TPU v7x, 256 devices: a whole 4x4x8 slice. The times are simulated.
256 devices in a mesh: dp: 16 (over x, z_hi), frame: 16 (over y, z_lo, core).
Axes of the slice: x: 4, y: 4, z: 8 (z_hi: 4, z_lo: 2; z = z_hi * 2 + z_lo), core: 2. Of those that a mesh axis runs over, the one named last changes fastest.
Arguments:
- video: bfloat16 [32, 16, 256, 1024], P('dp', 'frame'), may hold values from -96 to 96
- cotangent: bfloat16 [32, 16, 256, 1024], P('dp', 'frame'), may hold values from -6 to 6
- norm_gain: float32 [1024], replicated, may hold values from 0.1 to 1.9
- norm_bias: float32 [1024], replicated, may hold values from -3 to 3
- qkv_weight: bfloat16 [1024, 3072], replicated, may hold values from -1 to 1
- out_weight: bfloat16 [1024, 1024], replicated, may hold values from -0.1875 to 0.1875
Outputs:
- grad_video: bfloat16 [32, 16, 256, 1024], P('dp', 'frame')
- grad_qkv: float32 [1024, 3072], P('frame')
- grad_out: float32 [1024, 1024], P('frame')
- grad_gain: float32 [1024], P('frame')
- grad_bias: float32 [1024], P('frame')
All inputs are finite; a program needn't handle non-finite values.
Results may differ from a plain program's by a relative error of at most 0.004.
The roundings to bfloat16 on the way count: a program that leaves them out, or rounds other values in their place, can miss the bound.
Values may be sent and summed in bfloat16 or wider, within the bound.
No kernel may reach another device: no remote copies, remote signals or barrier semaphores. Data moves between devices by JAX's collectives and lax.ppermute only.
A program may use at most 128 MiB of HBM per device.

v0:
```python
import math

import jax
import jax.numpy as jnp
from jax import lax
from jax.sharding import PartitionSpec as P

HEADS = 16
HEAD_DIM = 64


def normalize(token_rows, norm_gain, norm_bias):
    values = token_rows.astype(jnp.float32)
    centered = values - jnp.mean(values, axis=-1, keepdims=True)
    inv_std = lax.rsqrt(jnp.mean(centered * centered, axis=-1, keepdims=True) + 1e-05)
    whitened = centered * inv_std
    normed = (whitened * norm_gain + norm_bias).astype(jnp.bfloat16)
    return (normed, whitened, inv_std)


def head_block(packed, offset):
    feat_width = packed.shape[-1] // 3
    column_block = packed[..., offset * feat_width : (offset + 1) * feat_width]
    return column_block.reshape(column_block.shape[:-1] + (HEADS, HEAD_DIM))


def attend(packed):
    query_part = head_block(packed, 0)
    key_part = head_block(packed, 1)
    value_part = head_block(packed, 2)
    scores = jnp.einsum(
        "cflhd,cglhd->clhfg", query_part, key_part, preferred_element_type=jnp.float32
    ) * HEAD_DIM ** (-0.5)
    attn_probs = jax.nn.softmax(scores, axis=-1)
    mixed = jnp.einsum(
        "clhfg,cglhd->cflhd",
        attn_probs.astype(jnp.bfloat16),
        value_part,
        preferred_element_type=jnp.float32,
    )
    attended = mixed.astype(jnp.bfloat16).reshape(packed.shape[:-1] + (packed.shape[-1] // 3,))
    return (attended, attn_probs)


def attend_back(packed, attn_probs, d_attended):
    query_part = head_block(packed, 0)
    key_part = head_block(packed, 1)
    value_part = head_block(packed, 2)
    grad_heads = d_attended.reshape(d_attended.shape[:-1] + (HEADS, HEAD_DIM))
    probs_low = attn_probs.astype(jnp.bfloat16)
    d_value = jnp.einsum(
        "clhfg,cflhd->cglhd", probs_low, grad_heads, preferred_element_type=jnp.float32
    ).astype(jnp.bfloat16)
    d_probs = jnp.einsum(
        "cflhd,cglhd->clhfg", grad_heads, value_part, preferred_element_type=jnp.float32
    )
    inner = jnp.sum(d_probs * attn_probs, axis=-1, keepdims=True)
    d_scores = (attn_probs * (d_probs - inner) * HEAD_DIM ** (-0.5)).astype(jnp.bfloat16)
    d_query = jnp.einsum(
        "clhfg,cglhd->cflhd", d_scores, key_part, preferred_element_type=jnp.float32
    ).astype(jnp.bfloat16)
    d_key = jnp.einsum(
        "clhfg,cflhd->cglhd", d_scores, query_part, preferred_element_type=jnp.float32
    ).astype(jnp.bfloat16)
    flat_shape = packed.shape[:-1] + (packed.shape[-1] // 3,)
    return jnp.concatenate(
        [d_query.reshape(flat_shape), d_key.reshape(flat_shape), d_value.reshape(flat_shape)],
        axis=-1,
    )


def contract_rows(left_rows, right_rows):
    return lax.dot_general(
        left_rows, right_rows, (((0,), (0,)), ((), ())), preferred_element_type=jnp.float32
    )


def contract_cols(left_rows, weight):
    return lax.dot_general(
        left_rows, weight, (((1,), (1,)), ((), ())), preferred_element_type=jnp.float32
    )


def norm_back(d_normed, whitened, inv_std, norm_gain):
    scaled = d_normed * norm_gain
    first = jnp.mean(scaled, axis=-1, keepdims=True)
    second = jnp.mean(scaled * whitened, axis=-1, keepdims=True)
    return inv_std * (scaled - first - whitened * second)


def local(video, cotangent, norm_gain, norm_bias, qkv_weight, out_weight):
    clip_count, frames_here, positions, feat_width = video.shape
    token_count = (
        clip_count * frames_here * positions * lax.axis_size("frame") * lax.axis_size("dp")
    )
    grad_scale = 1.0 / math.sqrt(token_count)
    token_rows = video.reshape(-1, feat_width)
    grad_rows = cotangent.reshape(-1, feat_width)
    normed, whitened, inv_std = normalize(token_rows, norm_gain, norm_bias)
    packed = jnp.dot(normed, qkv_weight, preferred_element_type=jnp.float32).astype(jnp.bfloat16)
    packed = packed.reshape(clip_count, frames_here, positions, 3 * feat_width)
    placed = lax.all_to_all(packed, "frame", split_axis=2, concat_axis=1, tiled=True)
    attended, attn_probs = attend(placed)
    attended_rows = lax.all_to_all(
        attended, "frame", split_axis=1, concat_axis=2, tiled=True
    ).reshape(-1, feat_width)
    grad_out = contract_rows(attended_rows, grad_rows)
    d_attended = contract_cols(grad_rows, out_weight).astype(jnp.bfloat16)
    d_placed = lax.all_to_all(
        d_attended.reshape(clip_count, frames_here, positions, feat_width),
        "frame",
        split_axis=2,
        concat_axis=1,
        tiled=True,
    )
    d_back = attend_back(placed, attn_probs, d_placed)
    d_packed = lax.all_to_all(d_back, "frame", split_axis=1, concat_axis=2, tiled=True).reshape(
        -1, 3 * feat_width
    )
    grad_qkv = contract_rows(normed, d_packed)
    d_normed = contract_cols(d_packed, qkv_weight)
    grad_gain = jnp.sum(d_normed * whitened, axis=0)
    grad_bias = jnp.sum(d_normed, axis=0)
    grad_video = (
        grad_rows.astype(jnp.float32) + norm_back(d_normed, whitened, inv_std, norm_gain)
    ).astype(jnp.bfloat16)
    grad_video = grad_video.reshape(video.shape)
    terms = (grad_qkv, grad_out, grad_gain, grad_bias)
    shares = (
        lax.psum_scatter(terms[0], "frame", scatter_dimension=0, tiled=True),
        lax.psum_scatter(terms[1], "frame", scatter_dimension=0, tiled=True),
        lax.psum_scatter(terms[2], "frame", scatter_dimension=0, tiled=True),
        lax.psum_scatter(terms[3], "frame", scatter_dimension=0, tiled=True),
    )
    totals = lax.psum((shares[0], shares[1], shares[2], shares[3]), "dp")
    total_qkv, total_out, total_gain, total_bias = totals
    return (
        grad_video,
        total_qkv * grad_scale,
        total_out * grad_scale,
        total_gain * grad_scale,
        total_bias * grad_scale,
    )


def solution(mesh):
    in_specs = (P("dp", "frame", None, None), P("dp", "frame", None, None), P(), P(), P(), P())
    out_specs = (
        P("dp", "frame", None, None),
        P("frame", None),
        P("frame", None),
        P("frame"),
        P("frame"),
    )
    return jax.shard_map(local, mesh=mesh, in_specs=in_specs, out_specs=out_specs, check_vma=False)
```

profile of v0, /device:TPU:32, one launch (start us, length us, event | category | flops | bytes accessed | tf_op | source)
XLA Modules:
  0.0 581.5 jit_solution(12530854526690863246)
XLA Ops:
  7.2 1.6 convert_reduce_fusion
  8.8 1.6 multiply_reduce_fusion.4
  11.0 6.4 %convolution_convert_fusion = bf16[512,3072]{1,0:T(8,128)(2,1)S(1)} fusion(bf16[512,1024]{1,0:T(8,128)(2,1)S(1)} %add_convert_fusion.2, bf16[1024,3072]{1,0:T(8,128)(2,1)} %param.10), kind=kOutput, calls=%fused_computation.2 | convolution fusion | flops 3222798336 | bytes 10485760 | tf_op jit(solution)/shard_map/dot_general | solution.py:100
  17.4 4.9 copy.52
  22.3 6.1 %all-to-all-start = ((bf16[2,1,256,3072]{3,0,1,2:T(2,128)(2,1)}), bf16[2,1,256,3072]{3,0,1,2:T(2,128)(2,1)}, u32[]{:S(2)}, u32[]{:S(2)}) async-start(bf16[2,1,256,3072]{3,0,1,2:T(2,128)(2,1)} %copy.52), calls=%async_computation | async-start | bytes 6291456 | tf_op jit(solution)/shard_map/all_to_all | solution.py:102
  28.4 2.5 convolution_convert_fusion.1
  30.9 2.0 copy.57
  33.0 33.4 %all-to-all-done = bf16[2,1,256,3072]{3,0,1,2:T(2,128)(2,1)} async-done(((bf16[2,1,256,3072]{3,0,1,2:T(2,128)(2,1)}), bf16[2,1,256,3072]{3,0,1,2:T(2,128)(2,1)}, u32[]{:S(2)}, u32[]{:S(2)}) %all-to-all-start) | async-done | bytes 3145760 | tf_op jit(solution)/shard_map/all_to_all | solution.py:102
  66.4 6.1 %all-to-all-start.1 = ((bf16[2,1,256,1024]{3,0,1,2:T(2,128)(2,1)}), bf16[2,1,256,1024]{3,0,1,2:T(2,128)(2,1)}, u32[]{:S(2)}, u32[]{:S(2)}) async-start(bf16[2,1,256,1024]{3,0,1,2:T(2,128)(2,1)} %copy.57), calls=%async_computation.1 | async-start | bytes 2097152 | tf_op jit(solution)/shard_map/all_to_all | solution.py:109
  72.5 5.6 fusion.39
  78.1 2.2 reshape.168
  80.3 3.7 reshape.167
  84.1 5.0 reshape.166
  89.1 4.1 fusion.24
  93.2 17.7 %fusion.40 = (f32[2,16,16,16]{3,2,1,0:T(8,128)S(1)}, f32[2,16,16,16,16]{3,4,2,1,0:T(8,128)S(1)}) fusion(f32[2,16,16,16,16]{3,4,2,1,0:T(8,128)S(1)} %fusion.24), kind=kOutput, calls=%fused_computation.57 | output fusion | flops 524303 | bytes 1081344 | tf_op jit(solution)/shard_map/sub | solution.py:34
  110.9 1.8 convert_bitcast_fusion
  113.4 2.3 reshape.162
  115.7 5.8 all-to-all-start.3
  121.7 3.7 reshape.165
  125.4 11.5 %all-to-all-done.3 = bf16[2,16,16,1024]{3,2,0,1:T(8,128)(2,1)} async-done(((bf16[2,16,16,1024]{3,2,0,1:T(8,128)(2,1)}), bf16[2,16,16,1024]{3,2,0,1:T(8,128)(2,1)}, u32[]{:S(2)}, u32[]{:S(2)}) %all-to-all-start.3) | async-done | bytes 1048608 | tf_op jit(solution)/shard_map/all_to_all | solution.py:104
  136.9 1.4 copy.75
  138.5 3.3 fusion.42
  141.8 3.8 convert_bitcast_fusion.1
  146.1 2.3 reshape.156
  148.4 6.9 %fusion.21 = f32[2,16,16,16,16]{3,4,2,1,0:T(8,128)} fusion(bf16[2,16,16,16,64]{4,3,0,2,1:T(8,128)(2,1)} %reshape.168, bf16[2,16,16,16,64]{4,3,0,2,1:T(8,128)(2,1)} %copy-done.6), kind=kOutput, calls=%fused_computation.28 | convolution fusion | flops 16777216 | bytes 2621440 | tf_op jit(solution)/shard_map/cflhd,cglhd->clhfg/dot_general | solution.py:54
  155.3 9.2 %convert_bitcast_fusion.3 = bf16[2,16,16,16,64]{4,1,3,2,0:T(8,128)(2,1)} fusion(f32[2,16,16,16,16]{3,4,2,1,0:T(8,128)} %fusion.21, bf16[2,16,16,16,64]{4,3,0,2,1:T(8,128)(2,1)S(1)} %copy-done.5, f32[2,16,16,16,16]{3,4,2,1,0:T(8,128)} %copy-done.7, f32[2,16,16,16]{3,2,1,0:T(8,128)S(1)} %get-tuple-element.42), kind=kOutput, calls=%fused_computation.19 | convolution fusion | flops 18227216 | bytes 3178496 | tf_op jit(solution)/shard_map/clhfg,cglhd->cflhd/dot_general | solution.py:59
  164.5 2.2 copy.64
  166.7 2.5 reshape.154
  169.2 10.4 %convert_bitcast_fusion.2 = bf16[2,16,16,16,64]{4,1,3,2,0:T(8,128)(2,1)} fusion(f32[2,16,16,16,16]{3,4,2,1,0:T(8,128)} %fusion.21, bf16[2,16,16,16,64]{4,3,0,2,1:T(8,128)(2,1)} %copy-done.3, f32[2,16,16,16,16]{3,4,2,1,0:T(8,128)} %copy-done.7, f32[2,16,16,16]{3,2,1,0:T(8,128)S(1)} %get-tuple-element.42), kind=kOutput, calls=%fused_computation.18 | convolution fusion | flops 18227216 | bytes 3178496 | tf_op jit(solution)/shard_map/clhfg,cflhd->cglhd/dot_general | solution.py:62
  179.6 2.2 copy.66
  181.7 2.3 reshape.155
  184.0 2.0 pad_maximum_fusion
  186.0 2.0 copy.69
  188.1 5.5 all-to-all-start.2
  194.1 48.0 %all-to-all-done.2 = bf16[2,16,16,3072]{3,2,0,1:T(8,128)(2,1)} async-done(((bf16[2,16,16,3072]{3,2,0,1:T(8,128)(2,1)}), bf16[2,16,16,3072]{3,2,0,1:T(8,128)(2,1)}, u32[]{:S(2)}, u32[]{:S(2)}) %all-to-all-start.2) | async-done | bytes 3145760 | tf_op jit(solution)/shard_map/all_to_all | solution.py:117
  242.0 2.2 copy.70
  244.3 1.7 copy-done.9
  245.9 6.4 %fusion.41 = f32[1024,3072]{1,0:T(8,128)} fusion(bf16[512,1024]{1,0:T(8,128)(2,1)S(1)} %bitcast.72, bf16[512,3072]{1,0:T(8,128)(2,1)S(1)} %bitcast.69), kind=kOutput, calls=%fused_computation.58 | convolution fusion | flops 3221225472 | bytes 16777216 | tf_op jit(solution)/shard_map/dot_general | solution.py:73
  252.4 0.6 copy-done.12
  253.0 0.6 dynamic-slice
  254.2 141.7 %reduce-scatter.3.cloned.1.call-done = f32[64,3072]{1,0:T(8,128)} async-done(((f32[1024,3072]{1,0:T(8,128)}), f32[64,3072]{1,0:T(8,128)}) %reduce-scatter.3.cloned.1.call-update) | async-done | bytes 786448 | tf_op jit(solution)/shard_map/reduce_scatter | solution.py:130
  395.9 8.9 %multiply_reduce_fusion.2 = (f32[1024]{0:T(1024)S(1)}, f32[512]{0:T(512)S(1)}, f32[512]{0:T(512)S(1)}, f32[1024]{0:T(1024)S(1)}, f32[512,1024]{1,0:T(8,128)}) fusion(bf16[2,1,256,1024]{3,2,1,0:T(8,128)(2,1)S(1)} %copy-done.2, f32[512]{0:T(512)S(1)} %bitcast.76, f32[512]{0:T(512)S(1)} %bitcast.79, f32[1024]{0:T(1024)S(1)} %copy-done.10, ...), kind=kOutput, calls=%fused_computation.12 | convolution fusion | flops 3226465280 | bytes 12603392 | tf_op jit(solution)/shard_map/dot_general | solution.py:79
  404.8 28.3 %all-reduce.2 = (f32[1024]{0:T(1024)S(1)}, f32[1024]{0:T(1024)S(1)}) all-reduce(f32[1024]{0:T(1024)S(1)} %get-tuple-element.25, f32[1024]{0:T(1024)S(1)} %get-tuple-element.28), channel_id=4, replica_groups=mesh['dp'=16,'frame'=16] {'frame'}, use_global_device_ids=true, to_apply=%region_12.0.clone | all-reduce | flops 2048 | bytes 16384
  433.3 45.3 %all-reduce.3 = (f32[64]{0:T(128)S(1)}, f32[64]{0:T(128)S(1)}) all-reduce(f32[64]{0:T(128)S(1)} %dynamic-slice.1, f32[64]{0:T(128)S(1)} %dynamic-slice.3), channel_id=1, replica_groups=mesh['dp'=16,'frame'=16] {'dp'}, use_global_device_ids=true, to_apply=%region_13.0 | all-reduce | flops 128 | bytes 1024 | tf_op jit(solution)/shard_map/psum | solution.py:135
  479.2 3.8 add_convert_fusion.1
  483.0 88.0 %all-reduce.7.cloned.1.call-done = (f32[64,3072]{1,0:T(8,128)}, f32[64,1024]{1,0:T(8,128)}) async-done(((f32[64,3072]{1,0:T(8,128)}, f32[64,1024]{1,0:T(8,128)}), (f32[64,3072]{1,0:T(8,128)}, f32[64,1024]{1,0:T(8,128)})) %all-reduce.7.cloned.1.call-update) | async-done | bytes 1048592 | tf_op jit(solution)/shard_map/psum | solution.py:135
  571.0 2.1 broadcast_multiply_fusion
  573.0 1.7 broadcast_multiply_fusion.1
  (44 shorter events, 3.3 us)
Async XLA Ops:
  7.2 21.2 %copy-start = (bf16[1024,1024]{1,0:T(8,128)(2,1)S(1)}, bf16[1024,1024]{1,0:T(8,128)(2,1)}, u32[]{:S(2)}) copy-start(bf16[1024,1024]{1,0:T(8,128)(2,1)} %param.11) | copy-start | bytes 6291460
  7.2 3.3 copy-start.2
  7.2 3.3 copy-start.10
  7.2 3.3 copy-start.11
  22.3 44.1 %all-to-all-start = ((bf16[2,1,256,3072]{3,0,1,2:T(2,128)(2,1)}), bf16[2,1,256,3072]{3,0,1,2:T(2,128)(2,1)}, u32[]{:S(2)}, u32[]{:S(2)}) async-start(bf16[2,1,256,3072]{3,0,1,2:T(2,128)(2,1)} %copy.52), calls=%async_computation | async-start | bytes 6291456 | tf_op jit(solution)/shard_map/all_to_all | solution.py:102
  66.4 49.3 %all-to-all-start.1 = ((bf16[2,1,256,1024]{3,0,1,2:T(2,128)(2,1)}), bf16[2,1,256,1024]{3,0,1,2:T(2,128)(2,1)}, u32[]{:S(2)}, u32[]{:S(2)}) async-start(bf16[2,1,256,1024]{3,0,1,2:T(2,128)(2,1)} %copy.57), calls=%async_computation.1 | async-start | bytes 2097152 | tf_op jit(solution)/shard_map/all_to_all | solution.py:109
  84.1 9.1 %copy-start.3 = (bf16[2,16,16,16,64]{4,3,0,2,1:T(8,128)(2,1)}, bf16[2,16,16,16,64]{4,3,0,2,1:T(8,128)(2,1)S(1)}, u32[]{:S(2)}) copy-start(bf16[2,16,16,16,64]{4,3,0,2,1:T(8,128)(2,1)S(1)} %reshape.167) | copy-start | bytes 3145732
  93.2 17.7 %copy-start.4 = (bf16[2,16,16,16,64]{4,3,0,2,1:T(8,128)(2,1)S(1)}, bf16[2,16,16,16,64]{4,3,0,2,1:T(8,128)(2,1)}, u32[]{:S(2)}) copy-start(bf16[2,16,16,16,64]{4,3,0,2,1:T(8,128)(2,1)} %reshape.168) | copy-start | bytes 3145732
  110.9 1.9 copy-start.7
  115.7 21.2 %all-to-all-start.3 = ((bf16[2,16,16,1024]{3,2,0,1:T(8,128)(2,1)}), bf16[2,16,16,1024]{3,2,0,1:T(8,128)(2,1)}, u32[]{:S(2)}, u32[]{:S(2)}) async-start(bf16[2,16,16,1024]{3,2,0,1:T(8,128)(2,1)} %reshape.162), calls=%async_computation.4 | async-start | bytes 2097152 | tf_op jit(solution)/shard_map/all_to_all | solution.py:104
  121.5 132.8 %reduce-scatter.5.cloned.1.call-start = ((), (), s32[]{:S(2)}) async-start(), calls=%async_computation.7 | async-start | bytes 4456448 | tf_op jit(solution)/shard_map/reduce_scatter | solution.py:131
  125.4 16.3 %copy-start.6 = (bf16[2,16,16,16,64]{4,3,0,2,1:T(8,128)(2,1)}, bf16[2,16,16,16,64]{4,3,0,2,1:T(8,128)(2,1)S(1)}, u32[]{:S(2)}) copy-start(bf16[2,16,16,16,64]{4,3,0,2,1:T(8,128)(2,1)S(1)} %reshape.165) | copy-start | bytes 3145732
  136.9 1.5 copy-start.8
  148.4 6.9 %copy-start.5 = (bf16[2,16,16,16,64]{4,3,0,2,1:T(8,128)(2,1)S(1)}, bf16[2,16,16,16,64]{4,3,0,2,1:T(8,128)(2,1)}, u32[]{:S(2)}) copy-start(bf16[2,16,16,16,64]{4,3,0,2,1:T(8,128)(2,1)} %reshape.166) | copy-start | bytes 3145732
  188.1 53.9 %all-to-all-start.2 = ((bf16[2,16,16,3072]{3,2,0,1:T(8,128)(2,1)}), bf16[2,16,16,3072]{3,2,0,1:T(8,128)(2,1)}, u32[]{:S(2)}, u32[]{:S(2)}) async-start(bf16[2,16,16,3072]{3,2,0,1:T(8,128)(2,1)} %copy.69), calls=%async_computation.2 | async-start | bytes 6291456 | tf_op jit(solution)/shard_map/all_to_all | solution.py:117
  193.6 202.3 %reduce-scatter.3.cloned.1.call-start = ((), (), s32[]{:S(2)}) async-start(), calls=%async_computation.6 | async-start | bytes 13369344 | tf_op jit(solution)/shard_map/reduce_scatter | solution.py:130
  244.2 1.7 copy-start.9
  252.3 0.7 copy-start.12
  252.3 318.6 %all-reduce.7.cloned.1.call-start = ((), (), s32[]{:S(2)}) async-start(), calls=%async_computation.8 | async-start | bytes 2097152 | tf_op jit(solution)/shard_map/psum | solution.py:135
  479.2 95.6 %copy-start.1 = (bf16[1024,1024]{1,0:T(8,128)(2,1)S(1)}, bf16[1024,1024]{1,0:T(8,128)(2,1)}, u32[]{:S(2)}) copy-start(bf16[1024,1024]{1,0:T(8,128)(2,1)} %param.11) | copy-start | bytes 6291460
Sparse Core Ops, SparseCore 0:
  141.9 75.5 reduce-scatter.4
  252.4 143.4 reduce-scatter.2
  398.6 172.3 all-reduce.6
where the time goes:
time: 590 us; the launch traced here: 581 us
  waiting for transfers between devices  323 us (55%)
  blocking collectives  73.6 us (12%)
  matrix products  63.7 us (11%)
  local copies, waits for them, and re-layouts  50.9 us (9%)
  other arithmetic  32 us (5%)
  starting transfers between devices  23.7 us (4%)
  between operations  14.9 us (3%)
    reduce_scatter x1, waiting for transfers between devices, local(): lax.psum_scatter(terms[0], 'frame', scatter_dimension=0, tiled=True)  142 us
    psum x1, waiting for transfers between devices, local(): totals = lax.psum((shares[0], shares[1], shares[2], shares[3]), 'dp')  88 us
    all_to_all x1, waiting for transfers between devices, local(): lax.all_to_all(d_back, 'frame', split_axis=1, concat_axis=2, tiled=True)  48 us
    psum x1, blocking collectives, local(): totals = lax.psum((shares[0], shares[1], shares[2], shares[3]), 'dp')  45.3 us
    all_to_all x1, waiting for transfers between devices, local(): lax.all_to_all(packed, 'frame', split_axis=2, concat_axis=1, tiled=True)  33.4 us
    unnamed x1, blocking collectives  28.3 us
    sub x1, other arithmetic, attend(): attn_probs = jax.nn.softmax(scores, axis=-1)  17.7 us
  transfers between devices with their start and end apart: 7, of which 5 were waited for; matrix products, arithmetic and copies ran while one was open for 21% of the time, Pallas kernels for 0%

commit v1 on v0

v1 whole, which is shorter than its diff:
```python
import math

import jax
import jax.numpy as jnp
from jax import lax
from jax.experimental import pallas as pl
from jax.experimental.pallas import tpu as pltpu
from jax.sharding import PartitionSpec as P

F32 = jnp.float32
BF16 = jnp.bfloat16
MIB = 1024 * 1024


def dot_nn(a, b):
    return lax.dot_general(a, b, (((1,), (0,)), ((), ())), preferred_element_type=F32)


def dot_nt(a, b):
    return lax.dot_general(a, b, (((1,), (1,)), ((), ())), preferred_element_type=F32)


def dot_tn(a, b):
    return lax.dot_general(a, b, (((0,), (0,)), ((), ())), preferred_element_type=F32)


def main_kernel(
    tokens_ref, gain_ref, bias_ref, wqkv_ref, wout_ref,
    left_ref, right_ref, gv_ref, dgb_ref,
    normed_s, packed_s, datt_s, wh_s, inv_s, dn_s,
):
    clips, frames, positions, width = gv_ref.shape
    halves = positions // 8
    part = frames * 8
    rows = clips * frames * positions
    gain = gain_ref[...]
    bias = bias_ref[...]

    def norm_step(i, carry):
        c = i // (frames // 2)
        q = i % (frames // 2)
        x = tokens_ref[c, pl.ds(2 * q, 2)].astype(F32).reshape(2, halves, 8, width)
        g = tokens_ref[clips + c, pl.ds(2 * q, 2)].astype(F32).reshape(2, halves, 8, width)
        for h in range(halves):
            at = pl.multiple_of((c * halves + h) * part + q * 16, 16)
            xh = x[:, h].reshape(16, width)
            centred = xh - jnp.mean(xh, axis=-1, keepdims=True)
            inv = lax.rsqrt(jnp.mean(centred * centred, axis=-1, keepdims=True) + 1e-05)
            wh = centred * inv
            wh_s[pl.ds(at, 16), :] = wh
            inv_s[pl.ds(at, 16), :] = jnp.broadcast_to(inv, (16, 128))
            normed_s[pl.ds(at, 16), :] = (wh * gain + bias).astype(BF16)
            right_ref[pl.ds(at, 16), pl.ds(3 * width, width)] = g[:, h].reshape(16, width).astype(BF16)
        return carry

    lax.fori_loop(0, clips * frames // 2, norm_step, 0)

    def qkv_step(n, carry):
        cols = pl.ds(pl.multiple_of(n * 256, 256), 256)
        packed_s[:, cols] = dot_nn(normed_s[...], wqkv_ref[:, cols]).astype(BF16)
        return carry

    lax.fori_loop(0, 3 * width // 256, qkv_step, 0)

    def datt_step(n, carry):
        cols = pl.ds(pl.multiple_of(n * 256, 256), 256)
        datt_s[:, cols] = dot_nt(right_ref[:, pl.ds(3 * width, width)], wout_ref[cols, :]).astype(BF16)
        left_ref[0, cols, :] = normed_s[:, cols].T
        return carry

    lax.fori_loop(0, width // 256, datt_step, 0)

    lane = lax.broadcasted_iota(jnp.int32, (part, 128), 1)
    first = lane < 64
    same = lax.broadcasted_iota(jnp.int32, (1, 8, part), 1) == (
        lax.broadcasted_iota(jnp.int32, (1, 8, part), 2) % 8
    )
    zero = jnp.zeros((part, 128), BF16)

    def split(a):
        return jnp.concatenate([jnp.where(first, a, zero), jnp.where(first, zero, a)], axis=0)

    def attend_step(i, carry):
        t = i // (width // 128)
        hp = i % (width // 128)
        tok = pl.ds(pl.multiple_of(t * part, part), part)
        col = pl.multiple_of(hp * 128, 128)
        q = packed_s[tok, pl.ds(col, 128)]
        k = packed_s[tok, pl.ds(width + col, 128)]
        v = packed_s[tok, pl.ds(2 * width + col, 128)]
        da = datt_s[tok, pl.ds(col, 128)]
        k2 = split(k)
        v2 = split(v)
        scores = (dot_nt(k2, q) * 0.125).reshape(2, frames, 8, part)
        e = jnp.exp(scores - jnp.max(scores, axis=1, keepdims=True))
        probs = e * (1.0 / jnp.sum(e, axis=1, keepdims=True))
        probs = jnp.where(same[None], probs, 0.0)
        low = probs.astype(BF16).reshape(2, part, part)
        dp = dot_nt(v2, da).reshape(2, frames, 8, part)
        inner = jnp.sum(dp * probs, axis=1, keepdims=True)
        ds = (probs * (dp - inner) * 0.125).astype(BF16).reshape(2, part, part)
        left_ref[1, pl.ds(col, 128), tok] = dot_tn(v2, low.reshape(2 * part, part)).astype(BF16)
        right_ref[tok, pl.ds(col, 128)] = dot_tn(ds.reshape(2 * part, part), k2).astype(BF16)
        right_ref[tok, pl.ds(width + col, 128)] = dot_nn(
            jnp.concatenate([ds[0], ds[1]], axis=1), split(q)
        ).astype(BF16)
        right_ref[tok, pl.ds(2 * width + col, 128)] = dot_nn(
            jnp.concatenate([low[0], low[1]], axis=1), split(da)
        ).astype(BF16)
        return carry

    lax.fori_loop(0, clips * halves * (width // 128), attend_step, 0)

    def dn_step(n, carry):
        cols = pl.ds(pl.multiple_of(n * 256, 256), 256)
        dn_s[:, cols] = dot_nt(right_ref[:, pl.ds(0, 3 * width)], wqkv_ref[cols, :])
        return carry

    lax.fori_loop(0, width // 256, dn_step, 0)

    def back_step(i, carry):
        dgain, dbias = carry
        c = i // (frames // 2)
        q = i % (frames // 2)
        outs = []
        for h in range(halves):
            at = pl.multiple_of((c * halves + h) * part + q * 16, 16)
            dn = dn_s[pl.ds(at, 16), :]
            wh = wh_s[pl.ds(at, 16), :]
            inv = inv_s[pl.ds(at, 16), :][:, :1]
            dw = dn * wh
            dgain = dgain + dw[:8] + dw[8:]
            dbias = dbias + dn[:8] + dn[8:]
            scaled = dn * gain
            m1 = jnp.mean(scaled, axis=-1, keepdims=True)
            m2 = jnp.mean(scaled * wh, axis=-1, keepdims=True)
            gr = right_ref[pl.ds(at, 16), pl.ds(3 * width, width)].astype(F32)
            outs.append((gr + inv * (scaled - m1 - wh * m2)).reshape(2, 8, width))
        gv_ref[c, pl.ds(2 * q, 2)] = jnp.concatenate(outs, axis=1).astype(BF16)
        return dgain, dbias

    zeros = jnp.zeros((8, width), F32)
    dgain, dbias = lax.fori_loop(0, clips * frames // 2, back_step, (zeros, zeros))
    dgb_ref[0:1, :] = jnp.sum(dgain, axis=0, keepdims=True)
    dgb_ref[1:2, :] = jnp.sum(dbias, axis=0, keepdims=True)


def run_main(tokens, gain, bias, wqkv, wout):
    clips, frames, positions, width = tokens.shape
    clips = clips // 2
    rows = clips * frames * positions
    vm = pl.BlockSpec(memory_space=pltpu.VMEM)
    return pl.pallas_call(
        main_kernel,
        out_shape=(
            jax.ShapeDtypeStruct((2, width, rows), BF16),
            jax.ShapeDtypeStruct((rows, 4 * width), BF16),
            jax.ShapeDtypeStruct((clips, frames, positions, width), BF16),
            jax.ShapeDtypeStruct((2, width), F32),
        ),
        in_specs=[vm] * 5,
        out_specs=(vm,) * 4,
        scratch_shapes=[
            pltpu.VMEM((rows, width), BF16),
            pltpu.VMEM((rows, 3 * width), BF16),
            pltpu.VMEM((rows, width), BF16),
            pltpu.VMEM((rows, width), F32),
            pltpu.VMEM((rows, 128), F32),
            pltpu.VMEM((rows, width), F32),
        ],
        compiler_params=pltpu.CompilerParams(vmem_limit_bytes=40 * MIB),
        name="sublayer",
    )(tokens, gain.reshape(1, -1), bias.reshape(1, -1), wqkv, wout)


def grads_kernel(core_ref, left_ref, right_ref, send_ref, keep_ref):
    width, rows = left_ref.shape[1:]
    blocks, shard, cols = send_ref.shape
    core = core_ref[0]
    for b in range(4):
        per = width // 4
        g = dot_nn(left_ref[0, b * per:(b + 1) * per, :], right_ref[...])
        g = g.reshape(blocks // 4, 2, shard, cols)
        at = pl.ds(b * (blocks // 4), blocks // 4)
        mine = jnp.where(core == 0, g[:, 0], g[:, 1])
        other = jnp.where(core == 0, g[:, 1], g[:, 0])
        keep_ref[at] = mine
        send_ref[at] = other.astype(BF16)


def run_grads(core, left, right):
    _, width, rows = left.shape
    total = right.shape[1]
    n = 512
    blocks = width // 128
    return pl.pallas_call(
        grads_kernel,
        grid=(total // n,),
        out_shape=(
            jax.ShapeDtypeStruct((blocks, 64, total), BF16),
            jax.ShapeDtypeStruct((blocks, 64, total), F32),
        ),
        in_specs=[
            pl.BlockSpec(memory_space=pltpu.SMEM),
            pl.BlockSpec((1, width, rows), lambda i: (i // (3 * width // n), 0, 0)),
            pl.BlockSpec((rows, n), lambda i: (0, i)),
        ],
        out_specs=(
            pl.BlockSpec((blocks, 64, n), lambda i: (0, 0, i)),
            pl.BlockSpec((blocks, 64, n), lambda i: (0, 0, i)),
        ),
        compiler_params=pltpu.CompilerParams(vmem_limit_bytes=40 * MIB),
        name="weight_grads",
    )(core, left, right)


def frame_pairs(move):
    pairs = []
    for i in range(16):
        y, z, core = move(i // 4, i // 2 % 2, i % 2)
        pairs.append((i, y % 4 * 4 + z % 2 * 2 + core % 2))
    return pairs


def dp_pairs(move):
    pairs = []
    for i in range(16):
        x, h = move(i // 4, i % 4)
        pairs.append((i, x % 4 * 4 + h % 4))
    return pairs


def pick(array, index, axis):
    return lax.dynamic_index_in_dim(array, index, axis, keepdims=False)


def reduce_pieces(array, me, count, axis, name, pairs_of, dtype):
    total = pick(array, me, axis)
    got = []
    for k in range(1, count):
        piece = pick(array, (me + k) % count, axis).astype(dtype)
        got.append(lax.ppermute(piece, name, pairs_of(k)))
    for piece in got:
        total = total + piece.astype(F32)
    return total


def gather_pieces(piece, me, count, name, pairs_of):
    got = [piece]
    for k in range(1, count):
        got.append(lax.ppermute(piece, name, pairs_of(k)))
    stacked = jnp.stack(got)
    order = (me - jnp.arange(count)) % count
    return jnp.take(stacked, order, axis=0)


def step_y(k):
    return frame_pairs(lambda y, z, c: (y + k, z, c))


def step_z(k):
    return frame_pairs(lambda y, z, c: (y, z + k, c))


def step_x(k):
    return dp_pairs(lambda x, h: (x + k, h))


def step_h(k):
    return dp_pairs(lambda x, h: (x, h + k))


def reduce_grads(send, keep):
    frame = lax.axis_index("frame")
    dp = lax.axis_index("dp")
    y, z = frame // 4, frame // 2 % 2
    x, h = dp // 4, dp % 4
    cols = keep.shape[-1]
    half, part = cols // 2, cols // 8
    other = lax.ppermute(send, "frame", frame_pairs(lambda y, z, c: (y, z, 1 - c)))
    own = keep + other.astype(F32)
    own = own.reshape(4, 2, 64, cols)
    a = reduce_pieces(own[..., :half], y, 4, 0, "frame", step_y, BF16)
    b = reduce_pieces(own[..., half:].reshape(4, 2, 64, 4, part), x, 4, 3, "dp", step_x, BF16)
    a = reduce_pieces(a.reshape(2, 64, 4, part), x, 4, 2, "dp", step_x, F32)
    b = reduce_pieces(b, y, 4, 0, "frame", step_y, F32)
    both = jnp.concatenate([a, b], axis=-1)
    both = reduce_pieces(both, z, 2, 0, "frame", step_z, F32)
    both = reduce_pieces(both.reshape(4, 16, 2 * part), h, 4, 0, "dp", step_h, F32)
    both = gather_pieces(both, h, 4, "dp", step_h).reshape(64, 2 * part)
    both = gather_pieces(both, x, 4, "dp", step_x)
    both = both.reshape(4, 64, 2, part).transpose(1, 2, 0, 3)
    return both.reshape(64, cols)


def reduce_small(dgb):
    share = dgb.reshape(2, 16, 64).transpose(1, 0, 2).reshape(16, 1, 128)
    share = lax.all_to_all(share, "frame", 0, 0, tiled=True)
    share = jnp.sum(share, axis=0, keepdims=True)
    share = lax.all_to_all(jnp.broadcast_to(share, (16, 1, 128)), "dp", 0, 0, tiled=True)
    return jnp.sum(share, axis=0).reshape(2, 64)


def local(video, cotangent, norm_gain, norm_bias, qkv_weight, out_weight):
    clips, frames_here, positions, width = video.shape
    token_count = clips * positions * 256
    grad_scale = 1.0 / math.sqrt(token_count)
    tokens = jnp.concatenate([video, cotangent], axis=0)
    tokens = lax.all_to_all(tokens, "frame", split_axis=2, concat_axis=1, tiled=True)
    left, right, grad_video, dgb = run_main(tokens, norm_gain, norm_bias, qkv_weight, out_weight)
    grad_video = lax.all_to_all(grad_video, "frame", split_axis=1, concat_axis=2, tiled=True)
    core = (lax.axis_index("frame") % 2).reshape(1)
    send, keep = run_grads(core, left, right)
    total = reduce_grads(send, keep) * grad_scale
    small = reduce_small(dgb) * grad_scale
    return grad_video, total[:, : 3 * width], total[:, 3 * width :], small[0], small[1]


def solution(mesh):
    in_specs = (P("dp", "frame", None, None), P("dp", "frame", None, None), P(), P(), P(), P())
    out_specs = (
        P("dp", "frame", None, None),
        P("frame", None),
        P("frame", None),
        P("frame"),
        P("frame"),
    )
    return jax.shard_map(local, mesh=mesh, in_specs=in_specs, out_specs=out_specs, check_vma=False)
```

time: 590 us -> 257 us (0.44)
  the two profiles are of different devices: /device:TPU:32 before, /device:TPU:72 now
where the time goes in v1:
time: 257 us; the launch traced here: 256 us
  waiting for transfers between devices  88.2 us (34%)
  starting transfers between devices  61.2 us (24%)
  local copies, waits for them, and re-layouts  45.8 us (18%)
  Pallas kernels  44.6 us (17%)
  other arithmetic  15.6 us (6%)
    pallas_call x1, Pallas kernels, run_main(): pl.pallas_call(main_kernel, out_shape=(jax.ShapeDtypeStruct((2, width, ro...  35.9 us
    ppermute x16, waiting for transfers between devices, reduce_pieces(): got.append(lax.ppermute(piece, name, pairs_of(k)))  31.2 us
    all_to_all x1, waiting for transfers between devices, local(): lax.all_to_all(tokens, 'frame', split_axis=2, concat_axis=1, tiled=True)  26.4 us
    ppermute x16, starting transfers between devices, reduce_pieces(): got.append(lax.ppermute(piece, name, pairs_of(k)))  25.8 us
    ppermute x6, waiting for transfers between devices, gather_pieces(): got.append(lax.ppermute(piece, name, pairs_of(k)))  16.5 us
    ppermute x6, starting transfers between devices, gather_pieces(): got.append(lax.ppermute(piece, name, pairs_of(k)))  9.77 us
    all_to_all x1, starting transfers between devices, reduce_small(): lax.all_to_all(jnp.broadcast_to(share, (16, 1, 128)), 'dp', 0, 0, tiled=T...  9.7 us
    convert_element_type x2, local copies, waits for them, and re-layouts, reduce_pieces(): piece = pick(array, (me + k) % count, axis).astype(dtype)  9.33 us
  transfers between devices with their start and end apart: 27, of which 14 were waited for; matrix products, arithmetic and copies ran while one was open for 15% of the time, Pallas kernels for 0%

profile of v1, /device:TPU:72, one launch (start us, length us, event | category | flops | bytes accessed | tf_op | source)
XLA Modules:
  0.0 256.4 jit_solution(1674076633164001159)
XLA Ops:
  0.6 1.7 pad_maximum_fusion
  2.4 3.0 %copy.58 = bf16[4,1,256,1024]{3,0,1,2:T(4,128)(2,1)} copy(bf16[4,1,256,1024]{3,2,1,0:T(8,128)(2,1)S(1)} %pad_maximum_fusion) | data formatting | bytes 4194304 | tf_op jit(solution)/shard_map/concatenate | solution.py:308
  5.3 6.4 %all-to-all-start = ((bf16[4,1,256,1024]{3,0,1,2:T(4,128)(2,1)}), bf16[4,1,256,1024]{3,0,1,2:T(4,128)(2,1)}, u32[]{:S(2)}, u32[]{:S(2)}) async-start(bf16[4,1,256,1024]{3,0,1,2:T(4,128)(2,1)} %copy.58), calls=%async_computation | async-start | bytes 4194304 | tf_op jit(solution)/shard_map/all_to_all | solution.py:309
  11.7 26.4 %all-to-all-done = bf16[4,1,256,1024]{3,0,1,2:T(4,128)(2,1)} async-done(((bf16[4,1,256,1024]{3,0,1,2:T(4,128)(2,1)}), bf16[4,1,256,1024]{3,0,1,2:T(4,128)(2,1)}, u32[]{:S(2)}, u32[]{:S(2)}) %all-to-all-start) | async-done | bytes 2097184 | tf_op jit(solution)/shard_map/all_to_all | solution.py:309
  38.1 2.2 copy.59
  40.4 35.9 %sublayer.1 = (bf16[2,1024,512]{2,1,0:T(8,128)(2,1)S(1)}, bf16[512,4096]{1,0:T(8,128)(2,1)S(1)}, bf16[2,16,16,1024]{3,2,1,0:T(8,128)(2,1)S(1)}, f32[2,1024]{1,0:T(2,128)S(1)}) custom-call(bf16[4,16,16,1024]{3,2,1,0:T(8,128)(2,1)S(1)} %bitcast.106, f32[1,1024]{1,0:T(1,128)S(1)} %bitcast.107, f32[1,1024]{1,0:T(1,128)S(1)} %bitcast.108, ...), custom_call_target="tpu_custom_call" | custom-call | tf_op jit(solution)/shard_map/sublayer/pallas_call | solution.py:153
  76.3 8.7 %weight_grads.1 = (bf16[8,64,4096]{2,1,0:T(8,128)(2,1)}, f32[8,64,4096]{2,1,0:T(8,128)}) custom-call(s32[1]{0:T(128)} %bitcast.5.core_ref, bf16[2,1024,512]{2,1,0:T(8,128)(2,1)S(1)} %get-tuple-element.12.left_ref, bf16[512,4096]{1,0:T(8,128)(2,1)S(1)} %get-tuple-element.13.right_ref), custom_call_target="tpu_custom_call" | custom-call | tf_op jit(solution)/shard_map/weight_grads/pallas_call | solution.py:196
  85.1 7.5 %collective-permute-done = bf16[8,64,4096]{2,1,0:T(8,128)(2,1)} collective-permute-done((bf16[8,64,4096]{2,1,0:T(8,128)(2,1)}, bf16[8,64,4096]{2,1,0:T(8,128)(2,1)}, u32[]{:S(2)}, u32[]{:S(2)}) %collective-permute-start) | collective-permute-done | bytes 4194336 | tf_op jit(solution)/shard_map/ppermute | solution.py:280
  92.6 5.7 %convert_add_fusion = f32[8,64,4096]{2,1,0:T(8,128)S(1)} fusion(f32[8,64,4096]{2,1,0:T(8,128)} %get-tuple-element.14, bf16[8,64,4096]{2,1,0:T(8,128)(2,1)} %collective-permute-done), kind=kLoop, calls=%fused_computation.2 | loop fusion | flops 4194304 | bytes 20971520 | tf_op jit(solution)/shard_map/add | solution.py:281
  98.2 2.8 %fusion.24 = (f32[4,2,64,2048]{3,2,1,0:T(8,128)}, f32[4,2,64,2048]{3,2,1,0:T(8,128)S(1)}) fusion(f32[4,2,64,4096]{3,2,1,0:T(8,128)S(1)} %bitcast.109), kind=kLoop, calls=%fused_computation.87 | loop fusion | bytes 16777216 | tf_op jit(solution)/shard_map/slice | solution.py:284
  101.0 2.0 copy-done.3
  103.0 1.2 fusion.4
  104.7 3.2 %collective-permute-start.2 = (bf16[2,64,2048]{2,1,0:T(8,128)(2,1)}, bf16[2,64,2048]{2,1,0:T(8,128)(2,1)}, u32[]{:S(2)}, u32[]{:S(2)}) collective-permute-start(bf16[2,64,2048]{2,1,0:T(8,128)(2,1)} %get-tuple-element.69), channel_id=1, source_target_pairs={{0,8},{1,9},{2,10},{3,11},{4,12},{5,13},{6,14},{7,15},{8,0},{9,1},... | collective-permute-start | bytes 1572872 | tf_op jit(solution)/shard_map/ppermute | solution.py:242
  109.6 4.6 %all-to-all-start.2 = ((f32[16,1,128]{2,1,0:T(1,128)}), f32[16,1,128]{2,1,0:T(1,128)S(1)}, u32[]{:S(2)}, u32[]{:S(2)}) async-start(f32[16,1,128]{2,1,0:T(1,128)} %bitcast.35), calls=%async_computation.2 | async-start | bytes 16384 | tf_op jit(solution)/shard_map/all_to_all | solution.py:298
  114.2 6.0 %reshape.216 = f32[4,2,64,4,512]{4,3,2,1,0:T(4,128)} reshape(f32[4,2,64,2048]{3,2,1,0:T(8,128)} %get-tuple-element.62) | data formatting | bytes 8388608 | tf_op jit(solution)/shard_map/reshape | solution.py:284
  120.2 8.2 %dynamic-slice_convert_fusion.2 = (bf16[4,2,64,1,512]{4,3,2,1,0:T(2,128)(2,1)S(1)}, bf16[4,2,64,1,512]{4,3,2,1,0:T(2,128)(2,1)S(1)}, bf16[4,2,64,1,512]{4,3,2,1,0:T(2,128)(2,1)S(1)}) fusion(f32[4,2,64,4,512]{4,3,2,1,0:T(4,128)} %reshape.216, s32[]{:T(128)S(6)} %select_n.232, s32[]{:T(128)S(6)} %select_n.236, s32[]{:T(128)S(6)} %select_n.234), kind=kLoop, calls=%fused_computation.14 | loop fusion | bytes 3145740 | tf_op jit(solution)/shard_map/convert_element_type | solution.py:241
  128.4 0.9 copy.86
  129.3 1.5 collective-permute-start.7
  130.8 0.9 copy.85
  131.8 2.7 %collective-permute-start.8 = (bf16[4,2,64,512]{3,2,1,0:T(8,128)(2,1)}, bf16[4,2,64,512]{3,2,1,0:T(8,128)(2,1)}, u32[]{:S(2)}, u32[]{:S(2)}) collective-permute-start(bf16[4,2,64,512]{3,2,1,0:T(8,128)(2,1)} %bitcast.99), channel_id=1, source_target_pairs={{0,128},{16,144},{32,160},{48,176},{64,192},{80,208},{96,224},{112... | collective-permute-start | bytes 1572872 | tf_op jit(solution)/shard_map/ppermute | solution.py:242
  135.4 3.3 %constant_dynamic-slice_fusion = f32[4,2,64,1,512]{4,3,2,1,0:T(1,128)S(1)} fusion(f32[4,2,64,4,512]{4,3,2,1,0:T(4,128)} %reshape.216, s32[]{:T(128)S(6)} %select_n.230), kind=kLoop, calls=%fused_computation.55 | loop fusion | bytes 2097156 | tf_op jit(solution)/shard_map/jit(dynamic_index_in_dim)/dynamic_slice | solution.py:234
  138.7 1.5 collective-permute-start.9
  140.2 2.9 %fusion.3 = f32[2,64,2048]{2,1,0:T(8,128)} fusion(bf16[2,64,2048]{2,1,0:T(8,128)(2,1)} %collective-permute-done.3, bf16[2,64,2048]{2,1,0:T(8,128)(2,1)} %collective-permute-done.2, bf16[2,64,2048]{2,1,0:T(8,128)(2,1)} %collective-permute-done.1, f32[4,2,64,2048]{3,2,1,0:T(8,128)} %copy-done.3, s32[]{:T(128)S(6)} %select_n.223), kind=kLoop, calls=%fused_computation.10 | loop fusion | flops 1572864 | bytes 3670020 | tf_op jit(solution)/shard_map/add | solution.py:244
  143.2 1.9 reshape.215
  149.1 1.8 collective-permute-start.6
  150.8 7.1 %collective-permute-done.8 = bf16[4,2,64,512]{3,2,1,0:T(8,128)(2,1)} collective-permute-done((bf16[4,2,64,512]{3,2,1,0:T(8,128)(2,1)}, bf16[4,2,64,512]{3,2,1,0:T(8,128)(2,1)}, u32[]{:S(2)}, u32[]{:S(2)}) %collective-permute-start.8) | collective-permute-done | bytes 524320 | tf_op jit(solution)/shard_map/ppermute | solution.py:242
  158.8 1.7 fusion.1
  161.3 1.5 collective-permute-start.10
  163.4 2.5 collective-permute-start.12
  166.0 1.0 copy.60
  167.7 9.7 %all-to-all-start.3 = ((f32[16,1,128]{2,1,0:T(1,128)}), f32[16,1,128]{2,1,0:T(1,128)S(1)}, u32[]{:S(2)}, u32[]{:S(2)}) async-start(f32[16,1,128]{2,1,0:T(1,128)} %broadcast_in_dim.42), calls=%async_computation.3 | async-start | bytes 16384 | tf_op jit(solution)/shard_map/all_to_all | solution.py:300
  177.4 1.2 fusion.13
  178.6 6.5 %all-to-all-done.3 = f32[16,1,128]{2,1,0:T(1,128)S(1)} async-done(((f32[16,1,128]{2,1,0:T(1,128)}), f32[16,1,128]{2,1,0:T(1,128)S(1)}, u32[]{:S(2)}, u32[]{:S(2)}) %all-to-all-start.3) | async-done | bytes 8224 | tf_op jit(solution)/shard_map/all_to_all | solution.py:300
  185.1 4.9 %all-to-all-start.1 = ((bf16[2,16,16,1024]{3,2,0,1:T(8,128)(2,1)}), bf16[2,16,16,1024]{3,2,0,1:T(8,128)(2,1)S(1)}, u32[]{:S(2)}, u32[]{:S(2)}) async-start(bf16[2,16,16,1024]{3,2,0,1:T(8,128)(2,1)} %copy.60), calls=%async_computation.1 | async-start | bytes 2097152 | tf_op jit(solution)/shard_map/all_to_all | solution.py:311
  190.1 1.1 fusion.15
  191.2 1.6 collective-permute-start.13
  193.0 16.6 %collective-permute-done.13 = f32[64,1024]{1,0:T(8,128)S(1)} collective-permute-done((f32[64,1024]{1,0:T(8,128)S(1)}, f32[64,1024]{1,0:T(8,128)S(1)}, u32[]{:S(2)}, u32[]{:S(2)}) %collective-permute-start.13) | collective-permute-done | bytes 262176 | tf_op jit(solution)/shard_map/ppermute | solution.py:242
  210.4 5.2 %collective-permute-start.15 = (f32[16,1024]{1,0:T(8,128)S(1)}, f32[16,1024]{1,0:T(8,128)S(1)}, u32[]{:S(2)}, u32[]{:S(2)}) collective-permute-start(f32[16,1024]{1,0:T(8,128)S(1)} %get-tuple-element.79), channel_id=1, source_target_pairs={{0,32},{16,48},{32,0},{48,16},{64,96},{80,112},{96,64},{112,80},{1... | collective-permute-start | bytes 196616 | tf_op jit(solution)/shard_map/ppermute | solution.py:242
  215.8 3.7 %collective-permute-done.15 = f32[16,1024]{1,0:T(8,128)S(1)} collective-permute-done((f32[16,1024]{1,0:T(8,128)S(1)}, f32[16,1024]{1,0:T(8,128)S(1)}, u32[]{:S(2)}, u32[]{:S(2)}) %collective-permute-start.15) | collective-permute-done | bytes 65568 | tf_op jit(solution)/shard_map/ppermute | solution.py:242
  219.5 2.8 %collective-permute-done.16 = f32[16,1024]{1,0:T(8,128)S(1)} collective-permute-done((f32[16,1024]{1,0:T(8,128)S(1)}, f32[16,1024]{1,0:T(8,128)S(1)}, u32[]{:S(2)}, u32[]{:S(2)}) %collective-permute-start.16) | collective-permute-done | bytes 65568 | tf_op jit(solution)/shard_map/ppermute | solution.py:242
  222.3 1.2 collective-permute-start.17
  223.5 4.1 %collective-permute-start.18 = (f32[16,1024]{1,0:T(8,128)S(1)}, f32[16,1024]{1,0:T(8,128)S(1)}, u32[]{:S(2)}, u32[]{:S(2)}) collective-permute-start(f32[16,1024]{1,0:T(8,128)S(1)} %fusion.17), channel_id=1, source_target_pairs={{0,32},{16,48},{32,0},{48,16},{64,96},{80,112},{96,64},{112,80},{1... | collective-permute-start | bytes 196616 | tf_op jit(solution)/shard_map/ppermute | solution.py:251
  228.5 4.6 %collective-permute-done.18 = f32[16,1024]{1,0:T(8,128)S(1)} collective-permute-done((f32[16,1024]{1,0:T(8,128)S(1)}, f32[16,1024]{1,0:T(8,128)S(1)}, u32[]{:S(2)}, u32[]{:S(2)}) %collective-permute-start.18) | collective-permute-done | bytes 65568 | tf_op jit(solution)/shard_map/ppermute | solution.py:251
  233.1 1.4 collective-permute-done.19
  236.0 1.9 collective-permute-start.21
  238.0 1.3 collective-permute-start.22
  239.9 1.0 copy.61
  241.0 9.3 %collective-permute-done.20 = f32[64,1024]{1,0:T(8,128)S(1)} collective-permute-done((f32[64,1024]{1,0:T(8,128)S(1)}, f32[64,1024]{1,0:T(8,128)S(1)}, u32[]{:S(2)}, u32[]{:S(2)}) %collective-permute-start.20) | collective-permute-done | bytes 262176 | tf_op jit(solution)/shard_map/ppermute | solution.py:251
  (72 shorter events, 20.3 us)
Async XLA Ops:
  5.3 35.1 %copy-start = (bf16[1024,1024]{1,0:T(8,128)(2,1)S(1)}, bf16[1024,1024]{1,0:T(8,128)(2,1)}, u32[]{:S(2)}) copy-start(bf16[1024,1024]{1,0:T(8,128)(2,1)} %wout_ref.1) | copy-start | bytes 6291460
  5.3 35.1 %copy-start.1 = (f32[1024]{0:T(1024)S(1)}, f32[1024]{0:T(1024)}, u32[]{:S(2)}) copy-start(f32[1024]{0:T(1024)} %param.8) | copy-start | bytes 12292
  5.3 35.1 %copy-start.2 = (f32[1024]{0:T(1024)S(1)}, f32[1024]{0:T(1024)}, u32[]{:S(2)}) copy-start(f32[1024]{0:T(1024)} %param.9) | copy-start | bytes 12292
  5.3 32.8 %all-to-all-start = ((bf16[4,1,256,1024]{3,0,1,2:T(4,128)(2,1)}), bf16[4,1,256,1024]{3,0,1,2:T(4,128)(2,1)}, u32[]{:S(2)}, u32[]{:S(2)}) async-start(bf16[4,1,256,1024]{3,0,1,2:T(4,128)(2,1)} %copy.58), calls=%async_computation | async-start | bytes 4194304 | tf_op jit(solution)/shard_map/all_to_all | solution.py:309
  85.0 7.5 %collective-permute-start = (bf16[8,64,4096]{2,1,0:T(8,128)(2,1)}, bf16[8,64,4096]{2,1,0:T(8,128)(2,1)}, u32[]{:S(2)}, u32[]{:S(2)}) collective-permute-start(bf16[8,64,4096]{2,1,0:T(8,128)(2,1)} %get-tuple-element.15), channel_id=1, source_target_pairs={{0,1},{1,0},{2,3},{3,2},{4,5},{5,4},{6,7},{7,6},{8,9},{9,8},{10,11... | collective-permute-start | bytes 12582920 | tf_op jit(solution)/shard_map/ppermute | solution.py:280
  101.0 2.0 copy-start.3
  104.2 34.5 %collective-permute-start.1 = (bf16[2,64,2048]{2,1,0:T(8,128)(2,1)}, bf16[2,64,2048]{2,1,0:T(8,128)(2,1)}, u32[]{:S(2)}, u32[]{:S(2)}) collective-permute-start(bf16[2,64,2048]{2,1,0:T(8,128)(2,1)} %get-tuple-element.67), channel_id=1, source_target_pairs={{0,4},{1,5},{2,6},{3,7},{4,8},{5,9},{6,10},{7,11},{8,12},{9,13},{1... | collective-permute-start | bytes 1572872 | tf_op jit(solution)/shard_map/ppermute | solution.py:242
  104.7 35.6 %collective-permute-start.2 = (bf16[2,64,2048]{2,1,0:T(8,128)(2,1)}, bf16[2,64,2048]{2,1,0:T(8,128)(2,1)}, u32[]{:S(2)}, u32[]{:S(2)}) collective-permute-start(bf16[2,64,2048]{2,1,0:T(8,128)(2,1)} %get-tuple-element.69), channel_id=1, source_target_pairs={{0,8},{1,9},{2,10},{3,11},{4,12},{5,13},{6,14},{7,15},{8,0},{9,1},... | collective-permute-start | bytes 1572872 | tf_op jit(solution)/shard_map/ppermute | solution.py:242
  107.9 32.3 %collective-permute-start.3 = (bf16[2,64,2048]{2,1,0:T(8,128)(2,1)S(1)}, bf16[2,64,2048]{2,1,0:T(8,128)(2,1)}, u32[]{:S(2)}, u32[]{:S(2)}) collective-permute-start(bf16[2,64,2048]{2,1,0:T(8,128)(2,1)S(1)} %get-tuple-element.68), channel_id=1, source_target_pairs={{0,12},{1,13},{2,14},{3,15},{4,0},{5,1},{6,2},{7,3},{8,4},{9,5},{1... | collective-permute-start | bytes 1572872 | tf_op jit(solution)/shard_map/ppermute | solution.py:242
  109.6 57.5 %all-to-all-start.2 = ((f32[16,1,128]{2,1,0:T(1,128)}), f32[16,1,128]{2,1,0:T(1,128)S(1)}, u32[]{:S(2)}, u32[]{:S(2)}) async-start(f32[16,1,128]{2,1,0:T(1,128)} %bitcast.35), calls=%async_computation.2 | async-start | bytes 16384 | tf_op jit(solution)/shard_map/all_to_all | solution.py:298
  129.3 19.7 %collective-permute-start.7 = (bf16[4,2,64,512]{3,2,1,0:T(8,128)(2,1)}, bf16[4,2,64,512]{3,2,1,0:T(8,128)(2,1)}, u32[]{:S(2)}, u32[]{:S(2)}) collective-permute-start(bf16[4,2,64,512]{3,2,1,0:T(8,128)(2,1)} %bitcast.100), channel_id=1, source_target_pairs={{0,64},{16,80},{32,96},{48,112},{64,128},{80,144},{96,160},{112,17... | collective-permute-start | bytes 1572872 | tf_op jit(solution)/shard_map/ppermute | solution.py:242
  131.8 26.1 %collective-permute-start.8 = (bf16[4,2,64,512]{3,2,1,0:T(8,128)(2,1)}, bf16[4,2,64,512]{3,2,1,0:T(8,128)(2,1)}, u32[]{:S(2)}, u32[]{:S(2)}) collective-permute-start(bf16[4,2,64,512]{3,2,1,0:T(8,128)(2,1)} %bitcast.99), channel_id=1, source_target_pairs={{0,128},{16,144},{32,160},{48,176},{64,192},{80,208},{96,224},{112... | collective-permute-start | bytes 1572872 | tf_op jit(solution)/shard_map/ppermute | solution.py:242
  138.7 20.1 %collective-permute-start.9 = (bf16[4,2,64,512]{3,2,1,0:T(8,128)(2,1)}, bf16[4,2,64,512]{3,2,1,0:T(8,128)(2,1)}, u32[]{:S(2)}, u32[]{:S(2)}) collective-permute-start(bf16[4,2,64,512]{3,2,1,0:T(8,128)(2,1)} %bitcast.98), channel_id=1, source_target_pairs={{0,192},{16,208},{32,224},{48,240},{64,0},{80,16},{96,32},{112,48}... | collective-permute-start | bytes 1572872 | tf_op jit(solution)/shard_map/ppermute | solution.py:242
  146.0 17.4 %collective-permute-start.4 = (f32[2,64,512]{2,1,0:T(8,128)S(1)}, f32[2,64,512]{2,1,0:T(8,128)}, u32[]{:S(2)}, u32[]{:S(2)}) collective-permute-start(f32[2,64,512]{2,1,0:T(8,128)S(1)} %bitcast.114), channel_id=1, source_target_pairs={{0,64},{16,80},{32,96},{48,112},{64,128},{80,144},{96,160},{112,17... | collective-permute-start | bytes 786440 | tf_op jit(solution)/shard_map/ppermute | solution.py:242
  147.4 30.0 %collective-permute-start.5 = (f32[2,64,512]{2,1,0:T(8,128)}, f32[2,64,512]{2,1,0:T(8,128)}, u32[]{:S(2)}, u32[]{:S(2)}) collective-permute-start(f32[2,64,512]{2,1,0:T(8,128)} %bitcast.102), channel_id=1, source_target_pairs={{0,128},{16,144},{32,160},{48,176},{64,192},{80,208},{96,224},{112... | collective-permute-start | bytes 786440 | tf_op jit(solution)/shard_map/ppermute | solution.py:242
  149.1 28.3 %collective-permute-start.6 = (f32[2,64,512]{2,1,0:T(8,128)}, f32[2,64,512]{2,1,0:T(8,128)}, u32[]{:S(2)}, u32[]{:S(2)}) collective-permute-start(f32[2,64,512]{2,1,0:T(8,128)} %bitcast.101), channel_id=1, source_target_pairs={{0,192},{16,208},{32,224},{48,240},{64,0},{80,16},{96,32},{112,48}... | collective-permute-start | bytes 786440 | tf_op jit(solution)/shard_map/ppermute | solution.py:242
  161.3 28.8 %collective-permute-start.10 = (f32[2,64,512]{2,1,0:T(8,128)}, f32[2,64,512]{2,1,0:T(8,128)S(1)}, u32[]{:S(2)}, u32[]{:S(2)}) collective-permute-start(f32[2,64,512]{2,1,0:T(8,128)} %get-tuple-element.70), channel_id=1, source_target_pairs={{0,4},{1,5},{2,6},{3,7},{4,8},{5,9},{6,10},{7,11},{8,12},{9,13},{1... | collective-permute-start | bytes 786440 | tf_op jit(solution)/shard_map/ppermute | solution.py:242
  162.7 27.3 %collective-permute-start.11 = (f32[2,64,512]{2,1,0:T(8,128)S(1)}, f32[2,64,512]{2,1,0:T(8,128)}, u32[]{:S(2)}, u32[]{:S(2)}) collective-permute-start(f32[2,64,512]{2,1,0:T(8,128)S(1)} %get-tuple-element.72), channel_id=1, source_target_pairs={{0,8},{1,9},{2,10},{3,11},{4,12},{5,13},{6,14},{7,15},{8,0},{9,1},... | collective-permute-start | bytes 786440 | tf_op jit(solution)/shard_map/ppermute | solution.py:242
  163.4 26.6 %collective-permute-start.12 = (f32[2,64,512]{2,1,0:T(8,128)S(1)}, f32[2,64,512]{2,1,0:T(8,128)}, u32[]{:S(2)}, u32[]{:S(2)}) collective-permute-start(f32[2,64,512]{2,1,0:T(8,128)S(1)} %get-tuple-element.71), channel_id=1, source_target_pairs={{0,12},{1,13},{2,14},{3,15},{4,0},{5,1},{6,2},{7,3},{8,4},{9,5},{1... | collective-permute-start | bytes 786440 | tf_op jit(solution)/shard_map/ppermute | solution.py:242
  167.7 17.4 %all-to-all-start.3 = ((f32[16,1,128]{2,1,0:T(1,128)}), f32[16,1,128]{2,1,0:T(1,128)S(1)}, u32[]{:S(2)}, u32[]{:S(2)}) async-start(f32[16,1,128]{2,1,0:T(1,128)} %broadcast_in_dim.42), calls=%async_computation.3 | async-start | bytes 16384 | tf_op jit(solution)/shard_map/all_to_all | solution.py:300
  185.1 54.8 %all-to-all-start.1 = ((bf16[2,16,16,1024]{3,2,0,1:T(8,128)(2,1)}), bf16[2,16,16,1024]{3,2,0,1:T(8,128)(2,1)S(1)}, u32[]{:S(2)}, u32[]{:S(2)}) async-start(bf16[2,16,16,1024]{3,2,0,1:T(8,128)(2,1)} %copy.60), calls=%async_computation.1 | async-start | bytes 2097152 | tf_op jit(solution)/shard_map/all_to_all | solution.py:311
  191.2 18.5 %collective-permute-start.13 = (f32[64,1024]{1,0:T(8,128)S(1)}, f32[64,1024]{1,0:T(8,128)S(1)}, u32[]{:S(2)}, u32[]{:S(2)}) collective-permute-start(f32[64,1024]{1,0:T(8,128)S(1)} %fusion.8), channel_id=1, source_target_pairs={{0,2},{1,3},{2,0},{3,1},{4,6},{5,7},{6,4},{7,5},{8,10},{9,11},{10,... | collective-permute-start | bytes 786440 | tf_op jit(solution)/shard_map/ppermute | solution.py:242
  209.8 6.0 %collective-permute-start.14 = (f32[16,1024]{1,0:T(8,128)S(1)}, f32[16,1024]{1,0:T(8,128)S(1)}, u32[]{:S(2)}, u32[]{:S(2)}) collective-permute-start(f32[16,1024]{1,0:T(8,128)S(1)} %get-tuple-element.77), channel_id=1, source_target_pairs={{0,16},{16,32},{32,48},{48,0},{64,80},{80,96},{96,112},{112,64},{1... | collective-permute-start | bytes 196616 | tf_op jit(solution)/shard_map/ppermute | solution.py:242
  210.4 9.0 %collective-permute-start.15 = (f32[16,1024]{1,0:T(8,128)S(1)}, f32[16,1024]{1,0:T(8,128)S(1)}, u32[]{:S(2)}, u32[]{:S(2)}) collective-permute-start(f32[16,1024]{1,0:T(8,128)S(1)} %get-tuple-element.79), channel_id=1, source_target_pairs={{0,32},{16,48},{32,0},{48,16},{64,96},{80,112},{96,64},{112,80},{1... | collective-permute-start | bytes 196616 | tf_op jit(solution)/shard_map/ppermute | solution.py:242
  215.6 6.6 %collective-permute-start.16 = (f32[16,1024]{1,0:T(8,128)S(1)}, f32[16,1024]{1,0:T(8,128)S(1)}, u32[]{:S(2)}, u32[]{:S(2)}) collective-permute-start(f32[16,1024]{1,0:T(8,128)S(1)} %get-tuple-element.78), channel_id=1, source_target_pairs={{0,48},{16,0},{32,16},{48,32},{64,112},{80,64},{96,80},{112,96},{1... | collective-permute-start | bytes 196616 | tf_op jit(solution)/shard_map/ppermute | solution.py:242
  222.3 6.3 %collective-permute-start.17 = (f32[16,1024]{1,0:T(8,128)S(1)}, f32[16,1024]{1,0:T(8,128)S(1)}, u32[]{:S(2)}, u32[]{:S(2)}) collective-permute-start(f32[16,1024]{1,0:T(8,128)S(1)} %fusion.17), channel_id=1, source_target_pairs={{0,16},{16,32},{32,48},{48,0},{64,80},{80,96},{96,112},{112,64},{1... | collective-permute-start | bytes 196616 | tf_op jit(solution)/shard_map/ppermute | solution.py:251
  223.5 9.6 %collective-permute-start.18 = (f32[16,1024]{1,0:T(8,128)S(1)}, f32[16,1024]{1,0:T(8,128)S(1)}, u32[]{:S(2)}, u32[]{:S(2)}) collective-permute-start(f32[16,1024]{1,0:T(8,128)S(1)} %fusion.17), channel_id=1, source_target_pairs={{0,32},{16,48},{32,0},{48,16},{64,96},{80,112},{96,64},{112,80},{1... | collective-permute-start | bytes 196616 | tf_op jit(solution)/shard_map/ppermute | solution.py:251
  227.7 6.9 %collective-permute-start.19 = (f32[16,1024]{1,0:T(8,128)S(1)}, f32[16,1024]{1,0:T(8,128)S(1)}, u32[]{:S(2)}, u32[]{:S(2)}) collective-permute-start(f32[16,1024]{1,0:T(8,128)S(1)} %fusion.17), channel_id=1, source_target_pairs={{0,48},{16,0},{32,16},{48,32},{64,112},{80,64},{96,80},{112,96},{1... | collective-permute-start | bytes 196616 | tf_op jit(solution)/shard_map/ppermute | solution.py:251
  235.3 15.1 %collective-permute-start.20 = (f32[64,1024]{1,0:T(8,128)S(1)}, f32[64,1024]{1,0:T(8,128)S(1)}, u32[]{:S(2)}, u32[]{:S(2)}) collective-permute-start(f32[64,1024]{1,0:T(8,128)S(1)} %bitcast_select_fusion), channel_id=1, source_target_pairs={{0,64},{16,80},{32,96},{48,112},{64,128},{80,144},{96,160},{112,17... | collective-permute-start | bytes 786440 | tf_op jit(solution)/shard_map/ppermute | solution.py:251
  236.0 14.3 %collective-permute-start.21 = (f32[64,1024]{1,0:T(8,128)S(1)}, f32[64,1024]{1,0:T(8,128)S(1)}, u32[]{:S(2)}, u32[]{:S(2)}) collective-permute-start(f32[64,1024]{1,0:T(8,128)S(1)} %bitcast_select_fusion), channel_id=1, source_target_pairs={{0,128},{16,144},{32,160},{48,176},{64,192},{80,208},{96,224},{112... | collective-permute-start | bytes 786440 | tf_op jit(solution)/shard_map/ppermute | solution.py:251
  238.0 13.0 %collective-permute-start.22 = (f32[64,1024]{1,0:T(8,128)S(1)}, f32[64,1024]{1,0:T(8,128)S(1)}, u32[]{:S(2)}, u32[]{:S(2)}) collective-permute-start(f32[64,1024]{1,0:T(8,128)S(1)} %bitcast_select_fusion), channel_id=1, source_target_pairs={{0,192},{16,208},{32,224},{48,240},{64,0},{80,16},{96,32},{112,48}... | collective-permute-start | bytes 786440 | tf_op jit(solution)/shard_map/ppermute | solution.py:251

commit v2 on v1

v2 whole, which is shorter than its diff:
```python
import functools
import math

import jax
import jax.numpy as jnp
from jax import lax
from jax.experimental import pallas as pl
from jax.experimental.pallas import tpu as pltpu
from jax.sharding import PartitionSpec as P

F32 = jnp.float32
BF16 = jnp.bfloat16
MIB = 1024 * 1024
CHUNK = 512


def dot_nn(a, b):
    return lax.dot_general(a, b, (((1,), (0,)), ((), ())), preferred_element_type=F32)


def dot_nt(a, b):
    return lax.dot_general(a, b, (((1,), (1,)), ((), ())), preferred_element_type=F32)


def dot_tn(a, b):
    return lax.dot_general(a, b, (((0,), (0,)), ((), ())), preferred_element_type=F32)


def chunk(n):
    return pl.ds(pl.multiple_of(n * CHUNK, CHUNK), CHUNK)


def block_row(block, place):
    x, h, y, z, core = place
    dh = (block % 4 - h) % 4
    dcore = (block // 4 % 2 - core) % 2
    dz = (block // 8 % 2 - z) % 2
    dy = (block // 16 - y) % 4
    return pl.multiple_of((((dcore * 4 + dy) * 2 + dz) * 4 + dh) * 16, 16)


def read_place(place_ref):
    return tuple(place_ref[i] for i in range(5))


def whiten(xh):
    centred = xh - jnp.mean(xh, axis=-1, keepdims=True)
    inv = lax.rsqrt(jnp.mean(centred * centred, axis=-1, keepdims=True) + 1e-05)
    return centred * inv, inv


def main_kernel(
    place_ref, tokens_ref, gain_ref, bias_ref, wqkv_ref, wout_ref,
    send_hbm, keep_hbm, left_hbm, right_hbm,
    left_s, right_s, normed_s, packed_s, datt_s, send_s, keep_s, sems,
):
    place = read_place(place_ref)
    frames, clips, positions, width = tokens_ref.shape
    clips = clips // 2
    halves = positions // 8
    part = frames * 8
    gain = gain_ref[...]
    bias = bias_ref[...]

    def norm_step(i, carry):
        c = i // (frames // 2)
        q = i % (frames // 2)
        x = tokens_ref[pl.ds(2 * q, 2), c].astype(F32).reshape(2, halves, 8, width)
        g = tokens_ref[pl.ds(2 * q, 2), clips + c].astype(F32).reshape(2, halves, 8, width)
        for hf in range(halves):
            at = pl.multiple_of((c * halves + hf) * part + q * 16, 16)
            wh, _ = whiten(x[:, hf].reshape(16, width))
            normed_s[pl.ds(at, 16), :] = (wh * gain + bias).astype(BF16)
            right_s[pl.ds(at, 16), pl.ds(3 * width, width)] = g[:, hf].reshape(16, width).astype(BF16)
        return carry

    lax.fori_loop(0, clips * frames // 2, norm_step, 0)

    def qkv_step(n, carry):
        packed_s[:, chunk(n)] = dot_nn(normed_s[...], wqkv_ref[:, chunk(n)]).astype(BF16)
        return carry

    lax.fori_loop(0, 3 * width // CHUNK, qkv_step, 0, unroll=2)

    for n in range(width // CHUNK):
        cols = slice(n * CHUNK, (n + 1) * CHUNK)
        datt_s[:, cols] = dot_nt(right_s[:, 3 * width:], wout_ref[cols, :]).astype(BF16)
        turned = normed_s[:, cols].T
        for b in range(CHUNK // 16):
            at = block_row(n * (CHUNK // 16) + b, place)
            left_s[0, pl.ds(at, 16), :] = turned[b * 16:(b + 1) * 16]

    lane = lax.broadcasted_iota(jnp.int32, (part, 128), 1)
    first = lane < 64
    same = lax.broadcasted_iota(jnp.int32, (1, 8, part), 1) == (
        lax.broadcasted_iota(jnp.int32, (1, 8, part), 2) % 8
    )
    zero = jnp.zeros((part, 128), BF16)

    def split(a):
        return jnp.concatenate([jnp.where(first, a, zero), jnp.where(first, zero, a)], axis=0)

    def attend_step(i, carry):
        t = i // (width // 128)
        hp = i % (width // 128)
        tok = pl.ds(pl.multiple_of(t * part, part), part)
        col = pl.multiple_of(hp * 128, 128)
        q = packed_s[tok, pl.ds(col, 128)]
        k = packed_s[tok, pl.ds(width + col, 128)]
        v = packed_s[tok, pl.ds(2 * width + col, 128)]
        da = datt_s[tok, pl.ds(col, 128)]
        k2 = split(k)
        v2 = split(v)
        scores = (dot_nt(k2, q) * 0.125).reshape(2, frames, 8, part)
        e = jnp.exp(scores - jnp.max(scores, axis=1, keepdims=True))
        probs = e * (1.0 / jnp.sum(e, axis=1, keepdims=True))
        probs = jnp.where(same[None], probs, 0.0)
        low = probs.astype(BF16).reshape(2, part, part)
        dp = dot_nt(v2, da).reshape(2, frames, 8, part)
        inner = jnp.sum(dp * probs, axis=1, keepdims=True)
        ds = (probs * (dp - inner) * 0.125).astype(BF16).reshape(2, part, part)
        attended = dot_tn(v2, low.reshape(2 * part, part)).astype(BF16)
        for b in range(8):
            left_s[1, pl.ds(block_row(hp * 8 + b, place), 16), tok] = attended[b * 16:(b + 1) * 16]
        right_s[tok, pl.ds(col, 128)] = dot_tn(ds.reshape(2 * part, part), k2).astype(BF16)
        right_s[tok, pl.ds(width + col, 128)] = dot_nn(
            jnp.concatenate([ds[0], ds[1]], axis=1), split(q)
        ).astype(BF16)
        right_s[tok, pl.ds(2 * width + col, 128)] = dot_nn(
            jnp.concatenate([low[0], low[1]], axis=1), split(da)
        ).astype(BF16)
        return carry

    lax.fori_loop(0, clips * halves * (width // 128), attend_step, 0, unroll=4)

    copies = [
        pltpu.make_async_copy(left_s, left_hbm, sems.at[0]),
        pltpu.make_async_copy(right_s, right_hbm, sems.at[1]),
    ]
    for copy in copies:
        copy.start()
    half = width // 2
    for k in range(4):
        rhs = right_s[:, chunk((place[0] + k) % 4)]
        g = dot_nn(left_s[0, half:, :], rhs)
        send_s[:, k] = g.reshape(4, 128, CHUNK).astype(BF16)
        copies.append(pltpu.make_async_copy(send_s.at[:, k], send_hbm.at[:, k], sems.at[2 + k]))
        copies[-1].start()
        g = dot_nn(left_s[0, :half, :], rhs)
        keep_s[:, k] = g.reshape(4, 128, CHUNK)
        copies.append(pltpu.make_async_copy(keep_s.at[:, k], keep_hbm.at[:, k], sems.at[6 + k]))
        copies[-1].start()
    for copy in copies:
        copy.wait()


def run_main(place, tokens, gain, bias, wqkv, wout):
    frames, clips, positions, width = tokens.shape
    rows = clips // 2 * frames * positions
    vm = pl.BlockSpec(memory_space=pltpu.VMEM)
    hbm = pl.BlockSpec(memory_space=pl.ANY)
    piece = (4, 4, 128, CHUNK)
    return pl.pallas_call(
        main_kernel,
        out_shape=(
            jax.ShapeDtypeStruct(piece, BF16),
            jax.ShapeDtypeStruct(piece, F32),
            jax.ShapeDtypeStruct((2, width, rows), BF16),
            jax.ShapeDtypeStruct((rows, 4 * width), BF16),
        ),
        in_specs=[pl.BlockSpec(memory_space=pltpu.SMEM)] + [vm] * 5,
        out_specs=(hbm,) * 4,
        scratch_shapes=[
            pltpu.VMEM((2, width, rows), BF16),
            pltpu.VMEM((rows, 4 * width), BF16),
            pltpu.VMEM((rows, width), BF16),
            pltpu.VMEM((rows, 3 * width), BF16),
            pltpu.VMEM((rows, width), BF16),
            pltpu.VMEM(piece, BF16),
            pltpu.VMEM(piece, F32),
            pltpu.SemaphoreType.DMA((10,)),
        ],
        compiler_params=pltpu.CompilerParams(vmem_limit_bytes=36 * MIB),
        cost_estimate=pl.CostEstimate(flops=12 * 1024**3, bytes_accessed=20 * MIB, transcendentals=MIB),
        name="sublayer",
    )(place, tokens, gain, bias, wqkv, wout)


def grads_kernel(place_ref, left_ref, right_ref, send_ref, keep_ref):
    half = left_ref.shape[1] // 2
    rhs = right_ref[...]
    send_ref[0] = dot_nn(left_ref[0, half:, :], rhs).reshape(4, 128, CHUNK).astype(BF16)
    keep_ref[0] = dot_nn(left_ref[0, :half, :], rhs).reshape(4, 128, CHUNK)


def run_grads(place, left, right):
    _, width, rows = left.shape
    piece = (4, 4, 128, CHUNK)
    out = pl.BlockSpec((1, 4, 128, CHUNK), lambda k, place: (k, 0, 0, 0))
    return pl.pallas_call(
        grads_kernel,
        grid_spec=pltpu.PrefetchScalarGridSpec(
            num_scalar_prefetch=1,
            grid=(4,),
            in_specs=[
                pl.BlockSpec((1, width, rows), lambda k, place: ((place[0] + k) % 4 // 2, 0, 0)),
                pl.BlockSpec((rows, CHUNK), lambda k, place: (0, 4 + (place[0] + k) % 4)),
            ],
            out_specs=(out, out),
        ),
        out_shape=(
            jax.ShapeDtypeStruct(piece, BF16),
            jax.ShapeDtypeStruct(piece, F32),
        ),
        compiler_params=pltpu.CompilerParams(vmem_limit_bytes=24 * MIB),
        cost_estimate=pl.CostEstimate(flops=2 * 1024**3, bytes_accessed=12 * MIB, transcendentals=0),
        name="weight_grads",
    )(place, left, right)


def back_kernel(tokens_ref, gain_ref, dpk_ref, wqkv_ref, gv_ref, dn_s):
    frames, clips, positions, width = tokens_ref.shape
    clips = clips // 2
    halves = positions // 8
    part = frames * 8
    gain = gain_ref[...]
    for n in range(width // CHUNK):
        cols = slice(n * CHUNK, (n + 1) * CHUNK)
        dn_s[:, cols] = dot_nt(dpk_ref[...], wqkv_ref[cols, :])

    def back_step(i, carry):
        dgain, dbias = carry
        c = i // (frames // 2)
        q = i % (frames // 2)
        x = tokens_ref[pl.ds(2 * q, 2), c].astype(F32).reshape(2, halves, 8, width)
        g = tokens_ref[pl.ds(2 * q, 2), clips + c].astype(F32).reshape(2, halves, 8, width)
        outs = []
        for hf in range(halves):
            at = pl.multiple_of((c * halves + hf) * part + q * 16, 16)
            dn = dn_s[pl.ds(at, 16), :]
            wh, inv = whiten(x[:, hf].reshape(16, width))
            dw = dn * wh
            dgain = dgain + dw[:8] + dw[8:]
            dbias = dbias + dn[:8] + dn[8:]
            scaled = dn * gain
            m1 = jnp.mean(scaled, axis=-1, keepdims=True)
            m2 = jnp.mean(scaled * wh, axis=-1, keepdims=True)
            grad = g[:, hf].reshape(16, width) + inv * (scaled - m1 - wh * m2)
            outs.append(grad.reshape(2, 8, width))
        cols = pl.ds(pl.multiple_of(c * width, width), width)
        gv_ref[pl.ds(2 * q, 2), :, cols] = jnp.concatenate(outs, axis=1).astype(BF16)
        return dgain, dbias

    zeros = jnp.zeros((8, width), F32)
    dgain, dbias = lax.fori_loop(0, clips * frames // 2, back_step, (zeros, zeros))
    dgain = jnp.sum(dgain, axis=0, keepdims=True)
    dbias = jnp.sum(dbias, axis=0, keepdims=True)
    lane = lax.broadcasted_iota(jnp.int32, (1, 128), 1)
    row = lax.broadcasted_iota(jnp.int32, (16, 128), 0)
    for f in range(frames):
        at = f // 2 * 128
        a = dgain[:, at:at + 128]
        b = dbias[:, at:at + 128]
        if f % 2 == 0:
            b = jnp.concatenate([b[:, 64:], b[:, :64]], axis=1)
        else:
            a = jnp.concatenate([a[:, 64:], a[:, :64]], axis=1)
        both = jnp.where(lane < 64, a, b)
        hi = both.astype(BF16).astype(F32)
        mid = (both - hi).astype(BF16).astype(F32)
        low = both - hi - mid
        terms = jnp.where(row == 0, hi, jnp.where(row == 1, mid, jnp.where(row == 2, low, 0.0)))
        gv_ref[f, :, clips * width:] = terms.astype(BF16)


def run_back(tokens, gain, right, wqkv):
    frames, clips, positions, width = tokens.shape
    clips = clips // 2
    rows = clips * frames * positions
    whole = lambda *shape: pl.BlockSpec(shape, lambda i: (0,) * len(shape))
    message = (frames, positions, clips * width + 128)
    return pl.pallas_call(
        back_kernel,
        grid=(1,),
        out_shape=jax.ShapeDtypeStruct(message, BF16),
        in_specs=[
            whole(*tokens.shape),
            whole(1, width),
            whole(rows, 3 * width),
            whole(width, 3 * width),
        ],
        out_specs=whole(*message),
        scratch_shapes=[pltpu.VMEM((rows, width), F32)],
        compiler_params=pltpu.CompilerParams(vmem_limit_bytes=40 * MIB),
        cost_estimate=pl.CostEstimate(flops=4 * 1024**3, bytes_accessed=12 * MIB, transcendentals=0),
        name="video_grads",
    )(tokens, gain, right, wqkv)


def place_kernel(scale, place_ref, d0, d1, d2, d3, qkv_ref, out_ref, small_ref):
    x, h = place_ref[0], place_ref[1]
    small = jnp.zeros((8, 128), F32)
    for j, d in enumerate((d0, d1, d2, d3)):
        block = (x - j) % 4
        for k in range(4):
            rows = pl.ds(pl.multiple_of((h - k) % 4 * 16, 16), 16)
            qkv_ref[rows, chunk(block)] = d[k * 32:k * 32 + 16, :] * scale
            b = d[k * 32 + 16:k * 32 + 32, :] * scale

            @pl.when(block < 2)
            def _():
                qkv_ref[rows, chunk(4 + block)] = b

            @pl.when(block >= 2)
            def _():
                out_ref[rows, chunk(block - 2)] = b

        small = small + d[128:136, :128] * scale
    small_ref[...] = small


def run_place(place, scale, pieces):
    vm = pl.BlockSpec(memory_space=pltpu.VMEM)
    return pl.pallas_call(
        functools.partial(place_kernel, scale),
        out_shape=(
            jax.ShapeDtypeStruct((64, 6 * CHUNK), F32),
            jax.ShapeDtypeStruct((64, 2 * CHUNK), F32),
            jax.ShapeDtypeStruct((8, 128), F32),
        ),
        in_specs=[pl.BlockSpec(memory_space=pltpu.SMEM)] + [vm] * 4,
        out_specs=(vm,) * 3,
        name="place_grads",
    )(place, *pieces)


def frame_pairs(move):
    pairs = []
    for i in range(16):
        y, z, core = move(i // 4, i // 2 % 2, i % 2)
        pairs.append((i, y % 4 * 4 + z % 2 * 2 + core % 2))
    return pairs


def dp_pairs(move):
    pairs = []
    for i in range(16):
        x, h = move(i // 4, i % 4)
        pairs.append((i, x % 4 * 4 + h % 4))
    return pairs


def go_core(a):
    return lax.ppermute(a, "frame", frame_pairs(lambda y, z, c: (y, z, c + 1)))


def go_y(a, k):
    return lax.ppermute(a, "frame", frame_pairs(lambda y, z, c: (y + k, z, c)))


def go_z(a):
    return lax.ppermute(a, "frame", frame_pairs(lambda y, z, c: (y, z + 1, c)))


def go_x(a, k):
    return lax.ppermute(a, "dp", dp_pairs(lambda x, h: (x + k, h)))


def go_h(a, k):
    return lax.ppermute(a, "dp", dp_pairs(lambda x, h: (x, h + k)))


def reduce_ring(piece, go, dtype):
    got = [go(piece(k).astype(dtype), k) for k in range(1, 4)]
    total = piece(0)
    for part in got:
        total = total + part.astype(F32)
    return total


def reduce_grads(send_a, keep_a, send_b, keep_b, small):
    got_a = go_core(send_a)
    got_b = go_core(send_b)
    a = reduce_ring(lambda k: keep_a[k] + got_a[k].astype(F32), go_y, BF16)
    b = reduce_ring(lambda k: keep_b[k] + got_b[k].astype(F32), go_x, BF16)
    a = reduce_second(a, go_x)
    b = reduce_second(b, go_y)
    away = jnp.stack([a[64:], b[64:]])
    both = jnp.stack([a[:64], b[:64]]) + go_z(away)
    both = both.reshape(2, 4, 16, CHUNK)
    both = reduce_ring(lambda k: both[:, k], go_h, F32)
    message = jnp.concatenate([both.reshape(32, CHUNK), small], axis=0)
    got = [message] + [go_h(message, k) for k in range(1, 4)]
    small = got[0][32:] + got[1][32:] + got[2][32:] + got[3][32:]
    message = jnp.concatenate([g[:32] for g in got] + [small], axis=0)
    return [message] + [go_x(message, k) for k in range(1, 4)]


def reduce_second(total, go):
    return reduce_ring(lambda k: total[k], go, F32)


def local(video, cotangent, norm_gain, norm_bias, qkv_weight, out_weight):
    clips, frames_here, positions, width = video.shape
    grad_scale = 1.0 / math.sqrt(clips * positions * 256)
    frame = lax.axis_index("frame")
    dp = lax.axis_index("dp")
    place = jnp.stack([dp // 4, dp % 4, frame // 4, frame // 2 % 2, frame % 2]).astype(jnp.int32)
    gain = norm_gain.reshape(1, width)
    bias = norm_bias.reshape(1, width)
    tokens = jnp.concatenate([video, cotangent], axis=0).reshape(2 * clips, 16, positions // 16, width)
    tokens = lax.all_to_all(tokens.transpose(1, 0, 2, 3), "frame", 0, 0, tiled=True)
    send_a, keep_a, left, right = run_main(place, tokens, gain, bias, qkv_weight, out_weight)
    send_b, keep_b = run_grads(place, left, right)
    back = run_back(tokens, gain, right, qkv_weight)
    back = lax.all_to_all(back, "frame", 0, 0, tiled=True)
    grad_video = back[:, :, : clips * width].reshape(positions, clips, width)
    grad_video = grad_video.transpose(1, 0, 2).reshape(video.shape)
    small = jnp.sum(back[:, :3, clips * width :].astype(F32), axis=(0, 1))
    small = jnp.pad(small.reshape(1, 128), ((0, 7), (0, CHUNK - 128)))
    pieces = reduce_grads(send_a, keep_a, send_b, keep_b, small)
    grad_qkv, grad_out, small = run_place(place, grad_scale, pieces)
    return grad_video, grad_qkv, grad_out, small[0, :64], small[0, 64:]


def solution(mesh):
    in_specs = (P("dp", "frame", None, None), P("dp", "frame", None, None), P(), P(), P(), P())
    out_specs = (
        P("dp", "frame", None, None),
        P("frame", None),
        P("frame", None),
        P("frame"),
        P("frame"),
    )
    return jax.shard_map(local, mesh=mesh, in_specs=in_specs, out_specs=out_specs, check_vma=False)
```

time: 257 us -> 199 us (0.77)
  the two profiles are of different devices: /device:TPU:72 before, /device:TPU:32 now
where the time goes in v2:
time: 199 us; the launch traced here: 198 us
  starting transfers between devices  66.2 us (33%)
  waiting for transfers between devices  64.4 us (32%)
  Pallas kernels  44.6 us (22%)
  local copies, waits for them, and re-layouts  11 us (6%)
  other arithmetic  10.6 us (5%)
    pallas_call x1, Pallas kernels, run_main(): pl.pallas_call(main_kernel, out_shape=(jax.ShapeDtypeStruct(piece, BF16),...  28.7 us
    all_to_all x1, waiting for transfers between devices, local(): lax.all_to_all(tokens.transpose(1, 0, 2, 3), 'frame', 0, 0, tiled=True)  26.6 us
    ppermute x9, starting transfers between devices, go_x(): return lax.ppermute(a, 'dp', dp_pairs(lambda x, h: (x + k, h)))  25.7 us
    ppermute x6, starting transfers between devices, go_h(): return lax.ppermute(a, 'dp', dp_pairs(lambda x, h: (x, h + k)))  18.5 us
    ppermute x6, waiting for transfers between devices, go_y(): return lax.ppermute(a, 'frame', frame_pairs(lambda y, z, c: (y + k, z, c)))  12 us
    ppermute x6, waiting for transfers between devices, go_h(): return lax.ppermute(a, 'dp', dp_pairs(lambda x, h: (x, h + k)))  10.2 us
    ppermute x9, waiting for transfers between devices, go_x(): return lax.ppermute(a, 'dp', dp_pairs(lambda x, h: (x + k, h)))  9.81 us
    pallas_call x1, Pallas kernels, run_back(): pl.pallas_call(back_kernel, grid=(1,), out_shape=jax.ShapeDtypeStruct(mes...  9.28 us
  transfers between devices with their start and end apart: 26, of which 14 were waited for; matrix products, arithmetic and copies ran while one was open for 6% of the time, Pallas kernels for 7%

profile of v2, /device:TPU:32, one launch (start us, length us, event | category | flops | bytes accessed | tf_op | source)
XLA Modules:
  0.0 197.6 jit_solution(9118608040685996712)
XLA Ops:
  0.6 1.7 pad_maximum_fusion
  2.4 1.5 copy.30
  3.9 6.1 %all-to-all-start = ((bf16[16,4,16,1024]{3,2,1,0:T(8,128)(2,1)}), bf16[16,4,16,1024]{3,2,1,0:T(8,128)(2,1)S(1)}, u32[]{:S(2)}, u32[]{:S(2)}) async-start(bf16[16,4,16,1024]{3,2,1,0:T(8,128)(2,1)} %bitcast.110), calls=%async_computation | async-start | bytes 4194304 | tf_op jit(solution)/shard_map/all_to_all | solution.py:412
  10.0 26.6 %all-to-all-done.tokens_ref = bf16[16,4,16,1024]{3,2,1,0:T(8,128)(2,1)S(1)} async-done(((bf16[16,4,16,1024]{3,2,1,0:T(8,128)(2,1)}), bf16[16,4,16,1024]{3,2,1,0:T(8,128)(2,1)S(1)}, u32[]{:S(2)}, u32[]{:S(2)}) %all-to-all-start) | async-done | bytes 2097184 | tf_op jit(solution)/shard_map/all_to_all | solution.py:412
  36.6 1.6 copy-done.4
  38.2 28.7 %sublayer.1 = (bf16[4,4,128,512]{3,2,1,0:T(8,128)(2,1)S(1)}, f32[4,4,128,512]{3,2,1,0:T(8,128)S(1)}, bf16[2,1024,512]{2,1,0:T(8,128)(2,1)S(1)}, bf16[512,4096]{1,0:T(8,128)(2,1)S(1)}) custom-call(s32[5]{0:T(128)S(1)} %stack.41.place_ref, bf16[16,4,16,1024]{3,2,1,0:T(8,128)(2,1)S(1)} %all-to-all-done.tokens_ref, f32[1,1024]{1,0:T(1,128)S(1)} %bitcast.108, ...), custom_call_target="tpu_custom_call" | custom-call | flops 12884901888 | bytes 20971520 | tf_op jit(solution)/shard_map/sublayer/pallas_call | solution.py:163
  67.1 4.2 %weight_grads.1 = (bf16[4,4,128,512]{3,2,1,0:T(8,128)(2,1)}, f32[4,4,128,512]{3,2,1,0:T(8,128)S(1)}) custom-call(s32[5]{0:T(128)S(1)} %stack.41.place_ref, bf16[2,1024,512]{2,1,0:T(8,128)(2,1)S(1)} %get-tuple-element.17.left_ref, bf16[512,4096]{1,0:T(8,128)(2,1)S(1)} %get-tuple-element.14.dpk_ref.right_ref), custom_call_target="tpu_custom_call" | custom-call | flops 2147483648 | bytes 12582912 | tf_op jit(solution)/shard_map/weight_grads/pallas_call | solution.py:200
  71.7 1.8 fusion.4
  74.2 3.2 %collective-permute-start.3 = (bf16[4,128,512]{2,1,0:T(8,128)(2,1)S(1)}, bf16[4,128,512]{2,1,0:T(8,128)(2,1)}, u32[]{:S(2)}, u32[]{:S(2)}) collective-permute-start(bf16[4,128,512]{2,1,0:T(8,128)(2,1)S(1)} %get-tuple-element.24), channel_id=1, source_target_pairs={{0,12},{1,13},{2,14},{3,15},{4,0},{5,1},{6,2},{7,3},{8,4},{9,5},{1... | collective-permute-start | bytes 1572872 | tf_op jit(solution)/shard_map/ppermute | solution.py:358
  77.7 2.8 %copy-done.3 = bf16[1024,3072]{1,0:T(8,128)(2,1)S(1)} copy-done((bf16[1024,3072]{1,0:T(8,128)(2,1)S(1)}, bf16[1024,3072]{1,0:T(8,128)(2,1)}, u32[]{:S(2)}) %copy-start.3) | copy-done | bytes 6291480
  80.5 9.3 %video_grads.1 = bf16[16,16,2176]{2,1,0:T(8,128)(2,1)} custom-call(bf16[16,4,16,1024]{3,2,1,0:T(8,128)(2,1)S(1)} %all-to-all-done.tokens_ref, f32[1,1024]{1,0:T(1,128)S(1)} %bitcast.109, bf16[512,4096]{1,0:T(8,128)(2,1)S(1)} %get-tuple-element.14.dpk_ref.right_ref, bf16[1024,3072]{1,0:T(8,128)(2,1)S(1)} %copy-done.3), custom_call_target="tpu_custom_call" | custom-call | flops 4294967296 | bytes 12582912 | tf_op jit(solution)/shard_map/video_grads/pallas_call | solution.py:282
  89.8 6.0 %all-to-all-start.1 = ((bf16[16,16,2176]{2,1,0:T(8,128)(2,1)}), bf16[16,16,2176]{2,1,0:T(8,128)(2,1)S(1)}, u32[]{:S(2)}, u32[]{:S(2)}) async-start(bf16[16,16,2176]{2,1,0:T(8,128)(2,1)} %video_grads.1), calls=%async_computation.1 | async-start | bytes 2228224 | tf_op jit(solution)/shard_map/all_to_all | solution.py:416
  95.8 2.8 %fusion.7 = (bf16[4,128,512]{2,1,0:T(8,128)(2,1)S(1)}, bf16[4,128,512]{2,1,0:T(8,128)(2,1)S(1)}, bf16[4,128,512]{2,1,0:T(8,128)(2,1)S(1)}) fusion(f32[4,4,128,512]{3,2,1,0:T(8,128)} %copy-done, bf16[4,4,128,512]{3,2,1,0:T(8,128)(2,1)} %collective-permute-done.7), kind=kLoop, calls=%fused_computation.18 | loop fusion | flops 2359296 | bytes 6291456 | tf_op jit(solution)/shard_map/convert_element_type | solution.py:374
  98.6 1.6 collective-permute-start.8
  100.2 1.7 collective-permute-start.10
  101.9 6.2 %collective-permute-done.1 = bf16[4,128,512]{2,1,0:T(8,128)(2,1)} collective-permute-done((bf16[4,128,512]{2,1,0:T(8,128)(2,1)}, bf16[4,128,512]{2,1,0:T(8,128)(2,1)}, u32[]{:S(2)}, u32[]{:S(2)}) %collective-permute-start.1) | collective-permute-done | bytes 524320 | tf_op jit(solution)/shard_map/ppermute | solution.py:358
  108.1 3.0 %collective-permute-start.9 = (bf16[4,128,512]{2,1,0:T(8,128)(2,1)S(1)}, bf16[4,128,512]{2,1,0:T(8,128)(2,1)S(1)}, u32[]{:S(2)}, u32[]{:S(2)}) collective-permute-start(bf16[4,128,512]{2,1,0:T(8,128)(2,1)S(1)} %get-tuple-element.28), channel_id=1, source_target_pairs={{0,128},{16,144},{32,160},{48,176},{64,192},{80,208},{96,224},{112... | collective-permute-start | bytes 1572872 | tf_op jit(solution)/shard_map/ppermute | solution.py:366
  111.1 2.2 %fusion.3 = f32[4,128,512]{2,1,0:T(8,128)S(1)} fusion(bf16[4,128,512]{2,1,0:T(8,128)(2,1)} %collective-permute-done.3, bf16[4,128,512]{2,1,0:T(8,128)(2,1)} %collective-permute-done.2, bf16[4,128,512]{2,1,0:T(8,128)(2,1)} %collective-permute-done.1, f32[4,4,128,512]{3,2,1,0:T(8,128)} %copy-done.1, bf16[4,4,128,512]{3,2,1,0:T(8,128)(2,1)} %copy-done.7), kind=kLoop, calls=%fused_computation.7 | loop fusion | flops 2097152 | bytes 4194304 | tf_op jit(solution)/shard_map/add | solution.py:377
  113.4 0.7 collective-permute-start.4
  114.0 2.6 %collective-permute-start.6 = (f32[128,512]{1,0:T(8,128)S(1)}, f32[128,512]{1,0:T(8,128)S(1)}, u32[]{:S(2)}, u32[]{:S(2)}) collective-permute-start(f32[128,512]{1,0:T(8,128)S(1)} %get-tuple-element.30), channel_id=1, source_target_pairs={{0,192},{16,208},{32,224},{48,240},{64,0},{80,16},{96,32},{112,48}... | collective-permute-start | bytes 786440 | tf_op jit(solution)/shard_map/ppermute | solution.py:366
  116.7 11.0 %collective-permute-start.5 = (f32[128,512]{1,0:T(8,128)S(1)}, f32[128,512]{1,0:T(8,128)S(1)}, u32[]{:S(2)}, u32[]{:S(2)}) collective-permute-start(f32[128,512]{1,0:T(8,128)S(1)} %get-tuple-element.31), channel_id=1, source_target_pairs={{0,128},{16,144},{32,160},{48,176},{64,192},{80,208},{96,224},{112... | collective-permute-start | bytes 786440 | tf_op jit(solution)/shard_map/ppermute | solution.py:366
  127.7 1.7 fusion.1
  129.5 1.5 collective-permute-start.11
  131.1 1.8 collective-permute-start.13
  132.8 1.8 collective-permute-start.12
  134.6 2.8 %collective-permute-done.5 = f32[128,512]{1,0:T(8,128)S(1)} collective-permute-done((f32[128,512]{1,0:T(8,128)S(1)}, f32[128,512]{1,0:T(8,128)S(1)}, u32[]{:S(2)}, u32[]{:S(2)}) %collective-permute-start.5) | collective-permute-done | bytes 262176 | tf_op jit(solution)/shard_map/ppermute | solution.py:366
  137.5 2.5 %collective-permute-done.11 = f32[128,512]{1,0:T(8,128)S(1)} collective-permute-done((f32[128,512]{1,0:T(8,128)S(1)}, f32[128,512]{1,0:T(8,128)S(1)}, u32[]{:S(2)}, u32[]{:S(2)}) %collective-permute-start.11) | collective-permute-done | bytes 262176 | tf_op jit(solution)/shard_map/ppermute | solution.py:358
  140.0 1.7 collective-permute-done.13
  141.7 1.6 collective-permute-done.12
  144.1 5.8 %collective-permute-done.14 = f32[2,64,512]{2,1,0:T(8,128)S(1)} collective-permute-done((f32[2,64,512]{2,1,0:T(8,128)S(1)}, f32[2,64,512]{2,1,0:T(8,128)S(1)}, u32[]{:S(2)}, u32[]{:S(2)}) %collective-permute-start.14) | collective-permute-done | bytes 262176 | tf_op jit(solution)/shard_map/ppermute | solution.py:362
  150.0 4.3 %collective-permute-start.15 = (f32[2,16,512]{2,1,0:T(8,128)S(1)}, f32[2,16,512]{2,1,0:T(8,128)S(1)}, u32[]{:S(2)}, u32[]{:S(2)}) collective-permute-start(f32[2,16,512]{2,1,0:T(8,128)S(1)} %get-tuple-element.35), channel_id=1, source_target_pairs={{0,16},{16,32},{32,48},{48,0},{64,80},{80,96},{96,112},{112,64},{1... | collective-permute-start | bytes 196616 | tf_op jit(solution)/shard_map/ppermute | solution.py:370
  154.2 5.2 %collective-permute-start.16 = (f32[2,16,512]{2,1,0:T(8,128)S(1)}, f32[2,16,512]{2,1,0:T(8,128)S(1)}, u32[]{:S(2)}, u32[]{:S(2)}) collective-permute-start(f32[2,16,512]{2,1,0:T(8,128)S(1)} %get-tuple-element.36), channel_id=1, source_target_pairs={{0,32},{16,48},{32,0},{48,16},{64,96},{80,112},{96,64},{112,80},{1... | collective-permute-start | bytes 196616 | tf_op jit(solution)/shard_map/ppermute | solution.py:370
  159.4 1.8 collective-permute-start.17
  161.3 1.3 collective-permute-done.16
  162.6 3.0 %collective-permute-done.17 = f32[2,16,512]{2,1,0:T(8,128)S(1)} collective-permute-done((f32[2,16,512]{2,1,0:T(8,128)S(1)}, f32[2,16,512]{2,1,0:T(8,128)S(1)}, u32[]{:S(2)}, u32[]{:S(2)}) %collective-permute-start.17) | collective-permute-done | bytes 65568 | tf_op jit(solution)/shard_map/ppermute | solution.py:370
  165.7 4.8 %collective-permute-start.20 = (f32[40,512]{1,0:T(8,128)S(1)}, f32[40,512]{1,0:T(8,128)S(1)}, u32[]{:S(2)}, u32[]{:S(2)}) collective-permute-start(f32[40,512]{1,0:T(8,128)S(1)} %pad_maximum_fusion.2), channel_id=1, source_target_pairs={{0,48},{16,0},{32,16},{48,32},{64,112},{80,64},{96,80},{112,96},{1... | collective-permute-start | bytes 245768 | tf_op jit(solution)/shard_map/ppermute | solution.py:370
  170.7 2.3 %collective-permute-start.18 = (f32[40,512]{1,0:T(8,128)S(1)}, f32[40,512]{1,0:T(8,128)S(1)}, u32[]{:S(2)}, u32[]{:S(2)}) collective-permute-start(f32[40,512]{1,0:T(8,128)S(1)} %pad_maximum_fusion.2), channel_id=1, source_target_pairs={{0,16},{16,32},{32,48},{48,0},{64,80},{80,96},{96,112},{112,64},{1... | collective-permute-start | bytes 245768 | tf_op jit(solution)/shard_map/ppermute | solution.py:370
  172.9 5.2 %collective-permute-done.18 = f32[40,512]{1,0:T(8,128)S(1)} collective-permute-done((f32[40,512]{1,0:T(8,128)S(1)}, f32[40,512]{1,0:T(8,128)S(1)}, u32[]{:S(2)}, u32[]{:S(2)}) %collective-permute-start.18) | collective-permute-done | bytes 81952 | tf_op jit(solution)/shard_map/ppermute | solution.py:370
  178.9 3.2 %collective-permute-start.23 = (f32[136,512]{1,0:T(8,128)S(1)}, f32[136,512]{1,0:T(8,128)S(1)}, u32[]{:S(2)}, u32[]{:S(2)}) collective-permute-start(f32[136,512]{1,0:T(8,128)S(1)} %fusion.19.d0), channel_id=1, source_target_pairs={{0,192},{16,208},{32,224},{48,240},{64,0},{80,16},{96,32},{112,48}... | collective-permute-start | bytes 835592 | tf_op jit(solution)/shard_map/ppermute | solution.py:366
  182.1 1.8 collective-permute-start.22
  184.1 0.8 reshape.59
  184.9 1.2 copy.31
  186.1 3.1 %collective-permute-done.23.d3 = f32[136,512]{1,0:T(8,128)S(1)} collective-permute-done((f32[136,512]{1,0:T(8,128)S(1)}, f32[136,512]{1,0:T(8,128)S(1)}, u32[]{:S(2)}, u32[]{:S(2)}) %collective-permute-start.23) | collective-permute-done | bytes 278560 | tf_op jit(solution)/shard_map/ppermute | solution.py:366
  189.2 1.1 collective-permute-done.22.d2
  190.3 2.9 %collective-permute-done.21.d1 = f32[136,512]{1,0:T(8,128)S(1)} collective-permute-done((f32[136,512]{1,0:T(8,128)S(1)}, f32[136,512]{1,0:T(8,128)S(1)}, u32[]{:S(2)}, u32[]{:S(2)}) %collective-permute-start.21) | collective-permute-done | bytes 278560 | tf_op jit(solution)/shard_map/ppermute | solution.py:366
  193.2 0.7 copy-done.11
  193.9 2.4 %place_grads.1 = (f32[64,3072]{1,0:T(8,128)}, f32[64,1024]{1,0:T(8,128)}, f32[8,128]{1,0:T(8,128)}) custom-call(s32[5]{0:T(128)} %copy-done.2, f32[136,512]{1,0:T(8,128)} %copy-done.8, f32[136,512]{1,0:T(8,128)} %copy-done.11, f32[136,512]{1,0:T(8,128)} %copy-done.10, f32[136,512]{1,0:T(8,128)} %copy-done.9), custom_call_target="tpu_custom_call" | custom-call | tf_op jit(solution)/shard_map/place_grads/pallas_call | solution.py:324
  196.3 1.3 slice_bitcast_fusion.16
  (61 shorter events, 3.7 us)
Async XLA Ops:
  3.9 32.7 %copy-start.5 = (f32[1024]{0:T(1024)S(1)}, f32[1024]{0:T(1024)}, u32[]{:S(2)}) copy-start(f32[1024]{0:T(1024)} %param.9) | copy-start | bytes 12292
  3.9 32.7 %copy-start.6 = (f32[1024]{0:T(1024)S(1)}, f32[1024]{0:T(1024)}, u32[]{:S(2)}) copy-start(f32[1024]{0:T(1024)} %param.8) | copy-start | bytes 12292
  3.9 32.7 %all-to-all-start = ((bf16[16,4,16,1024]{3,2,1,0:T(8,128)(2,1)}), bf16[16,4,16,1024]{3,2,1,0:T(8,128)(2,1)S(1)}, u32[]{:S(2)}, u32[]{:S(2)}) async-start(bf16[16,4,16,1024]{3,2,1,0:T(8,128)(2,1)} %bitcast.110), calls=%async_computation | async-start | bytes 4194304 | tf_op jit(solution)/shard_map/all_to_all | solution.py:412
  10.0 57.1 %copy-start.2 = (s32[5]{0:T(128)}, s32[5]{0:T(128)S(1)}, u32[]{:S(2)}) copy-start(s32[5]{0:T(128)S(1)} %stack.41.place_ref) | copy-start | bytes 64
  36.6 1.6 copy-start.4
  66.9 4.8 %copy-start.1 = (f32[4,4,128,512]{3,2,1,0:T(8,128)}, f32[4,4,128,512]{3,2,1,0:T(8,128)S(1)}, u32[]{:S(2)}) copy-start(f32[4,4,128,512]{3,2,1,0:T(8,128)S(1)} %get-tuple-element.15) | copy-start | bytes 12582916
  66.9 4.8 %collective-permute-start = (bf16[4,4,128,512]{3,2,1,0:T(8,128)(2,1)S(1)}, bf16[4,4,128,512]{3,2,1,0:T(8,128)(2,1)S(1)}, u32[]{:S(2)}, u32[]{:S(2)}) collective-permute-start(bf16[4,4,128,512]{3,2,1,0:T(8,128)(2,1)S(1)} %get-tuple-element.16), channel_id=1, source_target_pairs={{0,1},{1,0},{2,3},{3,2},{4,5},{5,4},{6,7},{7,6},{8,9},{9,8},{10,11... | collective-permute-start | bytes 6291464 | tf_op jit(solution)/shard_map/ppermute | solution.py:354
  71.3 2.2 %copy-start = (f32[4,4,128,512]{3,2,1,0:T(8,128)}, f32[4,4,128,512]{3,2,1,0:T(8,128)S(1)}, u32[]{:S(2)}) copy-start(f32[4,4,128,512]{3,2,1,0:T(8,128)S(1)} %get-tuple-element.18) | copy-start | bytes 12582916
  71.3 24.4 %collective-permute-start.7 = (bf16[4,4,128,512]{3,2,1,0:T(8,128)(2,1)}, bf16[4,4,128,512]{3,2,1,0:T(8,128)(2,1)}, u32[]{:S(2)}, u32[]{:S(2)}) collective-permute-start(bf16[4,4,128,512]{3,2,1,0:T(8,128)(2,1)} %get-tuple-element.19), channel_id=1, source_target_pairs={{0,1},{1,0},{2,3},{3,2},{4,5},{5,4},{6,7},{7,6},{8,9},{9,8},{10,11... | collective-permute-start | bytes 6291464 | tf_op jit(solution)/shard_map/ppermute | solution.py:354
  71.7 2.4 %copy-start.7 = (bf16[4,4,128,512]{3,2,1,0:T(8,128)(2,1)}, bf16[4,4,128,512]{3,2,1,0:T(8,128)(2,1)S(1)}, u32[]{:S(2)}) copy-start(bf16[4,4,128,512]{3,2,1,0:T(8,128)(2,1)S(1)} %collective-permute-done) | copy-start | bytes 6291460
  74.2 33.9 %collective-permute-start.1 = (bf16[4,128,512]{2,1,0:T(8,128)(2,1)}, bf16[4,128,512]{2,1,0:T(8,128)(2,1)}, u32[]{:S(2)}, u32[]{:S(2)}) collective-permute-start(bf16[4,128,512]{2,1,0:T(8,128)(2,1)} %get-tuple-element.23), channel_id=1, source_target_pairs={{0,4},{1,5},{2,6},{3,7},{4,8},{5,9},{6,10},{7,11},{8,12},{9,13},{1... | collective-permute-start | bytes 1572872 | tf_op jit(solution)/shard_map/ppermute | solution.py:358
  74.2 36.9 %collective-permute-start.3 = (bf16[4,128,512]{2,1,0:T(8,128)(2,1)S(1)}, bf16[4,128,512]{2,1,0:T(8,128)(2,1)}, u32[]{:S(2)}, u32[]{:S(2)}) collective-permute-start(bf16[4,128,512]{2,1,0:T(8,128)(2,1)S(1)} %get-tuple-element.24), channel_id=1, source_target_pairs={{0,12},{1,13},{2,14},{3,15},{4,0},{5,1},{6,2},{7,3},{8,4},{9,5},{1... | collective-permute-start | bytes 1572872 | tf_op jit(solution)/shard_map/ppermute | solution.py:358
  77.4 33.7 %collective-permute-start.2 = (bf16[4,128,512]{2,1,0:T(8,128)(2,1)S(1)}, bf16[4,128,512]{2,1,0:T(8,128)(2,1)}, u32[]{:S(2)}, u32[]{:S(2)}) collective-permute-start(bf16[4,128,512]{2,1,0:T(8,128)(2,1)S(1)} %get-tuple-element.25), channel_id=1, source_target_pairs={{0,8},{1,9},{2,10},{3,11},{4,12},{5,13},{6,14},{7,15},{8,0},{9,1},... | collective-permute-start | bytes 1572872 | tf_op jit(solution)/shard_map/ppermute | solution.py:358
  77.7 2.8 %copy-start.3 = (bf16[1024,3072]{1,0:T(8,128)(2,1)S(1)}, bf16[1024,3072]{1,0:T(8,128)(2,1)}, u32[]{:S(2)}) copy-start(bf16[1024,3072]{1,0:T(8,128)(2,1)} %wqkv_ref.3) | copy-start | bytes 18874372
  89.8 71.4 %all-to-all-start.1 = ((bf16[16,16,2176]{2,1,0:T(8,128)(2,1)}), bf16[16,16,2176]{2,1,0:T(8,128)(2,1)S(1)}, u32[]{:S(2)}, u32[]{:S(2)}) async-start(bf16[16,16,2176]{2,1,0:T(8,128)(2,1)} %video_grads.1), calls=%async_computation.1 | async-start | bytes 2228224 | tf_op jit(solution)/shard_map/all_to_all | solution.py:416
  98.6 18.1 %collective-permute-start.8 = (bf16[4,128,512]{2,1,0:T(8,128)(2,1)S(1)}, bf16[4,128,512]{2,1,0:T(8,128)(2,1)S(1)}, u32[]{:S(2)}, u32[]{:S(2)}) collective-permute-start(bf16[4,128,512]{2,1,0:T(8,128)(2,1)S(1)} %get-tuple-element.26), channel_id=1, source_target_pairs={{0,64},{16,80},{32,96},{48,112},{64,128},{80,144},{96,160},{112,17... | collective-permute-start | bytes 1572872 | tf_op jit(solution)/shard_map/ppermute | solution.py:366
  100.2 27.5 %collective-permute-start.10 = (bf16[4,128,512]{2,1,0:T(8,128)(2,1)S(1)}, bf16[4,128,512]{2,1,0:T(8,128)(2,1)S(1)}, u32[]{:S(2)}, u32[]{:S(2)}) collective-permute-start(bf16[4,128,512]{2,1,0:T(8,128)(2,1)S(1)} %get-tuple-element.27), channel_id=1, source_target_pairs={{0,192},{16,208},{32,224},{48,240},{64,0},{80,16},{96,32},{112,48}... | collective-permute-start | bytes 1572872 | tf_op jit(solution)/shard_map/ppermute | solution.py:366
  108.1 19.6 %collective-permute-start.9 = (bf16[4,128,512]{2,1,0:T(8,128)(2,1)S(1)}, bf16[4,128,512]{2,1,0:T(8,128)(2,1)S(1)}, u32[]{:S(2)}, u32[]{:S(2)}) collective-permute-start(bf16[4,128,512]{2,1,0:T(8,128)(2,1)S(1)} %get-tuple-element.28), channel_id=1, source_target_pairs={{0,128},{16,144},{32,160},{48,176},{64,192},{80,208},{96,224},{112... | collective-permute-start | bytes 1572872 | tf_op jit(solution)/shard_map/ppermute | solution.py:366
  113.4 19.5 %collective-permute-start.4 = (f32[128,512]{1,0:T(8,128)S(1)}, f32[128,512]{1,0:T(8,128)S(1)}, u32[]{:S(2)}, u32[]{:S(2)}) collective-permute-start(f32[128,512]{1,0:T(8,128)S(1)} %get-tuple-element.29), channel_id=1, source_target_pairs={{0,64},{16,80},{32,96},{48,112},{64,128},{80,144},{96,160},{112,17... | collective-permute-start | bytes 786440 | tf_op jit(solution)/shard_map/ppermute | solution.py:366
  114.0 20.6 %collective-permute-start.6 = (f32[128,512]{1,0:T(8,128)S(1)}, f32[128,512]{1,0:T(8,128)S(1)}, u32[]{:S(2)}, u32[]{:S(2)}) collective-permute-start(f32[128,512]{1,0:T(8,128)S(1)} %get-tuple-element.30), channel_id=1, source_target_pairs={{0,192},{16,208},{32,224},{48,240},{64,0},{80,16},{96,32},{112,48}... | collective-permute-start | bytes 786440 | tf_op jit(solution)/shard_map/ppermute | solution.py:366
  116.7 20.7 %collective-permute-start.5 = (f32[128,512]{1,0:T(8,128)S(1)}, f32[128,512]{1,0:T(8,128)S(1)}, u32[]{:S(2)}, u32[]{:S(2)}) collective-permute-start(f32[128,512]{1,0:T(8,128)S(1)} %get-tuple-element.31), channel_id=1, source_target_pairs={{0,128},{16,144},{32,160},{48,176},{64,192},{80,208},{96,224},{112... | collective-permute-start | bytes 786440 | tf_op jit(solution)/shard_map/ppermute | solution.py:366
  129.5 10.4 %collective-permute-start.11 = (f32[128,512]{1,0:T(8,128)S(1)}, f32[128,512]{1,0:T(8,128)S(1)}, u32[]{:S(2)}, u32[]{:S(2)}) collective-permute-start(f32[128,512]{1,0:T(8,128)S(1)} %get-tuple-element.32), channel_id=1, source_target_pairs={{0,4},{1,5},{2,6},{3,7},{4,8},{5,9},{6,10},{7,11},{8,12},{9,13},{1... | collective-permute-start | bytes 786440 | tf_op jit(solution)/shard_map/ppermute | solution.py:358
  131.1 10.6 %collective-permute-start.13 = (f32[128,512]{1,0:T(8,128)S(1)}, f32[128,512]{1,0:T(8,128)S(1)}, u32[]{:S(2)}, u32[]{:S(2)}) collective-permute-start(f32[128,512]{1,0:T(8,128)S(1)} %get-tuple-element.33), channel_id=1, source_target_pairs={{0,12},{1,13},{2,14},{3,15},{4,0},{5,1},{6,2},{7,3},{8,4},{9,5},{1... | collective-permute-start | bytes 786440 | tf_op jit(solution)/shard_map/ppermute | solution.py:358
  132.8 10.5 %collective-permute-start.12 = (f32[128,512]{1,0:T(8,128)S(1)}, f32[128,512]{1,0:T(8,128)S(1)}, u32[]{:S(2)}, u32[]{:S(2)}) collective-permute-start(f32[128,512]{1,0:T(8,128)S(1)} %get-tuple-element.34), channel_id=1, source_target_pairs={{0,8},{1,9},{2,10},{3,11},{4,12},{5,13},{6,14},{7,15},{8,0},{9,1},... | collective-permute-start | bytes 786440 | tf_op jit(solution)/shard_map/ppermute | solution.py:358
  143.4 6.5 %collective-permute-start.14 = (f32[2,64,512]{2,1,0:T(8,128)S(1)}, f32[2,64,512]{2,1,0:T(8,128)S(1)}, u32[]{:S(2)}, u32[]{:S(2)}) collective-permute-start(f32[2,64,512]{2,1,0:T(8,128)S(1)} %pad_maximum_fusion.1), channel_id=1, source_target_pairs={{0,2},{1,3},{2,0},{3,1},{4,6},{5,7},{6,4},{7,5},{8,10},{9,11},{10,... | collective-permute-start | bytes 786440 | tf_op jit(solution)/shard_map/ppermute | solution.py:362
  150.0 11.3 %collective-permute-start.15 = (f32[2,16,512]{2,1,0:T(8,128)S(1)}, f32[2,16,512]{2,1,0:T(8,128)S(1)}, u32[]{:S(2)}, u32[]{:S(2)}) collective-permute-start(f32[2,16,512]{2,1,0:T(8,128)S(1)} %get-tuple-element.35), channel_id=1, source_target_pairs={{0,16},{16,32},{32,48},{48,0},{64,80},{80,96},{96,112},{112,64},{1... | collective-permute-start | bytes 196616 | tf_op jit(solution)/shard_map/ppermute | solution.py:370
  154.2 8.4 %collective-permute-start.16 = (f32[2,16,512]{2,1,0:T(8,128)S(1)}, f32[2,16,512]{2,1,0:T(8,128)S(1)}, u32[]{:S(2)}, u32[]{:S(2)}) collective-permute-start(f32[2,16,512]{2,1,0:T(8,128)S(1)} %get-tuple-element.36), channel_id=1, source_target_pairs={{0,32},{16,48},{32,0},{48,16},{64,96},{80,112},{96,64},{112,80},{1... | collective-permute-start | bytes 196616 | tf_op jit(solution)/shard_map/ppermute | solution.py:370
  159.4 6.2 %collective-permute-start.17 = (f32[2,16,512]{2,1,0:T(8,128)S(1)}, f32[2,16,512]{2,1,0:T(8,128)S(1)}, u32[]{:S(2)}, u32[]{:S(2)}) collective-permute-start(f32[2,16,512]{2,1,0:T(8,128)S(1)} %get-tuple-element.37), channel_id=1, source_target_pairs={{0,48},{16,0},{32,16},{48,32},{64,112},{80,64},{96,80},{112,96},{1... | collective-permute-start | bytes 196616 | tf_op jit(solution)/shard_map/ppermute | solution.py:370
  165.7 13.2 %collective-permute-start.20 = (f32[40,512]{1,0:T(8,128)S(1)}, f32[40,512]{1,0:T(8,128)S(1)}, u32[]{:S(2)}, u32[]{:S(2)}) collective-permute-start(f32[40,512]{1,0:T(8,128)S(1)} %pad_maximum_fusion.2), channel_id=1, source_target_pairs={{0,48},{16,0},{32,16},{48,32},{64,112},{80,64},{96,80},{112,96},{1... | collective-permute-start | bytes 245768 | tf_op jit(solution)/shard_map/ppermute | solution.py:370
  170.5 8.3 %collective-permute-start.19 = (f32[40,512]{1,0:T(8,128)S(1)}, f32[40,512]{1,0:T(8,128)S(1)}, u32[]{:S(2)}, u32[]{:S(2)}) collective-permute-start(f32[40,512]{1,0:T(8,128)S(1)} %pad_maximum_fusion.2), channel_id=1, source_target_pairs={{0,32},{16,48},{32,0},{48,16},{64,96},{80,112},{96,64},{112,80},{1... | collective-permute-start | bytes 245768 | tf_op jit(solution)/shard_map/ppermute | solution.py:370
  170.7 7.5 %collective-permute-start.18 = (f32[40,512]{1,0:T(8,128)S(1)}, f32[40,512]{1,0:T(8,128)S(1)}, u32[]{:S(2)}, u32[]{:S(2)}) collective-permute-start(f32[40,512]{1,0:T(8,128)S(1)} %pad_maximum_fusion.2), channel_id=1, source_target_pairs={{0,16},{16,32},{32,48},{48,0},{64,80},{80,96},{96,112},{112,64},{1... | collective-permute-start | bytes 245768 | tf_op jit(solution)/shard_map/ppermute | solution.py:370
  178.9 6.0 %copy-start.8 = (f32[136,512]{1,0:T(8,128)}, f32[136,512]{1,0:T(8,128)S(1)}, u32[]{:S(2)}) copy-start(f32[136,512]{1,0:T(8,128)S(1)} %fusion.19.d0) | copy-start | bytes 835588
  178.9 10.3 %collective-permute-start.23 = (f32[136,512]{1,0:T(8,128)S(1)}, f32[136,512]{1,0:T(8,128)S(1)}, u32[]{:S(2)}, u32[]{:S(2)}) collective-permute-start(f32[136,512]{1,0:T(8,128)S(1)} %fusion.19.d0), channel_id=1, source_target_pairs={{0,192},{16,208},{32,224},{48,240},{64,0},{80,16},{96,32},{112,48}... | collective-permute-start | bytes 835592 | tf_op jit(solution)/shard_map/ppermute | solution.py:366
  182.1 8.2 %collective-permute-start.22 = (f32[136,512]{1,0:T(8,128)S(1)}, f32[136,512]{1,0:T(8,128)S(1)}, u32[]{:S(2)}, u32[]{:S(2)}) collective-permute-start(f32[136,512]{1,0:T(8,128)S(1)} %fusion.19.d0), channel_id=1, source_target_pairs={{0,128},{16,144},{32,160},{48,176},{64,192},{80,208},{96,224},{112... | collective-permute-start | bytes 835592 | tf_op jit(solution)/shard_map/ppermute | solution.py:366
  183.9 9.2 %collective-permute-start.21 = (f32[136,512]{1,0:T(8,128)S(1)}, f32[136,512]{1,0:T(8,128)S(1)}, u32[]{:S(2)}, u32[]{:S(2)}) collective-permute-start(f32[136,512]{1,0:T(8,128)S(1)} %fusion.19.d0), channel_id=1, source_target_pairs={{0,64},{16,80},{32,96},{48,112},{64,128},{80,144},{96,160},{112,17... | collective-permute-start | bytes 835592 | tf_op jit(solution)/shard_map/ppermute | solution.py:366
  189.2 4.0 %copy-start.9 = (f32[136,512]{1,0:T(8,128)}, f32[136,512]{1,0:T(8,128)S(1)}, u32[]{:S(2)}) copy-start(f32[136,512]{1,0:T(8,128)S(1)} %collective-permute-done.23.d3) | copy-start | bytes 835588
  190.3 2.9 %copy-start.10 = (f32[136,512]{1,0:T(8,128)}, f32[136,512]{1,0:T(8,128)S(1)}, u32[]{:S(2)}) copy-start(f32[136,512]{1,0:T(8,128)S(1)} %collective-permute-done.22.d2) | copy-start | bytes 835588
  193.2 0.7 copy-start.11

commit v3 on v2

--- a/solution.py
+++ b/solution.py
@@ -31,16 +31,15 @@
 
 
 def block_row(block, place):
-    x, h, y, z, core = place
-    dh = (block % 4 - h) % 4
-    dcore = (block // 4 % 2 - core) % 2
-    dz = (block // 8 % 2 - z) % 2
-    dy = (block // 16 - y) % 4
-    return pl.multiple_of((((dcore * 4 + dy) * 2 + dz) * 4 + dh) * 16, 16)
+    x, y, z, core = place
+    dcore = (block % 2 - core) % 2
+    dz = (block // 2 % 2 - z) % 2
+    dy = (block // 4 - y) % 4
+    return pl.multiple_of(((dcore * 4 + dy) * 2 + dz) * 64, 64)
 
 
 def read_place(place_ref):
-    return tuple(place_ref[i] for i in range(5))
+    return tuple(place_ref[i] for i in range(4))
 
 
 def whiten(xh):
@@ -86,9 +85,9 @@
         cols = slice(n * CHUNK, (n + 1) * CHUNK)
         datt_s[:, cols] = dot_nt(right_s[:, 3 * width:], wout_ref[cols, :]).astype(BF16)
         turned = normed_s[:, cols].T
-        for b in range(CHUNK // 16):
-            at = block_row(n * (CHUNK // 16) + b, place)
-            left_s[0, pl.ds(at, 16), :] = turned[b * 16:(b + 1) * 16]
+        for b in range(CHUNK // 64):
+            at = block_row(n * (CHUNK // 64) + b, place)
+            left_s[0, pl.ds(at, 64), :] = turned[b * 64:(b + 1) * 64]
 
     lane = lax.broadcasted_iota(jnp.int32, (part, 128), 1)
     first = lane < 64
@@ -120,8 +119,8 @@
         inner = jnp.sum(dp * probs, axis=1, keepdims=True)
         ds = (probs * (dp - inner) * 0.125).astype(BF16).reshape(2, part, part)
         attended = dot_tn(v2, low.reshape(2 * part, part)).astype(BF16)
-        for b in range(8):
-            left_s[1, pl.ds(block_row(hp * 8 + b, place), 16), tok] = attended[b * 16:(b + 1) * 16]
+        for b in range(2):
+            left_s[1, pl.ds(block_row(hp * 2 + b, place), 64), tok] = attended[b * 64:(b + 1) * 64]
         right_s[tok, pl.ds(col, 128)] = dot_tn(ds.reshape(2 * part, part), k2).astype(BF16)
         right_s[tok, pl.ds(width + col, 128)] = dot_nn(
             jnp.concatenate([ds[0], ds[1]], axis=1), split(q)
@@ -297,26 +296,24 @@
     )(tokens, gain, right, wqkv)
 
 
-def place_kernel(scale, place_ref, d0, d1, d2, d3, qkv_ref, out_ref, small_ref):
-    x, h = place_ref[0], place_ref[1]
+def place_kernel(scale, place_ref, d0, d1, d2, d3, qkv_ref, out_ref, gain_ref, bias_ref):
+    x = place_ref[0]
     small = jnp.zeros((8, 128), F32)
     for j, d in enumerate((d0, d1, d2, d3)):
         block = (x - j) % 4
-        for k in range(4):
-            rows = pl.ds(pl.multiple_of((h - k) % 4 * 16, 16), 16)
-            qkv_ref[rows, chunk(block)] = d[k * 32:k * 32 + 16, :] * scale
-            b = d[k * 32 + 16:k * 32 + 32, :] * scale
-
-            @pl.when(block < 2)
-            def _():
-                qkv_ref[rows, chunk(4 + block)] = b
-
-            @pl.when(block >= 2)
-            def _():
-                out_ref[rows, chunk(block - 2)] = b
+        qkv_ref[:, chunk(block)] = d[:64, :] * scale
+
+        @pl.when(block < 2)
+        def _():
+            qkv_ref[:, chunk(4 + block)] = d[64:128, :] * scale
+
+        @pl.when(block >= 2)
+        def _():
+            out_ref[:, chunk(block - 2)] = d[64:128, :] * scale
 
         small = small + d[128:136, :128] * scale
-    small_ref[...] = small
+    gain_ref[...] = small[:1, :64]
+    bias_ref[...] = small[:1, 64:]
 
 
 def run_place(place, scale, pieces):
@@ -326,10 +323,11 @@
         out_shape=(
             jax.ShapeDtypeStruct((64, 6 * CHUNK), F32),
             jax.ShapeDtypeStruct((64, 2 * CHUNK), F32),
-            jax.ShapeDtypeStruct((8, 128), F32),
+            jax.ShapeDtypeStruct((1, 64), F32),
+            jax.ShapeDtypeStruct((1, 64), F32),
         ),
         in_specs=[pl.BlockSpec(memory_space=pltpu.SMEM)] + [vm] * 4,
-        out_specs=(vm,) * 3,
+        out_specs=(vm,) * 4,
         name="place_grads",
     )(place, *pieces)
 
@@ -370,34 +368,29 @@
     return lax.ppermute(a, "dp", dp_pairs(lambda x, h: (x, h + k)))
 
 
-def reduce_ring(piece, go, dtype):
-    got = [go(piece(k).astype(dtype), k) for k in range(1, 4)]
-    total = piece(0)
+def combine(own, got):
     for part in got:
-        total = total + part.astype(F32)
-    return total
-
-
-def reduce_grads(send_a, keep_a, send_b, keep_b, small):
-    got_a = go_core(send_a)
-    got_b = go_core(send_b)
-    a = reduce_ring(lambda k: keep_a[k] + got_a[k].astype(F32), go_y, BF16)
-    b = reduce_ring(lambda k: keep_b[k] + got_b[k].astype(F32), go_x, BF16)
-    a = reduce_second(a, go_x)
-    b = reduce_second(b, go_y)
-    away = jnp.stack([a[64:], b[64:]])
-    both = jnp.stack([a[:64], b[:64]]) + go_z(away)
-    both = both.reshape(2, 4, 16, CHUNK)
-    both = reduce_ring(lambda k: both[:, k], go_h, F32)
-    message = jnp.concatenate([both.reshape(32, CHUNK), small], axis=0)
-    got = [message] + [go_h(message, k) for k in range(1, 4)]
-    small = got[0][32:] + got[1][32:] + got[2][32:] + got[3][32:]
-    message = jnp.concatenate([g[:32] for g in got] + [small], axis=0)
-    return [message] + [go_x(message, k) for k in range(1, 4)]
-
-
-def reduce_second(total, go):
-    return reduce_ring(lambda k: total[k], go, F32)
+        own = own + part.astype(F32)
+    return own
+
+
+def exchange(pieces, go):
+    return [go(pieces[k], k) for k in range(1, 4)]
+
+
+def first_pieces(keep, got):
+    own = keep[0] + got[0].astype(F32)
+    return [own] + [(keep[k] + got[k].astype(F32)).astype(BF16) for k in range(1, 4)]
+
+
+def second_pieces(total):
+    return [total[0]] + [total[k].astype(BF16) for k in range(1, 4)]
+
+
+def three_terms(value):
+    hi = lax.reduce_precision(value, 8, 7)
+    mid = lax.reduce_precision(value - hi, 8, 7)
+    return jnp.concatenate([hi, mid, value - hi - mid], axis=0)
 
 
 def local(video, cotangent, norm_gain, norm_bias, qkv_weight, out_weight):
@@ -405,22 +398,41 @@
     grad_scale = 1.0 / math.sqrt(clips * positions * 256)
     frame = lax.axis_index("frame")
     dp = lax.axis_index("dp")
-    place = jnp.stack([dp // 4, dp % 4, frame // 4, frame // 2 % 2, frame % 2]).astype(jnp.int32)
+    place = jnp.stack([dp // 4, frame // 4, frame // 2 % 2, frame % 2]).astype(jnp.int32)
     gain = norm_gain.reshape(1, width)
     bias = norm_bias.reshape(1, width)
     tokens = jnp.concatenate([video, cotangent], axis=0).reshape(2 * clips, 16, positions // 16, width)
     tokens = lax.all_to_all(tokens.transpose(1, 0, 2, 3), "frame", 0, 0, tiled=True)
+
     send_a, keep_a, left, right = run_main(place, tokens, gain, bias, qkv_weight, out_weight)
     send_b, keep_b = run_grads(place, left, right)
+    pieces_a = first_pieces(keep_a, go_core(send_a))
+    pieces_b = first_pieces(keep_b, go_core(send_b))
+    got_a = exchange(pieces_a, go_y)
+    right, pieces_b = lax.optimization_barrier((right, pieces_b))
+    got_b = exchange(pieces_b, go_x)
+
     back = run_back(tokens, gain, right, qkv_weight)
     back = lax.all_to_all(back, "frame", 0, 0, tiled=True)
     grad_video = back[:, :, : clips * width].reshape(positions, clips, width)
     grad_video = grad_video.transpose(1, 0, 2).reshape(video.shape)
-    small = jnp.sum(back[:, :3, clips * width :].astype(F32), axis=(0, 1))
-    small = jnp.pad(small.reshape(1, 128), ((0, 7), (0, CHUNK - 128)))
-    pieces = reduce_grads(send_a, keep_a, send_b, keep_b, small)
-    grad_qkv, grad_out, small = run_place(place, grad_scale, pieces)
-    return grad_video, grad_qkv, grad_out, small[0, :64], small[0, 64:]
+    small = jnp.sum(back[:, :3, clips * width :].astype(F32), axis=(0, 1)).reshape(1, 128)
+
+    got_a, got_b[0], got_b[2] = lax.optimization_barrier((got_a, got_b[0], got_b[2]))
+    pieces_a = second_pieces(combine(pieces_a[0], got_a))
+    pieces_b = second_pieces(combine(pieces_b[0], got_b))
+    got_a = exchange(pieces_a, go_x)
+    got_b = exchange(pieces_b, go_y)
+    a = combine(pieces_a[0], got_a)
+    b = combine(pieces_b[0], got_b)
+    own = jnp.concatenate([a[:64], b[:64]], axis=0) + go_z(jnp.concatenate([a[64:], b[64:]], axis=0))
+    own = jnp.concatenate([own, jnp.pad(three_terms(small), ((0, 13), (0, CHUNK - 128)))], axis=0)
+    own = combine(own, exchange([own.astype(BF16)] * 4, go_h))
+    small = jnp.sum(own[128:131], axis=0, keepdims=True)
+    own = jnp.concatenate([own[:128], jnp.pad(small, ((0, 7), (0, 0)))], axis=0)
+    pieces = [own] + exchange([own] * 4, go_x)
+    grad_qkv, grad_out, total_gain, total_bias = run_place(place, grad_scale, pieces)
+    return grad_video, grad_qkv, grad_out, total_gain.reshape(64), total_bias.reshape(64)
 
 
 def solution(mesh):

time: 199 us -> 187 us (0.940)
  starting transfers between devices: 66.2 us -> 41.1 us
  waiting for transfers between devices: 64.4 us -> 84.4 us
  Pallas kernels: 44.6 us -> 41.9 us
  local copies, waits for them, and re-layouts: 11 us -> 8.44 us
    ppermute x6, waiting for transfers between devices: 12 us -> 26.7 us  [go_y(): return lax.ppermute(a, 'frame', frame_pairs(lambda y, z, c: (y + k, z, c)))]
    ppermute x9, starting transfers between devices: 25.7 us -> 12.9 us  [go_x(): return lax.ppermute(a, 'dp', dp_pairs(lambda x, h: (x + k, h)))]
    ppermute x6 -> x3, starting transfers between devices: 18.5 us -> 9.3 us  [go_h(): return lax.ppermute(a, 'dp', dp_pairs(lambda x, h: (x, h + k)))]
    another operation x1 -> x3, other arithmetic: 0.02 us -> 4.01 us  [reduce_grads(): away = jnp.stack([a[64:], b[64:]])]
    add x6 -> x4, other arithmetic: 4.15 us -> 0.24 us  [the longest x3 0.2 us: combine(): own = own + part.astype(F32)]
    ppermute x9, waiting for transfers between devices: 9.81 us -> 13.5 us  [go_x(): return lax.ppermute(a, 'dp', dp_pairs(lambda x, h: (x + k, h)))]
    ppermute x2, waiting for transfers between devices: 0.01 us -> 2.12 us  [go_core(): return lax.ppermute(a, 'frame', frame_pairs(lambda y, z, c: (y, z, c + 1)))]
    pallas_call x1, Pallas kernels: 28.7 us -> 26.6 us  [run_main(): pl.pallas_call(main_kernel, out_shape=(jax.ShapeDtypeStruct(piece, BF16),...]
  transfers between devices with their start and end apart: 26 -> 23, of which waited for: 14 -> 13; matrix products, arithmetic and copies ran while one was open for 6% -> 5% of each run, Pallas kernels for 7% -> 7%
where the time goes in v3:
time: 187 us; the launch traced here: 186 us
  waiting for transfers between devices  84.4 us (45%)
  Pallas kernels  41.9 us (22%)
  starting transfers between devices  41.1 us (22%)
  other arithmetic  9.38 us (5%)
  local copies, waits for them, and re-layouts  8.44 us (5%)
    ppermute x6, waiting for transfers between devices, go_y(): return lax.ppermute(a, 'frame', frame_pairs(lambda y, z, c: (y + k, z, c)))  26.7 us
    pallas_call x1, Pallas kernels, run_main(): pl.pallas_call(main_kernel, out_shape=(jax.ShapeDtypeStruct(piece, BF16),...  26.6 us
    all_to_all x1, waiting for transfers between devices, local(): lax.all_to_all(tokens.transpose(1, 0, 2, 3), 'frame', 0, 0, tiled=True)  26.6 us
    ppermute x9, waiting for transfers between devices, go_x(): return lax.ppermute(a, 'dp', dp_pairs(lambda x, h: (x + k, h)))  13.5 us
    ppermute x9, starting transfers between devices, go_x(): return lax.ppermute(a, 'dp', dp_pairs(lambda x, h: (x + k, h)))  12.9 us
    ppermute x3, waiting for transfers between devices, go_h(): return lax.ppermute(a, 'dp', dp_pairs(lambda x, h: (x, h + k)))  9.7 us
    pallas_call x1, Pallas kernels, run_back(): pl.pallas_call(back_kernel, grid=(1,), out_shape=jax.ShapeDtypeStruct(mes...  9.3 us
    ppermute x3, starting transfers between devices, go_h(): return lax.ppermute(a, 'dp', dp_pairs(lambda x, h: (x, h + k)))  9.3 us
  transfers between devices with their start and end apart: 23, of which 13 were waited for; matrix products, arithmetic and copies ran while one was open for 5% of the time, Pallas kernels for 7%

profile of v3, /device:TPU:32, one launch (start us, length us, event | category | flops | bytes accessed | tf_op | source)
XLA Modules:
  0.0 186.1 jit_solution(13811207822229122746)
XLA Ops:
  0.6 1.7 pad_maximum_fusion
  2.4 1.5 copy.18
  3.9 6.1 %all-to-all-start = ((bf16[16,4,16,1024]{3,2,1,0:T(8,128)(2,1)}), bf16[16,4,16,1024]{3,2,1,0:T(8,128)(2,1)S(1)}, u32[]{:S(2)}, u32[]{:S(2)}) async-start(bf16[16,4,16,1024]{3,2,1,0:T(8,128)(2,1)} %bitcast.87), calls=%async_computation | async-start | bytes 4194304 | tf_op jit(solution)/shard_map/all_to_all | solution.py:405
  10.0 26.6 %all-to-all-done.tokens_ref = bf16[16,4,16,1024]{3,2,1,0:T(8,128)(2,1)S(1)} async-done(((bf16[16,4,16,1024]{3,2,1,0:T(8,128)(2,1)}), bf16[16,4,16,1024]{3,2,1,0:T(8,128)(2,1)S(1)}, u32[]{:S(2)}, u32[]{:S(2)}) %all-to-all-start) | async-done | bytes 2097184 | tf_op jit(solution)/shard_map/all_to_all | solution.py:405
  36.6 1.6 copy-done.2
  38.2 26.6 %sublayer.1 = (bf16[4,4,128,512]{3,2,1,0:T(8,128)(2,1)S(1)}, f32[4,4,128,512]{3,2,1,0:T(8,128)S(1)}, bf16[2,1024,512]{2,1,0:T(8,128)(2,1)S(1)}, bf16[512,4096]{1,0:T(8,128)(2,1)S(1)}) custom-call(s32[4]{0:T(128)S(1)} %pad_add_fusion.place_ref, bf16[16,4,16,1024]{3,2,1,0:T(8,128)(2,1)S(1)} %all-to-all-done.tokens_ref, f32[1,1024]{1,0:T(1,128)S(1)} %bitcast.85, ...), custom_call_target="tpu_custom_call" | custom-call | flops 12884901888 | bytes 20971520 | tf_op jit(solution)/shard_map/sublayer/pallas_call | solution.py:162
  65.1 3.7 %weight_grads.1 = (bf16[4,4,128,512]{3,2,1,0:T(8,128)(2,1)S(1)}, f32[4,4,128,512]{3,2,1,0:T(8,128)S(1)}) custom-call(s32[4]{0:T(128)S(1)} %pad_add_fusion.place_ref, bf16[2,1024,512]{2,1,0:T(8,128)(2,1)S(1)} %get-tuple-element.26.left_ref, bf16[512,4096]{1,0:T(8,128)(2,1)S(1)} %get-tuple-element.29.right_ref.dpk_ref), custom_call_target="tpu_custom_call" | custom-call | flops 2147483648 | bytes 12582912 | tf_op jit(solution)/shard_map/weight_grads/pallas_call | solution.py:199
  68.8 2.0 %copy-done.5 = bf16[512,4096]{1,0:T(8,128)(2,1)} copy-done((bf16[512,4096]{1,0:T(8,128)(2,1)}, bf16[512,4096]{1,0:T(8,128)(2,1)S(1)}, u32[]{:S(2)}) %copy-start.5) | copy-done | bytes 4194328
  71.2 1.6 fusion.7
  72.8 2.1 %collective-permute-done = bf16[4,4,128,512]{3,2,1,0:T(8,128)(2,1)S(1)} collective-permute-done((bf16[4,4,128,512]{3,2,1,0:T(8,128)(2,1)S(1)}, bf16[4,4,128,512]{3,2,1,0:T(8,128)(2,1)S(1)}, u32[]{:S(2)}, u32[]{:S(2)}) %collective-permute-start) | collective-permute-done | bytes 2097184 | tf_op jit(solution)/shard_map/ppermute | solution.py:352
  75.0 1.7 fusion.4
  76.7 1.6 collective-permute-start.3
  78.3 0.7 collective-permute-start.4
  79.0 1.5 collective-permute-start.5
  80.5 1.7 collective-permute-start.6
  82.2 17.1 %collective-permute-done.2 = bf16[4,128,512]{2,1,0:T(8,128)(2,1)} collective-permute-done((bf16[4,128,512]{2,1,0:T(8,128)(2,1)S(1)}, bf16[4,128,512]{2,1,0:T(8,128)(2,1)}, u32[]{:S(2)}, u32[]{:S(2)}) %collective-permute-start.2) | collective-permute-done | bytes 524320 | tf_op jit(solution)/shard_map/ppermute | solution.py:356
  99.3 3.0 %collective-permute-start.10 = (bf16[4,128,512]{2,1,0:T(8,128)(2,1)}, bf16[4,128,512]{2,1,0:T(8,128)(2,1)}, u32[]{:S(2)}, u32[]{:S(2)}) collective-permute-start(bf16[4,128,512]{2,1,0:T(8,128)(2,1)} %get-tuple-element.39), channel_id=1, source_target_pairs={{0,128},{16,144},{32,160},{48,176},{64,192},{80,208},{96,224},{112... | collective-permute-start | bytes 1572872 | tf_op jit(solution)/shard_map/ppermute | solution.py:364
  102.4 9.3 %video_grads.1 = bf16[16,16,2176]{2,1,0:T(8,128)(2,1)} custom-call(bf16[16,4,16,1024]{3,2,1,0:T(8,128)(2,1)S(1)} %all-to-all-done.tokens_ref, f32[1,1024]{1,0:T(1,128)S(1)} %bitcast.86, bf16[512,4096]{1,0:T(8,128)(2,1)S(1)} %copy-done.6, bf16[1024,3072]{1,0:T(8,128)(2,1)S(1)} %bitcast.83), custom_call_target="tpu_custom_call" | custom-call | flops 4294967296 | bytes 12582912 | tf_op jit(solution)/shard_map/video_grads/pallas_call | solution.py:281
  111.7 4.7 %all-to-all-start.1 = ((bf16[16,16,2176]{2,1,0:T(8,128)(2,1)}), bf16[16,16,2176]{2,1,0:T(8,128)(2,1)S(1)}, u32[]{:S(2)}, u32[]{:S(2)}) async-start(bf16[16,16,2176]{2,1,0:T(8,128)(2,1)} %video_grads.1), calls=%async_computation.1 | async-start | bytes 2228224 | tf_op jit(solution)/shard_map/all_to_all | solution.py:416
  116.5 1.7 fusion.19
  118.2 2.8 %collective-permute-start.13 = (bf16[128,512]{1,0:T(8,128)(2,1)S(1)}, bf16[128,512]{1,0:T(8,128)(2,1)S(1)}, u32[]{:S(2)}, u32[]{:S(2)}) collective-permute-start(bf16[128,512]{1,0:T(8,128)(2,1)S(1)} %get-tuple-element.60), channel_id=1, source_target_pairs={{0,12},{1,13},{2,14},{3,15},{4,0},{5,1},{6,2},{7,3},{8,4},{9,5},{1... | collective-permute-start | bytes 393224 | tf_op jit(solution)/shard_map/ppermute | solution.py:356
  121.0 0.8 collective-permute-start.12
  121.9 0.9 collective-permute-start.11
  122.7 2.2 %fusion.17 = (bf16[4,128,512]{2,1,0:T(8,128)(2,1)S(1)}, f32[4,128,512]{2,1,0:T(8,128)S(1)}) fusion(bf16[4,128,512]{2,1,0:T(8,128)(2,1)} %collective-permute-done.4, bf16[4,128,512]{2,1,0:T(8,128)(2,1)} %collective-permute-done.3, bf16[4,128,512]{2,1,0:T(8,128)(2,1)} %collective-permute-done.2, bf16[4,4,128,512]{3,2,1,0:T(8,128)(2,1)} %copy-done.7, ...), kind=kLoop, calls=%fused_computation.52 | loop fusion | flops 2359296 | bytes 4718592 | tf_op jit(solution)/shard_map/convert.5
  125.0 1.2 collective-permute-start.9
  126.2 1.5 collective-permute-start.8
  127.7 6.6 %collective-permute-done.13 = bf16[128,512]{1,0:T(8,128)(2,1)S(1)} collective-permute-done((bf16[128,512]{1,0:T(8,128)(2,1)S(1)}, bf16[128,512]{1,0:T(8,128)(2,1)S(1)}, u32[]{:S(2)}, u32[]{:S(2)}) %collective-permute-start.13) | collective-permute-done | bytes 131104 | tf_op jit(solution)/shard_map/ppermute | solution.py:356
  134.4 0.6 collective-permute-start.7
  135.0 0.5 collective-permute-done.12
  135.4 2.5 %collective-permute-done.11 = bf16[128,512]{1,0:T(8,128)(2,1)S(1)} collective-permute-done((bf16[128,512]{1,0:T(8,128)(2,1)S(1)}, bf16[128,512]{1,0:T(8,128)(2,1)S(1)}, u32[]{:S(2)}, u32[]{:S(2)}) %collective-permute-start.11) | collective-permute-done | bytes 131104 | tf_op jit(solution)/shard_map/ppermute | solution.py:356
  138.0 2.5 %collective-permute-done.7 = bf16[128,512]{1,0:T(8,128)(2,1)S(1)} collective-permute-done((bf16[128,512]{1,0:T(8,128)(2,1)S(1)}, bf16[128,512]{1,0:T(8,128)(2,1)S(1)}, u32[]{:S(2)}, u32[]{:S(2)}) %collective-permute-start.7) | collective-permute-done | bytes 131104 | tf_op jit(solution)/shard_map/ppermute | solution.py:364
  140.7 0.7 collective-permute-start.14
  141.3 5.8 %collective-permute-done.14 = f32[128,512]{1,0:T(8,128)S(1)} collective-permute-done((f32[128,512]{1,0:T(8,128)S(1)}, f32[128,512]{1,0:T(8,128)S(1)}, u32[]{:S(2)}, u32[]{:S(2)}) %collective-permute-start.14) | collective-permute-done | bytes 262176 | tf_op jit(solution)/shard_map/ppermute | solution.py:360
  147.3 5.6 %collective-permute-start.17 = (bf16[144,512]{1,0:T(8,128)(2,1)S(1)}, bf16[144,512]{1,0:T(8,128)(2,1)S(1)}, u32[]{:S(2)}, u32[]{:S(2)}) collective-permute-start(bf16[144,512]{1,0:T(8,128)(2,1)S(1)} %fusion.14), channel_id=1, source_target_pairs={{0,48},{16,0},{32,16},{48,32},{64,112},{80,64},{96,80},{112,96},{1... | collective-permute-start | bytes 442376 | tf_op jit(solution)/shard_map/ppermute | solution.py:368
  152.9 1.3 collective-permute-start.16
  154.2 2.4 %collective-permute-start.15 = (bf16[144,512]{1,0:T(8,128)(2,1)S(1)}, bf16[144,512]{1,0:T(8,128)(2,1)S(1)}, u32[]{:S(2)}, u32[]{:S(2)}) collective-permute-start(bf16[144,512]{1,0:T(8,128)(2,1)S(1)} %fusion.14), channel_id=1, source_target_pairs={{0,16},{16,32},{32,48},{48,0},{64,80},{80,96},{96,112},{112,64},{1... | collective-permute-start | bytes 442376 | tf_op jit(solution)/shard_map/ppermute | solution.py:368
  156.6 1.6 collective-permute-done.17
  158.2 7.0 %collective-permute-done.16 = bf16[144,512]{1,0:T(8,128)(2,1)S(1)} collective-permute-done((bf16[144,512]{1,0:T(8,128)(2,1)S(1)}, bf16[144,512]{1,0:T(8,128)(2,1)S(1)}, u32[]{:S(2)}, u32[]{:S(2)}) %collective-permute-start.16) | collective-permute-done | bytes 147488 | tf_op jit(solution)/shard_map/ppermute | solution.py:368
  165.2 1.1 collective-permute-done.15
  166.4 0.4 collective-permute-start.18
  166.8 2.0 %collective-permute-start.19 = (f32[136,512]{1,0:T(8,128)S(1)}, f32[136,512]{1,0:T(8,128)S(1)}, u32[]{:S(2)}, u32[]{:S(2)}) collective-permute-start(f32[136,512]{1,0:T(8,128)S(1)} %select_maximum_fusion.d0), channel_id=1, source_target_pairs={{0,128},{16,144},{32,160},{48,176},{64,192},{80,208},{96,224},{112... | collective-permute-start | bytes 835592 | tf_op jit(solution)/shard_map/ppermute | solution.py:364
  168.9 0.9 collective-permute-start.20
  169.9 0.8 reshape.91
  170.7 1.2 copy.19
  171.9 10.3 %collective-permute-done.18.d1 = f32[136,512]{1,0:T(8,128)S(1)} collective-permute-done((f32[136,512]{1,0:T(8,128)S(1)}, f32[136,512]{1,0:T(8,128)S(1)}, u32[]{:S(2)}, u32[]{:S(2)}) %collective-permute-start.18) | collective-permute-done | bytes 278560 | tf_op jit(solution)/shard_map/ppermute | solution.py:364
  182.3 0.6 collective-permute-done.20.d3
  183.1 0.7 copy-done.11
  183.8 2.3 %place_grads.1 = (f32[64,3072]{1,0:T(8,128)}, f32[64,1024]{1,0:T(8,128)}, f32[1,64]{1,0:T(1,128)}, f32[1,64]{1,0:T(1,128)}) custom-call(s32[4]{0:T(128)} %copy-done.1, f32[136,512]{1,0:T(8,128)} %copy-done.8, f32[136,512]{1,0:T(8,128)} %copy-done.9, f32[136,512]{1,0:T(8,128)} %copy-done.10, f32[136,512]{1,0:T(8,128)} %copy-done.11), custom_call_target="tpu_custom_call" | custom-call | tf_op jit(solution)/shard_map/place_grads/pallas_call | solution.py:321
  (57 shorter events, 1.6 us)
Async XLA Ops:
  3.9 32.7 %copy-start.3 = (f32[1024]{0:T(1024)S(1)}, f32[1024]{0:T(1024)}, u32[]{:S(2)}) copy-start(f32[1024]{0:T(1024)} %param.9) | copy-start | bytes 12292
  3.9 32.7 %copy-start.4 = (f32[1024]{0:T(1024)S(1)}, f32[1024]{0:T(1024)}, u32[]{:S(2)}) copy-start(f32[1024]{0:T(1024)} %param.8) | copy-start | bytes 12292
  3.9 32.7 %all-to-all-start = ((bf16[16,4,16,1024]{3,2,1,0:T(8,128)(2,1)}), bf16[16,4,16,1024]{3,2,1,0:T(8,128)(2,1)S(1)}, u32[]{:S(2)}, u32[]{:S(2)}) async-start(bf16[16,4,16,1024]{3,2,1,0:T(8,128)(2,1)} %bitcast.87), calls=%async_computation | async-start | bytes 4194304 | tf_op jit(solution)/shard_map/all_to_all | solution.py:405
  10.0 55.0 %copy-start.1 = (s32[4]{0:T(128)}, s32[4]{0:T(128)S(1)}, u32[]{:S(2)}) copy-start(s32[4]{0:T(128)S(1)} %pad_add_fusion.place_ref) | copy-start | bytes 52
  36.6 1.6 copy-start.2
  64.9 6.3 %copy-start = (f32[4,4,128,512]{3,2,1,0:T(8,128)}, f32[4,4,128,512]{3,2,1,0:T(8,128)S(1)}, u32[]{:S(2)}) copy-start(f32[4,4,128,512]{3,2,1,0:T(8,128)S(1)} %get-tuple-element.30) | copy-start | bytes 12582916
  64.9 6.3 %collective-permute-start.1 = (bf16[4,4,128,512]{3,2,1,0:T(8,128)(2,1)S(1)}, bf16[4,4,128,512]{3,2,1,0:T(8,128)(2,1)S(1)}, u32[]{:S(2)}, u32[]{:S(2)}) collective-permute-start(bf16[4,4,128,512]{3,2,1,0:T(8,128)(2,1)S(1)} %get-tuple-element.31), channel_id=1, source_target_pairs={{0,1},{1,0},{2,3},{3,2},{4,5},{5,4},{6,7},{7,6},{8,9},{9,8},{10,11... | collective-permute-start | bytes 6291464 | tf_op jit(solution)/shard_map/ppermute | solution.py:352
  68.8 2.0 %copy-start.5 = (bf16[512,4096]{1,0:T(8,128)(2,1)}, bf16[512,4096]{1,0:T(8,128)(2,1)S(1)}, u32[]{:S(2)}) copy-start(bf16[512,4096]{1,0:T(8,128)(2,1)S(1)} %get-tuple-element.29.right_ref.dpk_ref) | copy-start | bytes 12582916
  70.8 4.2 %collective-permute-start = (bf16[4,4,128,512]{3,2,1,0:T(8,128)(2,1)S(1)}, bf16[4,4,128,512]{3,2,1,0:T(8,128)(2,1)S(1)}, u32[]{:S(2)}, u32[]{:S(2)}) collective-permute-start(bf16[4,4,128,512]{3,2,1,0:T(8,128)(2,1)S(1)} %get-tuple-element.28), channel_id=1, source_target_pairs={{0,1},{1,0},{2,3},{3,2},{4,5},{5,4},{6,7},{7,6},{8,9},{9,8},{10,11... | collective-permute-start | bytes 6291464 | tf_op jit(solution)/shard_map/ppermute | solution.py:352
  71.2 1.7 copy-start.7
  71.2 31.2 %slice-start = ((s8[6291456]{0:T(1024)(128)(4,1)}), s8[4194304]{0:T(1024)(128)(4,1)S(1)}, s32[]{:S(2)}) async-start(s8[6291456]{0:T(1024)(128)(4,1)} %bitcast.82), calls=%async_computation.2 | async-start | bytes 8388608
  72.8 26.5 %collective-permute-start.2 = (bf16[4,128,512]{2,1,0:T(8,128)(2,1)S(1)}, bf16[4,128,512]{2,1,0:T(8,128)(2,1)}, u32[]{:S(2)}, u32[]{:S(2)}) collective-permute-start(bf16[4,128,512]{2,1,0:T(8,128)(2,1)S(1)} %get-tuple-element.51), channel_id=1, source_target_pairs={{0,4},{1,5},{2,6},{3,7},{4,8},{5,9},{6,10},{7,11},{8,12},{9,13},{1... | collective-permute-start | bytes 1572872 | tf_op jit(solution)/shard_map/ppermute | solution.py:356
  75.0 27.4 %slice-start.1 = ((s8[6291456]{0:T(1024)(128)(4,1)}), s8[2097152]{0:T(1024)(128)(4,1)S(1)}, s32[]{:S(2)}) async-start(s8[6291456]{0:T(1024)(128)(4,1)} %bitcast.82), calls=%async_computation.3 | async-start | bytes 4194304
  75.0 27.4 %copy-start.6 = (bf16[512,4096]{1,0:T(8,128)(2,1)S(1)}, bf16[512,4096]{1,0:T(8,128)(2,1)}, u32[]{:S(2)}) copy-start(bf16[512,4096]{1,0:T(8,128)(2,1)} %copy-done.5) | copy-start | bytes 12582916
  76.7 39.8 %collective-permute-start.3 = (bf16[4,128,512]{2,1,0:T(8,128)(2,1)}, bf16[4,128,512]{2,1,0:T(8,128)(2,1)}, u32[]{:S(2)}, u32[]{:S(2)}) collective-permute-start(bf16[4,128,512]{2,1,0:T(8,128)(2,1)} %get-tuple-element.50), channel_id=1, source_target_pairs={{0,8},{1,9},{2,10},{3,11},{4,12},{5,13},{6,14},{7,15},{8,0},{9,1},... | collective-permute-start | bytes 1572872 | tf_op jit(solution)/shard_map/ppermute | solution.py:356
  78.3 38.1 %collective-permute-start.4 = (bf16[4,128,512]{2,1,0:T(8,128)(2,1)}, bf16[4,128,512]{2,1,0:T(8,128)(2,1)}, u32[]{:S(2)}, u32[]{:S(2)}) collective-permute-start(bf16[4,128,512]{2,1,0:T(8,128)(2,1)} %get-tuple-element.49), channel_id=1, source_target_pairs={{0,12},{1,13},{2,14},{3,15},{4,0},{5,1},{6,2},{7,3},{8,4},{9,5},{1... | collective-permute-start | bytes 1572872 | tf_op jit(solution)/shard_map/ppermute | solution.py:356
  79.0 37.4 %collective-permute-start.5 = (bf16[4,128,512]{2,1,0:T(8,128)(2,1)}, bf16[4,128,512]{2,1,0:T(8,128)(2,1)}, u32[]{:S(2)}, u32[]{:S(2)}) collective-permute-start(bf16[4,128,512]{2,1,0:T(8,128)(2,1)} %get-tuple-element.32), channel_id=1, source_target_pairs={{0,64},{16,80},{32,96},{48,112},{64,128},{80,144},{96,160},{112,17... | collective-permute-start | bytes 1572872 | tf_op jit(solution)/shard_map/ppermute | solution.py:364
  80.5 36.0 %collective-permute-start.6 = (bf16[4,128,512]{2,1,0:T(8,128)(2,1)}, bf16[4,128,512]{2,1,0:T(8,128)(2,1)}, u32[]{:S(2)}, u32[]{:S(2)}) collective-permute-start(bf16[4,128,512]{2,1,0:T(8,128)(2,1)} %get-tuple-element.33), channel_id=1, source_target_pairs={{0,192},{16,208},{32,224},{48,240},{64,0},{80,16},{96,32},{112,48}... | collective-permute-start | bytes 1572872 | tf_op jit(solution)/shard_map/ppermute | solution.py:364
  99.3 17.1 %collective-permute-start.10 = (bf16[4,128,512]{2,1,0:T(8,128)(2,1)}, bf16[4,128,512]{2,1,0:T(8,128)(2,1)}, u32[]{:S(2)}, u32[]{:S(2)}) collective-permute-start(bf16[4,128,512]{2,1,0:T(8,128)(2,1)} %get-tuple-element.39), channel_id=1, source_target_pairs={{0,128},{16,144},{32,160},{48,176},{64,192},{80,208},{96,224},{112... | collective-permute-start | bytes 1572872 | tf_op jit(solution)/shard_map/ppermute | solution.py:364
  111.7 35.5 %all-to-all-start.1 = ((bf16[16,16,2176]{2,1,0:T(8,128)(2,1)}), bf16[16,16,2176]{2,1,0:T(8,128)(2,1)S(1)}, u32[]{:S(2)}, u32[]{:S(2)}) async-start(bf16[16,16,2176]{2,1,0:T(8,128)(2,1)} %video_grads.1), calls=%async_computation.1 | async-start | bytes 2228224 | tf_op jit(solution)/shard_map/all_to_all | solution.py:416
  118.2 16.2 %collective-permute-start.13 = (bf16[128,512]{1,0:T(8,128)(2,1)S(1)}, bf16[128,512]{1,0:T(8,128)(2,1)S(1)}, u32[]{:S(2)}, u32[]{:S(2)}) collective-permute-start(bf16[128,512]{1,0:T(8,128)(2,1)S(1)} %get-tuple-element.60), channel_id=1, source_target_pairs={{0,12},{1,13},{2,14},{3,15},{4,0},{5,1},{6,2},{7,3},{8,4},{9,5},{1... | collective-permute-start | bytes 393224 | tf_op jit(solution)/shard_map/ppermute | solution.py:356
  121.0 14.4 %collective-permute-start.12 = (bf16[128,512]{1,0:T(8,128)(2,1)S(1)}, bf16[128,512]{1,0:T(8,128)(2,1)S(1)}, u32[]{:S(2)}, u32[]{:S(2)}) collective-permute-start(bf16[128,512]{1,0:T(8,128)(2,1)S(1)} %get-tuple-element.61), channel_id=1, source_target_pairs={{0,8},{1,9},{2,10},{3,11},{4,12},{5,13},{6,14},{7,15},{8,0},{9,1},... | collective-permute-start | bytes 393224 | tf_op jit(solution)/shard_map/ppermute | solution.py:356
  121.9 16.1 %collective-permute-start.11 = (bf16[128,512]{1,0:T(8,128)(2,1)S(1)}, bf16[128,512]{1,0:T(8,128)(2,1)S(1)}, u32[]{:S(2)}, u32[]{:S(2)}) collective-permute-start(bf16[128,512]{1,0:T(8,128)(2,1)S(1)} %get-tuple-element.59), channel_id=1, source_target_pairs={{0,4},{1,5},{2,6},{3,7},{4,8},{5,9},{6,10},{7,11},{8,12},{9,13},{1... | collective-permute-start | bytes 393224 | tf_op jit(solution)/shard_map/ppermute | solution.py:356
  125.0 13.0 %collective-permute-start.9 = (bf16[128,512]{1,0:T(8,128)(2,1)S(1)}, bf16[128,512]{1,0:T(8,128)(2,1)S(1)}, u32[]{:S(2)}, u32[]{:S(2)}) collective-permute-start(bf16[128,512]{1,0:T(8,128)(2,1)S(1)} %get-tuple-element.57), channel_id=1, source_target_pairs={{0,192},{16,208},{32,224},{48,240},{64,0},{80,16},{96,32},{112,48}... | collective-permute-start | bytes 393224 | tf_op jit(solution)/shard_map/ppermute | solution.py:364
  126.2 11.8 %collective-permute-start.8 = (bf16[128,512]{1,0:T(8,128)(2,1)S(1)}, bf16[128,512]{1,0:T(8,128)(2,1)S(1)}, u32[]{:S(2)}, u32[]{:S(2)}) collective-permute-start(bf16[128,512]{1,0:T(8,128)(2,1)S(1)} %get-tuple-element.58), channel_id=1, source_target_pairs={{0,128},{16,144},{32,160},{48,176},{64,192},{80,208},{96,224},{112... | collective-permute-start | bytes 393224 | tf_op jit(solution)/shard_map/ppermute | solution.py:364
  134.4 6.2 %collective-permute-start.7 = (bf16[128,512]{1,0:T(8,128)(2,1)S(1)}, bf16[128,512]{1,0:T(8,128)(2,1)S(1)}, u32[]{:S(2)}, u32[]{:S(2)}) collective-permute-start(bf16[128,512]{1,0:T(8,128)(2,1)S(1)} %get-tuple-element.56), channel_id=1, source_target_pairs={{0,64},{16,80},{32,96},{48,112},{64,128},{80,144},{96,160},{112,17... | collective-permute-start | bytes 393224 | tf_op jit(solution)/shard_map/ppermute | solution.py:364
  140.7 6.5 %collective-permute-start.14 = (f32[128,512]{1,0:T(8,128)S(1)}, f32[128,512]{1,0:T(8,128)S(1)}, u32[]{:S(2)}, u32[]{:S(2)}) collective-permute-start(f32[128,512]{1,0:T(8,128)S(1)} %pad_maximum_fusion.2), channel_id=1, source_target_pairs={{0,2},{1,3},{2,0},{3,1},{4,6},{5,7},{6,4},{7,5},{8,10},{9,11},{10,... | collective-permute-start | bytes 786440 | tf_op jit(solution)/shard_map/ppermute | solution.py:360
  147.3 10.9 %collective-permute-start.17 = (bf16[144,512]{1,0:T(8,128)(2,1)S(1)}, bf16[144,512]{1,0:T(8,128)(2,1)S(1)}, u32[]{:S(2)}, u32[]{:S(2)}) collective-permute-start(bf16[144,512]{1,0:T(8,128)(2,1)S(1)} %fusion.14), channel_id=1, source_target_pairs={{0,48},{16,0},{32,16},{48,32},{64,112},{80,64},{96,80},{112,96},{1... | collective-permute-start | bytes 442376 | tf_op jit(solution)/shard_map/ppermute | solution.py:368
  152.9 12.3 %collective-permute-start.16 = (bf16[144,512]{1,0:T(8,128)(2,1)S(1)}, bf16[144,512]{1,0:T(8,128)(2,1)S(1)}, u32[]{:S(2)}, u32[]{:S(2)}) collective-permute-start(bf16[144,512]{1,0:T(8,128)(2,1)S(1)} %fusion.14), channel_id=1, source_target_pairs={{0,32},{16,48},{32,0},{48,16},{64,96},{80,112},{96,64},{112,80},{1... | collective-permute-start | bytes 442376 | tf_op jit(solution)/shard_map/ppermute | solution.py:368
  154.2 12.1 %collective-permute-start.15 = (bf16[144,512]{1,0:T(8,128)(2,1)S(1)}, bf16[144,512]{1,0:T(8,128)(2,1)S(1)}, u32[]{:S(2)}, u32[]{:S(2)}) collective-permute-start(bf16[144,512]{1,0:T(8,128)(2,1)S(1)} %fusion.14), channel_id=1, source_target_pairs={{0,16},{16,32},{32,48},{48,0},{64,80},{80,96},{96,112},{112,64},{1... | collective-permute-start | bytes 442376 | tf_op jit(solution)/shard_map/ppermute | solution.py:368
  166.4 4.3 %copy-start.8 = (f32[136,512]{1,0:T(8,128)}, f32[136,512]{1,0:T(8,128)S(1)}, u32[]{:S(2)}) copy-start(f32[136,512]{1,0:T(8,128)S(1)} %select_maximum_fusion.d0) | copy-start | bytes 835588
  166.4 15.8 %collective-permute-start.18 = (f32[136,512]{1,0:T(8,128)S(1)}, f32[136,512]{1,0:T(8,128)S(1)}, u32[]{:S(2)}, u32[]{:S(2)}) collective-permute-start(f32[136,512]{1,0:T(8,128)S(1)} %select_maximum_fusion.d0), channel_id=1, source_target_pairs={{0,64},{16,80},{32,96},{48,112},{64,128},{80,144},{96,160},{112,17... | collective-permute-start | bytes 835592 | tf_op jit(solution)/shard_map/ppermute | solution.py:364
  166.8 15.4 %collective-permute-start.19 = (f32[136,512]{1,0:T(8,128)S(1)}, f32[136,512]{1,0:T(8,128)S(1)}, u32[]{:S(2)}, u32[]{:S(2)}) collective-permute-start(f32[136,512]{1,0:T(8,128)S(1)} %select_maximum_fusion.d0), channel_id=1, source_target_pairs={{0,128},{16,144},{32,160},{48,176},{64,192},{80,208},{96,224},{112... | collective-permute-start | bytes 835592 | tf_op jit(solution)/shard_map/ppermute | solution.py:364
  168.9 14.0 %collective-permute-start.20 = (f32[136,512]{1,0:T(8,128)S(1)}, f32[136,512]{1,0:T(8,128)S(1)}, u32[]{:S(2)}, u32[]{:S(2)}) collective-permute-start(f32[136,512]{1,0:T(8,128)S(1)} %select_maximum_fusion.d0), channel_id=1, source_target_pairs={{0,192},{16,208},{32,224},{48,240},{64,0},{80,16},{96,32},{112,48}... | collective-permute-start | bytes 835592 | tf_op jit(solution)/shard_map/ppermute | solution.py:364
  182.3 0.7 copy-start.9
  182.3 0.8 copy-start.10
  183.1 0.7 copy-start.11

commit v4 on v3

--- a/solution.py
+++ b/solution.py
@@ -31,15 +31,11 @@
 
 
 def block_row(block, place):
-    x, y, z, core = place
-    dcore = (block % 2 - core) % 2
-    dz = (block // 2 % 2 - z) % 2
-    dy = (block // 4 - y) % 4
-    return pl.multiple_of(((dcore * 4 + dy) * 2 + dz) * 64, 64)
+    return pl.multiple_of(((block % 2 - place[1]) % 2 * 8 + block // 2) * 64, 64)
 
 
 def read_place(place_ref):
-    return tuple(place_ref[i] for i in range(4))
+    return tuple(place_ref[i] for i in range(2))
 
 
 def whiten(xh):
@@ -142,11 +138,11 @@
     for k in range(4):
         rhs = right_s[:, chunk((place[0] + k) % 4)]
         g = dot_nn(left_s[0, half:, :], rhs)
-        send_s[:, k] = g.reshape(4, 128, CHUNK).astype(BF16)
+        send_s[:, k] = g.reshape(8, 64, CHUNK).astype(BF16)
         copies.append(pltpu.make_async_copy(send_s.at[:, k], send_hbm.at[:, k], sems.at[2 + k]))
         copies[-1].start()
         g = dot_nn(left_s[0, :half, :], rhs)
-        keep_s[:, k] = g.reshape(4, 128, CHUNK)
+        keep_s[:, k] = g.reshape(8, 64, CHUNK)
         copies.append(pltpu.make_async_copy(keep_s.at[:, k], keep_hbm.at[:, k], sems.at[6 + k]))
         copies[-1].start()
     for copy in copies:
@@ -158,7 +154,7 @@
     rows = clips // 2 * frames * positions
     vm = pl.BlockSpec(memory_space=pltpu.VMEM)
     hbm = pl.BlockSpec(memory_space=pl.ANY)
-    piece = (4, 4, 128, CHUNK)
+    piece = (8, 4, 64, CHUNK)
     return pl.pallas_call(
         main_kernel,
         out_shape=(
@@ -188,14 +184,14 @@
 def grads_kernel(place_ref, left_ref, right_ref, send_ref, keep_ref):
     half = left_ref.shape[1] // 2
     rhs = right_ref[...]
-    send_ref[0] = dot_nn(left_ref[0, half:, :], rhs).reshape(4, 128, CHUNK).astype(BF16)
-    keep_ref[0] = dot_nn(left_ref[0, :half, :], rhs).reshape(4, 128, CHUNK)
+    send_ref[0] = dot_nn(left_ref[0, half:, :], rhs).reshape(8, 64, CHUNK).astype(BF16)
+    keep_ref[0] = dot_nn(left_ref[0, :half, :], rhs).reshape(8, 64, CHUNK)
 
 
 def run_grads(place, left, right):
     _, width, rows = left.shape
-    piece = (4, 4, 128, CHUNK)
-    out = pl.BlockSpec((1, 4, 128, CHUNK), lambda k, place: (k, 0, 0, 0))
+    piece = (4, 8, 64, CHUNK)
+    out = pl.BlockSpec((1, 8, 64, CHUNK), lambda k, place: (k, 0, 0, 0))
     return pl.pallas_call(
         grads_kernel,
         grid_spec=pltpu.PrefetchScalarGridSpec(
@@ -296,24 +292,18 @@
     )(tokens, gain, right, wqkv)
 
 
-def place_kernel(scale, place_ref, d0, d1, d2, d3, qkv_ref, out_ref, gain_ref, bias_ref):
-    x = place_ref[0]
-    small = jnp.zeros((8, 128), F32)
+def place_kernel(scale, place_ref, d0, d1, d2, d3, qkv_ref, out_ref):
     for j, d in enumerate((d0, d1, d2, d3)):
-        block = (x - j) % 4
+        block = (place_ref[0] - j) % 4
         qkv_ref[:, chunk(block)] = d[:64, :] * scale
 
         @pl.when(block < 2)
         def _():
-            qkv_ref[:, chunk(4 + block)] = d[64:128, :] * scale
+            qkv_ref[:, chunk(4 + block)] = d[64:, :] * scale
 
         @pl.when(block >= 2)
         def _():
-            out_ref[:, chunk(block - 2)] = d[64:128, :] * scale
-
-        small = small + d[128:136, :128] * scale
-    gain_ref[...] = small[:1, :64]
-    bias_ref[...] = small[:1, 64:]
+            out_ref[:, chunk(block - 2)] = d[64:, :] * scale
 
 
 def run_place(place, scale, pieces):
@@ -323,11 +313,9 @@
         out_shape=(
             jax.ShapeDtypeStruct((64, 6 * CHUNK), F32),
             jax.ShapeDtypeStruct((64, 2 * CHUNK), F32),
-            jax.ShapeDtypeStruct((1, 64), F32),
-            jax.ShapeDtypeStruct((1, 64), F32),
         ),
         in_specs=[pl.BlockSpec(memory_space=pltpu.SMEM)] + [vm] * 4,
-        out_specs=(vm,) * 4,
+        out_specs=(vm,) * 2,
         name="place_grads",
     )(place, *pieces)
 
@@ -352,12 +340,9 @@
     return lax.ppermute(a, "frame", frame_pairs(lambda y, z, c: (y, z, c + 1)))
 
 
-def go_y(a, k):
-    return lax.ppermute(a, "frame", frame_pairs(lambda y, z, c: (y + k, z, c)))
-
-
-def go_z(a):
-    return lax.ppermute(a, "frame", frame_pairs(lambda y, z, c: (y, z + 1, c)))
+def trade_yz(a):
+    groups = [[2 * i + core for i in range(8)] for core in range(2)]
+    return lax.all_to_all(a, "frame", 0, 0, tiled=True, axis_index_groups=groups)
 
 
 def go_x(a, k):
@@ -378,19 +363,13 @@
     return [go(pieces[k], k) for k in range(1, 4)]
 
 
-def first_pieces(keep, got):
-    own = keep[0] + got[0].astype(F32)
-    return [own] + [(keep[k] + got[k].astype(F32)).astype(BF16) for k in range(1, 4)]
-
-
-def second_pieces(total):
-    return [total[0]] + [total[k].astype(BF16) for k in range(1, 4)]
-
-
-def three_terms(value):
-    hi = lax.reduce_precision(value, 8, 7)
-    mid = lax.reduce_precision(value - hi, 8, 7)
-    return jnp.concatenate([hi, mid, value - hi - mid], axis=0)
+def pick(array, index):
+    return lax.dynamic_index_in_dim(array, index, 0, keepdims=False)
+
+
+def reduce_yz(own, got, yz):
+    mine = (jnp.arange(8) == yz).reshape((8,) + (1,) * own.ndim)
+    return jnp.sum(jnp.where(mine, own[None], got.astype(F32)), axis=0)
 
 
 def local(video, cotangent, norm_gain, norm_bias, qkv_weight, out_weight):
@@ -398,7 +377,8 @@
     grad_scale = 1.0 / math.sqrt(clips * positions * 256)
     frame = lax.axis_index("frame")
     dp = lax.axis_index("dp")
-    place = jnp.stack([dp // 4, frame // 4, frame // 2 % 2, frame % 2]).astype(jnp.int32)
+    yz, core = frame // 2, frame % 2
+    place = jnp.stack([dp // 4, core]).astype(jnp.int32)
     gain = norm_gain.reshape(1, width)
     bias = norm_bias.reshape(1, width)
     tokens = jnp.concatenate([video, cotangent], axis=0).reshape(2 * clips, 16, positions // 16, width)
@@ -406,33 +386,38 @@
 
     send_a, keep_a, left, right = run_main(place, tokens, gain, bias, qkv_weight, out_weight)
     send_b, keep_b = run_grads(place, left, right)
-    pieces_a = first_pieces(keep_a, go_core(send_a))
-    pieces_b = first_pieces(keep_b, go_core(send_b))
-    got_a = exchange(pieces_a, go_y)
-    right, pieces_b = lax.optimization_barrier((right, pieces_b))
-    got_b = exchange(pieces_b, go_x)
-
+    got_a, send_b = lax.optimization_barrier((go_core(send_a), send_b))
+    got_b = go_core(send_b)
+    own_a = pick(keep_a, yz) + pick(got_a, yz).astype(F32)
+    terms_a = (keep_a + got_a.astype(F32)).astype(BF16)
+    terms_b = [keep_b[0] + got_b[0].astype(F32)]
+    terms_b += [(keep_b[k] + got_b[k].astype(F32)).astype(BF16) for k in range(1, 4)]
+    got_a = trade_yz(terms_a)
+    got_b = exchange(terms_b, go_x)
     back = run_back(tokens, gain, right, qkv_weight)
+    back, got_a, got_b = lax.optimization_barrier((back, got_a, got_b))
+    a = reduce_yz(own_a, got_a, yz)
+    b = combine(terms_b[0], got_b)
+    got_a = exchange([a[0]] + [a[k].astype(BF16) for k in range(1, 4)], go_x)
+    got_b = trade_yz(b.astype(BF16))
+
+    back, got_a, got_b = lax.optimization_barrier((back, got_a, got_b))
     back = lax.all_to_all(back, "frame", 0, 0, tiled=True)
-    grad_video = back[:, :, : clips * width].reshape(positions, clips, width)
-    grad_video = grad_video.transpose(1, 0, 2).reshape(video.shape)
-    small = jnp.sum(back[:, :3, clips * width :].astype(F32), axis=(0, 1)).reshape(1, 128)
-
-    got_a, got_b[0], got_b[2] = lax.optimization_barrier((got_a, got_b[0], got_b[2]))
-    pieces_a = second_pieces(combine(pieces_a[0], got_a))
-    pieces_b = second_pieces(combine(pieces_b[0], got_b))
-    got_a = exchange(pieces_a, go_x)
-    got_b = exchange(pieces_b, go_y)
-    a = combine(pieces_a[0], got_a)
-    b = combine(pieces_b[0], got_b)
-    own = jnp.concatenate([a[:64], b[:64]], axis=0) + go_z(jnp.concatenate([a[64:], b[64:]], axis=0))
-    own = jnp.concatenate([own, jnp.pad(three_terms(small), ((0, 13), (0, CHUNK - 128)))], axis=0)
+
+    a = combine(a[0], got_a)
+    b = reduce_yz(pick(b, yz), got_b, yz)
+    own = jnp.concatenate([a, b], axis=0)
     own = combine(own, exchange([own.astype(BF16)] * 4, go_h))
-    small = jnp.sum(own[128:131], axis=0, keepdims=True)
-    own = jnp.concatenate([own[:128], jnp.pad(small, ((0, 7), (0, 0)))], axis=0)
     pieces = [own] + exchange([own] * 4, go_x)
-    grad_qkv, grad_out, total_gain, total_bias = run_place(place, grad_scale, pieces)
-    return grad_video, grad_qkv, grad_out, total_gain.reshape(64), total_bias.reshape(64)
+    parts = [back[:, :, c * width : (c + 1) * width].reshape(positions, width) for c in range(clips)]
+    grad_video = jnp.stack(parts).reshape(video.shape)
+    pieces, grad_video = lax.optimization_barrier((pieces, grad_video))
+    grad_qkv, grad_out = run_place(place, grad_scale, pieces)
+
+    small = jnp.sum(back[:, :3, clips * width :].astype(F32), axis=(0, 1)).reshape(1, 1, 128)
+    small = lax.all_to_all(jnp.broadcast_to(small, (16, 1, 128)), "dp", 0, 0, tiled=True)
+    small = jnp.sum(small, axis=(0, 1)) * grad_scale
+    return grad_video, grad_qkv, grad_out, small[:64], small[64:]
 
 
 def solution(mesh):

time: 187 us -> 198 us (1.059)
  waiting for transfers between devices: 84.4 us -> 72.6 us
  starting transfers between devices: 41.1 us -> 50.9 us
  local copies, waits for them, and re-layouts: 8.44 us -> 14.6 us
  other arithmetic: 9.38 us -> 15.1 us
    ppermute x7 -> x0, waiting for transfers between devices: 32.5 us -> none  [the longest x6 26.7 us: go_y(): return lax.ppermute(a, 'frame', frame_pairs(lambda y, z, c: (y + k, z, c)))]
    all_to_all x0 -> x3, starting transfers between devices: none -> 19.9 us  [the longest x2 11.2 us: trade_yz(): lax.all_to_all(a, 'frame', 0, 0, tiled=True, axis_index_groups=groups)]
    ppermute x3, waiting for transfers between devices: 9.7 us -> 18.3 us  [go_h(): return lax.ppermute(a, 'dp', dp_pairs(lambda x, h: (x, h + k)))]
    ppermute x9, waiting for transfers between devices: 13.5 us -> 21.2 us  [go_x(): return lax.ppermute(a, 'dp', dp_pairs(lambda x, h: (x + k, h)))]
    ppermute x7 -> x0, starting transfers between devices: 7.5 us -> none  [the longest x6 6.85 us: go_y(): return lax.ppermute(a, 'frame', frame_pairs(lambda y, z, c: (y + k, z, c)))]
    unnamed x28 -> x32, local copies, waits for them, and re-layouts: 4.64 us -> 11.8 us
    convert_element_type x2 -> x3, other arithmetic: 3.27 us -> 8.49 us  [the longest x1 3.22 us: local(): (keep_b[k] + got_b[k].astype(F32)).astype(BF16)]
    another operation x3 -> x2, other arithmetic: 4.01 us -> 0.11 us  [the longest x1 0.07 us: local(): place = jnp.stack([dp // 4, core]).astype(jnp.int32)]
  transfers between devices with their start and end apart: 23 -> 19, of which waited for: 13 -> 11; matrix products, arithmetic and copies ran while one was open for 5% -> 4% of each run, Pallas kernels for 7% -> 8%
where the time goes in v4:
time: 198 us; the launch traced here: 196 us
  waiting for transfers between devices  72.6 us (37%)
  starting transfers between devices  50.9 us (26%)
  Pallas kernels  41.8 us (21%)
  other arithmetic  15.1 us (8%)
  local copies, waits for them, and re-layouts  14.6 us (7%)
    pallas_call x1, Pallas kernels, run_main(): pl.pallas_call(main_kernel, out_shape=(jax.ShapeDtypeStruct(piece, BF16),...  26.6 us
    all_to_all x1, waiting for transfers between devices, local(): lax.all_to_all(tokens.transpose(1, 0, 2, 3), 'frame', 0, 0, tiled=True)  26.6 us
    ppermute x9, waiting for transfers between devices, go_x(): return lax.ppermute(a, 'dp', dp_pairs(lambda x, h: (x + k, h)))  21.2 us
    ppermute x3, waiting for transfers between devices, go_h(): return lax.ppermute(a, 'dp', dp_pairs(lambda x, h: (x, h + k)))  18.3 us
    unnamed x32, local copies, waits for them, and re-layouts  11.8 us
    all_to_all x2, starting transfers between devices, trade_yz(): lax.all_to_all(a, 'frame', 0, 0, tiled=True, axis_index_groups=groups)  11.2 us
    ppermute x9, starting transfers between devices, go_x(): return lax.ppermute(a, 'dp', dp_pairs(lambda x, h: (x + k, h)))  9.47 us
    ppermute x3, starting transfers between devices, go_h(): return lax.ppermute(a, 'dp', dp_pairs(lambda x, h: (x, h + k)))  9.3 us
  transfers between devices with their start and end apart: 19, of which 11 were waited for; matrix products, arithmetic and copies ran while one was open for 4% of the time, Pallas kernels for 8%

profile of v4, /device:TPU:32, one launch (start us, length us, event | category | flops | bytes accessed | tf_op | source)
XLA Modules:
  0.0 195.8 jit_solution(12670591950715970525)
XLA Ops:
  0.6 1.7 pad_maximum_fusion
  2.4 1.5 copy.22
  3.9 6.1 %all-to-all-start = ((bf16[16,4,16,1024]{3,2,1,0:T(8,128)(2,1)}), bf16[16,4,16,1024]{3,2,1,0:T(8,128)(2,1)S(1)}, u32[]{:S(2)}, u32[]{:S(2)}) async-start(bf16[16,4,16,1024]{3,2,1,0:T(8,128)(2,1)} %bitcast.49), calls=%async_computation | async-start | bytes 4194304 | tf_op jit(solution)/shard_map/all_to_all | solution.py:385
  10.0 26.6 %all-to-all-done.tokens_ref = bf16[16,4,16,1024]{3,2,1,0:T(8,128)(2,1)S(1)} async-done(((bf16[16,4,16,1024]{3,2,1,0:T(8,128)(2,1)}), bf16[16,4,16,1024]{3,2,1,0:T(8,128)(2,1)S(1)}, u32[]{:S(2)}, u32[]{:S(2)}) %all-to-all-start) | async-done | bytes 2097184 | tf_op jit(solution)/shard_map/all_to_all | solution.py:385
  36.6 1.6 copy-done.4
  38.2 26.6 %sublayer.1 = (bf16[8,4,64,512]{3,2,1,0:T(8,128)(2,1)S(1)}, f32[8,4,64,512]{3,2,1,0:T(8,128)S(1)}, bf16[2,1024,512]{2,1,0:T(8,128)(2,1)S(1)}, bf16[512,4096]{1,0:T(8,128)(2,1)S(1)}) custom-call(s32[2]{0:T(128)S(1)} %pad_add_fusion.place_ref, bf16[16,4,16,1024]{3,2,1,0:T(8,128)(2,1)S(1)} %all-to-all-done.tokens_ref, f32[1,1024]{1,0:T(1,128)S(1)} %bitcast.47, ...), custom_call_target="tpu_custom_call" | custom-call | flops 12884901888 | bytes 20971520 | tf_op jit(solution)/shard_map/sublayer/pallas_call | solution.py:158
  65.0 3.6 %weight_grads.1 = (bf16[4,8,64,512]{3,2,1,0:T(8,128)(2,1)S(1)}, f32[4,8,64,512]{3,2,1,0:T(8,128)S(1)}) custom-call(s32[2]{0:T(128)S(1)} %pad_add_fusion.place_ref, bf16[2,1024,512]{2,1,0:T(8,128)(2,1)S(1)} %get-tuple-element.32.left_ref, bf16[512,4096]{1,0:T(8,128)(2,1)S(1)} %get-tuple-element.33.right_ref.dpk_ref), custom_call_target="tpu_custom_call" | custom-call | flops 2147483648 | bytes 12582912 | tf_op jit(solution)/shard_map/weight_grads/pallas_call | solution.py:195
  68.7 2.0 %copy-done.1 = f32[4,8,64,512]{3,2,1,0:T(8,128)} copy-done((f32[4,8,64,512]{3,2,1,0:T(8,128)}, f32[4,8,64,512]{3,2,1,0:T(8,128)S(1)}, u32[]{:S(2)}) %copy-start.1) | copy-done | bytes 4194328
  70.7 1.3 copy-done.5
  72.0 2.0 %copy-done.8 = bf16[512,4096]{1,0:T(8,128)(2,1)} copy-done((bf16[512,4096]{1,0:T(8,128)(2,1)}, bf16[512,4096]{1,0:T(8,128)(2,1)S(1)}, u32[]{:S(2)}) %copy-start.8) | copy-done | bytes 4194328
  74.0 1.3 copy-done.10
  75.3 2.2 %add_convert_fusion = bf16[8,4,64,512]{3,2,1,0:T(8,128)(2,1)} fusion(f32[8,4,64,512]{3,2,1,0:T(8,128)S(1)} %get-tuple-element.30, bf16[8,4,64,512]{3,2,1,0:T(8,128)(2,1)S(1)} %collective-permute-done), kind=kLoop, calls=%fused_computation.1 | loop fusion | flops 3145728 | bytes 8388608 | tf_op jit(solution)/shard_map/convert_element_type | solution.py:392
  77.6 5.5 %all-to-all-start.1 = ((bf16[8,4,64,512]{3,2,1,0:T(8,128)(2,1)}), bf16[8,4,64,512]{3,2,1,0:T(8,128)(2,1)}, u32[]{:S(2)}, u32[]{:S(2)}) async-start(bf16[8,4,64,512]{3,2,1,0:T(8,128)(2,1)} %add_convert_fusion), calls=%async_computation.1 | async-start | bytes 4194304 | tf_op jit(solution)/shard_map/all_to_all | solution.py:345
  83.3 4.2 %collective-permute-done.1 = bf16[4,8,64,512]{3,2,1,0:T(8,128)(2,1)S(1)} collective-permute-done((bf16[4,8,64,512]{3,2,1,0:T(8,128)(2,1)}, bf16[4,8,64,512]{3,2,1,0:T(8,128)(2,1)S(1)}, u32[]{:S(2)}, u32[]{:S(2)}) %collective-permute-start.1) | collective-permute-done | bytes 2097184 | tf_op jit(solution)/shard_map/ppermute | solution.py:340
  87.4 3.2 %fusion.4 = (bf16[8,64,512]{2,1,0:T(8,128)(2,1)S(1)}, bf16[8,64,512]{2,1,0:T(8,128)(2,1)S(1)}, bf16[8,64,512]{2,1,0:T(8,128)(2,1)S(1)}) fusion(f32[4,8,64,512]{3,2,1,0:T(8,128)} %copy-done.1, bf16[4,8,64,512]{3,2,1,0:T(8,128)(2,1)S(1)} %collective-permute-done.1), kind=kLoop, calls=%fused_computation.14 | loop fusion | flops 2359296 | bytes 6291456 | tf_op jit(solution)/shard_map/convert_element_type | solution.py:394
  90.7 2.8 %collective-permute-start.4 = (bf16[8,64,512]{2,1,0:T(8,128)(2,1)S(1)}, bf16[8,64,512]{2,1,0:T(8,128)(2,1)}, u32[]{:S(2)}, u32[]{:S(2)}) collective-permute-start(bf16[8,64,512]{2,1,0:T(8,128)(2,1)S(1)} %get-tuple-element.57), channel_id=1, source_target_pairs={{0,192},{16,208},{32,224},{48,240},{64,0},{80,16},{96,32},{112,48}... | collective-permute-start | bytes 1572872 | tf_op jit(solution)/shard_map/ppermute | solution.py:349
  93.5 0.8 collective-permute-start.3
  94.3 0.9 collective-permute-start.2
  95.2 2.8 %copy-done.3 = bf16[1024,3072]{1,0:T(8,128)(2,1)S(1)} copy-done((bf16[1024,3072]{1,0:T(8,128)(2,1)S(1)}, bf16[1024,3072]{1,0:T(8,128)(2,1)}, u32[]{:S(2)}) %copy-start.3) | copy-done | bytes 6291480
  98.0 9.3 %video_grads.1 = bf16[16,16,2176]{2,1,0:T(8,128)(2,1)} custom-call(bf16[16,4,16,1024]{3,2,1,0:T(8,128)(2,1)S(1)} %all-to-all-done.tokens_ref, f32[1,1024]{1,0:T(1,128)S(1)} %bitcast.48, bf16[512,4096]{1,0:T(8,128)(2,1)S(1)} %copy-done.9, bf16[1024,3072]{1,0:T(8,128)(2,1)S(1)} %copy-done.3), custom_call_target="tpu_custom_call" | custom-call | flops 4294967296 | bytes 12582912 | tf_op jit(solution)/shard_map/video_grads/pallas_call | solution.py:277
  107.3 9.1 %collective-permute-done.4 = bf16[8,64,512]{2,1,0:T(8,128)(2,1)} collective-permute-done((bf16[8,64,512]{2,1,0:T(8,128)(2,1)S(1)}, bf16[8,64,512]{2,1,0:T(8,128)(2,1)}, u32[]{:S(2)}, u32[]{:S(2)}) %collective-permute-start.4) | collective-permute-done | bytes 524320 | tf_op jit(solution)/shard_map/ppermute | solution.py:349
  116.3 3.8 %collective-permute-done.2 = bf16[8,64,512]{2,1,0:T(8,128)(2,1)} collective-permute-done((bf16[8,64,512]{2,1,0:T(8,128)(2,1)S(1)}, bf16[8,64,512]{2,1,0:T(8,128)(2,1)}, u32[]{:S(2)}, u32[]{:S(2)}) %collective-permute-start.2) | collective-permute-done | bytes 524320 | tf_op jit(solution)/shard_map/ppermute | solution.py:349
  120.1 3.0 %fusion.9 = (bf16[8,64,512]{2,1,0:T(8,128)(2,1)}, f32[8,64,512]{2,1,0:T(8,128)S(1)}) fusion(bf16[8,64,512]{2,1,0:T(8,128)(2,1)} %collective-permute-done.4, bf16[8,64,512]{2,1,0:T(8,128)(2,1)} %collective-permute-done.3, bf16[8,64,512]{2,1,0:T(8,128)(2,1)} %collective-permute-done.2, bf16[4,8,64,512]{3,2,1,0:T(8,128)(2,1)} %copy-done.11, ...), kind=kLoop, calls=%fused_computation.31 | loop fusion | flops 2359296 | bytes 4718592 | tf_op jit(solution)/shard_map/convert_element_type | solution.py:402
  123.2 5.7 %all-to-all-start.2 = ((bf16[8,64,512]{2,1,0:T(8,128)(2,1)}), bf16[8,64,512]{2,1,0:T(8,128)(2,1)S(1)}, u32[]{:S(2)}, u32[]{:S(2)}) async-start(bf16[8,64,512]{2,1,0:T(8,128)(2,1)} %get-tuple-element.55), calls=%async_computation.2 | async-start | bytes 1048576 | tf_op jit(solution)/shard_map/all_to_all | solution.py:345
  128.9 1.2 add_bitcast_fusion
  130.1 2.1 %select_reduce_fusion = f32[4,64,512]{2,1,0:T(8,128)S(1)} fusion(bf16[8,4,64,512]{3,2,1,0:T(8,128)(2,1)} %all-to-all-done.1, f32[4,64,512]{2,1,0:T(8,128)S(1)} %add_bitcast_fusion, pred[8]{0:T(512)(128)(4,1)S(1)} %iota_compare_fusion), kind=kLoop, calls=%fused_computation | loop fusion | flops 3014656 | bytes 3145736 | tf_op jit(solution)/shard_map/reduce_sum | solution.py:372
  132.3 0.7 collective-permute-start.7
  133.0 0.8 collective-permute-start.6
  133.8 0.8 collective-permute-start.5
  134.6 2.0 %collective-permute-done.7 = bf16[64,512]{1,0:T(8,128)(2,1)S(1)} collective-permute-done((bf16[64,512]{1,0:T(8,128)(2,1)S(1)}, bf16[64,512]{1,0:T(8,128)(2,1)S(1)}, u32[]{:S(2)}, u32[]{:S(2)}) %collective-permute-start.7) | collective-permute-done | bytes 65568 | tf_op jit(solution)/shard_map/ppermute | solution.py:349
  136.6 2.9 %collective-permute-done.6 = bf16[64,512]{1,0:T(8,128)(2,1)S(1)} collective-permute-done((bf16[64,512]{1,0:T(8,128)(2,1)S(1)}, bf16[64,512]{1,0:T(8,128)(2,1)S(1)}, u32[]{:S(2)}, u32[]{:S(2)}) %collective-permute-start.6) | collective-permute-done | bytes 65568 | tf_op jit(solution)/shard_map/ppermute | solution.py:349
  139.5 0.2 collective-permute-done.5
  139.7 5.7 %all-to-all-start.3 = ((bf16[16,16,2176]{2,1,0:T(8,128)(2,1)}), bf16[16,16,2176]{2,1,0:T(8,128)(2,1)S(1)}, u32[]{:S(2)}, u32[]{:S(2)}) async-start(bf16[16,16,2176]{2,1,0:T(8,128)(2,1)} %video_grads.1), calls=%async_computation.3 | async-start | bytes 2228224 | tf_op jit(solution)/shard_map/all_to_all | solution.py:405
  145.7 5.5 %collective-permute-start.10 = (bf16[128,512]{1,0:T(8,128)(2,1)S(1)}, bf16[128,512]{1,0:T(8,128)(2,1)S(1)}, u32[]{:S(2)}, u32[]{:S(2)}) collective-permute-start(bf16[128,512]{1,0:T(8,128)(2,1)S(1)} %fusion.5), channel_id=1, source_target_pairs={{0,48},{16,0},{32,16},{48,32},{64,112},{80,64},{96,80},{112,96},{1... | collective-permute-start | bytes 393224 | tf_op jit(solution)/shard_map/ppermute | solution.py:353
  151.2 1.4 collective-permute-start.9
  152.6 2.4 %collective-permute-start.8 = (bf16[128,512]{1,0:T(8,128)(2,1)S(1)}, bf16[128,512]{1,0:T(8,128)(2,1)S(1)}, u32[]{:S(2)}, u32[]{:S(2)}) collective-permute-start(bf16[128,512]{1,0:T(8,128)(2,1)S(1)} %fusion.5), channel_id=1, source_target_pairs={{0,16},{16,32},{32,48},{48,0},{64,80},{80,96},{96,112},{112,64},{1... | collective-permute-start | bytes 393224 | tf_op jit(solution)/shard_map/ppermute | solution.py:353
  155.0 13.0 %collective-permute-done.10 = bf16[128,512]{1,0:T(8,128)(2,1)S(1)} collective-permute-done((bf16[128,512]{1,0:T(8,128)(2,1)S(1)}, bf16[128,512]{1,0:T(8,128)(2,1)S(1)}, u32[]{:S(2)}, u32[]{:S(2)}) %collective-permute-start.10) | collective-permute-done | bytes 131104 | tf_op jit(solution)/shard_map/ppermute | solution.py:353
  168.0 5.4 %collective-permute-done.9 = bf16[128,512]{1,0:T(8,128)(2,1)S(1)} collective-permute-done((bf16[128,512]{1,0:T(8,128)(2,1)S(1)}, bf16[128,512]{1,0:T(8,128)(2,1)S(1)}, u32[]{:S(2)}, u32[]{:S(2)}) %collective-permute-start.9) | collective-permute-done | bytes 131104 | tf_op jit(solution)/shard_map/ppermute | solution.py:353
  173.4 1.7 collective-permute-start.13
  175.1 0.9 collective-permute-start.12
  176.1 0.6 broadcast_in_dim.49
  176.7 8.7 %all-to-all-start.4 = ((f32[16,1,128]{2,1,0:T(1,128)}), f32[16,1,128]{2,1,0:T(1,128)S(1)}, u32[]{:S(2)}, u32[]{:S(2)}) async-start(f32[16,1,128]{2,1,0:T(1,128)} %broadcast_in_dim.49), calls=%async_computation.4 | async-start | bytes 16384 | tf_op jit(solution)/shard_map/all_to_all | solution.py:418
  185.5 1.1 maximum_bitcast_fusion
  186.6 3.2 %collective-permute-done.11.d1 = f32[128,512]{1,0:T(8,128)S(1)} collective-permute-done((f32[128,512]{1,0:T(8,128)S(1)}, f32[128,512]{1,0:T(8,128)S(1)}, u32[]{:S(2)}, u32[]{:S(2)}) %collective-permute-start.11) | collective-permute-done | bytes 262176 | tf_op jit(solution)/shard_map/ppermute | solution.py:349
  189.8 0.7 copy-done.15
  190.5 2.3 %place_grads.1 = (f32[64,3072]{1,0:T(8,128)}, f32[64,1024]{1,0:T(8,128)}) custom-call(s32[2]{0:T(128)} %copy-done.2, f32[128,512]{1,0:T(8,128)} %copy-done.12, f32[128,512]{1,0:T(8,128)} %copy-done.15, f32[128,512]{1,0:T(8,128)} %copy-done.14, f32[128,512]{1,0:T(8,128)} %copy-done.13), custom_call_target="tpu_custom_call" | custom-call | tf_op jit(solution)/shard_map/place_grads/pallas_call | solution.py:311
  192.8 2.4 %all-to-all-done.4 = f32[16,1,128]{2,1,0:T(1,128)S(1)} async-done(((f32[16,1,128]{2,1,0:T(1,128)}), f32[16,1,128]{2,1,0:T(1,128)S(1)}, u32[]{:S(2)}, u32[]{:S(2)}) %all-to-all-start.4) | async-done | bytes 8224 | tf_op jit(solution)/shard_map/all_to_all | solution.py:418
  195.2 0.6 fusion.12
  (49 shorter events, 1.1 us)
Async XLA Ops:
  3.9 32.7 %copy-start.6 = (f32[1024]{0:T(1024)S(1)}, f32[1024]{0:T(1024)}, u32[]{:S(2)}) copy-start(f32[1024]{0:T(1024)} %param.9) | copy-start | bytes 12292
  3.9 32.7 %copy-start.7 = (f32[1024]{0:T(1024)S(1)}, f32[1024]{0:T(1024)}, u32[]{:S(2)}) copy-start(f32[1024]{0:T(1024)} %param.8) | copy-start | bytes 12292
  3.9 32.7 %all-to-all-start = ((bf16[16,4,16,1024]{3,2,1,0:T(8,128)(2,1)}), bf16[16,4,16,1024]{3,2,1,0:T(8,128)(2,1)S(1)}, u32[]{:S(2)}, u32[]{:S(2)}) async-start(bf16[16,4,16,1024]{3,2,1,0:T(8,128)(2,1)} %bitcast.49), calls=%async_computation | async-start | bytes 4194304 | tf_op jit(solution)/shard_map/all_to_all | solution.py:385
  10.0 55.0 %copy-start.2 = (s32[2]{0:T(128)}, s32[2]{0:T(128)S(1)}, u32[]{:S(2)}) copy-start(s32[2]{0:T(128)S(1)} %pad_add_fusion.place_ref) | copy-start | bytes 28
  36.6 1.6 copy-start.4
  64.8 9.2 %copy-start = (f32[8,4,64,512]{3,2,1,0:T(8,128)}, f32[8,4,64,512]{3,2,1,0:T(8,128)S(1)}, u32[]{:S(2)}) copy-start(f32[8,4,64,512]{3,2,1,0:T(8,128)S(1)} %get-tuple-element.30) | copy-start | bytes 12582916
  64.8 9.2 %collective-permute-start = (bf16[8,4,64,512]{3,2,1,0:T(8,128)(2,1)S(1)}, bf16[8,4,64,512]{3,2,1,0:T(8,128)(2,1)S(1)}, u32[]{:S(2)}, u32[]{:S(2)}) collective-permute-start(bf16[8,4,64,512]{3,2,1,0:T(8,128)(2,1)S(1)} %get-tuple-element.31), channel_id=1, source_target_pairs={{0,1},{1,0},{2,3},{3,2},{4,5},{5,4},{6,7},{7,6},{8,9},{9,8},{10,11... | collective-permute-start | bytes 6291464 | tf_op jit(solution)/shard_map/ppermute | solution.py:340
  68.7 2.0 %copy-start.1 = (f32[4,8,64,512]{3,2,1,0:T(8,128)}, f32[4,8,64,512]{3,2,1,0:T(8,128)S(1)}, u32[]{:S(2)}) copy-start(f32[4,8,64,512]{3,2,1,0:T(8,128)S(1)} %get-tuple-element.36) | copy-start | bytes 12582916
  70.7 1.3 copy-start.5
  72.0 2.0 %copy-start.8 = (bf16[512,4096]{1,0:T(8,128)(2,1)}, bf16[512,4096]{1,0:T(8,128)(2,1)S(1)}, u32[]{:S(2)}) copy-start(bf16[512,4096]{1,0:T(8,128)(2,1)S(1)} %get-tuple-element.33.right_ref.dpk_ref) | copy-start | bytes 12582916
  74.0 1.3 copy-start.10
  77.6 42.5 %all-to-all-start.1 = ((bf16[8,4,64,512]{3,2,1,0:T(8,128)(2,1)}), bf16[8,4,64,512]{3,2,1,0:T(8,128)(2,1)}, u32[]{:S(2)}, u32[]{:S(2)}) async-start(bf16[8,4,64,512]{3,2,1,0:T(8,128)(2,1)} %add_convert_fusion), calls=%async_computation.1 | async-start | bytes 4194304 | tf_op jit(solution)/shard_map/all_to_all | solution.py:345
  83.1 4.4 %collective-permute-start.1 = (bf16[4,8,64,512]{3,2,1,0:T(8,128)(2,1)}, bf16[4,8,64,512]{3,2,1,0:T(8,128)(2,1)S(1)}, u32[]{:S(2)}, u32[]{:S(2)}) collective-permute-start(bf16[4,8,64,512]{3,2,1,0:T(8,128)(2,1)} %copy-done.5), channel_id=1, source_target_pairs={{0,1},{1,0},{2,3},{3,2},{4,5},{5,4},{6,7},{7,6},{8,9},{9,8},{10,11... | collective-permute-start | bytes 6291464 | tf_op jit(solution)/shard_map/ppermute | solution.py:340
  87.4 3.2 %copy-start.11 = (bf16[4,8,64,512]{3,2,1,0:T(8,128)(2,1)}, bf16[4,8,64,512]{3,2,1,0:T(8,128)(2,1)S(1)}, u32[]{:S(2)}) copy-start(bf16[4,8,64,512]{3,2,1,0:T(8,128)(2,1)S(1)} %collective-permute-done.1) | copy-start | bytes 6291460
  87.4 7.8 %copy-start.9 = (bf16[512,4096]{1,0:T(8,128)(2,1)S(1)}, bf16[512,4096]{1,0:T(8,128)(2,1)}, u32[]{:S(2)}) copy-start(bf16[512,4096]{1,0:T(8,128)(2,1)} %copy-done.8) | copy-start | bytes 12582916
  90.7 25.7 %collective-permute-start.4 = (bf16[8,64,512]{2,1,0:T(8,128)(2,1)S(1)}, bf16[8,64,512]{2,1,0:T(8,128)(2,1)}, u32[]{:S(2)}, u32[]{:S(2)}) collective-permute-start(bf16[8,64,512]{2,1,0:T(8,128)(2,1)S(1)} %get-tuple-element.57), channel_id=1, source_target_pairs={{0,192},{16,208},{32,224},{48,240},{64,0},{80,16},{96,32},{112,48}... | collective-permute-start | bytes 1572872 | tf_op jit(solution)/shard_map/ppermute | solution.py:349
  93.5 22.8 %collective-permute-start.3 = (bf16[8,64,512]{2,1,0:T(8,128)(2,1)S(1)}, bf16[8,64,512]{2,1,0:T(8,128)(2,1)}, u32[]{:S(2)}, u32[]{:S(2)}) collective-permute-start(bf16[8,64,512]{2,1,0:T(8,128)(2,1)S(1)} %get-tuple-element.58), channel_id=1, source_target_pairs={{0,128},{16,144},{32,160},{48,176},{64,192},{80,208},{96,224},{112... | collective-permute-start | bytes 1572872 | tf_op jit(solution)/shard_map/ppermute | solution.py:349
  94.3 25.8 %collective-permute-start.2 = (bf16[8,64,512]{2,1,0:T(8,128)(2,1)S(1)}, bf16[8,64,512]{2,1,0:T(8,128)(2,1)}, u32[]{:S(2)}, u32[]{:S(2)}) collective-permute-start(bf16[8,64,512]{2,1,0:T(8,128)(2,1)S(1)} %get-tuple-element.59), channel_id=1, source_target_pairs={{0,64},{16,80},{32,96},{48,112},{64,128},{80,144},{96,160},{112,17... | collective-permute-start | bytes 1572872 | tf_op jit(solution)/shard_map/ppermute | solution.py:349
  95.2 2.8 %copy-start.3 = (bf16[1024,3072]{1,0:T(8,128)(2,1)S(1)}, bf16[1024,3072]{1,0:T(8,128)(2,1)}, u32[]{:S(2)}) copy-start(bf16[1024,3072]{1,0:T(8,128)(2,1)} %wqkv_ref.3) | copy-start | bytes 18874372
  123.2 16.6 %all-to-all-start.2 = ((bf16[8,64,512]{2,1,0:T(8,128)(2,1)}), bf16[8,64,512]{2,1,0:T(8,128)(2,1)S(1)}, u32[]{:S(2)}, u32[]{:S(2)}) async-start(bf16[8,64,512]{2,1,0:T(8,128)(2,1)} %get-tuple-element.55), calls=%async_computation.2 | async-start | bytes 1048576 | tf_op jit(solution)/shard_map/all_to_all | solution.py:345
  132.3 4.3 %collective-permute-start.7 = (bf16[64,512]{1,0:T(8,128)(2,1)S(1)}, bf16[64,512]{1,0:T(8,128)(2,1)S(1)}, u32[]{:S(2)}, u32[]{:S(2)}) collective-permute-start(bf16[64,512]{1,0:T(8,128)(2,1)S(1)} %get-tuple-element.62), channel_id=1, source_target_pairs={{0,192},{16,208},{32,224},{48,240},{64,0},{80,16},{96,32},{112,48}... | collective-permute-start | bytes 196616 | tf_op jit(solution)/shard_map/ppermute | solution.py:349
  133.0 6.5 %collective-permute-start.6 = (bf16[64,512]{1,0:T(8,128)(2,1)S(1)}, bf16[64,512]{1,0:T(8,128)(2,1)S(1)}, u32[]{:S(2)}, u32[]{:S(2)}) collective-permute-start(bf16[64,512]{1,0:T(8,128)(2,1)S(1)} %get-tuple-element.63), channel_id=1, source_target_pairs={{0,128},{16,144},{32,160},{48,176},{64,192},{80,208},{96,224},{112... | collective-permute-start | bytes 196616 | tf_op jit(solution)/shard_map/ppermute | solution.py:349
  133.8 5.9 %collective-permute-start.5 = (bf16[64,512]{1,0:T(8,128)(2,1)S(1)}, bf16[64,512]{1,0:T(8,128)(2,1)S(1)}, u32[]{:S(2)}, u32[]{:S(2)}) collective-permute-start(bf16[64,512]{1,0:T(8,128)(2,1)S(1)} %get-tuple-element.64), channel_id=1, source_target_pairs={{0,64},{16,80},{32,96},{48,112},{64,128},{80,144},{96,160},{112,17... | collective-permute-start | bytes 196616 | tf_op jit(solution)/shard_map/ppermute | solution.py:349
  139.7 36.3 %all-to-all-start.3 = ((bf16[16,16,2176]{2,1,0:T(8,128)(2,1)}), bf16[16,16,2176]{2,1,0:T(8,128)(2,1)S(1)}, u32[]{:S(2)}, u32[]{:S(2)}) async-start(bf16[16,16,2176]{2,1,0:T(8,128)(2,1)} %video_grads.1), calls=%async_computation.3 | async-start | bytes 2228224 | tf_op jit(solution)/shard_map/all_to_all | solution.py:405
  145.7 22.3 %collective-permute-start.10 = (bf16[128,512]{1,0:T(8,128)(2,1)S(1)}, bf16[128,512]{1,0:T(8,128)(2,1)S(1)}, u32[]{:S(2)}, u32[]{:S(2)}) collective-permute-start(bf16[128,512]{1,0:T(8,128)(2,1)S(1)} %fusion.5), channel_id=1, source_target_pairs={{0,48},{16,0},{32,16},{48,32},{64,112},{80,64},{96,80},{112,96},{1... | collective-permute-start | bytes 393224 | tf_op jit(solution)/shard_map/ppermute | solution.py:353
  151.2 22.2 %collective-permute-start.9 = (bf16[128,512]{1,0:T(8,128)(2,1)S(1)}, bf16[128,512]{1,0:T(8,128)(2,1)S(1)}, u32[]{:S(2)}, u32[]{:S(2)}) collective-permute-start(bf16[128,512]{1,0:T(8,128)(2,1)S(1)} %fusion.5), channel_id=1, source_target_pairs={{0,32},{16,48},{32,0},{48,16},{64,96},{80,112},{96,64},{112,80},{1... | collective-permute-start | bytes 393224 | tf_op jit(solution)/shard_map/ppermute | solution.py:353
  152.6 20.7 %collective-permute-start.8 = (bf16[128,512]{1,0:T(8,128)(2,1)S(1)}, bf16[128,512]{1,0:T(8,128)(2,1)S(1)}, u32[]{:S(2)}, u32[]{:S(2)}) collective-permute-start(bf16[128,512]{1,0:T(8,128)(2,1)S(1)} %fusion.5), channel_id=1, source_target_pairs={{0,16},{16,32},{32,48},{48,0},{64,80},{80,96},{96,112},{112,64},{1... | collective-permute-start | bytes 393224 | tf_op jit(solution)/shard_map/ppermute | solution.py:353
  173.4 13.2 %copy-start.12 = (f32[128,512]{1,0:T(8,128)}, f32[128,512]{1,0:T(8,128)S(1)}, u32[]{:S(2)}) copy-start(f32[128,512]{1,0:T(8,128)S(1)} %convert_add_fusion.d0) | copy-start | bytes 786436
  173.4 13.2 %collective-permute-start.13 = (f32[128,512]{1,0:T(8,128)S(1)}, f32[128,512]{1,0:T(8,128)S(1)}, u32[]{:S(2)}, u32[]{:S(2)}) collective-permute-start(f32[128,512]{1,0:T(8,128)S(1)} %convert_add_fusion.d0), channel_id=1, source_target_pairs={{0,192},{16,208},{32,224},{48,240},{64,0},{80,16},{96,32},{112,48}... | collective-permute-start | bytes 786440 | tf_op jit(solution)/shard_map/ppermute | solution.py:349
  175.1 11.5 %collective-permute-start.12 = (f32[128,512]{1,0:T(8,128)S(1)}, f32[128,512]{1,0:T(8,128)S(1)}, u32[]{:S(2)}, u32[]{:S(2)}) collective-permute-start(f32[128,512]{1,0:T(8,128)S(1)} %convert_add_fusion.d0), channel_id=1, source_target_pairs={{0,128},{16,144},{32,160},{48,176},{64,192},{80,208},{96,224},{112... | collective-permute-start | bytes 786440 | tf_op jit(solution)/shard_map/ppermute | solution.py:349
  176.0 13.8 %collective-permute-start.11 = (f32[128,512]{1,0:T(8,128)S(1)}, f32[128,512]{1,0:T(8,128)S(1)}, u32[]{:S(2)}, u32[]{:S(2)}) collective-permute-start(f32[128,512]{1,0:T(8,128)S(1)} %convert_add_fusion.d0), channel_id=1, source_target_pairs={{0,64},{16,80},{32,96},{48,112},{64,128},{80,144},{96,160},{112,17... | collective-permute-start | bytes 786440 | tf_op jit(solution)/shard_map/ppermute | solution.py:349
  176.7 18.5 %all-to-all-start.4 = ((f32[16,1,128]{2,1,0:T(1,128)}), f32[16,1,128]{2,1,0:T(1,128)S(1)}, u32[]{:S(2)}, u32[]{:S(2)}) async-start(f32[16,1,128]{2,1,0:T(1,128)} %broadcast_in_dim.49), calls=%async_computation.4 | async-start | bytes 16384 | tf_op jit(solution)/shard_map/all_to_all | solution.py:418
  186.6 3.2 %copy-start.13 = (f32[128,512]{1,0:T(8,128)}, f32[128,512]{1,0:T(8,128)S(1)}, u32[]{:S(2)}) copy-start(f32[128,512]{1,0:T(8,128)S(1)} %collective-permute-done.13.d3) | copy-start | bytes 786436
  186.6 3.2 %copy-start.14 = (f32[128,512]{1,0:T(8,128)}, f32[128,512]{1,0:T(8,128)S(1)}, u32[]{:S(2)}) copy-start(f32[128,512]{1,0:T(8,128)S(1)} %collective-permute-done.12.d2) | copy-start | bytes 786436
  189.8 0.7 copy-start.15

commit v5 on v4

v5 whole, which is shorter than its diff:
```python
import functools
import math

import jax
import jax.numpy as jnp
from jax import lax
from jax.experimental import pallas as pl
from jax.experimental.pallas import tpu as pltpu
from jax.sharding import PartitionSpec as P

F32 = jnp.float32
BF16 = jnp.bfloat16
MIB = 1024 * 1024
CHUNK = 512


def dot_nn(a, b):
    return lax.dot_general(a, b, (((1,), (0,)), ((), ())), preferred_element_type=F32)


def dot_nt(a, b):
    return lax.dot_general(a, b, (((1,), (1,)), ((), ())), preferred_element_type=F32)


def dot_tn(a, b):
    return lax.dot_general(a, b, (((0,), (0,)), ((), ())), preferred_element_type=F32)


def chunk(n):
    return pl.ds(pl.multiple_of(n * CHUNK, CHUNK), CHUNK)


def block_row(block, place):
    return pl.multiple_of(((block % 2 - place[1]) % 2 * 8 + block // 2) * 64, 64)


def read_place(place_ref):
    return tuple(place_ref[i] for i in range(2))


def whiten(xh):
    centred = xh - jnp.mean(xh, axis=-1, keepdims=True)
    inv = lax.rsqrt(jnp.mean(centred * centred, axis=-1, keepdims=True) + 1e-05)
    return centred * inv, inv


def main_kernel(
    place_ref, tokens_ref, gain_ref, bias_ref, wqkv_ref, wout_ref,
    back_ref, left_hbm, right_hbm,
    left_s, right_s, normed_s, packed_s, datt_s, wh_s, inv_s, dn_s, sems,
):
    place = read_place(place_ref)
    frames, clips, positions, width = tokens_ref.shape
    clips = clips // 2
    halves = positions // 8
    part = frames * 8
    gain = gain_ref[...]
    bias = bias_ref[...]

    def norm_step(i, carry):
        c = i // (frames // 2)
        q = i % (frames // 2)
        x = tokens_ref[pl.ds(2 * q, 2), c].astype(F32).reshape(2, halves, 8, width)
        g = tokens_ref[pl.ds(2 * q, 2), clips + c].astype(F32).reshape(2, halves, 8, width)
        for hf in range(halves):
            at = pl.multiple_of((c * halves + hf) * part + q * 16, 16)
            wh, inv = whiten(x[:, hf].reshape(16, width))
            wh_s[pl.ds(at, 16), :] = wh
            inv_s[pl.ds(at, 16), :] = jnp.broadcast_to(inv, (16, 128))
            normed_s[pl.ds(at, 16), :] = (wh * gain + bias).astype(BF16)
            right_s[pl.ds(at, 16), pl.ds(3 * width, width)] = g[:, hf].reshape(16, width).astype(BF16)
        return carry

    lax.fori_loop(0, clips * frames // 2, norm_step, 0)

    def qkv_step(n, carry):
        packed_s[:, chunk(n)] = dot_nn(normed_s[...], wqkv_ref[:, chunk(n)]).astype(BF16)
        return carry

    lax.fori_loop(0, 3 * width // CHUNK, qkv_step, 0, unroll=2)

    for n in range(width // CHUNK):
        cols = slice(n * CHUNK, (n + 1) * CHUNK)
        datt_s[:, cols] = dot_nt(right_s[:, 3 * width:], wout_ref[cols, :]).astype(BF16)
        turned = normed_s[:, cols].T
        for b in range(CHUNK // 64):
            at = block_row(n * (CHUNK // 64) + b, place)
            left_s[0, pl.ds(at, 64), :] = turned[b * 64:(b + 1) * 64]

    lane = lax.broadcasted_iota(jnp.int32, (part, 128), 1)
    first = lane < 64
    same = lax.broadcasted_iota(jnp.int32, (1, 8, part), 1) == (
        lax.broadcasted_iota(jnp.int32, (1, 8, part), 2) % 8
    )
    zero = jnp.zeros((part, 128), BF16)

    def split(a):
        return jnp.concatenate([jnp.where(first, a, zero), jnp.where(first, zero, a)], axis=0)

    def attend_step(i, carry):
        t = i // (width // 128)
        hp = i % (width // 128)
        tok = pl.ds(pl.multiple_of(t * part, part), part)
        col = pl.multiple_of(hp * 128, 128)
        q = packed_s[tok, pl.ds(col, 128)]
        k = packed_s[tok, pl.ds(width + col, 128)]
        v = packed_s[tok, pl.ds(2 * width + col, 128)]
        da = datt_s[tok, pl.ds(col, 128)]
        k2 = split(k)
        v2 = split(v)
        scores = (dot_nt(k2, q) * 0.125).reshape(2, frames, 8, part)
        e = jnp.exp(scores - jnp.max(scores, axis=1, keepdims=True))
        probs = e * (1.0 / jnp.sum(e, axis=1, keepdims=True))
        probs = jnp.where(same[None], probs, 0.0)
        low = probs.astype(BF16).reshape(2, part, part)
        dp = dot_nt(v2, da).reshape(2, frames, 8, part)
        inner = jnp.sum(dp * probs, axis=1, keepdims=True)
        ds = (probs * (dp - inner) * 0.125).astype(BF16).reshape(2, part, part)
        attended = dot_tn(v2, low.reshape(2 * part, part)).astype(BF16)
        for b in range(2):
            left_s[1, pl.ds(block_row(hp * 2 + b, place), 64), tok] = attended[b * 64:(b + 1) * 64]
        right_s[tok, pl.ds(col, 128)] = dot_tn(ds.reshape(2 * part, part), k2).astype(BF16)
        right_s[tok, pl.ds(width + col, 128)] = dot_nn(
            jnp.concatenate([ds[0], ds[1]], axis=1), split(q)
        ).astype(BF16)
        right_s[tok, pl.ds(2 * width + col, 128)] = dot_nn(
            jnp.concatenate([low[0], low[1]], axis=1), split(da)
        ).astype(BF16)
        return carry

    lax.fori_loop(0, clips * halves * (width // 128), attend_step, 0, unroll=4)

    copies = [
        pltpu.make_async_copy(left_s, left_hbm, sems.at[0]),
        pltpu.make_async_copy(right_s, right_hbm, sems.at[1]),
    ]
    for copy in copies:
        copy.start()

    for n in range(width // CHUNK):
        cols = slice(n * CHUNK, (n + 1) * CHUNK)
        dn_s[:, cols] = dot_nt(right_s[:, :3 * width], wqkv_ref[cols, :])

    def back_step(i, carry):
        dgain, dbias = carry
        c = i // (frames // 2)
        q = i % (frames // 2)
        outs = []
        for hf in range(halves):
            at = pl.multiple_of((c * halves + hf) * part + q * 16, 16)
            dn = dn_s[pl.ds(at, 16), :]
            wh = wh_s[pl.ds(at, 16), :]
            inv = inv_s[pl.ds(at, 16), :][:, :1]
            dw = dn * wh
            dgain = dgain + dw[:8] + dw[8:]
            dbias = dbias + dn[:8] + dn[8:]
            scaled = dn * gain
            m1 = jnp.mean(scaled, axis=-1, keepdims=True)
            m2 = jnp.mean(scaled * wh, axis=-1, keepdims=True)
            g = right_s[pl.ds(at, 16), pl.ds(3 * width, width)].astype(F32)
            outs.append((g + inv * (scaled - m1 - wh * m2)).reshape(2, 8, width))
        grads = jnp.concatenate(outs, axis=1).astype(BF16)
        at = pl.ds(pl.multiple_of(c * positions, positions), positions)
        for f in range(2):
            back_ref[(f - place[1]) % 2, q, at, :width] = grads[f]
        return dgain, dbias

    zeros = jnp.zeros((8, width), F32)
    dgain, dbias = lax.fori_loop(0, clips * frames // 2, back_step, (zeros, zeros))
    dgain = jnp.sum(dgain, axis=0, keepdims=True)
    dbias = jnp.sum(dbias, axis=0, keepdims=True)
    lane = lax.broadcasted_iota(jnp.int32, (1, 128), 1)
    row = lax.broadcasted_iota(jnp.int32, (16, 128), 0)
    back_ref[:, :, 16:, width:] = jnp.zeros((2, 8, clips * positions - 16, 128), BF16)
    for f in range(frames):
        at = f // 2 * 128
        a = dgain[:, at:at + 128]
        b = dbias[:, at:at + 128]
        if f % 2 == 0:
            b = jnp.concatenate([b[:, 64:], b[:, :64]], axis=1)
        else:
            a = jnp.concatenate([a[:, 64:], a[:, :64]], axis=1)
        both = jnp.where(lane < 64, a, b)
        hi = both.astype(BF16).astype(F32)
        mid = (both - hi).astype(BF16).astype(F32)
        low = both - hi - mid
        terms = jnp.where(row == 0, hi, jnp.where(row == 1, mid, jnp.where(row == 2, low, 0.0)))
        back_ref[(f % 2 - place[1]) % 2, f // 2, :16, width:] = terms.astype(BF16)
    for copy in copies:
        copy.wait()


def run_main(place, tokens, gain, bias, wqkv, wout):
    frames, clips, positions, width = tokens.shape
    clips = clips // 2
    rows = clips * frames * positions
    vm = pl.BlockSpec(memory_space=pltpu.VMEM)
    hbm = pl.BlockSpec(memory_space=pl.ANY)
    return pl.pallas_call(
        main_kernel,
        out_shape=(
            jax.ShapeDtypeStruct((2, frames // 2, clips * positions, width + 128), BF16),
            jax.ShapeDtypeStruct((2, width, rows), BF16),
            jax.ShapeDtypeStruct((rows, 4 * width), BF16),
        ),
        in_specs=[pl.BlockSpec(memory_space=pltpu.SMEM)] + [vm] * 5,
        out_specs=(vm, hbm, hbm),
        scratch_shapes=[
            pltpu.VMEM((2, width, rows), BF16),
            pltpu.VMEM((rows, 4 * width), BF16),
            pltpu.VMEM((rows, width), BF16),
            pltpu.VMEM((rows, 3 * width), BF16),
            pltpu.VMEM((rows, width), BF16),
            pltpu.VMEM((rows, width), F32),
            pltpu.VMEM((rows, 128), F32),
            pltpu.VMEM((rows, width), F32),
            pltpu.SemaphoreType.DMA((2,)),
        ],
        compiler_params=pltpu.CompilerParams(vmem_limit_bytes=36 * MIB),
        cost_estimate=pl.CostEstimate(flops=12 * 1024**3, bytes_accessed=20 * MIB, transcendentals=MIB),
        name="sublayer",
    )(place, tokens, gain, bias, wqkv, wout)


def rows_of(left_ref, sibling):
    half = left_ref.shape[1] // 2
    return left_ref[0, half:, :] if sibling else left_ref[0, :half, :]


def send_b_kernel(place_ref, left_ref, right_ref, send_ref):
    send_ref[0] = dot_nn(rows_of(left_ref, True), right_ref[...]).reshape(send_ref.shape[1:]).astype(BF16)


def own_b_kernel(place_ref, left_ref, right_ref, got_ref, own_ref, *term_refs):
    k = pl.program_id(0)
    g = dot_nn(rows_of(left_ref, False), right_ref[...]).reshape(own_ref.shape) + got_ref[0].astype(F32)

    @pl.when(k == 0)
    def _():
        own_ref[...] = g

    for i, term_ref in enumerate(term_refs):
        @pl.when(k == i + 1)
        def _():
            term_ref[...] = g.astype(BF16)


def send_a_kernel(place_ref, left_ref, right_ref, send_ref):
    send_ref[...] = dot_nn(rows_of(left_ref, True), right_ref[...]).reshape(send_ref.shape).astype(BF16)


def own_a_kernel(place_ref, left_ref, right_ref, got_ref, back_ref, theirs_ref, own_ref, message_ref, g_s):
    g = dot_nn(rows_of(left_ref, False), right_ref[...]).reshape(got_ref.shape) + got_ref[...].astype(F32)
    width = got_ref.shape[2]
    message_ref[:, :64, :width] = g.astype(BF16)
    message_ref[:, :64, width:] = jnp.zeros((8, 64, 128), BF16)
    message_ref[:, 64:96, :] = back_ref[0]
    message_ref[:, 96:, :] = theirs_ref[...]
    g_s[...] = g
    own_ref[...] = g_s[place_ref[2]]


def grads_call(kernel, name, grid, in_specs, outs, scratch=()):
    return pl.pallas_call(
        kernel,
        grid_spec=pltpu.PrefetchScalarGridSpec(
            num_scalar_prefetch=1,
            grid=grid,
            in_specs=in_specs,
            out_specs=tuple(spec for spec, _ in outs),
            scratch_shapes=scratch,
        ),
        out_shape=tuple(shape for _, shape in outs),
        compiler_params=pltpu.CompilerParams(vmem_limit_bytes=24 * MIB),
        cost_estimate=pl.CostEstimate(flops=2 * 1024**3, bytes_accessed=8 * MIB, transcendentals=0),
        name=name,
    )


def whole(*shape):
    return pl.BlockSpec(shape, lambda k, place: (0,) * len(shape))


def run_send_b(place, left, right):
    _, width, rows = left.shape
    block = (1, 8, 64, 768)
    ins = [
        whole(1, width, rows),
        pl.BlockSpec((rows, 768), lambda k, place: (0, (place[0] + k) % 4)),
    ]
    out = pl.BlockSpec(block, lambda k, place: (k, 0, 0, 0))
    outs = [(out, jax.ShapeDtypeStruct((4, 8, 64, 768), BF16))]
    return grads_call(send_b_kernel, "send_b", (4,), ins, outs)(place, left, right)[0]


def run_own_b(place, left, right, got):
    _, width, rows = left.shape
    ins = [
        whole(1, width, rows),
        pl.BlockSpec((rows, 768), lambda k, place: (0, (place[0] + k) % 4)),
        pl.BlockSpec((1, 8, 64, 768), lambda k, place: (k, 0, 0, 0)),
    ]
    outs = [(whole(8, 64, 768), jax.ShapeDtypeStruct((8, 64, 768), t)) for t in (F32, BF16, BF16, BF16)]
    return grads_call(own_b_kernel, "own_b", (4,), ins, outs)(place, left, right, got)


def run_send_a(place, left, right):
    _, width, rows = left.shape
    ins = [
        pl.BlockSpec((1, width, rows), lambda k, place: (1, 0, 0)),
        pl.BlockSpec((rows, width), lambda k, place: (0, 3)),
    ]
    outs = [(whole(8, 64, width), jax.ShapeDtypeStruct((8, 64, width), BF16))]
    return grads_call(send_a_kernel, "send_a", (1,), ins, outs)(place, left, right)[0]


def run_own_a(place, left, right, got, back, theirs):
    _, width, rows = left.shape
    ins = [
        pl.BlockSpec((1, width, rows), lambda k, place: (1, 0, 0)),
        pl.BlockSpec((rows, width), lambda k, place: (0, 3)),
        whole(8, 64, width),
        whole(1, 8, 32, width + 128),
        whole(8, 32, width + 128),
    ]
    outs = [
        (whole(64, width), jax.ShapeDtypeStruct((64, width), F32)),
        (whole(8, 128, width + 128), jax.ShapeDtypeStruct((8, 128, width + 128), BF16)),
    ]
    scratch = (pltpu.VMEM((8, 64, width), F32),)
    return grads_call(own_a_kernel, "own_a", (1,), ins, outs, scratch)(place, left, right, got, back, theirs)


def unpack_kernel(place_ref, message_ref, out_ref):
    clips = out_ref.shape[0]
    core = place_ref[1]
    for i in range(8):
        for which in range(2):
            at = pl.multiple_of(i * 32 + (which + core) % 2 * 16, 16)
            for c in range(clips):
                row = 64 + which * 32 + c * 16
                out_ref[c, pl.ds(at, 16), :] = message_ref[i, row:row + 16, :out_ref.shape[2]]


def run_unpack(place, message, clips):
    width = message.shape[2] - 128
    return pl.pallas_call(
        unpack_kernel,
        out_shape=jax.ShapeDtypeStruct((clips, 256, width), BF16),
        in_specs=[pl.BlockSpec(memory_space=pltpu.SMEM), pl.BlockSpec(memory_space=pltpu.VMEM)],
        out_specs=pl.BlockSpec(memory_space=pltpu.VMEM),
        name="unpack",
    )(place, message)


def place_kernel(scale, place_ref, d0, d1, d2, d3, qkv_ref, out_ref):
    for j, d in enumerate((d0, d1, d2, d3)):
        block = (place_ref[0] - j) % 4
        qkv_ref[:, pl.ds(pl.multiple_of(block * 768, 256), 768)] = d[:, :768] * scale
        out_ref[:, pl.ds(pl.multiple_of(block * 256, 256), 256)] = d[:, 768:] * scale


def run_place(place, scale, pieces):
    vm = pl.BlockSpec(memory_space=pltpu.VMEM)
    return pl.pallas_call(
        functools.partial(place_kernel, scale),
        out_shape=(
            jax.ShapeDtypeStruct((64, 6 * CHUNK), F32),
            jax.ShapeDtypeStruct((64, 2 * CHUNK), F32),
        ),
        in_specs=[pl.BlockSpec(memory_space=pltpu.SMEM)] + [vm] * 4,
        out_specs=(vm,) * 2,
        name="place_grads",
    )(place, *pieces)


def frame_pairs(move):
    pairs = []
    for i in range(16):
        y, z, core = move(i // 4, i // 2 % 2, i % 2)
        pairs.append((i, y % 4 * 4 + z % 2 * 2 + core % 2))
    return pairs


def dp_pairs(move):
    pairs = []
    for i in range(16):
        x, h = move(i // 4, i % 4)
        pairs.append((i, x % 4 * 4 + h % 4))
    return pairs


def go_core(a):
    return lax.ppermute(a, "frame", frame_pairs(lambda y, z, c: (y, z, c + 1)))


def trade_yz(a):
    groups = [[2 * i + core for i in range(8)] for core in range(2)]
    return lax.all_to_all(a, "frame", 0, 0, tiled=True, axis_index_groups=groups)


def go_x(a, k):
    return lax.ppermute(a, "dp", dp_pairs(lambda x, h: (x + k, h)))


def go_h(a, k):
    return lax.ppermute(a, "dp", dp_pairs(lambda x, h: (x, h + k)))


def combine(own, got):
    for part in got:
        own = own + part.astype(F32)
    return own


def exchange(pieces, go):
    return [go(pieces[k], k) for k in range(1, 4)]


def pick(array, index):
    return lax.dynamic_index_in_dim(array, index, 0, keepdims=False)


def reduce_yz(own, got, yz):
    mine = (jnp.arange(8) == yz).reshape((8,) + (1,) * own.ndim)
    return jnp.sum(jnp.where(mine, own[None], got.astype(F32)), axis=0)


def local(video, cotangent, norm_gain, norm_bias, qkv_weight, out_weight):
    clips, frames_here, positions, width = video.shape
    grad_scale = 1.0 / math.sqrt(clips * positions * 256)
    frame = lax.axis_index("frame")
    dp = lax.axis_index("dp")
    yz, core = frame // 2, frame % 2
    place = jnp.stack([dp // 4, core, yz]).astype(jnp.int32)
    gain = norm_gain.reshape(1, width)
    bias = norm_bias.reshape(1, width)
    tokens = jnp.concatenate([video, cotangent], axis=0).reshape(2 * clips, 16, positions // 16, width)
    tokens = lax.all_to_all(tokens.transpose(1, 0, 2, 3), "frame", 0, 0, tiled=True)

    back, left, right = run_main(place, tokens, gain, bias, qkv_weight, out_weight)
    theirs = go_core(back[1])

    got_a = go_core(run_send_a(place, left, right))
    send_b = run_send_b(place, left, right)
    got_a, send_b = lax.optimization_barrier((got_a, send_b))
    got_b = go_core(send_b)
    own_a, message = run_own_a(place, left, right, got_a, back, theirs)
    message = trade_yz(message)
    terms_b = run_own_b(place, left, right, got_b)
    got_b = exchange(terms_b, go_x)
    message, got_b = lax.optimization_barrier((message, got_b))

    b = combine(terms_b[0], got_b)
    got_b = trade_yz(b.astype(BF16))
    a = reduce_yz(own_a, message[:, :64, :width], yz).reshape(64, 4, 256)
    terms_a = [lax.dynamic_index_in_dim(a, (dp // 4 + k) % 4, 1, keepdims=False) for k in range(4)]
    got_a = exchange([t.astype(BF16) for t in terms_a], go_x)
    message, got_a, got_b = lax.optimization_barrier((message, got_a, got_b))

    a = combine(terms_a[0], got_a)
    b = reduce_yz(pick(b, yz), got_b, yz)
    own = jnp.concatenate([b, a], axis=1)
    own = combine(own, exchange([own.astype(BF16)] * 4, go_h))
    pieces = [own] + exchange([own] * 4, go_x)

    grad_video = run_unpack(place, message, clips).reshape(video.shape)
    small = jnp.sum(message[:, 64:, width:].astype(F32), axis=(0, 1)).reshape(1, 1, 128)
    small = lax.all_to_all(jnp.broadcast_to(small, (16, 1, 128)), "dp", 0, 0, tiled=True)
    small = jnp.sum(small, axis=(0, 1)) * grad_scale
    pieces, grad_video = lax.optimization_barrier((pieces, grad_video))
    grad_qkv, grad_out = run_place(place, grad_scale, pieces)
    return grad_video, grad_qkv, grad_out, small[:64], small[64:]


def solution(mesh):
    in_specs = (P("dp", "frame", None, None), P("dp", "frame", None, None), P(), P(), P(), P())
    out_specs = (
        P("dp", "frame", None, None),
        P("frame", None),
        P("frame", None),
        P("frame"),
        P("frame"),
    )
    return jax.shard_map(local, mesh=mesh, in_specs=in_specs, out_specs=out_specs, check_vma=False)
```

time: 198 us -> 198 us (level)
  other arithmetic: 15.1 us -> 7.83 us
  waiting for transfers between devices: 72.6 us -> 77.4 us
  local copies, waits for them, and re-layouts: 14.6 us -> 17.5 us
  starting transfers between devices: 50.9 us -> 48.7 us
    ppermute x9, waiting for transfers between devices: 21.2 us -> 42 us  [go_x(): return lax.ppermute(a, 'dp', dp_pairs(lambda x, h: (x + k, h)))]
    ppermute x3, waiting for transfers between devices: 18.3 us -> 0.01 us  [go_h(): return lax.ppermute(a, 'dp', dp_pairs(lambda x, h: (x, h + k)))]
    all_to_all x1 -> x0, starting transfers between devices: 5.72 us -> none  [local(): back = lax.all_to_all(back, 'frame', 0, 0, tiled=True)]
    convert_element_type x2 -> x0, other arithmetic: 5.44 us -> none  [the longest x1 3.22 us: local(): (keep_b[k] + got_b[k].astype(F32)).astype(BF16)]
    ppermute x9, starting transfers between devices: 9.47 us -> 14.9 us  [go_x(): return lax.ppermute(a, 'dp', dp_pairs(lambda x, h: (x + k, h)))]
    all_to_all x1, waiting for transfers between devices: 2.4 us -> 7.16 us  [local(): lax.all_to_all(jnp.broadcast_to(small, (16, 1, 128)), 'dp', 0, 0, tiled=T...]
    ppermute x2 -> x3, waiting for transfers between devices: 4.17 us -> 0.01 us  [go_core(): return lax.ppermute(a, 'frame', frame_pairs(lambda y, z, c: (y, z, c + 1)))]
    all_to_all x1, starting transfers between devices: 8.69 us -> 6.38 us  [local(): lax.all_to_all(jnp.broadcast_to(small, (16, 1, 128)), 'dp', 0, 0, tiled=T...]
  transfers between devices with their start and end apart: 19 -> 19, of which waited for: 11 -> 9; matrix products, arithmetic and copies ran while one was open for 4% -> 3% of each run, Pallas kernels for 8% -> 7%
where the time goes in v5:
time: 198 us; the launch traced here: 196 us
  waiting for transfers between devices  77.4 us (39%)
  starting transfers between devices  48.7 us (25%)
  Pallas kernels  43.7 us (22%)
  local copies, waits for them, and re-layouts  17.5 us (9%)
  other arithmetic  7.83 us (4%)
    ppermute x9, waiting for transfers between devices, go_x(): return lax.ppermute(a, 'dp', dp_pairs(lambda x, h: (x + k, h)))  42 us
    all_to_all x1, waiting for transfers between devices, local(): lax.all_to_all(tokens.transpose(1, 0, 2, 3), 'frame', 0, 0, tiled=True)  26.6 us
    pallas_call x1, Pallas kernels, run_main(): pl.pallas_call(main_kernel, out_shape=(jax.ShapeDtypeStruct((2, frames //...  26.2 us
    ppermute x9, starting transfers between devices, go_x(): return lax.ppermute(a, 'dp', dp_pairs(lambda x, h: (x + k, h)))  14.9 us
    unnamed x33, local copies, waits for them, and re-layouts  13.4 us
    all_to_all x2, starting transfers between devices, trade_yz(): lax.all_to_all(a, 'frame', 0, 0, tiled=True, axis_index_groups=groups)  11.2 us
    ppermute x3, starting transfers between devices, go_h(): return lax.ppermute(a, 'dp', dp_pairs(lambda x, h: (x, h + k)))  9.31 us
    all_to_all x1, waiting for transfers between devices, local(): lax.all_to_all(jnp.broadcast_to(small, (16, 1, 128)), 'dp', 0, 0, tiled=T...  7.16 us
  transfers between devices with their start and end apart: 19, of which 9 were waited for; matrix products, arithmetic and copies ran while one was open for 3% of the time, Pallas kernels for 7%

profile of v5, /device:TPU:32, one launch (start us, length us, event | category | flops | bytes accessed | tf_op | source)
XLA Modules:
  0.0 195.9 jit_solution(5498128087978786096)
XLA Ops:
  0.6 1.7 pad_maximum_fusion
  2.4 1.5 copy.49
  3.9 6.1 %all-to-all-start = ((bf16[16,4,16,1024]{3,2,1,0:T(8,128)(2,1)}), bf16[16,4,16,1024]{3,2,1,0:T(8,128)(2,1)S(1)}, u32[]{:S(2)}, u32[]{:S(2)}) async-start(bf16[16,4,16,1024]{3,2,1,0:T(8,128)(2,1)} %bitcast.35), calls=%async_computation | async-start | bytes 4194304 | tf_op jit(solution)/shard_map/all_to_all | solution.py:439
  10.0 26.6 %all-to-all-done.tokens_ref = bf16[16,4,16,1024]{3,2,1,0:T(8,128)(2,1)S(1)} async-done(((bf16[16,4,16,1024]{3,2,1,0:T(8,128)(2,1)}), bf16[16,4,16,1024]{3,2,1,0:T(8,128)(2,1)S(1)}, u32[]{:S(2)}, u32[]{:S(2)}) %all-to-all-start) | async-done | bytes 2097184 | tf_op jit(solution)/shard_map/all_to_all | solution.py:439
  36.6 1.4 copy-done.3
  38.0 1.6 copy-done.4
  39.6 2.8 %copy-done.7 = bf16[1024,3072]{1,0:T(8,128)(2,1)S(1)} copy-done((bf16[1024,3072]{1,0:T(8,128)(2,1)S(1)}, bf16[1024,3072]{1,0:T(8,128)(2,1)}, u32[]{:S(2)}) %copy-start.7) | copy-done | bytes 6291480
  42.3 1.6 copy-done.8
  43.9 26.2 %sublayer.1 = (bf16[2,8,32,1152]{3,2,1,0:T(8,128)(2,1)S(1)}, bf16[2,1024,512]{2,1,0:T(8,128)(2,1)S(1)}, bf16[512,4096]{1,0:T(8,128)(2,1)S(1)}) custom-call(s32[3]{0:T(128)S(1)} %pad_add_fusion.place_ref, bf16[16,4,16,1024]{3,2,1,0:T(8,128)(2,1)S(1)} %copy-done.4, f32[1,1024]{1,0:T(1,128)S(1)} %bitcast.33, f32[1,1024]{1,0:T(1,128)S(1)} %bitcast.34, ...), custom_call_target="tpu_custom_call" | custom-call | flops 12884901888 | bytes 20971520 | tf_op jit(solution)/shard_map/sublayer/pallas_call | solution.py:199
  70.1 1.2 send_a.1
  72.1 4.6 %send_b.1 = bf16[4,8,64,768]{3,2,1,0:T(8,128)(2,1)} custom-call(s32[3]{0:T(128)S(1)} %pad_add_fusion.place_ref, bf16[2,1024,512]{2,1,0:T(8,128)(2,1)S(1)} %get-tuple-element.32.left_ref, bf16[512,4096]{1,0:T(8,128)(2,1)S(1)} %get-tuple-element.33.right_ref), custom_call_target="tpu_custom_call" | custom-call | flops 2147483648 | bytes 8388608 | tf_op jit(solution)/shard_map/send_b/pallas_call | solution.py:293
  76.8 1.4 own_a.1
  78.2 1.4 copy-done.2
  79.6 5.5 %all-to-all-start.1 = ((bf16[8,128,1152]{2,1,0:T(8,128)(2,1)}), bf16[8,128,1152]{2,1,0:T(8,128)(2,1)}, u32[]{:S(2)}, u32[]{:S(2)}) async-start(bf16[8,128,1152]{2,1,0:T(8,128)(2,1)} %copy-done.2), calls=%async_computation.1 | async-start | bytes 4718592 | tf_op jit(solution)/shard_map/all_to_all | solution.py:399
  85.1 2.2 %copy-done.1 = bf16[512,4096]{1,0:T(8,128)(2,1)S(1)} copy-done((bf16[512,4096]{1,0:T(8,128)(2,1)S(1)}, bf16[512,4096]{1,0:T(8,128)(2,1)}, u32[]{:S(2)}) %copy-start.1) | copy-done | bytes 4194328
  87.3 5.3 %own_b.1 = (f32[8,64,768]{2,1,0:T(8,128)S(1)}, bf16[8,64,768]{2,1,0:T(8,128)(2,1)S(1)}, bf16[8,64,768]{2,1,0:T(8,128)(2,1)S(1)}, bf16[8,64,768]{2,1,0:T(8,128)(2,1)S(1)}) custom-call(s32[3]{0:T(128)S(1)} %pad_add_fusion.place_ref, bf16[2,1024,512]{2,1,0:T(8,128)(2,1)S(1)} %get-tuple-element.32.left_ref, bf16[512,4096]{1,0:T(8,128)(2,1)S(1)} %copy-done.1, ...), custom_call_target="tpu_custom_call" | custom-call | flops 2147483648 | bytes 8388608 | tf_op jit(solution)/shard_map/own_b/pallas_call | solution.py:304
  92.6 1.2 copy-done.5
  93.8 0.6 copy-done.6
  94.4 1.5 collective-permute-start.3
  95.9 2.7 %collective-permute-start.4 = (bf16[8,64,768]{2,1,0:T(8,128)(2,1)S(1)}, bf16[8,64,768]{2,1,0:T(8,128)(2,1)S(1)}, u32[]{:S(2)}, u32[]{:S(2)}) collective-permute-start(bf16[8,64,768]{2,1,0:T(8,128)(2,1)S(1)} %get-tuple-element.40), channel_id=1, source_target_pairs={{0,128},{16,144},{32,160},{48,176},{64,192},{80,208},{96,224},{112... | collective-permute-start | bytes 2359304 | tf_op jit(solution)/shard_map/ppermute | solution.py:403
  98.6 1.4 collective-permute-start.5
  100.1 15.2 %collective-permute-done.3 = bf16[8,64,768]{2,1,0:T(8,128)(2,1)S(1)} collective-permute-done((bf16[8,64,768]{2,1,0:T(8,128)(2,1)S(1)}, bf16[8,64,768]{2,1,0:T(8,128)(2,1)S(1)}, u32[]{:S(2)}, u32[]{:S(2)}) %collective-permute-start.3) | collective-permute-done | bytes 786464 | tf_op jit(solution)/shard_map/ppermute | solution.py:403
  115.3 17.8 %collective-permute-done.4 = bf16[8,64,768]{2,1,0:T(8,128)(2,1)S(1)} collective-permute-done((bf16[8,64,768]{2,1,0:T(8,128)(2,1)S(1)}, bf16[8,64,768]{2,1,0:T(8,128)(2,1)S(1)}, u32[]{:S(2)}, u32[]{:S(2)}) %collective-permute-start.4) | collective-permute-done | bytes 786464 | tf_op jit(solution)/shard_map/ppermute | solution.py:403
  133.1 3.2 %fusion.6 = (bf16[8,64,768]{2,1,0:T(8,128)(2,1)}, f32[8,64,768]{2,1,0:T(8,128)}) fusion(bf16[8,64,768]{2,1,0:T(8,128)(2,1)S(1)} %collective-permute-done.5, bf16[8,64,768]{2,1,0:T(8,128)(2,1)S(1)} %collective-permute-done.4, f32[8,64,768]{2,1,0:T(8,128)} %copy-done.5, bf16[8,64,768]{2,1,0:T(8,128)(2,1)S(1)} %collective-permute-done.3), kind=kLoop, calls=%fused_computation.27 | loop fusion | flops 2752512 | bytes 6291456 | tf_op jit(solution)/shard_map/convert_element_type | solution.py:455
  136.3 5.7 %all-to-all-start.2 = ((bf16[8,64,768]{2,1,0:T(8,128)(2,1)}), bf16[8,64,768]{2,1,0:T(8,128)(2,1)S(1)}, u32[]{:S(2)}, u32[]{:S(2)}) async-start(bf16[8,64,768]{2,1,0:T(8,128)(2,1)} %get-tuple-element.79), calls=%async_computation.2 | async-start | bytes 1572864 | tf_op jit(solution)/shard_map/all_to_all | solution.py:399
  142.0 1.5 select_reduce_fusion
  143.9 1.4 collective-permute-start.6
  145.3 2.4 %collective-permute-start.7 = (bf16[64,256]{1,0:T(8,128)(2,1)S(1)}, bf16[64,256]{1,0:T(8,128)(2,1)S(1)}, u32[]{:S(2)}, u32[]{:S(2)}) collective-permute-start(bf16[64,256]{1,0:T(8,128)(2,1)S(1)} %bitcast.41), channel_id=1, source_target_pairs={{0,128},{16,144},{32,160},{48,176},{64,192},{80,208},{96,224},{112... | collective-permute-start | bytes 98312 | tf_op jit(solution)/shard_map/ppermute | solution.py:403
  147.7 1.6 collective-permute-start.8
  149.3 0.9 dynamic-slice_bitcast_fusion
  150.7 0.9 collective-permute-done.8
  151.6 1.7 all-to-all-done.2
  153.6 6.4 %collective-permute-start.10 = (bf16[64,1024]{1,0:T(8,128)(2,1)S(1)}, bf16[64,1024]{1,0:T(8,128)(2,1)S(1)}, u32[]{:S(2)}, u32[]{:S(2)}) collective-permute-start(bf16[64,1024]{1,0:T(8,128)(2,1)S(1)} %fusion), channel_id=1, source_target_pairs={{0,32},{16,48},{32,0},{48,16},{64,96},{80,112},{96,64},{112,80},{1... | collective-permute-start | bytes 393224 | tf_op jit(solution)/shard_map/ppermute | solution.py:407
  159.9 0.5 collective-permute-start.11
  160.5 2.4 %collective-permute-start.9 = (bf16[64,1024]{1,0:T(8,128)(2,1)S(1)}, bf16[64,1024]{1,0:T(8,128)(2,1)S(1)}, u32[]{:S(2)}, u32[]{:S(2)}) collective-permute-start(bf16[64,1024]{1,0:T(8,128)(2,1)S(1)} %fusion), channel_id=1, source_target_pairs={{0,16},{16,32},{32,48},{48,0},{64,80},{80,96},{96,112},{112,64},{1... | collective-permute-start | bytes 393224 | tf_op jit(solution)/shard_map/ppermute | solution.py:407
  162.9 1.0 convert_reduce_fusion
  163.9 0.6 broadcast_in_dim.46
  164.5 6.4 %all-to-all-start.3 = ((f32[16,1,128]{2,1,0:T(1,128)}), f32[16,1,128]{2,1,0:T(1,128)S(1)}, u32[]{:S(2)}, u32[]{:S(2)}) async-start(f32[16,1,128]{2,1,0:T(1,128)} %broadcast_in_dim.46), calls=%async_computation.3 | async-start | bytes 16384 | tf_op jit(solution)/shard_map/all_to_all | solution.py:469
  170.9 2.7 %unpack.1 = bf16[2,256,1024]{2,1,0:T(8,128)(2,1)} custom-call(s32[3]{0:T(128)} %copy-done.6, bf16[8,128,1152]{2,1,0:T(8,128)(2,1)} %all-to-all-done.1.message_ref), custom_call_target="tpu_custom_call" | custom-call | tf_op jit(solution)/shard_map/unpack/pallas_call | solution.py:347
  173.6 7.2 %all-to-all-done.3 = f32[16,1,128]{2,1,0:T(1,128)S(1)} async-done(((f32[16,1,128]{2,1,0:T(1,128)}), f32[16,1,128]{2,1,0:T(1,128)S(1)}, u32[]{:S(2)}, u32[]{:S(2)}) %all-to-all-start.3) | async-done | bytes 8224 | tf_op jit(solution)/shard_map/all_to_all | solution.py:469
  180.9 0.6 collective-permute-start.12
  181.5 2.1 %collective-permute-start.13 = (f32[64,1024]{1,0:T(8,128)S(1)}, f32[64,1024]{1,0:T(8,128)S(1)}, u32[]{:S(2)}, u32[]{:S(2)}) collective-permute-start(f32[64,1024]{1,0:T(8,128)S(1)} %convert_add_fusion.1.d0), channel_id=1, source_target_pairs={{0,128},{16,144},{32,160},{48,176},{64,192},{80,208},{96,224},{112... | collective-permute-start | bytes 786440 | tf_op jit(solution)/shard_map/ppermute | solution.py:403
  183.6 1.2 collective-permute-start.14
  184.8 0.6 fusion.7
  185.3 7.0 %collective-permute-done.12.d1 = f32[64,1024]{1,0:T(8,128)S(1)} collective-permute-done((f32[64,1024]{1,0:T(8,128)S(1)}, f32[64,1024]{1,0:T(8,128)S(1)}, u32[]{:S(2)}, u32[]{:S(2)}) %collective-permute-start.12) | collective-permute-done | bytes 262176 | tf_op jit(solution)/shard_map/ppermute | solution.py:403
  192.3 0.7 collective-permute-done.14.d3
  193.1 0.6 copy-done.14
  193.7 2.2 %place_grads.1 = (f32[64,3072]{1,0:T(8,128)}, f32[64,1024]{1,0:T(8,128)}) custom-call(s32[3]{0:T(128)} %copy-done.6, f32[64,1024]{1,0:T(8,128)} %copy-done.11, f32[64,1024]{1,0:T(8,128)} %copy-done.12, f32[64,1024]{1,0:T(8,128)} %copy-done.13, f32[64,1024]{1,0:T(8,128)} %copy-done.14), custom_call_target="tpu_custom_call" | custom-call | tf_op jit(solution)/shard_map/place_grads/pallas_call | solution.py:365
  (50 shorter events, 2.3 us)
Async XLA Ops:
  3.9 34.1 %copy-start.9 = (f32[1024]{0:T(1024)S(1)}, f32[1024]{0:T(1024)}, u32[]{:S(2)}) copy-start(f32[1024]{0:T(1024)} %param.8) | copy-start | bytes 12292
  3.9 34.1 %copy-start.10 = (f32[1024]{0:T(1024)S(1)}, f32[1024]{0:T(1024)}, u32[]{:S(2)}) copy-start(f32[1024]{0:T(1024)} %param.9) | copy-start | bytes 12292
  3.9 32.7 %all-to-all-start = ((bf16[16,4,16,1024]{3,2,1,0:T(8,128)(2,1)}), bf16[16,4,16,1024]{3,2,1,0:T(8,128)(2,1)S(1)}, u32[]{:S(2)}, u32[]{:S(2)}) async-start(bf16[16,4,16,1024]{3,2,1,0:T(8,128)(2,1)} %bitcast.35), calls=%async_computation | async-start | bytes 4194304 | tf_op jit(solution)/shard_map/all_to_all | solution.py:439
  36.6 1.4 copy-start.3
  38.0 1.6 copy-start.4
  39.6 2.8 %copy-start.7 = (bf16[1024,3072]{1,0:T(8,128)(2,1)S(1)}, bf16[1024,3072]{1,0:T(8,128)(2,1)}, u32[]{:S(2)}) copy-start(bf16[1024,3072]{1,0:T(8,128)(2,1)} %wqkv_ref.1) | copy-start | bytes 18874372
  42.3 1.6 copy-start.8
  70.1 6.7 %copy-start = (bf16[512,4096]{1,0:T(8,128)(2,1)}, bf16[512,4096]{1,0:T(8,128)(2,1)S(1)}, u32[]{:S(2)}) copy-start(bf16[512,4096]{1,0:T(8,128)(2,1)S(1)} %get-tuple-element.33.right_ref) | copy-start | bytes 12582916
  71.4 5.3 %collective-permute-start = (bf16[8,64,1024]{2,1,0:T(8,128)(2,1)S(1)}, bf16[8,64,1024]{2,1,0:T(8,128)(2,1)S(1)}, u32[]{:S(2)}, u32[]{:S(2)}) collective-permute-start(bf16[8,64,1024]{2,1,0:T(8,128)(2,1)S(1)} %send_a.1), channel_id=1, source_target_pairs={{0,1},{1,0},{2,3},{3,2},{4,5},{5,4},{6,7},{7,6},{8,9},{9,8},{10,11... | collective-permute-start | bytes 3145736 | tf_op jit(solution)/shard_map/ppermute | solution.py:394
  71.6 5.2 %collective-permute-start.2 = (bf16[8,32,1152]{2,1,0:T(8,128)(2,1)S(1)}, bf16[8,32,1152]{2,1,0:T(8,128)(2,1)S(1)}, u32[]{:S(2)}, u32[]{:S(2)}) collective-permute-start(bf16[8,32,1152]{2,1,0:T(8,128)(2,1)S(1)} %slice_bitcast_fusion), channel_id=1, source_target_pairs={{0,1},{1,0},{2,3},{3,2},{4,5},{5,4},{6,7},{7,6},{8,9},{9,8},{10,11... | collective-permute-start | bytes 1769480 | tf_op jit(solution)/shard_map/ppermute | solution.py:394
  76.7 8.4 %collective-permute-start.1 = (bf16[4,8,64,768]{3,2,1,0:T(8,128)(2,1)}, bf16[4,8,64,768]{3,2,1,0:T(8,128)(2,1)}, u32[]{:S(2)}, u32[]{:S(2)}) collective-permute-start(bf16[4,8,64,768]{3,2,1,0:T(8,128)(2,1)} %send_b.1), channel_id=1, source_target_pairs={{0,1},{1,0},{2,3},{3,2},{4,5},{5,4},{6,7},{7,6},{8,9},{9,8},{10,11... | collective-permute-start | bytes 9437192 | tf_op jit(solution)/shard_map/ppermute | solution.py:394
  78.2 1.4 copy-start.2
  79.6 53.5 %all-to-all-start.1 = ((bf16[8,128,1152]{2,1,0:T(8,128)(2,1)}), bf16[8,128,1152]{2,1,0:T(8,128)(2,1)}, u32[]{:S(2)}, u32[]{:S(2)}) async-start(bf16[8,128,1152]{2,1,0:T(8,128)(2,1)} %copy-done.2), calls=%async_computation.1 | async-start | bytes 4718592 | tf_op jit(solution)/shard_map/all_to_all | solution.py:399
  85.1 2.2 %copy-start.1 = (bf16[512,4096]{1,0:T(8,128)(2,1)S(1)}, bf16[512,4096]{1,0:T(8,128)(2,1)}, u32[]{:S(2)}) copy-start(bf16[512,4096]{1,0:T(8,128)(2,1)} %copy-done) | copy-start | bytes 12582916
  92.6 1.2 copy-start.5
  93.8 0.6 copy-start.6
  94.4 20.9 %collective-permute-start.3 = (bf16[8,64,768]{2,1,0:T(8,128)(2,1)S(1)}, bf16[8,64,768]{2,1,0:T(8,128)(2,1)S(1)}, u32[]{:S(2)}, u32[]{:S(2)}) collective-permute-start(bf16[8,64,768]{2,1,0:T(8,128)(2,1)S(1)} %get-tuple-element.39), channel_id=1, source_target_pairs={{0,64},{16,80},{32,96},{48,112},{64,128},{80,144},{96,160},{112,17... | collective-permute-start | bytes 2359304 | tf_op jit(solution)/shard_map/ppermute | solution.py:403
  95.9 37.2 %collective-permute-start.4 = (bf16[8,64,768]{2,1,0:T(8,128)(2,1)S(1)}, bf16[8,64,768]{2,1,0:T(8,128)(2,1)S(1)}, u32[]{:S(2)}, u32[]{:S(2)}) collective-permute-start(bf16[8,64,768]{2,1,0:T(8,128)(2,1)S(1)} %get-tuple-element.40), channel_id=1, source_target_pairs={{0,128},{16,144},{32,160},{48,176},{64,192},{80,208},{96,224},{112... | collective-permute-start | bytes 2359304 | tf_op jit(solution)/shard_map/ppermute | solution.py:403
  98.6 34.5 %collective-permute-start.5 = (bf16[8,64,768]{2,1,0:T(8,128)(2,1)S(1)}, bf16[8,64,768]{2,1,0:T(8,128)(2,1)S(1)}, u32[]{:S(2)}, u32[]{:S(2)}) collective-permute-start(bf16[8,64,768]{2,1,0:T(8,128)(2,1)S(1)} %get-tuple-element.41), channel_id=1, source_target_pairs={{0,192},{16,208},{32,224},{48,240},{64,0},{80,16},{96,32},{112,48}... | collective-permute-start | bytes 2359304 | tf_op jit(solution)/shard_map/ppermute | solution.py:403
  136.3 17.0 %all-to-all-start.2 = ((bf16[8,64,768]{2,1,0:T(8,128)(2,1)}), bf16[8,64,768]{2,1,0:T(8,128)(2,1)S(1)}, u32[]{:S(2)}, u32[]{:S(2)}) async-start(bf16[8,64,768]{2,1,0:T(8,128)(2,1)} %get-tuple-element.79), calls=%async_computation.2 | async-start | bytes 1572864 | tf_op jit(solution)/shard_map/all_to_all | solution.py:399
  143.9 6.4 %collective-permute-start.6 = (bf16[64,256]{1,0:T(8,128)(2,1)S(1)}, bf16[64,256]{1,0:T(8,128)(2,1)S(1)}, u32[]{:S(2)}, u32[]{:S(2)}) collective-permute-start(bf16[64,256]{1,0:T(8,128)(2,1)S(1)} %bitcast.40), channel_id=1, source_target_pairs={{0,64},{16,80},{32,96},{48,112},{64,128},{80,144},{96,160},{112,17... | collective-permute-start | bytes 98312 | tf_op jit(solution)/shard_map/ppermute | solution.py:403
  145.3 5.4 %collective-permute-start.7 = (bf16[64,256]{1,0:T(8,128)(2,1)S(1)}, bf16[64,256]{1,0:T(8,128)(2,1)S(1)}, u32[]{:S(2)}, u32[]{:S(2)}) collective-permute-start(bf16[64,256]{1,0:T(8,128)(2,1)S(1)} %bitcast.41), channel_id=1, source_target_pairs={{0,128},{16,144},{32,160},{48,176},{64,192},{80,208},{96,224},{112... | collective-permute-start | bytes 98312 | tf_op jit(solution)/shard_map/ppermute | solution.py:403
  147.7 3.9 %collective-permute-start.8 = (bf16[64,256]{1,0:T(8,128)(2,1)S(1)}, bf16[64,256]{1,0:T(8,128)(2,1)S(1)}, u32[]{:S(2)}, u32[]{:S(2)}) collective-permute-start(bf16[64,256]{1,0:T(8,128)(2,1)S(1)} %bitcast.42), channel_id=1, source_target_pairs={{0,192},{16,208},{32,224},{48,240},{64,0},{80,16},{96,32},{112,48}... | collective-permute-start | bytes 98312 | tf_op jit(solution)/shard_map/ppermute | solution.py:403
  153.6 27.2 %collective-permute-start.10 = (bf16[64,1024]{1,0:T(8,128)(2,1)S(1)}, bf16[64,1024]{1,0:T(8,128)(2,1)S(1)}, u32[]{:S(2)}, u32[]{:S(2)}) collective-permute-start(bf16[64,1024]{1,0:T(8,128)(2,1)S(1)} %fusion), channel_id=1, source_target_pairs={{0,32},{16,48},{32,0},{48,16},{64,96},{80,112},{96,64},{112,80},{1... | collective-permute-start | bytes 393224 | tf_op jit(solution)/shard_map/ppermute | solution.py:407
  159.9 20.8 %collective-permute-start.11 = (bf16[64,1024]{1,0:T(8,128)(2,1)S(1)}, bf16[64,1024]{1,0:T(8,128)(2,1)S(1)}, u32[]{:S(2)}, u32[]{:S(2)}) collective-permute-start(bf16[64,1024]{1,0:T(8,128)(2,1)S(1)} %fusion), channel_id=1, source_target_pairs={{0,48},{16,0},{32,16},{48,32},{64,112},{80,64},{96,80},{112,96},{1... | collective-permute-start | bytes 393224 | tf_op jit(solution)/shard_map/ppermute | solution.py:407
  160.5 20.3 %collective-permute-start.9 = (bf16[64,1024]{1,0:T(8,128)(2,1)S(1)}, bf16[64,1024]{1,0:T(8,128)(2,1)S(1)}, u32[]{:S(2)}, u32[]{:S(2)}) collective-permute-start(bf16[64,1024]{1,0:T(8,128)(2,1)S(1)} %fusion), channel_id=1, source_target_pairs={{0,16},{16,32},{32,48},{48,0},{64,80},{80,96},{96,112},{112,64},{1... | collective-permute-start | bytes 393224 | tf_op jit(solution)/shard_map/ppermute | solution.py:407
  164.5 16.3 %all-to-all-start.3 = ((f32[16,1,128]{2,1,0:T(1,128)}), f32[16,1,128]{2,1,0:T(1,128)S(1)}, u32[]{:S(2)}, u32[]{:S(2)}) async-start(f32[16,1,128]{2,1,0:T(1,128)} %broadcast_in_dim.46), calls=%async_computation.3 | async-start | bytes 16384 | tf_op jit(solution)/shard_map/all_to_all | solution.py:469
  180.9 12.1 %copy-start.11 = (f32[64,1024]{1,0:T(8,128)}, f32[64,1024]{1,0:T(8,128)S(1)}, u32[]{:S(2)}) copy-start(f32[64,1024]{1,0:T(8,128)S(1)} %convert_add_fusion.1.d0) | copy-start | bytes 786436
  180.9 11.4 %collective-permute-start.12 = (f32[64,1024]{1,0:T(8,128)S(1)}, f32[64,1024]{1,0:T(8,128)S(1)}, u32[]{:S(2)}, u32[]{:S(2)}) collective-permute-start(f32[64,1024]{1,0:T(8,128)S(1)} %convert_add_fusion.1.d0), channel_id=1, source_target_pairs={{0,64},{16,80},{32,96},{48,112},{64,128},{80,144},{96,160},{112,17... | collective-permute-start | bytes 786440 | tf_op jit(solution)/shard_map/ppermute | solution.py:403
  181.5 10.8 %collective-permute-start.13 = (f32[64,1024]{1,0:T(8,128)S(1)}, f32[64,1024]{1,0:T(8,128)S(1)}, u32[]{:S(2)}, u32[]{:S(2)}) collective-permute-start(f32[64,1024]{1,0:T(8,128)S(1)} %convert_add_fusion.1.d0), channel_id=1, source_target_pairs={{0,128},{16,144},{32,160},{48,176},{64,192},{80,208},{96,224},{112... | collective-permute-start | bytes 786440 | tf_op jit(solution)/shard_map/ppermute | solution.py:403
  183.6 9.4 %collective-permute-start.14 = (f32[64,1024]{1,0:T(8,128)S(1)}, f32[64,1024]{1,0:T(8,128)S(1)}, u32[]{:S(2)}, u32[]{:S(2)}) collective-permute-start(f32[64,1024]{1,0:T(8,128)S(1)} %convert_add_fusion.1.d0), channel_id=1, source_target_pairs={{0,192},{16,208},{32,224},{48,240},{64,0},{80,16},{96,32},{112,48}... | collective-permute-start | bytes 786440 | tf_op jit(solution)/shard_map/ppermute | solution.py:403
  192.3 0.7 copy-start.12
  192.3 0.8 copy-start.13
  193.0 0.7 copy-start.14

commit v6 on v5

--- a/solution.py
+++ b/solution.py
@@ -45,43 +45,62 @@
 
 
 def main_kernel(
-    place_ref, tokens_ref, gain_ref, bias_ref, wqkv_ref, wout_ref,
-    back_ref, left_hbm, right_hbm,
-    left_s, right_s, normed_s, packed_s, datt_s, wh_s, inv_s, dn_s, sems,
+    place_ref, tokens_hbm, gain_ref, bias_ref, wqkv_hbm, wout_hbm,
+    left_hbm, right_hbm, send_a_hbm, send_b_hbm,
+    tokens_s, wqkv_s, wout_s, left_s, right_s, normed_s, packed_s, datt_s, send_a_s, send_b_s,
+    token_sems, weight_sems, out_sems,
 ):
     place = read_place(place_ref)
-    frames, clips, positions, width = tokens_ref.shape
+    frames, clips, positions, width = tokens_s.shape
     clips = clips // 2
     halves = positions // 8
     part = frames * 8
     gain = gain_ref[...]
     bias = bias_ref[...]
 
-    def norm_step(i, carry):
-        c = i // (frames // 2)
-        q = i % (frames // 2)
-        x = tokens_ref[pl.ds(2 * q, 2), c].astype(F32).reshape(2, halves, 8, width)
-        g = tokens_ref[pl.ds(2 * q, 2), clips + c].astype(F32).reshape(2, halves, 8, width)
-        for hf in range(halves):
-            at = pl.multiple_of((c * halves + hf) * part + q * 16, 16)
-            wh, inv = whiten(x[:, hf].reshape(16, width))
-            wh_s[pl.ds(at, 16), :] = wh
-            inv_s[pl.ds(at, 16), :] = jnp.broadcast_to(inv, (16, 128))
-            normed_s[pl.ds(at, 16), :] = (wh * gain + bias).astype(BF16)
-            right_s[pl.ds(at, 16), pl.ds(3 * width, width)] = g[:, hf].reshape(16, width).astype(BF16)
+    def load_tokens(q):
+        pair = pl.ds(2 * q, 2)
+        return pltpu.make_async_copy(tokens_hbm.at[pair], tokens_s.at[pair], token_sems.at[q])
+
+    def load_wqkv(n):
+        return pltpu.make_async_copy(wqkv_hbm.at[:, chunk(n)], wqkv_s.at[:, chunk(n)], weight_sems.at[n])
+
+    blocks = 3 * width // CHUNK
+    load_wout = pltpu.make_async_copy(wout_hbm, wout_s, weight_sems.at[blocks])
+    for q in range(frames // 2):
+        load_tokens(q).start()
+    for n in range(blocks):
+        load_wqkv(n).start()
+    load_wout.start()
+
+    def norm_step(q, carry):
+        load_tokens(q).wait()
+        for c in range(clips):
+            x = tokens_s[pl.ds(2 * q, 2), c].astype(F32).reshape(2, halves, 8, width)
+            g = tokens_s[pl.ds(2 * q, 2), clips + c].astype(F32).reshape(2, halves, 8, width)
+            for hf in range(halves):
+                at = pl.multiple_of((c * halves + hf) * part + q * 16, 16)
+                wh, _ = whiten(x[:, hf].reshape(16, width))
+                normed_s[pl.ds(at, 16), :] = (wh * gain + bias).astype(BF16)
+                right_s[pl.ds(at, 16), pl.ds(3 * width, width)] = g[:, hf].reshape(16, width).astype(BF16)
         return carry
 
-    lax.fori_loop(0, clips * frames // 2, norm_step, 0)
+    lax.fori_loop(0, frames // 2, norm_step, 0)
 
     def qkv_step(n, carry):
-        packed_s[:, chunk(n)] = dot_nn(normed_s[...], wqkv_ref[:, chunk(n)]).astype(BF16)
+        for i in range(2):
+            load_wqkv(2 * n + i).wait()
+        for i in range(2):
+            cols = chunk(2 * n + i)
+            packed_s[:, cols] = dot_nn(normed_s[...], wqkv_s[:, cols]).astype(BF16)
         return carry
 
-    lax.fori_loop(0, 3 * width // CHUNK, qkv_step, 0, unroll=2)
+    lax.fori_loop(0, blocks // 2, qkv_step, 0)
+    load_wout.wait()
 
     for n in range(width // CHUNK):
         cols = slice(n * CHUNK, (n + 1) * CHUNK)
-        datt_s[:, cols] = dot_nt(right_s[:, 3 * width:], wout_ref[cols, :]).astype(BF16)
+        datt_s[:, cols] = dot_nt(right_s[:, 3 * width:], wout_s[cols, :]).astype(BF16)
         turned = normed_s[:, cols].T
         for b in range(CHUNK // 64):
             at = block_row(n * (CHUNK // 64) + b, place)
@@ -131,38 +150,106 @@
     lax.fori_loop(0, clips * halves * (width // 128), attend_step, 0, unroll=4)
 
     copies = [
-        pltpu.make_async_copy(left_s, left_hbm, sems.at[0]),
-        pltpu.make_async_copy(right_s, right_hbm, sems.at[1]),
+        pltpu.make_async_copy(left_s, left_hbm, out_sems.at[0]),
+        pltpu.make_async_copy(right_s, right_hbm, out_sems.at[1]),
     ]
+    g = dot_nn(left_s[1, width // 2:, :], right_s[:, 3 * width:])
+    send_a_s[...] = g.reshape(send_a_s.shape).astype(BF16)
+    copies.append(pltpu.make_async_copy(send_a_s, send_a_hbm, out_sems.at[2]))
+    copies[-1].start()
+    for k in range(4):
+        cols = pl.ds(pl.multiple_of((place[0] + k) % 4 * 768, 256), 768)
+        g = dot_nn(left_s[0, width // 2:, :], right_s[:, cols])
+        send_b_s[k] = g.reshape(send_b_s.shape[1:]).astype(BF16)
+        copies.append(pltpu.make_async_copy(send_b_s.at[k], send_b_hbm.at[k], out_sems.at[3 + k]))
+        copies[-1].start()
+    for copy in copies[:2]:
+        copy.start()
     for copy in copies:
-        copy.start()
-
+        copy.wait()
+
+
+def run_main(place, tokens, gain, bias, wqkv, wout):
+    frames, clips, positions, width = tokens.shape
+    rows = clips // 2 * frames * positions
+    vm = pl.BlockSpec(memory_space=pltpu.VMEM)
+    hbm = pl.BlockSpec(memory_space=pl.ANY)
+    outs = [(2, width, rows), (rows, 4 * width), (8, 64, width), (4, 8, 64, 768)]
+    return pl.pallas_call(
+        main_kernel,
+        out_shape=tuple(jax.ShapeDtypeStruct(shape, BF16) for shape in outs),
+        in_specs=[pl.BlockSpec(memory_space=pltpu.SMEM), hbm, vm, vm, hbm, hbm],
+        out_specs=(hbm,) * 4,
+        scratch_shapes=[
+            pltpu.VMEM(tokens.shape, BF16),
+            pltpu.VMEM(wqkv.shape, BF16),
+            pltpu.VMEM(wout.shape, BF16),
+            pltpu.VMEM(outs[0], BF16),
+            pltpu.VMEM(outs[1], BF16),
+            pltpu.VMEM((rows, width), BF16),
+            pltpu.VMEM((rows, 3 * width), BF16),
+            pltpu.VMEM((rows, width), BF16),
+            pltpu.VMEM(outs[2], BF16),
+            pltpu.VMEM(outs[3], BF16),
+            pltpu.SemaphoreType.DMA((frames // 2,)),
+            pltpu.SemaphoreType.DMA((3 * width // CHUNK + 1,)),
+            pltpu.SemaphoreType.DMA((7,)),
+        ],
+        compiler_params=pltpu.CompilerParams(vmem_limit_bytes=63 * MIB),
+        cost_estimate=pl.CostEstimate(flops=12 * 1024**3, bytes_accessed=20 * MIB, transcendentals=MIB),
+        name="sublayer",
+    )(place, tokens, gain, bias, wqkv, wout)
+
+
+def back_kernel(
+    place_ref, tokens_hbm, gain_ref, right_hbm, wqkv_hbm, back_ref,
+    tokens_s, right_s, wqkv_s, dn_s, sems,
+):
+    core = place_ref[1]
+    frames, clips, positions, width = tokens_s.shape
+    clips = clips // 2
+    halves = positions // 8
+    part = frames * 8
+    gain = gain_ref[...]
+    load_right = pltpu.make_async_copy(right_hbm.at[:, pl.ds(0, 3 * width)], right_s, sems.at[0])
+    load_right.start()
+    loads = []
     for n in range(width // CHUNK):
+        rows = pl.ds(n * CHUNK, CHUNK)
+        loads.append(pltpu.make_async_copy(wqkv_hbm.at[rows], wqkv_s.at[rows], sems.at[1 + n]))
+        loads[-1].start()
+    load_tokens = pltpu.make_async_copy(tokens_hbm, tokens_s, sems.at[1 + len(loads)])
+    load_tokens.start()
+    load_right.wait()
+    for n, load in enumerate(loads):
         cols = slice(n * CHUNK, (n + 1) * CHUNK)
-        dn_s[:, cols] = dot_nt(right_s[:, :3 * width], wqkv_ref[cols, :])
+        load.wait()
+        dn_s[:, cols] = dot_nt(right_s[...], wqkv_s[cols, :])
+    load_tokens.wait()
 
     def back_step(i, carry):
         dgain, dbias = carry
         c = i // (frames // 2)
         q = i % (frames // 2)
+        x = tokens_s[pl.ds(2 * q, 2), c].astype(F32).reshape(2, halves, 8, width)
+        g = tokens_s[pl.ds(2 * q, 2), clips + c].astype(F32).reshape(2, halves, 8, width)
         outs = []
         for hf in range(halves):
             at = pl.multiple_of((c * halves + hf) * part + q * 16, 16)
             dn = dn_s[pl.ds(at, 16), :]
-            wh = wh_s[pl.ds(at, 16), :]
-            inv = inv_s[pl.ds(at, 16), :][:, :1]
+            wh, inv = whiten(x[:, hf].reshape(16, width))
             dw = dn * wh
             dgain = dgain + dw[:8] + dw[8:]
             dbias = dbias + dn[:8] + dn[8:]
             scaled = dn * gain
             m1 = jnp.mean(scaled, axis=-1, keepdims=True)
             m2 = jnp.mean(scaled * wh, axis=-1, keepdims=True)
-            g = right_s[pl.ds(at, 16), pl.ds(3 * width, width)].astype(F32)
-            outs.append((g + inv * (scaled - m1 - wh * m2)).reshape(2, 8, width))
+            grad = g[:, hf].reshape(16, width) + inv * (scaled - m1 - wh * m2)
+            outs.append(grad.reshape(2, 8, width))
         grads = jnp.concatenate(outs, axis=1).astype(BF16)
         at = pl.ds(pl.multiple_of(c * positions, positions), positions)
         for f in range(2):
-            back_ref[(f - place[1]) % 2, q, at, :width] = grads[f]
+            back_ref[(f - core) % 2, q, at, :width] = grads[f]
         return dgain, dbias
 
     zeros = jnp.zeros((8, width), F32)
@@ -185,41 +272,31 @@
         mid = (both - hi).astype(BF16).astype(F32)
         low = both - hi - mid
         terms = jnp.where(row == 0, hi, jnp.where(row == 1, mid, jnp.where(row == 2, low, 0.0)))
-        back_ref[(f % 2 - place[1]) % 2, f // 2, :16, width:] = terms.astype(BF16)
-    for copy in copies:
-        copy.wait()
-
-
-def run_main(place, tokens, gain, bias, wqkv, wout):
+        back_ref[(f % 2 - core) % 2, f // 2, :16, width:] = terms.astype(BF16)
+
+
+def run_back(place, tokens, gain, right, wqkv):
     frames, clips, positions, width = tokens.shape
     clips = clips // 2
     rows = clips * frames * positions
     vm = pl.BlockSpec(memory_space=pltpu.VMEM)
     hbm = pl.BlockSpec(memory_space=pl.ANY)
     return pl.pallas_call(
-        main_kernel,
-        out_shape=(
-            jax.ShapeDtypeStruct((2, frames // 2, clips * positions, width + 128), BF16),
-            jax.ShapeDtypeStruct((2, width, rows), BF16),
-            jax.ShapeDtypeStruct((rows, 4 * width), BF16),
-        ),
-        in_specs=[pl.BlockSpec(memory_space=pltpu.SMEM)] + [vm] * 5,
-        out_specs=(vm, hbm, hbm),
+        back_kernel,
+        out_shape=jax.ShapeDtypeStruct((2, frames // 2, clips * positions, width + 128), BF16),
+        in_specs=[pl.BlockSpec(memory_space=pltpu.SMEM), hbm, vm, hbm, hbm],
+        out_specs=vm,
         scratch_shapes=[
-            pltpu.VMEM((2, width, rows), BF16),
-            pltpu.VMEM((rows, 4 * width), BF16),
-            pltpu.VMEM((rows, width), BF16),
+            pltpu.VMEM(tokens.shape, BF16),
             pltpu.VMEM((rows, 3 * width), BF16),
-            pltpu.VMEM((rows, width), BF16),
+            pltpu.VMEM(wqkv.shape, BF16),
             pltpu.VMEM((rows, width), F32),
-            pltpu.VMEM((rows, 128), F32),
-            pltpu.VMEM((rows, width), F32),
-            pltpu.SemaphoreType.DMA((2,)),
+            pltpu.SemaphoreType.DMA((4,)),
         ],
-        compiler_params=pltpu.CompilerParams(vmem_limit_bytes=36 * MIB),
-        cost_estimate=pl.CostEstimate(flops=12 * 1024**3, bytes_accessed=20 * MIB, transcendentals=MIB),
-        name="sublayer",
-    )(place, tokens, gain, bias, wqkv, wout)
+        compiler_params=pltpu.CompilerParams(vmem_limit_bytes=63 * MIB),
+        cost_estimate=pl.CostEstimate(flops=4 * 1024**3, bytes_accessed=12 * MIB, transcendentals=0),
+        name="video_grads",
+    )(place, tokens, gain, right, wqkv)
 
 
 def rows_of(left_ref, sibling):
@@ -227,26 +304,28 @@
     return left_ref[0, half:, :] if sibling else left_ref[0, :half, :]
 
 
-def send_b_kernel(place_ref, left_ref, right_ref, send_ref):
-    send_ref[0] = dot_nn(rows_of(left_ref, True), right_ref[...]).reshape(send_ref.shape[1:]).astype(BF16)
-
-
-def own_b_kernel(place_ref, left_ref, right_ref, got_ref, own_ref, *term_refs):
+def own_b_kernel(place_ref, left_ref, right_ref, got_ref, own_hbm, t1, t2, t3, own_s, terms_s, sems):
     k = pl.program_id(0)
-    g = dot_nn(rows_of(left_ref, False), right_ref[...]).reshape(own_ref.shape) + got_ref[0].astype(F32)
+    g = dot_nn(rows_of(left_ref, False), right_ref[...]).reshape(own_s.shape) + got_ref[0].astype(F32)
+    copies = [pltpu.make_async_copy(own_s, own_hbm, sems.at[0])]
+    for i, term in enumerate((t1, t2, t3)):
+        copies.append(pltpu.make_async_copy(terms_s.at[i], term, sems.at[i + 1]))
 
     @pl.when(k == 0)
     def _():
-        own_ref[...] = g
-
-    for i, term_ref in enumerate(term_refs):
-        @pl.when(k == i + 1)
+        own_s[...] = g
+        copies[0].start()
+
+    for i in range(1, 4):
+        @pl.when(k == i)
         def _():
-            term_ref[...] = g.astype(BF16)
-
-
-def send_a_kernel(place_ref, left_ref, right_ref, send_ref):
-    send_ref[...] = dot_nn(rows_of(left_ref, True), right_ref[...]).reshape(send_ref.shape).astype(BF16)
+            terms_s[i - 1] = g.astype(BF16)
+            copies[i].start()
+
+    @pl.when(k == 3)
+    def _():
+        for copy in copies:
+            copy.wait()
 
 
 def own_a_kernel(place_ref, left_ref, right_ref, got_ref, back_ref, theirs_ref, own_ref, message_ref, g_s):
@@ -271,7 +350,7 @@
             scratch_shapes=scratch,
         ),
         out_shape=tuple(shape for _, shape in outs),
-        compiler_params=pltpu.CompilerParams(vmem_limit_bytes=24 * MIB),
+        compiler_params=pltpu.CompilerParams(vmem_limit_bytes=63 * MIB),
         cost_estimate=pl.CostEstimate(flops=2 * 1024**3, bytes_accessed=8 * MIB, transcendentals=0),
         name=name,
     )
@@ -279,18 +358,6 @@
 
 def whole(*shape):
     return pl.BlockSpec(shape, lambda k, place: (0,) * len(shape))
-
-
-def run_send_b(place, left, right):
-    _, width, rows = left.shape
-    block = (1, 8, 64, 768)
-    ins = [
-        whole(1, width, rows),
-        pl.BlockSpec((rows, 768), lambda k, place: (0, (place[0] + k) % 4)),
-    ]
-    out = pl.BlockSpec(block, lambda k, place: (k, 0, 0, 0))
-    outs = [(out, jax.ShapeDtypeStruct((4, 8, 64, 768), BF16))]
-    return grads_call(send_b_kernel, "send_b", (4,), ins, outs)(place, left, right)[0]
 
 
 def run_own_b(place, left, right, got):
@@ -300,18 +367,14 @@
         pl.BlockSpec((rows, 768), lambda k, place: (0, (place[0] + k) % 4)),
         pl.BlockSpec((1, 8, 64, 768), lambda k, place: (k, 0, 0, 0)),
     ]
-    outs = [(whole(8, 64, 768), jax.ShapeDtypeStruct((8, 64, 768), t)) for t in (F32, BF16, BF16, BF16)]
-    return grads_call(own_b_kernel, "own_b", (4,), ins, outs)(place, left, right, got)
-
-
-def run_send_a(place, left, right):
-    _, width, rows = left.shape
-    ins = [
-        pl.BlockSpec((1, width, rows), lambda k, place: (1, 0, 0)),
-        pl.BlockSpec((rows, width), lambda k, place: (0, 3)),
-    ]
-    outs = [(whole(8, 64, width), jax.ShapeDtypeStruct((8, 64, width), BF16))]
-    return grads_call(send_a_kernel, "send_a", (1,), ins, outs)(place, left, right)[0]
+    hbm = pl.BlockSpec(memory_space=pl.ANY)
+    outs = [(hbm, jax.ShapeDtypeStruct((8, 64, 768), t)) for t in (F32, BF16, BF16, BF16)]
+    scratch = (
+        pltpu.VMEM((8, 64, 768), F32),
+        pltpu.VMEM((3, 8, 64, 768), BF16),
+        pltpu.SemaphoreType.DMA((4,)),
+    )
+    return grads_call(own_b_kernel, "own_b", (4,), ins, outs, scratch)(place, left, right, got)
 
 
 def run_own_a(place, left, right, got, back, theirs):
@@ -353,11 +416,16 @@
     )(place, message)
 
 
-def place_kernel(scale, place_ref, d0, d1, d2, d3, qkv_ref, out_ref):
+def place_kernel(scale, place_ref, d0, d1, d2, d3, qkv_ref, out_ref, gain_ref, bias_ref):
+    small = jnp.zeros((8, 128), F32)
     for j, d in enumerate((d0, d1, d2, d3)):
         block = (place_ref[0] - j) % 4
         qkv_ref[:, pl.ds(pl.multiple_of(block * 768, 256), 768)] = d[:, :768] * scale
-        out_ref[:, pl.ds(pl.multiple_of(block * 256, 256), 256)] = d[:, 768:] * scale
+        out_ref[:, pl.ds(pl.multiple_of(block * 256, 256), 256)] = d[:, 768:1024] * scale
+        small = small + d[:8, 1024:]
+    small = jnp.sum(small, axis=0, keepdims=True) * scale
+    gain_ref[...] = small[:, :64]
+    bias_ref[...] = small[:, 64:]
 
 
 def run_place(place, scale, pieces):
@@ -365,11 +433,13 @@
     return pl.pallas_call(
         functools.partial(place_kernel, scale),
         out_shape=(
-            jax.ShapeDtypeStruct((64, 6 * CHUNK), F32),
-            jax.ShapeDtypeStruct((64, 2 * CHUNK), F32),
+            jax.ShapeDtypeStruct((64, 3072), F32),
+            jax.ShapeDtypeStruct((64, 1024), F32),
+            jax.ShapeDtypeStruct((1, 64), F32),
+            jax.ShapeDtypeStruct((1, 64), F32),
         ),
         in_specs=[pl.BlockSpec(memory_space=pltpu.SMEM)] + [vm] * 4,
-        out_specs=(vm,) * 2,
+        out_specs=(vm,) * 4,
         name="place_grads",
     )(place, *pieces)
 
@@ -424,6 +494,12 @@
 def reduce_yz(own, got, yz):
     mine = (jnp.arange(8) == yz).reshape((8,) + (1,) * own.ndim)
     return jnp.sum(jnp.where(mine, own[None], got.astype(F32)), axis=0)
+
+
+def three_terms(value):
+    hi = lax.reduce_precision(value, 8, 7)
+    mid = lax.reduce_precision(value - hi, 8, 7)
+    return jnp.pad(jnp.concatenate([hi, mid, value - hi - mid], axis=0), ((0, 61), (0, 0)))
 
 
 def local(video, cotangent, norm_gain, norm_bias, qkv_weight, out_weight):
@@ -438,16 +514,17 @@
     tokens = jnp.concatenate([video, cotangent], axis=0).reshape(2 * clips, 16, positions // 16, width)
     tokens = lax.all_to_all(tokens.transpose(1, 0, 2, 3), "frame", 0, 0, tiled=True)
 
-    back, left, right = run_main(place, tokens, gain, bias, qkv_weight, out_weight)
+    left, right, send_a, send_b = run_main(place, tokens, gain, bias, qkv_weight, out_weight)
+
+    got_b = go_core(send_b)
+    got_a = go_core(send_a)
+    back = run_back(place, tokens, gain, right, qkv_weight)
+    back, got_b = lax.optimization_barrier((back, got_b))
+    terms_b = run_own_b(place, left, right, got_b)
     theirs = go_core(back[1])
-
-    got_a = go_core(run_send_a(place, left, right))
-    send_b = run_send_b(place, left, right)
-    got_a, send_b = lax.optimization_barrier((got_a, send_b))
-    got_b = go_core(send_b)
+    terms_b, got_a = lax.optimization_barrier((terms_b, got_a))
     own_a, message = run_own_a(place, left, right, got_a, back, theirs)
     message = trade_yz(message)
-    terms_b = run_own_b(place, left, right, got_b)
     got_b = exchange(terms_b, go_x)
     message, got_b = lax.optimization_barrier((message, got_b))
 
@@ -460,17 +537,15 @@
 
     a = combine(terms_a[0], got_a)
     b = reduce_yz(pick(b, yz), got_b, yz)
-    own = jnp.concatenate([b, a], axis=1)
+    small = jnp.sum(message[:, 64:, width:].astype(F32), axis=(0, 1)).reshape(1, 128)
+    own = jnp.concatenate([b, a, three_terms(small)], axis=1)
     own = combine(own, exchange([own.astype(BF16)] * 4, go_h))
     pieces = [own] + exchange([own] * 4, go_x)
 
     grad_video = run_unpack(place, message, clips).reshape(video.shape)
-    small = jnp.sum(message[:, 64:, width:].astype(F32), axis=(0, 1)).reshape(1, 1, 128)
-    small = lax.all_to_all(jnp.broadcast_to(small, (16, 1, 128)), "dp", 0, 0, tiled=True)
-    small = jnp.sum(small, axis=(0, 1)) * grad_scale
     pieces, grad_video = lax.optimization_barrier((pieces, grad_video))
-    grad_qkv, grad_out = run_place(place, grad_scale, pieces)
-    return grad_video, grad_qkv, grad_out, small[:64], small[64:]
+    grad_qkv, grad_out, total_gain, total_bias = run_place(place, grad_scale, pieces)
+    return grad_video, grad_qkv, grad_out, total_gain.reshape(64), total_bias.reshape(64)
 
 
 def solution(mesh):

time: 198 us -> 200 us (1.010)
  Pallas kernels: 43.7 us -> 56.7 us
  local copies, waits for them, and re-layouts: 17.5 us -> 8.95 us
  starting transfers between devices: 48.7 us -> 41.3 us
  waiting for transfers between devices: 77.4 us -> 82 us
  other arithmetic: 7.83 us -> 9.98 us
    unnamed x33 -> x19, local copies, waits for them, and re-layouts: 13.4 us -> 2.53 us
    ppermute x3, waiting for transfers between devices: 0.01 us -> 10.1 us  [go_h(): return lax.ppermute(a, 'dp', dp_pairs(lambda x, h: (x, h + k)))]
    pallas_call x4 -> x3, Pallas kernels: 37.4 us -> 46.6 us  [the longest x1 25.9 us: run_main(): pl.pallas_call(main_kernel, out_shape=tuple((jax.ShapeDtypeStruct(shape,...]
    all_to_all x1 -> x0, waiting for transfers between devices: 7.16 us -> none  [local(): lax.all_to_all(jnp.broadcast_to(small, (16, 1, 128)), 'dp', 0, 0, tiled=T...]
    all_to_all x1 -> x0, starting transfers between devices: 6.38 us -> none  [local(): lax.all_to_all(jnp.broadcast_to(small, (16, 1, 128)), 'dp', 0, 0, tiled=T...]
    pallas_call x1, Pallas kernels: 1.36 us -> 5.15 us  [run_own_a(): grads_call(own_a_kernel, 'own_a', (1,), ins, outs, scratch)]
    ppermute x9, waiting for transfers between devices: 42 us -> 44 us  [go_x(): return lax.ppermute(a, 'dp', dp_pairs(lambda x, h: (x + k, h)))]
  transfers between devices with their start and end apart: 19 -> 18, of which waited for: 9 -> 9; matrix products, arithmetic and copies ran while one was open for 3% -> 3% of each run, Pallas kernels for 7% -> 12%
where the time goes in v6:
time: 200 us
  waiting for transfers between devices  82 us (41%)
  Pallas kernels  56.7 us (28%)
  starting transfers between devices  41.3 us (21%)
  other arithmetic  9.98 us (5%)
  local copies, waits for them, and re-layouts  8.95 us (4%)
    ppermute x9, waiting for transfers between devices, go_x(): return lax.ppermute(a, 'dp', dp_pairs(lambda x, h: (x + k, h)))  44 us
    all_to_all x1, waiting for transfers between devices, local(): lax.all_to_all(tokens.transpose(1, 0, 2, 3), 'frame', 0, 0, tiled=True)  26.1 us
    pallas_call x1, Pallas kernels, run_main(): pl.pallas_call(main_kernel, out_shape=tuple((jax.ShapeDtypeStruct(shape,...  25.9 us
    ppermute x9, starting transfers between devices, go_x(): return lax.ppermute(a, 'dp', dp_pairs(lambda x, h: (x + k, h)))  14.6 us
    pallas_call x1, Pallas kernels, run_back(): pl.pallas_call(back_kernel, out_shape=jax.ShapeDtypeStruct((2, frames //...  13 us
    all_to_all x2, starting transfers between devices, trade_yz(): lax.all_to_all(a, 'frame', 0, 0, tiled=True, axis_index_groups=groups)  10.6 us
    ppermute x3, waiting for transfers between devices, go_h(): return lax.ppermute(a, 'dp', dp_pairs(lambda x, h: (x, h + k)))  10.1 us
    ppermute x3, starting transfers between devices, go_h(): return lax.ppermute(a, 'dp', dp_pairs(lambda x, h: (x, h + k)))  9.29 us
  transfers between devices with their start and end apart: 18, of which 9 were waited for; matrix products, arithmetic and copies ran while one was open for 3% of the time, Pallas kernels for 12%

profile of v6, /device:TPU:32, one launch (start us, length us, event | category | flops | bytes accessed | tf_op | source)
XLA Modules:
  0.0 199.7 jit_solution(9591069078404526333)
XLA Ops:
  0.6 1.7 pad_maximum_fusion
  2.4 1.5 copy.34
  3.9 6.0 %all-to-all-start = ((bf16[16,4,16,1024]{3,2,1,0:T(8,128)(2,1)}), bf16[16,4,16,1024]{3,2,1,0:T(8,128)(2,1)}, u32[]{:S(2)}, u32[]{:S(2)}) async-start(bf16[16,4,16,1024]{3,2,1,0:T(8,128)(2,1)} %bitcast.43), calls=%async_computation | async-start | bytes 4194304 | tf_op jit(solution)/shard_map/all_to_all | solution.py:515
  9.9 0.7 pad_add_fusion.place_ref
  10.5 26.1 %all-to-all-done.tokens_hbm = bf16[16,4,16,1024]{3,2,1,0:T(8,128)(2,1)} async-done(((bf16[16,4,16,1024]{3,2,1,0:T(8,128)(2,1)}), bf16[16,4,16,1024]{3,2,1,0:T(8,128)(2,1)}, u32[]{:S(2)}, u32[]{:S(2)}) %all-to-all-start) | async-done | bytes 2097184 | tf_op jit(solution)/shard_map/all_to_all | solution.py:515
  36.7 25.9 %sublayer.1 = (bf16[2,1024,512]{2,1,0:T(8,128)(2,1)}, bf16[512,4096]{1,0:T(8,128)(2,1)}, bf16[8,64,1024]{2,1,0:T(8,128)(2,1)}, bf16[4,8,64,768]{3,2,1,0:T(8,128)(2,1)}) custom-call(s32[3]{0:T(128)} %pad_add_fusion.place_ref, bf16[16,4,16,1024]{3,2,1,0:T(8,128)(2,1)} %all-to-all-done.tokens_hbm, f32[1,1024]{1,0:T(1,128)} %bitcast.55, f32[1,1024]{1,0:T(1,128)} %bitcast.54, ...), custom_call_target="tpu_custom_call" | custom-call | flops 12884901888 | bytes 20971520 | tf_op jit(solution)/shard_map/sublayer/pallas_call | solution.py:178
  62.6 0.2 collective-permute-start
  62.8 0.4 collective-permute-start.1
  63.2 13.0 %video_grads.1.back_ref = bf16[2,8,32,1152]{3,2,1,0:T(8,128)(2,1)} custom-call(s32[3]{0:T(128)} %pad_add_fusion.place_ref, bf16[16,4,16,1024]{3,2,1,0:T(8,128)(2,1)} %all-to-all-done.tokens_hbm, f32[1,1024]{1,0:T(1,128)} %bitcast.56, bf16[512,4096]{1,0:T(8,128)(2,1)} %get-tuple-element.41.right_hbm.right_ref, bf16[1024,3072]{1,0:T(8,128)(2,1)} %wqkv_hbm.3), custom_call_target="tpu_custom_call" | custom-call | flops 4294967296 | bytes 12582912 | tf_op jit(solution)/shard_map/video_grads/pallas_call | solution.py:284
  76.2 2.0 slice_bitcast_fusion
  78.2 0.1 collective-permute-start.2
  78.3 7.6 %own_b.1 = (f32[8,64,768]{2,1,0:T(8,128)}, bf16[8,64,768]{2,1,0:T(8,128)(2,1)}, bf16[8,64,768]{2,1,0:T(8,128)(2,1)}, bf16[8,64,768]{2,1,0:T(8,128)(2,1)}) custom-call(s32[3]{0:T(128)} %pad_add_fusion.place_ref, bf16[2,1024,512]{2,1,0:T(8,128)(2,1)} %get-tuple-element.40.left_ref, bf16[512,4096]{1,0:T(8,128)(2,1)} %get-tuple-element.41.right_hbm.right_ref, ...), custom_call_target="tpu_custom_call" | custom-call | flops 2147483648 | bytes 8388608 | tf_op jit(solution)/shard_map/own_b/pallas_call | solution.py:377
  86.0 0.8 copy-done.3
  86.8 5.1 %own_a.1 = (f32[64,1024]{1,0:T(8,128)}, bf16[8,128,1152]{2,1,0:T(8,128)(2,1)}) custom-call(s32[3]{0:T(128)} %pad_add_fusion.place_ref, bf16[2,1024,512]{2,1,0:T(8,128)(2,1)} %get-tuple-element.40.left_ref, bf16[512,4096]{1,0:T(8,128)(2,1)} %get-tuple-element.41.right_hbm.right_ref, bf16[8,64,1024]{2,1,0:T(8,128)(2,1)} %collective-permute-done.1.got_ref, ...), custom_call_target="tpu_custom_call" | custom-call | flops 2147483648 | bytes 8388608 | tf_op jit(solution)/shard_map/own_a/pallas_call | solution.py:394
  91.9 4.9 %all-to-all-start.1 = ((bf16[8,128,1152]{2,1,0:T(8,128)(2,1)}), bf16[8,128,1152]{2,1,0:T(8,128)(2,1)S(1)}, u32[]{:S(2)}, u32[]{:S(2)}) async-start(bf16[8,128,1152]{2,1,0:T(8,128)(2,1)} %get-tuple-element.52), calls=%async_computation.1 | async-start | bytes 4718592 | tf_op jit(solution)/shard_map/all_to_all | solution.py:469
  96.9 1.3 collective-permute-start.3
  98.2 2.7 %collective-permute-start.4 = (bf16[8,64,768]{2,1,0:T(8,128)(2,1)}, bf16[8,64,768]{2,1,0:T(8,128)(2,1)S(1)}, u32[]{:S(2)}, u32[]{:S(2)}) collective-permute-start(bf16[8,64,768]{2,1,0:T(8,128)(2,1)} %get-tuple-element.54), channel_id=1, source_target_pairs={{0,128},{16,144},{32,160},{48,176},{64,192},{80,208},{96,224},{112... | collective-permute-start | bytes 2359304 | tf_op jit(solution)/shard_map/ppermute | solution.py:473
  100.9 1.4 collective-permute-start.5
  102.3 15.5 %collective-permute-done.3 = bf16[8,64,768]{2,1,0:T(8,128)(2,1)S(1)} collective-permute-done((bf16[8,64,768]{2,1,0:T(8,128)(2,1)}, bf16[8,64,768]{2,1,0:T(8,128)(2,1)S(1)}, u32[]{:S(2)}, u32[]{:S(2)}) %collective-permute-start.3) | collective-permute-done | bytes 786464 | tf_op jit(solution)/shard_map/ppermute | solution.py:473
  117.9 17.7 %collective-permute-done.4 = bf16[8,64,768]{2,1,0:T(8,128)(2,1)S(1)} collective-permute-done((bf16[8,64,768]{2,1,0:T(8,128)(2,1)}, bf16[8,64,768]{2,1,0:T(8,128)(2,1)S(1)}, u32[]{:S(2)}, u32[]{:S(2)}) %collective-permute-start.4) | collective-permute-done | bytes 786464 | tf_op jit(solution)/shard_map/ppermute | solution.py:473
  135.5 0.9 copy-done.2
  136.4 4.5 %fusion.8 = (bf16[8,64,768]{2,1,0:T(8,128)(2,1)}, f32[8,64,768]{2,1,0:T(8,128)}) fusion(bf16[8,64,768]{2,1,0:T(8,128)(2,1)} %collective-permute-done.5, bf16[8,64,768]{2,1,0:T(8,128)(2,1)} %copy-done.2, f32[8,64,768]{2,1,0:T(8,128)} %get-tuple-element.49, bf16[8,64,768]{2,1,0:T(8,128)(2,1)S(1)} %collective-permute-done.3), kind=kLoop, calls=%fused_computation.33 | loop fusion | flops 2752512 | bytes 6291456 | tf_op jit(solution)/shard_map/convert_element_type | solution.py:532
  140.9 5.7 %all-to-all-start.2 = ((bf16[8,64,768]{2,1,0:T(8,128)(2,1)}), bf16[8,64,768]{2,1,0:T(8,128)(2,1)S(1)}, u32[]{:S(2)}, u32[]{:S(2)}) async-start(bf16[8,64,768]{2,1,0:T(8,128)(2,1)} %get-tuple-element.85), calls=%async_computation.2 | async-start | bytes 1572864 | tf_op jit(solution)/shard_map/all_to_all | solution.py:469
  146.6 1.0 select_reduce_fusion
  147.6 1.1 reshape.73
  148.7 0.2 constant_dynamic-slice_fusion.1
  148.9 0.8 collective-permute-start.6
  149.7 2.4 %collective-permute-start.7 = (bf16[64,256]{1,0:T(8,128)(2,1)S(1)}, bf16[64,256]{1,0:T(8,128)(2,1)S(1)}, u32[]{:S(2)}, u32[]{:S(2)}) collective-permute-start(bf16[64,256]{1,0:T(8,128)(2,1)S(1)} %bitcast.52), channel_id=1, source_target_pairs={{0,128},{16,144},{32,160},{48,176},{64,192},{80,208},{96,224},{112... | collective-permute-start | bytes 98312 | tf_op jit(solution)/shard_map/ppermute | solution.py:473
  152.1 1.4 collective-permute-start.8
  153.5 1.6 dynamic-slice_bitcast_fusion
  155.2 0.9 collective-permute-done.8
  156.1 1.7 all-to-all-done.2
  157.8 0.1 convert_reduce_fusion
  157.9 1.2 select_reduce_fusion.1
  159.1 0.8 fusion.2
  159.9 5.5 %collective-permute-start.11 = (bf16[64,1152]{1,0:T(8,128)(2,1)S(1)}, bf16[64,1152]{1,0:T(8,128)(2,1)S(1)}, u32[]{:S(2)}, u32[]{:S(2)}) collective-permute-start(bf16[64,1152]{1,0:T(8,128)(2,1)S(1)} %fusion), channel_id=1, source_target_pairs={{0,48},{16,0},{32,16},{48,32},{64,112},{80,64},{96,80},{112,96},{1... | collective-permute-start | bytes 442376 | tf_op jit(solution)/shard_map/ppermute | solution.py:477
  165.4 1.4 collective-permute-start.10
  166.8 2.4 %collective-permute-start.9 = (bf16[64,1152]{1,0:T(8,128)(2,1)S(1)}, bf16[64,1152]{1,0:T(8,128)(2,1)S(1)}, u32[]{:S(2)}, u32[]{:S(2)}) collective-permute-start(bf16[64,1152]{1,0:T(8,128)(2,1)S(1)} %fusion), channel_id=1, source_target_pairs={{0,16},{16,32},{32,48},{48,0},{64,80},{80,96},{96,112},{112,64},{1... | collective-permute-start | bytes 442376 | tf_op jit(solution)/shard_map/ppermute | solution.py:477
  169.2 4.2 %collective-permute-done.11 = bf16[64,1152]{1,0:T(8,128)(2,1)S(1)} collective-permute-done((bf16[64,1152]{1,0:T(8,128)(2,1)S(1)}, bf16[64,1152]{1,0:T(8,128)(2,1)S(1)}, u32[]{:S(2)}, u32[]{:S(2)}) %collective-permute-start.11) | collective-permute-done | bytes 147488 | tf_op jit(solution)/shard_map/ppermute | solution.py:477
  173.4 5.9 %collective-permute-done.10 = bf16[64,1152]{1,0:T(8,128)(2,1)S(1)} collective-permute-done((bf16[64,1152]{1,0:T(8,128)(2,1)S(1)}, bf16[64,1152]{1,0:T(8,128)(2,1)S(1)}, u32[]{:S(2)}, u32[]{:S(2)}) %collective-permute-start.10) | collective-permute-done | bytes 147488 | tf_op jit(solution)/shard_map/ppermute | solution.py:477
  179.4 0.7 collective-permute-start.12
  180.1 3.9 %collective-permute-start.13 = (f32[64,1152]{1,0:T(8,128)S(1)}, f32[64,1152]{1,0:T(8,128)S(1)}, u32[]{:S(2)}, u32[]{:S(2)}) collective-permute-start(f32[64,1152]{1,0:T(8,128)S(1)} %convert_add_fusion.1.d0), channel_id=1, source_target_pairs={{0,128},{16,144},{32,160},{48,176},{64,192},{80,208},{96,224},{112... | collective-permute-start | bytes 884744 | tf_op jit(solution)/shard_map/ppermute | solution.py:473
  184.0 2.7 %unpack.1 = bf16[2,256,1024]{2,1,0:T(8,128)(2,1)} custom-call(s32[3]{0:T(128)} %pad_add_fusion.place_ref, bf16[8,128,1152]{2,1,0:T(8,128)(2,1)} %copy-done), custom_call_target="tpu_custom_call" | custom-call | tf_op jit(solution)/shard_map/unpack/pallas_call | solution.py:410
  186.7 2.8 %collective-permute-done.12.d1 = f32[64,1152]{1,0:T(8,128)S(1)} collective-permute-done((f32[64,1152]{1,0:T(8,128)S(1)}, f32[64,1152]{1,0:T(8,128)S(1)}, u32[]{:S(2)}, u32[]{:S(2)}) %collective-permute-start.12) | collective-permute-done | bytes 294944 | tf_op jit(solution)/shard_map/ppermute | solution.py:473
  189.5 7.0 %collective-permute-done.13.d2 = f32[64,1152]{1,0:T(8,128)S(1)} collective-permute-done((f32[64,1152]{1,0:T(8,128)S(1)}, f32[64,1152]{1,0:T(8,128)S(1)}, u32[]{:S(2)}, u32[]{:S(2)}) %collective-permute-start.13) | collective-permute-done | bytes 294944 | tf_op jit(solution)/shard_map/ppermute | solution.py:473
  196.6 0.7 copy-done.5
  197.3 0.1 copy-done.6
  197.4 2.3 %place_grads.1 = (f32[64,3072]{1,0:T(8,128)}, f32[64,1024]{1,0:T(8,128)}, f32[1,64]{1,0:T(1,128)}, f32[1,64]{1,0:T(1,128)}) custom-call(s32[3]{0:T(128)} %pad_add_fusion.place_ref, f32[64,1152]{1,0:T(8,128)} %copy-done.1, f32[64,1152]{1,0:T(8,128)} %copy-done.4, f32[64,1152]{1,0:T(8,128)} %copy-done.5, f32[64,1152]{1,0:T(8,128)} %copy-done.6), custom_call_target="tpu_custom_call" | custom-call | tf_op jit(solution)/shard_map/place_grads/pallas_call | solution.py:433
  (31 shorter events, 0.2 us)
Async XLA Ops:
  3.9 32.8 %all-to-all-start = ((bf16[16,4,16,1024]{3,2,1,0:T(8,128)(2,1)}), bf16[16,4,16,1024]{3,2,1,0:T(8,128)(2,1)}, u32[]{:S(2)}, u32[]{:S(2)}) async-start(bf16[16,4,16,1024]{3,2,1,0:T(8,128)(2,1)} %bitcast.43), calls=%async_computation | async-start | bytes 4194304 | tf_op jit(solution)/shard_map/all_to_all | solution.py:515
  62.6 13.7 %collective-permute-start = (bf16[4,8,64,768]{3,2,1,0:T(8,128)(2,1)}, bf16[4,8,64,768]{3,2,1,0:T(8,128)(2,1)}, u32[]{:S(2)}, u32[]{:S(2)}) collective-permute-start(bf16[4,8,64,768]{3,2,1,0:T(8,128)(2,1)} %get-tuple-element.42), channel_id=1, source_target_pairs={{0,1},{1,0},{2,3},{3,2},{4,5},{5,4},{6,7},{7,6},{8,9},{9,8},{10,11... | collective-permute-start | bytes 9437192 | tf_op jit(solution)/shard_map/ppermute | solution.py:464
  62.8 23.2 %collective-permute-start.1 = (bf16[8,64,1024]{2,1,0:T(8,128)(2,1)}, bf16[8,64,1024]{2,1,0:T(8,128)(2,1)}, u32[]{:S(2)}, u32[]{:S(2)}) collective-permute-start(bf16[8,64,1024]{2,1,0:T(8,128)(2,1)} %get-tuple-element.48), channel_id=1, source_target_pairs={{0,1},{1,0},{2,3},{3,2},{4,5},{5,4},{6,7},{7,6},{8,9},{9,8},{10,11... | collective-permute-start | bytes 3145736 | tf_op jit(solution)/shard_map/ppermute | solution.py:464
  78.2 7.7 %collective-permute-start.2 = (bf16[8,32,1152]{2,1,0:T(8,128)(2,1)}, bf16[8,32,1152]{2,1,0:T(8,128)(2,1)S(1)}, u32[]{:S(2)}, u32[]{:S(2)}) collective-permute-start(bf16[8,32,1152]{2,1,0:T(8,128)(2,1)} %slice_bitcast_fusion), channel_id=1, source_target_pairs={{0,1},{1,0},{2,3},{3,2},{4,5},{5,4},{6,7},{7,6},{8,9},{9,8},{10,11... | collective-permute-start | bytes 1769480 | tf_op jit(solution)/shard_map/ppermute | solution.py:464
  86.0 0.8 copy-start.3
  91.9 44.5 %all-to-all-start.1 = ((bf16[8,128,1152]{2,1,0:T(8,128)(2,1)}), bf16[8,128,1152]{2,1,0:T(8,128)(2,1)S(1)}, u32[]{:S(2)}, u32[]{:S(2)}) async-start(bf16[8,128,1152]{2,1,0:T(8,128)(2,1)} %get-tuple-element.52), calls=%async_computation.1 | async-start | bytes 4718592 | tf_op jit(solution)/shard_map/all_to_all | solution.py:469
  96.8 49.8 %copy-start.7 = (f32[64,1024]{1,0:T(8,128)S(1)}, f32[64,1024]{1,0:T(8,128)}, u32[]{:S(2)}) copy-start(f32[64,1024]{1,0:T(8,128)} %get-tuple-element.60) | copy-start | bytes 786436
  96.9 21.0 %collective-permute-start.3 = (bf16[8,64,768]{2,1,0:T(8,128)(2,1)}, bf16[8,64,768]{2,1,0:T(8,128)(2,1)S(1)}, u32[]{:S(2)}, u32[]{:S(2)}) collective-permute-start(bf16[8,64,768]{2,1,0:T(8,128)(2,1)} %get-tuple-element.53), channel_id=1, source_target_pairs={{0,64},{16,80},{32,96},{48,112},{64,128},{80,144},{96,160},{112,17... | collective-permute-start | bytes 2359304 | tf_op jit(solution)/shard_map/ppermute | solution.py:473
  98.2 37.4 %collective-permute-start.4 = (bf16[8,64,768]{2,1,0:T(8,128)(2,1)}, bf16[8,64,768]{2,1,0:T(8,128)(2,1)S(1)}, u32[]{:S(2)}, u32[]{:S(2)}) collective-permute-start(bf16[8,64,768]{2,1,0:T(8,128)(2,1)} %get-tuple-element.54), channel_id=1, source_target_pairs={{0,128},{16,144},{32,160},{48,176},{64,192},{80,208},{96,224},{112... | collective-permute-start | bytes 2359304 | tf_op jit(solution)/shard_map/ppermute | solution.py:473
  100.9 35.5 %collective-permute-start.5 = (bf16[8,64,768]{2,1,0:T(8,128)(2,1)}, bf16[8,64,768]{2,1,0:T(8,128)(2,1)}, u32[]{:S(2)}, u32[]{:S(2)}) collective-permute-start(bf16[8,64,768]{2,1,0:T(8,128)(2,1)} %get-tuple-element.55), channel_id=1, source_target_pairs={{0,192},{16,208},{32,224},{48,240},{64,0},{80,16},{96,32},{112,48}... | collective-permute-start | bytes 2359304 | tf_op jit(solution)/shard_map/ppermute | solution.py:473
  135.5 0.9 copy-start.2
  136.4 21.4 %copy-start = (bf16[8,128,1152]{2,1,0:T(8,128)(2,1)}, bf16[8,128,1152]{2,1,0:T(8,128)(2,1)S(1)}, u32[]{:S(2)}) copy-start(bf16[8,128,1152]{2,1,0:T(8,128)(2,1)S(1)} %all-to-all-done.1.message_ref) | copy-start | bytes 7077892
  140.9 16.9 %all-to-all-start.2 = ((bf16[8,64,768]{2,1,0:T(8,128)(2,1)}), bf16[8,64,768]{2,1,0:T(8,128)(2,1)S(1)}, u32[]{:S(2)}, u32[]{:S(2)}) async-start(bf16[8,64,768]{2,1,0:T(8,128)(2,1)} %get-tuple-element.85), calls=%async_computation.2 | async-start | bytes 1572864 | tf_op jit(solution)/shard_map/all_to_all | solution.py:469
  148.9 6.3 %collective-permute-start.6 = (bf16[64,256]{1,0:T(8,128)(2,1)S(1)}, bf16[64,256]{1,0:T(8,128)(2,1)S(1)}, u32[]{:S(2)}, u32[]{:S(2)}) collective-permute-start(bf16[64,256]{1,0:T(8,128)(2,1)S(1)} %bitcast.51), channel_id=1, source_target_pairs={{0,64},{16,80},{32,96},{48,112},{64,128},{80,144},{96,160},{112,17... | collective-permute-start | bytes 98312 | tf_op jit(solution)/shard_map/ppermute | solution.py:473
  149.7 5.5 %collective-permute-start.7 = (bf16[64,256]{1,0:T(8,128)(2,1)S(1)}, bf16[64,256]{1,0:T(8,128)(2,1)S(1)}, u32[]{:S(2)}, u32[]{:S(2)}) collective-permute-start(bf16[64,256]{1,0:T(8,128)(2,1)S(1)} %bitcast.52), channel_id=1, source_target_pairs={{0,128},{16,144},{32,160},{48,176},{64,192},{80,208},{96,224},{112... | collective-permute-start | bytes 98312 | tf_op jit(solution)/shard_map/ppermute | solution.py:473
  152.1 4.0 %collective-permute-start.8 = (bf16[64,256]{1,0:T(8,128)(2,1)S(1)}, bf16[64,256]{1,0:T(8,128)(2,1)}, u32[]{:S(2)}, u32[]{:S(2)}) collective-permute-start(bf16[64,256]{1,0:T(8,128)(2,1)S(1)} %bitcast.53), channel_id=1, source_target_pairs={{0,192},{16,208},{32,224},{48,240},{64,0},{80,16},{96,32},{112,48}... | collective-permute-start | bytes 98312 | tf_op jit(solution)/shard_map/ppermute | solution.py:473
  159.9 13.5 %collective-permute-start.11 = (bf16[64,1152]{1,0:T(8,128)(2,1)S(1)}, bf16[64,1152]{1,0:T(8,128)(2,1)S(1)}, u32[]{:S(2)}, u32[]{:S(2)}) collective-permute-start(bf16[64,1152]{1,0:T(8,128)(2,1)S(1)} %fusion), channel_id=1, source_target_pairs={{0,48},{16,0},{32,16},{48,32},{64,112},{80,64},{96,80},{112,96},{1... | collective-permute-start | bytes 442376 | tf_op jit(solution)/shard_map/ppermute | solution.py:477
  165.4 13.9 %collective-permute-start.10 = (bf16[64,1152]{1,0:T(8,128)(2,1)S(1)}, bf16[64,1152]{1,0:T(8,128)(2,1)S(1)}, u32[]{:S(2)}, u32[]{:S(2)}) collective-permute-start(bf16[64,1152]{1,0:T(8,128)(2,1)S(1)} %fusion), channel_id=1, source_target_pairs={{0,32},{16,48},{32,0},{48,16},{64,96},{80,112},{96,64},{112,80},{1... | collective-permute-start | bytes 442376 | tf_op jit(solution)/shard_map/ppermute | solution.py:477
  166.8 12.5 %collective-permute-start.9 = (bf16[64,1152]{1,0:T(8,128)(2,1)S(1)}, bf16[64,1152]{1,0:T(8,128)(2,1)S(1)}, u32[]{:S(2)}, u32[]{:S(2)}) collective-permute-start(bf16[64,1152]{1,0:T(8,128)(2,1)S(1)} %fusion), channel_id=1, source_target_pairs={{0,16},{16,32},{32,48},{48,0},{64,80},{80,96},{96,112},{112,64},{1... | collective-permute-start | bytes 442376 | tf_op jit(solution)/shard_map/ppermute | solution.py:477
  179.4 17.2 %copy-start.1 = (f32[64,1152]{1,0:T(8,128)}, f32[64,1152]{1,0:T(8,128)S(1)}, u32[]{:S(2)}) copy-start(f32[64,1152]{1,0:T(8,128)S(1)} %convert_add_fusion.1.d0) | copy-start | bytes 884740
  179.4 10.1 %collective-permute-start.12 = (f32[64,1152]{1,0:T(8,128)S(1)}, f32[64,1152]{1,0:T(8,128)S(1)}, u32[]{:S(2)}, u32[]{:S(2)}) collective-permute-start(f32[64,1152]{1,0:T(8,128)S(1)} %convert_add_fusion.1.d0), channel_id=1, source_target_pairs={{0,64},{16,80},{32,96},{48,112},{64,128},{80,144},{96,160},{112,17... | collective-permute-start | bytes 884744 | tf_op jit(solution)/shard_map/ppermute | solution.py:473
  180.1 16.5 %collective-permute-start.13 = (f32[64,1152]{1,0:T(8,128)S(1)}, f32[64,1152]{1,0:T(8,128)S(1)}, u32[]{:S(2)}, u32[]{:S(2)}) collective-permute-start(f32[64,1152]{1,0:T(8,128)S(1)} %convert_add_fusion.1.d0), channel_id=1, source_target_pairs={{0,128},{16,144},{32,160},{48,176},{64,192},{80,208},{96,224},{112... | collective-permute-start | bytes 884744 | tf_op jit(solution)/shard_map/ppermute | solution.py:473
  184.0 12.6 %collective-permute-start.14 = (f32[64,1152]{1,0:T(8,128)S(1)}, f32[64,1152]{1,0:T(8,128)S(1)}, u32[]{:S(2)}, u32[]{:S(2)}) collective-permute-start(f32[64,1152]{1,0:T(8,128)S(1)} %convert_add_fusion.1.d0), channel_id=1, source_target_pairs={{0,192},{16,208},{32,224},{48,240},{64,0},{80,16},{96,32},{112,48}... | collective-permute-start | bytes 884744 | tf_op jit(solution)/shard_map/ppermute | solution.py:473
  189.5 7.0 %copy-start.4 = (f32[64,1152]{1,0:T(8,128)}, f32[64,1152]{1,0:T(8,128)S(1)}, u32[]{:S(2)}) copy-start(f32[64,1152]{1,0:T(8,128)S(1)} %collective-permute-done.12.d1) | copy-start | bytes 884740
  196.6 0.7 copy-start.5
  196.6 0.8 copy-start.6

commit v7 on v5

v7 whole, which is shorter than its diff:
```python
import functools
import math

import jax
import jax.numpy as jnp
from jax import lax
from jax.experimental import pallas as pl
from jax.experimental.pallas import tpu as pltpu
from jax.sharding import PartitionSpec as P

F32 = jnp.float32
BF16 = jnp.bfloat16
MIB = 1024 * 1024
CHUNK = 512


def dot_nn(a, b):
    return lax.dot_general(a, b, (((1,), (0,)), ((), ())), preferred_element_type=F32)


def dot_nt(a, b):
    return lax.dot_general(a, b, (((1,), (1,)), ((), ())), preferred_element_type=F32)


def dot_tn(a, b):
    return lax.dot_general(a, b, (((0,), (0,)), ((), ())), preferred_element_type=F32)


def chunk(n):
    return pl.ds(pl.multiple_of(n * CHUNK, CHUNK), CHUNK)


def block_row(block, place):
    return pl.multiple_of(((block % 2 - place[1]) % 2 * 8 + block // 2) * 64, 64)


def read_place(place_ref):
    return tuple(place_ref[i] for i in range(2))


def whiten(xh):
    centred = xh - jnp.mean(xh, axis=-1, keepdims=True)
    inv = lax.rsqrt(jnp.mean(centred * centred, axis=-1, keepdims=True) + 1e-05)
    return centred * inv, inv


def main_kernel(
    place_ref, tokens_hbm, gain_ref, bias_ref, wqkv_hbm, wout_hbm,
    back_ref, send_a_hbm, send_b_hbm, keep_a_hbm, keep_b_hbm,
    tokens_s, wqkv_s, wout_s, left_s, right_s, normed_s, packed_s, datt_s, wh_s, inv_s, dn_s,
    send_a_s, send_b_s, keep_a_s, keep_b_s,
    token_sems, weight_sems, out_sems,
):
    place = read_place(place_ref)
    frames, clips, positions, width = tokens_s.shape
    clips = clips // 2
    halves = positions // 8
    part = frames * 8
    gain = gain_ref[...]
    bias = bias_ref[...]

    def load_tokens(q):
        pair = pl.ds(2 * q, 2)
        return pltpu.make_async_copy(tokens_hbm.at[pair], tokens_s.at[pair], token_sems.at[q])

    def load_wqkv(n):
        return pltpu.make_async_copy(wqkv_hbm.at[:, chunk(n)], wqkv_s.at[:, chunk(n)], weight_sems.at[n])

    blocks = 3 * width // CHUNK
    load_wout = pltpu.make_async_copy(wout_hbm, wout_s, weight_sems.at[blocks])
    for q in range(frames // 2):
        load_tokens(q).start()
    for n in range(blocks):
        load_wqkv(n).start()
    load_wout.start()

    def norm_step(q, carry):
        load_tokens(q).wait()
        for c in range(clips):
            x = tokens_s[pl.ds(2 * q, 2), c].astype(F32).reshape(2, halves, 8, width)
            g = tokens_s[pl.ds(2 * q, 2), clips + c].astype(F32).reshape(2, halves, 8, width)
            for hf in range(halves):
                at = pl.multiple_of((c * halves + hf) * part + q * 16, 16)
                wh, inv = whiten(x[:, hf].reshape(16, width))
                wh_s[pl.ds(at, 16), :] = wh
                inv_s[pl.ds(at, 16), :] = jnp.broadcast_to(inv, (16, 128))
                normed_s[pl.ds(at, 16), :] = (wh * gain + bias).astype(BF16)
                right_s[pl.ds(at, 16), pl.ds(3 * width, width)] = g[:, hf].reshape(16, width).astype(BF16)
        return carry

    lax.fori_loop(0, frames // 2, norm_step, 0)

    def qkv_step(n, carry):
        for i in range(2):
            load_wqkv(2 * n + i).wait()
        for i in range(2):
            cols = chunk(2 * n + i)
            packed_s[:, cols] = dot_nn(normed_s[...], wqkv_s[:, cols]).astype(BF16)
        return carry

    lax.fori_loop(0, blocks // 2, qkv_step, 0)
    load_wout.wait()

    for n in range(width // CHUNK):
        cols = slice(n * CHUNK, (n + 1) * CHUNK)
        datt_s[:, cols] = dot_nt(right_s[:, 3 * width:], wout_s[cols, :]).astype(BF16)
        turned = normed_s[:, cols].T
        for b in range(CHUNK // 64):
            at = block_row(n * (CHUNK // 64) + b, place)
            left_s[0, pl.ds(at, 64), :] = turned[b * 64:(b + 1) * 64]

    lane = lax.broadcasted_iota(jnp.int32, (part, 128), 1)
    first = lane < 64
    same = lax.broadcasted_iota(jnp.int32, (1, 8, part), 1) == (
        lax.broadcasted_iota(jnp.int32, (1, 8, part), 2) % 8
    )
    zero = jnp.zeros((part, 128), BF16)

    def split(a):
        return jnp.concatenate([jnp.where(first, a, zero), jnp.where(first, zero, a)], axis=0)

    def attend_step(i, carry):
        t = i // (width // 128)
        hp = i % (width // 128)
        tok = pl.ds(pl.multiple_of(t * part, part), part)
        col = pl.multiple_of(hp * 128, 128)
        q = packed_s[tok, pl.ds(col, 128)]
        k = packed_s[tok, pl.ds(width + col, 128)]
        v = packed_s[tok, pl.ds(2 * width + col, 128)]
        da = datt_s[tok, pl.ds(col, 128)]
        k2 = split(k)
        v2 = split(v)
        scores = (dot_nt(k2, q) * 0.125).reshape(2, frames, 8, part)
        e = jnp.exp(scores - jnp.max(scores, axis=1, keepdims=True))
        probs = e * (1.0 / jnp.sum(e, axis=1, keepdims=True))
        probs = jnp.where(same[None], probs, 0.0)
        low = probs.astype(BF16).reshape(2, part, part)
        dp = dot_nt(v2, da).reshape(2, frames, 8, part)
        inner = jnp.sum(dp * probs, axis=1, keepdims=True)
        ds = (probs * (dp - inner) * 0.125).astype(BF16).reshape(2, part, part)
        attended = dot_tn(v2, low.reshape(2 * part, part)).astype(BF16)
        for b in range(2):
            left_s[1, pl.ds(block_row(hp * 2 + b, place), 64), tok] = attended[b * 64:(b + 1) * 64]
        right_s[tok, pl.ds(col, 128)] = dot_tn(ds.reshape(2 * part, part), k2).astype(BF16)
        right_s[tok, pl.ds(width + col, 128)] = dot_nn(
            jnp.concatenate([ds[0], ds[1]], axis=1), split(q)
        ).astype(BF16)
        right_s[tok, pl.ds(2 * width + col, 128)] = dot_nn(
            jnp.concatenate([low[0], low[1]], axis=1), split(da)
        ).astype(BF16)
        return carry

    lax.fori_loop(0, clips * halves * (width // 128), attend_step, 0, unroll=4)

    half = width // 2
    copies = []

    def write(src, dst):
        copies.append(pltpu.make_async_copy(src, dst, out_sems.at[len(copies)]))
        copies[-1].start()

    for k in range(4):
        block = (place[0] + k) % 4
        lanes = slice(k * 384, k * 384 + 128)
        rhs = right_s[:, pl.ds(pl.multiple_of(2560 + block * 128, 128), 128)]
        send_a_s[:, :, lanes] = dot_nn(left_s[0, half:, :], rhs).reshape(8, 64, 128).astype(BF16)
        keep_a_s[:, :, lanes] = dot_nn(left_s[0, :half, :], rhs).reshape(8, 64, 128)
        lanes = slice(k * 384 + 128, k * 384 + 384)
        rhs = right_s[:, pl.ds(pl.multiple_of(3072 + block * 256, 256), 256)]
        send_a_s[:, :, lanes] = dot_nn(left_s[1, half:, :], rhs).reshape(8, 64, 256).astype(BF16)
        keep_a_s[:, :, lanes] = dot_nn(left_s[1, :half, :], rhs).reshape(8, 64, 256)
    write(send_a_s, send_a_hbm)
    for k in range(4):
        block = (place[0] + k) % 4
        rhs = right_s[:, pl.ds(pl.multiple_of(block * 640, 128), 640)]
        send_b_s[k] = dot_nn(left_s[0, half:, :], rhs).reshape(8, 64, 640).astype(BF16)
        write(send_b_s.at[k], send_b_hbm.at[k])
        keep_b_s[k] = dot_nn(left_s[0, :half, :], rhs).reshape(8, 64, 640)
        write(keep_b_s.at[k], keep_b_hbm.at[k])
    write(keep_a_s, keep_a_hbm)

    for n in range(width // CHUNK):
        cols = slice(n * CHUNK, (n + 1) * CHUNK)
        dn_s[:, cols] = dot_nt(right_s[:, :3 * width], wqkv_s[cols, :])

    def back_step(i, carry):
        dgain, dbias = carry
        c = i // (frames // 2)
        q = i % (frames // 2)
        outs = []
        for hf in range(halves):
            at = pl.multiple_of((c * halves + hf) * part + q * 16, 16)
            dn = dn_s[pl.ds(at, 16), :]
            wh = wh_s[pl.ds(at, 16), :]
            inv = inv_s[pl.ds(at, 16), :][:, :1]
            dw = dn * wh
            dgain = dgain + dw[:8] + dw[8:]
            dbias = dbias + dn[:8] + dn[8:]
            scaled = dn * gain
            m1 = jnp.mean(scaled, axis=-1, keepdims=True)
            m2 = jnp.mean(scaled * wh, axis=-1, keepdims=True)
            g = right_s[pl.ds(at, 16), pl.ds(3 * width, width)].astype(F32)
            outs.append((g + inv * (scaled - m1 - wh * m2)).reshape(2, 8, width))
        grads = jnp.concatenate(outs, axis=1).astype(BF16)
        at = pl.ds(pl.multiple_of(c * positions, positions), positions)
        for f in range(2):
            back_ref[(f - place[1]) % 2, q, at, :width] = grads[f]
        return dgain, dbias

    zeros = jnp.zeros((8, width), F32)
    dgain, dbias = lax.fori_loop(0, clips * frames // 2, back_step, (zeros, zeros))
    dgain = jnp.sum(dgain, axis=0, keepdims=True)
    dbias = jnp.sum(dbias, axis=0, keepdims=True)
    lane = lax.broadcasted_iota(jnp.int32, (1, 128), 1)
    row = lax.broadcasted_iota(jnp.int32, (16, 128), 0)
    back_ref[:, :, 16:, width:] = jnp.zeros((2, 8, clips * positions - 16, 128), BF16)
    for f in range(frames):
        at = f // 2 * 128
        a = dgain[:, at:at + 128]
        b = dbias[:, at:at + 128]
        if f % 2 == 0:
            b = jnp.concatenate([b[:, 64:], b[:, :64]], axis=1)
        else:
            a = jnp.concatenate([a[:, 64:], a[:, :64]], axis=1)
        both = jnp.where(lane < 64, a, b)
        hi = both.astype(BF16).astype(F32)
        mid = (both - hi).astype(BF16).astype(F32)
        low = both - hi - mid
        terms = jnp.where(row == 0, hi, jnp.where(row == 1, mid, jnp.where(row == 2, low, 0.0)))
        back_ref[(f % 2 - place[1]) % 2, f // 2, :16, width:] = terms.astype(BF16)
    for copy in copies:
        copy.wait()


def run_main(place, tokens, gain, bias, wqkv, wout):
    frames, clips, positions, width = tokens.shape
    clips = clips // 2
    rows = clips * frames * positions
    vm = pl.BlockSpec(memory_space=pltpu.VMEM)
    hbm = pl.BlockSpec(memory_space=pl.ANY)
    a, b = (8, 64, 1536), (4, 8, 64, 640)
    return pl.pallas_call(
        main_kernel,
        out_shape=(
            jax.ShapeDtypeStruct((2, frames // 2, clips * positions, width + 128), BF16),
            jax.ShapeDtypeStruct(a, BF16),
            jax.ShapeDtypeStruct(b, BF16),
            jax.ShapeDtypeStruct(a, F32),
            jax.ShapeDtypeStruct(b, F32),
        ),
        in_specs=[pl.BlockSpec(memory_space=pltpu.SMEM), hbm, vm, vm, hbm, hbm],
        out_specs=(vm, hbm, hbm, hbm, hbm),
        scratch_shapes=[
            pltpu.VMEM(tokens.shape, BF16),
            pltpu.VMEM(wqkv.shape, BF16),
            pltpu.VMEM(wout.shape, BF16),
            pltpu.VMEM((2, width, rows), BF16),
            pltpu.VMEM((rows, 4 * width), BF16),
            pltpu.VMEM((rows, width), BF16),
            pltpu.VMEM((rows, 3 * width), BF16),
            pltpu.VMEM((rows, width), BF16),
            pltpu.VMEM((rows, width), F32),
            pltpu.VMEM((rows, 128), F32),
            pltpu.VMEM((rows, width), F32),
            pltpu.VMEM(a, BF16),
            pltpu.VMEM(b, BF16),
            pltpu.VMEM(a, F32),
            pltpu.VMEM(b, F32),
            pltpu.SemaphoreType.DMA((frames // 2,)),
            pltpu.SemaphoreType.DMA((3 * width // CHUNK + 1,)),
            pltpu.SemaphoreType.DMA((10,)),
        ],
        compiler_params=pltpu.CompilerParams(vmem_limit_bytes=63 * MIB),
        cost_estimate=pl.CostEstimate(flops=12 * 1024**3, bytes_accessed=20 * MIB, transcendentals=MIB),
        name="sublayer",
    )(place, tokens, gain, bias, wqkv, wout)


def message_kernel(place_ref, keep_ref, got_ref, back_ref, theirs_ref, own_ref, message_ref):
    g = keep_ref[0] + got_ref[0].astype(F32)
    message_ref[0, :, :1536] = g.astype(BF16)
    message_ref[0, :32, 1536:] = back_ref[0, 0]
    message_ref[0, 32:, 1536:] = theirs_ref[0]

    @pl.when(pl.program_id(0) == place_ref[2])
    def _():
        own_ref[...] = g


def run_message(place, keep, got, back, theirs):
    lanes = back.shape[3]
    rows = pl.BlockSpec((1, 64, 1536), lambda k, place: (k, 0, 0))
    return pl.pallas_call(
        message_kernel,
        grid_spec=pltpu.PrefetchScalarGridSpec(
            num_scalar_prefetch=1,
            grid=(8,),
            in_specs=[
                rows,
                rows,
                pl.BlockSpec((1, 1, 32, lanes), lambda k, place: (0, k, 0, 0)),
                pl.BlockSpec((1, 32, lanes), lambda k, place: (k, 0, 0)),
            ],
            out_specs=(
                pl.BlockSpec((64, 1536), lambda k, place: (0, 0)),
                pl.BlockSpec((1, 64, 1536 + lanes), lambda k, place: (k, 0, 0)),
            ),
        ),
        out_shape=(
            jax.ShapeDtypeStruct((64, 1536), F32),
            jax.ShapeDtypeStruct((8, 64, 1536 + lanes), BF16),
        ),
        compiler_params=pltpu.CompilerParams(vmem_limit_bytes=63 * MIB),
        cost_estimate=pl.CostEstimate(flops=MIB, bytes_accessed=9 * MIB, transcendentals=0),
        name="message",
    )(place, keep, got, back, theirs)


def unpack_kernel(place_ref, message_ref, out_ref):
    clips, _, width = out_ref.shape
    for which in range(2):
        at = pl.multiple_of((which + place_ref[1]) % 2 * 16, 16)
        for c in range(clips):
            row = which * 32 + c * 16
            out_ref[c, pl.ds(at, 16), :] = message_ref[0, row:row + 16, 1536:1536 + width]


def run_unpack(place, message, clips, width):
    return pl.pallas_call(
        unpack_kernel,
        grid_spec=pltpu.PrefetchScalarGridSpec(
            num_scalar_prefetch=1,
            grid=(8,),
            in_specs=[pl.BlockSpec((1,) + message.shape[1:], lambda k, place: (k, 0, 0))],
            out_specs=pl.BlockSpec((clips, 32, width), lambda k, place: (0, k, 0)),
        ),
        out_shape=jax.ShapeDtypeStruct((clips, 256, width), BF16),
        compiler_params=pltpu.CompilerParams(vmem_limit_bytes=63 * MIB),
        name="unpack",
    )(place, message)


def place_kernel(scale, place_ref, d0, d1, d2, d3, qkv_ref, out_ref, gain_ref, bias_ref):
    small = jnp.zeros((8, 128), F32)
    for j, d in enumerate((d0, d1, d2, d3)):
        block = (place_ref[0] - j) % 4
        qkv_ref[:, pl.ds(pl.multiple_of(block * 640, 128), 640)] = d[:, :640] * scale
        qkv_ref[:, pl.ds(pl.multiple_of(2560 + block * 128, 128), 128)] = d[:, 640:768] * scale
        out_ref[:, pl.ds(pl.multiple_of(block * 256, 256), 256)] = d[:, 768:1024] * scale
        small = small + d[:8, 1024:]
    small = jnp.sum(small, axis=0, keepdims=True) * scale
    gain_ref[...] = small[:, :64]
    bias_ref[...] = small[:, 64:]


def run_place(place, scale, pieces):
    vm = pl.BlockSpec(memory_space=pltpu.VMEM)
    return pl.pallas_call(
        functools.partial(place_kernel, scale),
        out_shape=(
            jax.ShapeDtypeStruct((64, 3072), F32),
            jax.ShapeDtypeStruct((64, 1024), F32),
            jax.ShapeDtypeStruct((1, 64), F32),
            jax.ShapeDtypeStruct((1, 64), F32),
        ),
        in_specs=[pl.BlockSpec(memory_space=pltpu.SMEM)] + [vm] * 4,
        out_specs=(vm,) * 4,
        name="place_grads",
    )(place, *pieces)


def frame_pairs(move):
    pairs = []
    for i in range(16):
        y, z, core = move(i // 4, i // 2 % 2, i % 2)
        pairs.append((i, y % 4 * 4 + z % 2 * 2 + core % 2))
    return pairs


def dp_pairs(move):
    pairs = []
    for i in range(16):
        x, h = move(i // 4, i % 4)
        pairs.append((i, x % 4 * 4 + h % 4))
    return pairs


def go_core(a):
    return lax.ppermute(a, "frame", frame_pairs(lambda y, z, c: (y, z, c + 1)))


def trade_yz(a):
    groups = [[2 * i + core for i in range(8)] for core in range(2)]
    return lax.all_to_all(a, "frame", 0, 0, tiled=True, axis_index_groups=groups)


def go_x(a, k):
    return lax.ppermute(a, "dp", dp_pairs(lambda x, h: (x + k, h)))


def go_h(a, k):
    return lax.ppermute(a, "dp", dp_pairs(lambda x, h: (x, h + k)))


def combine(own, got):
    for part in got:
        own = own + part.astype(F32)
    return own


def exchange(pieces, go):
    return [go(pieces[k], k) for k in range(1, 4)]


def pick(array, index):
    return lax.dynamic_index_in_dim(array, index, 0, keepdims=False)


def reduce_yz(own, got, yz):
    mine = (jnp.arange(8) == yz).reshape((8,) + (1,) * own.ndim)
    return jnp.sum(jnp.where(mine, own[None], got.astype(F32)), axis=0)


def three_terms(value):
    hi = lax.reduce_precision(value, 8, 7)
    mid = lax.reduce_precision(value - hi, 8, 7)
    return jnp.pad(jnp.concatenate([hi, mid, value - hi - mid], axis=0), ((0, 61), (0, 0)))


def local(video, cotangent, norm_gain, norm_bias, qkv_weight, out_weight):
    clips, frames_here, positions, width = video.shape
    grad_scale = 1.0 / math.sqrt(clips * positions * 256)
    frame = lax.axis_index("frame")
    dp = lax.axis_index("dp")
    yz, core = frame // 2, frame % 2
    place = jnp.stack([dp // 4, core, yz]).astype(jnp.int32)
    gain = norm_gain.reshape(1, width)
    bias = norm_bias.reshape(1, width)
    tokens = jnp.concatenate([video, cotangent], axis=0).reshape(2 * clips, 16, positions // 16, width)
    tokens = lax.all_to_all(tokens.transpose(1, 0, 2, 3), "frame", 0, 0, tiled=True)

    back, send_a, send_b, keep_a, keep_b = run_main(place, tokens, gain, bias, qkv_weight, out_weight)

    got_a = go_core(send_a)
    theirs = go_core(back[1])
    got_b = go_core(send_b)
    own_a, message = run_message(place, keep_a, got_a, back, theirs)
    message = trade_yz(message)
    terms_b = [keep_b[0] + got_b[0].astype(F32)]
    terms_b += [(keep_b[k] + got_b[k].astype(F32)).astype(BF16) for k in range(1, 4)]
    got_b = exchange(terms_b, go_x)
    message, got_b = lax.optimization_barrier((message, got_b))

    b = combine(terms_b[0], got_b)
    got_b = trade_yz(b.astype(BF16))
    a = reduce_yz(own_a, message[:, :, :1536], yz)
    terms_a = [a[:, k * 384 : (k + 1) * 384] for k in range(4)]
    got_a = exchange([t.astype(BF16) for t in terms_a], go_x)
    message, got_a, got_b = lax.optimization_barrier((message, got_a, got_b))

    a = combine(terms_a[0], got_a)
    b = reduce_yz(pick(b, yz), got_b, yz)
    small = jnp.sum(message[:, :, 1536 + width :].astype(F32), axis=(0, 1)).reshape(1, 128)
    own = jnp.concatenate([b, a, three_terms(small)], axis=1)
    own = combine(own, exchange([own.astype(BF16)] * 4, go_h))
    pieces = [own] + exchange([own] * 4, go_x)

    grad_video = run_unpack(place, message, clips, width).reshape(video.shape)
    pieces, grad_video = lax.optimization_barrier((pieces, grad_video))
    grad_qkv, grad_out, total_gain, total_bias = run_place(place, grad_scale, pieces)
    return grad_video, grad_qkv, grad_out, total_gain.reshape(64), total_bias.reshape(64)


def solution(mesh):
    in_specs = (P("dp", "frame", None, None), P("dp", "frame", None, None), P(), P(), P(), P())
    out_specs = (
        P("dp", "frame", None, None),
        P("frame", None),
        P("frame", None),
        P("frame"),
        P("frame"),
    )
    return jax.shard_map(local, mesh=mesh, in_specs=in_specs, out_specs=out_specs, check_vma=False)
```

time: 198 us -> 193 us (0.975)
  local copies, waits for them, and re-layouts: 17.5 us -> 6.61 us
  starting transfers between devices: 48.7 us -> 41.1 us
  other arithmetic: 7.83 us -> 14.3 us
  Pallas kernels: 43.7 us -> 48.9 us
  waiting for transfers between devices: 77.4 us -> 80.1 us
    unnamed x33 -> x18, local copies, waits for them, and re-layouts: 13.4 us -> 2.38 us
    ppermute x3, waiting for transfers between devices: 0.01 us -> 10.5 us  [go_h(): return lax.ppermute(a, 'dp', dp_pairs(lambda x, h: (x, h + k)))]
    ppermute x3, waiting for transfers between devices: 0.01 us -> 7.66 us  [go_core(): return lax.ppermute(a, 'frame', frame_pairs(lambda y, z, c: (y, z, c + 1)))]
    ppermute x9, waiting for transfers between devices: 42 us -> 34.8 us  [go_x(): return lax.ppermute(a, 'dp', dp_pairs(lambda x, h: (x + k, h)))]
    all_to_all x1 -> x0, waiting for transfers between devices: 7.16 us -> none  [local(): lax.all_to_all(jnp.broadcast_to(small, (16, 1, 128)), 'dp', 0, 0, tiled=T...]
    pallas_call x1, Pallas kernels: 26.2 us -> 33 us  [run_main(): pl.pallas_call(main_kernel, out_shape=(jax.ShapeDtypeStruct((2, frames //...]
    all_to_all x1 -> x0, starting transfers between devices: 6.38 us -> none  [local(): lax.all_to_all(jnp.broadcast_to(small, (16, 1, 128)), 'dp', 0, 0, tiled=T...]
    convert_element_type x0 -> x1, other arithmetic: none -> 3.62 us  [local(): (keep_b[k] + got_b[k].astype(F32)).astype(BF16)]
  transfers between devices with their start and end apart: 19 -> 18, of which waited for: 9 -> 12; matrix products, arithmetic and copies ran while one was open for 3% -> 4% of each run, Pallas kernels for 7% -> 3%
where the time goes in v7:
time: 193 us; the launch traced here: 192 us
  waiting for transfers between devices  80.1 us (42%)
  Pallas kernels  48.9 us (25%)
  starting transfers between devices  41.1 us (21%)
  other arithmetic  14.3 us (7%)
  local copies, waits for them, and re-layouts  6.61 us (3%)
    ppermute x9, waiting for transfers between devices, go_x(): return lax.ppermute(a, 'dp', dp_pairs(lambda x, h: (x + k, h)))  34.8 us
    pallas_call x1, Pallas kernels, run_main(): pl.pallas_call(main_kernel, out_shape=(jax.ShapeDtypeStruct((2, frames //...  33 us
    all_to_all x1, waiting for transfers between devices, local(): lax.all_to_all(tokens.transpose(1, 0, 2, 3), 'frame', 0, 0, tiled=True)  26.1 us
    ppermute x9, starting transfers between devices, go_x(): return lax.ppermute(a, 'dp', dp_pairs(lambda x, h: (x + k, h)))  14.4 us
    all_to_all x2, starting transfers between devices, trade_yz(): lax.all_to_all(a, 'frame', 0, 0, tiled=True, axis_index_groups=groups)  10.7 us
    ppermute x3, waiting for transfers between devices, go_h(): return lax.ppermute(a, 'dp', dp_pairs(lambda x, h: (x, h + k)))  10.5 us
    ppermute x3, starting transfers between devices, go_h(): return lax.ppermute(a, 'dp', dp_pairs(lambda x, h: (x, h + k)))  9.3 us
    ppermute x3, waiting for transfers between devices, go_core(): return lax.ppermute(a, 'frame', frame_pairs(lambda y, z, c: (y, z, c + 1)))  7.66 us
  transfers between devices with their start and end apart: 18, of which 12 were waited for; matrix products, arithmetic and copies ran while one was open for 4% of the time, Pallas kernels for 3%

profile of v7, /device:TPU:32, one launch (start us, length us, event | category | flops | bytes accessed | tf_op | source)
XLA Modules:
  0.0 191.8 jit_solution(2377754127888378799)
XLA Ops:
  0.6 1.7 pad_maximum_fusion
  2.4 1.5 copy.17
  3.9 6.0 %all-to-all-start = ((bf16[16,4,16,1024]{3,2,1,0:T(8,128)(2,1)}), bf16[16,4,16,1024]{3,2,1,0:T(8,128)(2,1)}, u32[]{:S(2)}, u32[]{:S(2)}) async-start(bf16[16,4,16,1024]{3,2,1,0:T(8,128)(2,1)} %bitcast.44), calls=%async_computation | async-start | bytes 4194304 | tf_op jit(solution)/shard_map/all_to_all | solution.py:440
  9.9 0.7 pad_add_fusion.place_ref
  10.5 26.1 %all-to-all-done.tokens_hbm = bf16[16,4,16,1024]{3,2,1,0:T(8,128)(2,1)} async-done(((bf16[16,4,16,1024]{3,2,1,0:T(8,128)(2,1)}), bf16[16,4,16,1024]{3,2,1,0:T(8,128)(2,1)}, u32[]{:S(2)}, u32[]{:S(2)}) %all-to-all-start) | async-done | bytes 2097184 | tf_op jit(solution)/shard_map/all_to_all | solution.py:440
  36.7 33.0 %sublayer.1 = (bf16[2,8,32,1152]{3,2,1,0:T(8,128)(2,1)}, bf16[8,64,1536]{2,1,0:T(8,128)(2,1)}, bf16[4,8,64,640]{3,2,1,0:T(8,128)(2,1)}, f32[8,64,1536]{2,1,0:T(8,128)}, f32[4,8,64,640]{3,2,1,0:T(8,128)}) custom-call(s32[3]{0:T(128)} %pad_add_fusion.place_ref, bf16[16,4,16,1024]{3,2,1,0:T(8,128)(2,1)} %all-to-all-done.tokens_hbm, f32[1,1024]{1,0:T(1,128)} %bitcast.49, ...), custom_call_target="tpu_custom_call" | custom-call | flops 12884901888 | bytes 20971520 | tf_op jit(solution)/shard_map/sublayer/pallas_call | solution.py:242
  69.7 0.2 collective-permute-start.1
  69.9 1.1 slice_bitcast_fusion
  71.0 0.5 collective-permute-start.2
  71.5 2.5 %collective-permute-done.2.theirs_ref = bf16[8,32,1152]{2,1,0:T(8,128)(2,1)S(1)} collective-permute-done((bf16[8,32,1152]{2,1,0:T(8,128)(2,1)S(1)}, bf16[8,32,1152]{2,1,0:T(8,128)(2,1)S(1)}, u32[]{:S(2)}, u32[]{:S(2)}) %collective-permute-start.2) | collective-permute-done | bytes 589856 | tf_op jit(solution)/shard_map/ppermute | solution.py:389
  74.0 0.8 copy-done.5
  74.8 7.4 %message.1 = (f32[64,1536]{1,0:T(8,128)}, bf16[8,64,2688]{2,1,0:T(8,128)(2,1)}) custom-call(s32[3]{0:T(128)} %pad_add_fusion.place_ref, f32[8,64,1536]{2,1,0:T(8,128)} %get-tuple-element.32.keep_ref, bf16[8,64,1536]{2,1,0:T(8,128)(2,1)} %collective-permute-done.1.got_ref, bf16[2,8,32,1152]{3,2,1,0:T(8,128)(2,1)} %get-tuple-element.34.back_ref, ...), custom_call_target="tpu_custom_call" | custom-call | flops 1048576 | bytes 9437184 | tf_op jit(solution)/shard_map/message/pallas_call | solution.py:293
  82.2 4.9 %all-to-all-start.1 = ((bf16[8,64,2688]{2,1,0:T(8,128)(2,1)}), bf16[8,64,2688]{2,1,0:T(8,128)(2,1)S(1)}, u32[]{:S(2)}, u32[]{:S(2)}) async-start(bf16[8,64,2688]{2,1,0:T(8,128)(2,1)} %get-tuple-element.35), calls=%async_computation.1 | async-start | bytes 5505024 | tf_op jit(solution)/shard_map/all_to_all | solution.py:394
  87.2 5.1 %collective-permute-done = bf16[4,8,64,640]{3,2,1,0:T(8,128)(2,1)S(1)} collective-permute-done((bf16[4,8,64,640]{3,2,1,0:T(8,128)(2,1)}, bf16[4,8,64,640]{3,2,1,0:T(8,128)(2,1)S(1)}, u32[]{:S(2)}, u32[]{:S(2)}) %collective-permute-start) | collective-permute-done | bytes 2621472 | tf_op jit(solution)/shard_map/ppermute | solution.py:389
  92.3 3.6 %fusion.4 = (bf16[8,64,640]{2,1,0:T(8,128)(2,1)S(1)}, bf16[8,64,640]{2,1,0:T(8,128)(2,1)S(1)}, bf16[8,64,640]{2,1,0:T(8,128)(2,1)S(1)}) fusion(f32[4,8,64,640]{3,2,1,0:T(8,128)} %get-tuple-element.30, bf16[4,8,64,640]{3,2,1,0:T(8,128)(2,1)S(1)} %collective-permute-done), kind=kLoop, calls=%fused_computation.12 | loop fusion | flops 2949120 | bytes 7864320 | tf_op jit(solution)/shard_map/convert_element_type | solution.py:450
  95.9 1.4 collective-permute-start.3
  97.4 2.7 %collective-permute-start.4 = (bf16[8,64,640]{2,1,0:T(8,128)(2,1)S(1)}, bf16[8,64,640]{2,1,0:T(8,128)(2,1)S(1)}, u32[]{:S(2)}, u32[]{:S(2)}) collective-permute-start(bf16[8,64,640]{2,1,0:T(8,128)(2,1)S(1)} %get-tuple-element.68), channel_id=1, source_target_pairs={{0,128},{16,144},{32,160},{48,176},{64,192},{80,208},{96,224},{112... | collective-permute-start | bytes 1966088 | tf_op jit(solution)/shard_map/ppermute | solution.py:398
  100.1 1.4 collective-permute-start.5
  101.5 12.5 %collective-permute-done.3 = bf16[8,64,640]{2,1,0:T(8,128)(2,1)S(1)} collective-permute-done((bf16[8,64,640]{2,1,0:T(8,128)(2,1)S(1)}, bf16[8,64,640]{2,1,0:T(8,128)(2,1)S(1)}, u32[]{:S(2)}, u32[]{:S(2)}) %collective-permute-start.3) | collective-permute-done | bytes 655392 | tf_op jit(solution)/shard_map/ppermute | solution.py:398
  114.0 14.9 %collective-permute-done.4 = bf16[8,64,640]{2,1,0:T(8,128)(2,1)S(1)} collective-permute-done((bf16[8,64,640]{2,1,0:T(8,128)(2,1)S(1)}, bf16[8,64,640]{2,1,0:T(8,128)(2,1)S(1)}, u32[]{:S(2)}, u32[]{:S(2)}) %collective-permute-start.4) | collective-permute-done | bytes 655392 | tf_op jit(solution)/shard_map/ppermute | solution.py:398
  128.9 0.8 copy-done.4
  129.7 4.6 %fusion.10 = (bf16[8,64,640]{2,1,0:T(8,128)(2,1)}, f32[8,64,640]{2,1,0:T(8,128)}) fusion(bf16[8,64,640]{2,1,0:T(8,128)(2,1)} %collective-permute-done.5, bf16[8,64,640]{2,1,0:T(8,128)(2,1)} %copy-done.4, bf16[8,64,640]{2,1,0:T(8,128)(2,1)S(1)} %collective-permute-done.3, bf16[4,8,64,640]{3,2,1,0:T(8,128)(2,1)} %copy-done.1, ...), kind=kLoop, calls=%fused_computation.31 | loop fusion | flops 2949120 | bytes 5898240 | tf_op jit(solution)/shard_map/convert_element_type | solution.py:455
  134.3 5.7 %all-to-all-start.2 = ((bf16[8,64,640]{2,1,0:T(8,128)(2,1)}), bf16[8,64,640]{2,1,0:T(8,128)(2,1)S(1)}, u32[]{:S(2)}, u32[]{:S(2)}) async-start(bf16[8,64,640]{2,1,0:T(8,128)(2,1)} %get-tuple-element.65), calls=%async_computation.2 | async-start | bytes 1310720 | tf_op jit(solution)/shard_map/all_to_all | solution.py:394
  140.1 1.4 select_reduce_fusion
  141.5 0.0 copy-start.2
  141.6 0.8 collective-permute-start.6
  142.4 2.4 %collective-permute-start.7 = (bf16[64,384]{1,0:T(8,128)(2,1)S(1)}, bf16[64,384]{1,0:T(8,128)(2,1)S(1)}, u32[]{:S(2)}, u32[]{:S(2)}) collective-permute-start(bf16[64,384]{1,0:T(8,128)(2,1)S(1)} %get-tuple-element.71), channel_id=1, source_target_pairs={{0,128},{16,144},{32,160},{48,176},{64,192},{80,208},{96,224},{112... | collective-permute-start | bytes 147464 | tf_op jit(solution)/shard_map/ppermute | solution.py:398
  144.8 1.4 collective-permute-start.8
  146.2 1.6 dynamic-slice_bitcast_fusion
  147.8 0.2 collective-permute-done.7
  148.0 0.9 collective-permute-done.8
  148.9 1.0 all-to-all-done.2
  149.8 0.1 convert_reduce_fusion
  149.9 1.1 select_reduce_fusion.1
  151.1 0.9 fusion.7
  152.0 5.5 %collective-permute-start.11 = (bf16[64,1152]{1,0:T(8,128)(2,1)S(1)}, bf16[64,1152]{1,0:T(8,128)(2,1)S(1)}, u32[]{:S(2)}, u32[]{:S(2)}) collective-permute-start(bf16[64,1152]{1,0:T(8,128)(2,1)S(1)} %fusion.5), channel_id=1, source_target_pairs={{0,48},{16,0},{32,16},{48,32},{64,112},{80,64},{96,80},{112,96},{1... | collective-permute-start | bytes 442376 | tf_op jit(solution)/shard_map/ppermute | solution.py:402
  157.5 1.4 collective-permute-start.10
  159.0 2.4 %collective-permute-start.9 = (bf16[64,1152]{1,0:T(8,128)(2,1)S(1)}, bf16[64,1152]{1,0:T(8,128)(2,1)S(1)}, u32[]{:S(2)}, u32[]{:S(2)}) collective-permute-start(bf16[64,1152]{1,0:T(8,128)(2,1)S(1)} %fusion.5), channel_id=1, source_target_pairs={{0,16},{16,32},{32,48},{48,0},{64,80},{80,96},{96,112},{112,64},{1... | collective-permute-start | bytes 442376 | tf_op jit(solution)/shard_map/ppermute | solution.py:402
  161.3 4.3 %collective-permute-done.11 = bf16[64,1152]{1,0:T(8,128)(2,1)S(1)} collective-permute-done((bf16[64,1152]{1,0:T(8,128)(2,1)S(1)}, bf16[64,1152]{1,0:T(8,128)(2,1)S(1)}, u32[]{:S(2)}, u32[]{:S(2)}) %collective-permute-start.11) | collective-permute-done | bytes 147488 | tf_op jit(solution)/shard_map/ppermute | solution.py:402
  165.7 5.8 %collective-permute-done.10 = bf16[64,1152]{1,0:T(8,128)(2,1)S(1)} collective-permute-done((bf16[64,1152]{1,0:T(8,128)(2,1)S(1)}, bf16[64,1152]{1,0:T(8,128)(2,1)S(1)}, u32[]{:S(2)}, u32[]{:S(2)}) %collective-permute-start.10) | collective-permute-done | bytes 147488 | tf_op jit(solution)/shard_map/ppermute | solution.py:402
  171.5 0.4 collective-permute-done.9
  171.9 0.1 convert_add_fusion.d0
  172.0 0.6 collective-permute-start.12
  172.6 3.6 %collective-permute-start.13 = (f32[64,1152]{1,0:T(8,128)S(1)}, f32[64,1152]{1,0:T(8,128)S(1)}, u32[]{:S(2)}, u32[]{:S(2)}) collective-permute-start(f32[64,1152]{1,0:T(8,128)S(1)} %convert_add_fusion.d0), channel_id=1, source_target_pairs={{0,128},{16,144},{32,160},{48,176},{64,192},{80,208},{96,224},{112... | collective-permute-start | bytes 884744 | tf_op jit(solution)/shard_map/ppermute | solution.py:398
  176.1 6.2 %unpack.1 = bf16[2,256,1024]{2,1,0:T(8,128)(2,1)} custom-call(s32[3]{0:T(128)} %pad_add_fusion.place_ref, bf16[8,64,2688]{2,1,0:T(8,128)(2,1)} %copy-done), custom_call_target="tpu_custom_call" | custom-call | tf_op jit(solution)/shard_map/unpack/pallas_call | solution.py:329
  182.3 6.4 %collective-permute-done.13.d2 = f32[64,1152]{1,0:T(8,128)S(1)} collective-permute-done((f32[64,1152]{1,0:T(8,128)S(1)}, f32[64,1152]{1,0:T(8,128)S(1)}, u32[]{:S(2)}, u32[]{:S(2)}) %collective-permute-start.13) | collective-permute-done | bytes 294944 | tf_op jit(solution)/shard_map/ppermute | solution.py:398
  188.7 0.7 copy-done.7
  189.4 2.3 %place_grads.1 = (f32[64,3072]{1,0:T(8,128)}, f32[64,1024]{1,0:T(8,128)}, f32[1,64]{1,0:T(1,128)}, f32[1,64]{1,0:T(1,128)}) custom-call(s32[3]{0:T(128)} %pad_add_fusion.place_ref, f32[64,1152]{1,0:T(8,128)} %copy-done.3, f32[64,1152]{1,0:T(8,128)} %copy-done.6, f32[64,1152]{1,0:T(8,128)} %copy-done.7, f32[64,1152]{1,0:T(8,128)} %collective-permute-done.14.d3), custom_call_target="tpu_custom_call" | custom-call | tf_op jit(solution)/shard_map/place_grads/pallas_call | solution.py:358
  (28 shorter events, 0.1 us)
Async XLA Ops:
  3.9 32.8 %all-to-all-start = ((bf16[16,4,16,1024]{3,2,1,0:T(8,128)(2,1)}), bf16[16,4,16,1024]{3,2,1,0:T(8,128)(2,1)}, u32[]{:S(2)}, u32[]{:S(2)}) async-start(bf16[16,4,16,1024]{3,2,1,0:T(8,128)(2,1)} %bitcast.44), calls=%async_computation | async-start | bytes 4194304 | tf_op jit(solution)/shard_map/all_to_all | solution.py:440
  69.7 4.3 %collective-permute-start.1 = (bf16[8,64,1536]{2,1,0:T(8,128)(2,1)}, bf16[8,64,1536]{2,1,0:T(8,128)(2,1)}, u32[]{:S(2)}, u32[]{:S(2)}) collective-permute-start(bf16[8,64,1536]{2,1,0:T(8,128)(2,1)} %get-tuple-element.33), channel_id=1, source_target_pairs={{0,1},{1,0},{2,3},{3,2},{4,5},{5,4},{6,7},{7,6},{8,9},{9,8},{10,11... | collective-permute-start | bytes 4718600 | tf_op jit(solution)/shard_map/ppermute | solution.py:389
  71.0 3.0 %collective-permute-start.2 = (bf16[8,32,1152]{2,1,0:T(8,128)(2,1)S(1)}, bf16[8,32,1152]{2,1,0:T(8,128)(2,1)S(1)}, u32[]{:S(2)}, u32[]{:S(2)}) collective-permute-start(bf16[8,32,1152]{2,1,0:T(8,128)(2,1)S(1)} %slice_bitcast_fusion), channel_id=1, source_target_pairs={{0,1},{1,0},{2,3},{3,2},{4,5},{5,4},{6,7},{7,6},{8,9},{9,8},{10,11... | collective-permute-start | bytes 1769480 | tf_op jit(solution)/shard_map/ppermute | solution.py:389
  74.0 0.8 copy-start.5
  82.2 47.5 %all-to-all-start.1 = ((bf16[8,64,2688]{2,1,0:T(8,128)(2,1)}), bf16[8,64,2688]{2,1,0:T(8,128)(2,1)S(1)}, u32[]{:S(2)}, u32[]{:S(2)}) async-start(bf16[8,64,2688]{2,1,0:T(8,128)(2,1)} %get-tuple-element.35), calls=%async_computation.1 | async-start | bytes 5505024 | tf_op jit(solution)/shard_map/all_to_all | solution.py:394
  87.2 5.1 %collective-permute-start = (bf16[4,8,64,640]{3,2,1,0:T(8,128)(2,1)}, bf16[4,8,64,640]{3,2,1,0:T(8,128)(2,1)S(1)}, u32[]{:S(2)}, u32[]{:S(2)}) collective-permute-start(bf16[4,8,64,640]{3,2,1,0:T(8,128)(2,1)} %get-tuple-element.31), channel_id=1, source_target_pairs={{0,1},{1,0},{2,3},{3,2},{4,5},{5,4},{6,7},{7,6},{8,9},{9,8},{10,11... | collective-permute-start | bytes 7864328 | tf_op jit(solution)/shard_map/ppermute | solution.py:389
  92.3 3.6 %copy-start.1 = (bf16[4,8,64,640]{3,2,1,0:T(8,128)(2,1)}, bf16[4,8,64,640]{3,2,1,0:T(8,128)(2,1)S(1)}, u32[]{:S(2)}) copy-start(bf16[4,8,64,640]{3,2,1,0:T(8,128)(2,1)S(1)} %collective-permute-done) | copy-start | bytes 7864324
  95.9 18.1 %collective-permute-start.3 = (bf16[8,64,640]{2,1,0:T(8,128)(2,1)S(1)}, bf16[8,64,640]{2,1,0:T(8,128)(2,1)S(1)}, u32[]{:S(2)}, u32[]{:S(2)}) collective-permute-start(bf16[8,64,640]{2,1,0:T(8,128)(2,1)S(1)} %get-tuple-element.69), channel_id=1, source_target_pairs={{0,64},{16,80},{32,96},{48,112},{64,128},{80,144},{96,160},{112,17... | collective-permute-start | bytes 1966088 | tf_op jit(solution)/shard_map/ppermute | solution.py:398
  97.4 31.5 %collective-permute-start.4 = (bf16[8,64,640]{2,1,0:T(8,128)(2,1)S(1)}, bf16[8,64,640]{2,1,0:T(8,128)(2,1)S(1)}, u32[]{:S(2)}, u32[]{:S(2)}) collective-permute-start(bf16[8,64,640]{2,1,0:T(8,128)(2,1)S(1)} %get-tuple-element.68), channel_id=1, source_target_pairs={{0,128},{16,144},{32,160},{48,176},{64,192},{80,208},{96,224},{112... | collective-permute-start | bytes 1966088 | tf_op jit(solution)/shard_map/ppermute | solution.py:398
  100.1 29.6 %collective-permute-start.5 = (bf16[8,64,640]{2,1,0:T(8,128)(2,1)S(1)}, bf16[8,64,640]{2,1,0:T(8,128)(2,1)}, u32[]{:S(2)}, u32[]{:S(2)}) collective-permute-start(bf16[8,64,640]{2,1,0:T(8,128)(2,1)S(1)} %get-tuple-element.67), channel_id=1, source_target_pairs={{0,192},{16,208},{32,224},{48,240},{64,0},{80,16},{96,32},{112,48}... | collective-permute-start | bytes 1966088 | tf_op jit(solution)/shard_map/ppermute | solution.py:398
  128.9 0.8 copy-start.4
  129.7 20.1 %copy-start = (bf16[8,64,2688]{2,1,0:T(8,128)(2,1)}, bf16[8,64,2688]{2,1,0:T(8,128)(2,1)S(1)}, u32[]{:S(2)}) copy-start(bf16[8,64,2688]{2,1,0:T(8,128)(2,1)S(1)} %all-to-all-done.1.message_ref) | copy-start | bytes 8257540
  134.3 15.5 %all-to-all-start.2 = ((bf16[8,64,640]{2,1,0:T(8,128)(2,1)}), bf16[8,64,640]{2,1,0:T(8,128)(2,1)S(1)}, u32[]{:S(2)}, u32[]{:S(2)}) async-start(bf16[8,64,640]{2,1,0:T(8,128)(2,1)} %get-tuple-element.65), calls=%async_computation.2 | async-start | bytes 1310720 | tf_op jit(solution)/shard_map/all_to_all | solution.py:394
  140.1 1.5 copy-start.8
  141.5 6.5 %copy-start.2 = (f32[64,1536]{1,0:T(8,128)}, f32[64,1536]{1,0:T(8,128)S(1)}, u32[]{:S(2)}) copy-start(f32[64,1536]{1,0:T(8,128)S(1)} %select_reduce_fusion) | copy-start | bytes 1179652
  141.6 6.2 %collective-permute-start.6 = (bf16[64,384]{1,0:T(8,128)(2,1)S(1)}, bf16[64,384]{1,0:T(8,128)(2,1)S(1)}, u32[]{:S(2)}, u32[]{:S(2)}) collective-permute-start(bf16[64,384]{1,0:T(8,128)(2,1)S(1)} %get-tuple-element.72), channel_id=1, source_target_pairs={{0,64},{16,80},{32,96},{48,112},{64,128},{80,144},{96,160},{112,17... | collective-permute-start | bytes 147464 | tf_op jit(solution)/shard_map/ppermute | solution.py:398
  142.4 5.6 %collective-permute-start.7 = (bf16[64,384]{1,0:T(8,128)(2,1)S(1)}, bf16[64,384]{1,0:T(8,128)(2,1)S(1)}, u32[]{:S(2)}, u32[]{:S(2)}) collective-permute-start(bf16[64,384]{1,0:T(8,128)(2,1)S(1)} %get-tuple-element.71), channel_id=1, source_target_pairs={{0,128},{16,144},{32,160},{48,176},{64,192},{80,208},{96,224},{112... | collective-permute-start | bytes 147464 | tf_op jit(solution)/shard_map/ppermute | solution.py:398
  144.8 4.1 %collective-permute-start.8 = (bf16[64,384]{1,0:T(8,128)(2,1)S(1)}, bf16[64,384]{1,0:T(8,128)(2,1)S(1)}, u32[]{:S(2)}, u32[]{:S(2)}) collective-permute-start(bf16[64,384]{1,0:T(8,128)(2,1)S(1)} %get-tuple-element.70), channel_id=1, source_target_pairs={{0,192},{16,208},{32,224},{48,240},{64,0},{80,16},{96,32},{112,48}... | collective-permute-start | bytes 147464 | tf_op jit(solution)/shard_map/ppermute | solution.py:398
  152.0 13.6 %collective-permute-start.11 = (bf16[64,1152]{1,0:T(8,128)(2,1)S(1)}, bf16[64,1152]{1,0:T(8,128)(2,1)S(1)}, u32[]{:S(2)}, u32[]{:S(2)}) collective-permute-start(bf16[64,1152]{1,0:T(8,128)(2,1)S(1)} %fusion.5), channel_id=1, source_target_pairs={{0,48},{16,0},{32,16},{48,32},{64,112},{80,64},{96,80},{112,96},{1... | collective-permute-start | bytes 442376 | tf_op jit(solution)/shard_map/ppermute | solution.py:402
  157.5 13.9 %collective-permute-start.10 = (bf16[64,1152]{1,0:T(8,128)(2,1)S(1)}, bf16[64,1152]{1,0:T(8,128)(2,1)S(1)}, u32[]{:S(2)}, u32[]{:S(2)}) collective-permute-start(bf16[64,1152]{1,0:T(8,128)(2,1)S(1)} %fusion.5), channel_id=1, source_target_pairs={{0,32},{16,48},{32,0},{48,16},{64,96},{80,112},{96,64},{112,80},{1... | collective-permute-start | bytes 442376 | tf_op jit(solution)/shard_map/ppermute | solution.py:402
  159.0 12.9 %collective-permute-start.9 = (bf16[64,1152]{1,0:T(8,128)(2,1)S(1)}, bf16[64,1152]{1,0:T(8,128)(2,1)S(1)}, u32[]{:S(2)}, u32[]{:S(2)}) collective-permute-start(bf16[64,1152]{1,0:T(8,128)(2,1)S(1)} %fusion.5), channel_id=1, source_target_pairs={{0,16},{16,32},{32,48},{48,0},{64,80},{80,96},{96,112},{112,64},{1... | collective-permute-start | bytes 442376 | tf_op jit(solution)/shard_map/ppermute | solution.py:402
  171.9 10.4 %copy-start.3 = (f32[64,1152]{1,0:T(8,128)}, f32[64,1152]{1,0:T(8,128)S(1)}, u32[]{:S(2)}) copy-start(f32[64,1152]{1,0:T(8,128)S(1)} %convert_add_fusion.d0) | copy-start | bytes 884740
  172.0 10.4 %collective-permute-start.12 = (f32[64,1152]{1,0:T(8,128)S(1)}, f32[64,1152]{1,0:T(8,128)S(1)}, u32[]{:S(2)}, u32[]{:S(2)}) collective-permute-start(f32[64,1152]{1,0:T(8,128)S(1)} %convert_add_fusion.d0), channel_id=1, source_target_pairs={{0,64},{16,80},{32,96},{48,112},{64,128},{80,144},{96,160},{112,17... | collective-permute-start | bytes 884744 | tf_op jit(solution)/shard_map/ppermute | solution.py:398
  172.6 16.1 %collective-permute-start.13 = (f32[64,1152]{1,0:T(8,128)S(1)}, f32[64,1152]{1,0:T(8,128)S(1)}, u32[]{:S(2)}, u32[]{:S(2)}) collective-permute-start(f32[64,1152]{1,0:T(8,128)S(1)} %convert_add_fusion.d0), channel_id=1, source_target_pairs={{0,128},{16,144},{32,160},{48,176},{64,192},{80,208},{96,224},{112... | collective-permute-start | bytes 884744 | tf_op jit(solution)/shard_map/ppermute | solution.py:398
  176.1 12.6 %collective-permute-start.14 = (f32[64,1152]{1,0:T(8,128)S(1)}, f32[64,1152]{1,0:T(8,128)}, u32[]{:S(2)}, u32[]{:S(2)}) collective-permute-start(f32[64,1152]{1,0:T(8,128)S(1)} %convert_add_fusion.d0), channel_id=1, source_target_pairs={{0,192},{16,208},{32,224},{48,240},{64,0},{80,16},{96,32},{112,48}... | collective-permute-start | bytes 884744 | tf_op jit(solution)/shard_map/ppermute | solution.py:398
  182.3 6.4 %copy-start.6 = (f32[64,1152]{1,0:T(8,128)}, f32[64,1152]{1,0:T(8,128)S(1)}, u32[]{:S(2)}) copy-start(f32[64,1152]{1,0:T(8,128)S(1)} %collective-permute-done.12.d1) | copy-start | bytes 884740
  188.7 0.7 copy-start.7

commit v8 on v7

--- a/solution.py
+++ b/solution.py
@@ -46,9 +46,9 @@
 
 def main_kernel(
     place_ref, tokens_hbm, gain_ref, bias_ref, wqkv_hbm, wout_hbm,
-    back_ref, send_a_hbm, send_b_hbm, keep_a_hbm, keep_b_hbm,
+    back_hbm, theirs_hbm, send_a_hbm, send_b_hbm, keep_a_hbm, keep_b_hbm,
     tokens_s, wqkv_s, wout_s, left_s, right_s, normed_s, packed_s, datt_s, wh_s, inv_s, dn_s,
-    send_a_s, send_b_s, keep_a_s, keep_b_s,
+    send_a_s, send_b_s, keep_a_s, keep_b_s, back_ref,
     token_sems, weight_sems, out_sems,
 ):
     place = read_place(place_ref)
@@ -88,7 +88,7 @@
                 right_s[pl.ds(at, 16), pl.ds(3 * width, width)] = g[:, hf].reshape(16, width).astype(BF16)
         return carry
 
-    lax.fori_loop(0, frames // 2, norm_step, 0)
+    lax.fori_loop(0, frames // 2, norm_step, 0, unroll=2)
 
     def qkv_step(n, carry):
         for i in range(2):
@@ -115,6 +115,7 @@
         lax.broadcasted_iota(jnp.int32, (1, 8, part), 2) % 8
     )
     zero = jnp.zeros((part, 128), BF16)
+    scale = jnp.asarray(0.125, BF16)
 
     def split(a):
         return jnp.concatenate([jnp.where(first, a, zero), jnp.where(first, zero, a)], axis=0)
@@ -130,14 +131,14 @@
         da = datt_s[tok, pl.ds(col, 128)]
         k2 = split(k)
         v2 = split(v)
-        scores = (dot_nt(k2, q) * 0.125).reshape(2, frames, 8, part)
+        scores = dot_nt(k2, q * scale).reshape(2, frames, 8, part)
         e = jnp.exp(scores - jnp.max(scores, axis=1, keepdims=True))
         probs = e * (1.0 / jnp.sum(e, axis=1, keepdims=True))
         probs = jnp.where(same[None], probs, 0.0)
         low = probs.astype(BF16).reshape(2, part, part)
-        dp = dot_nt(v2, da).reshape(2, frames, 8, part)
+        dp = dot_nt(v2, da * scale).reshape(2, frames, 8, part)
         inner = jnp.sum(dp * probs, axis=1, keepdims=True)
-        ds = (probs * (dp - inner) * 0.125).astype(BF16).reshape(2, part, part)
+        ds = (probs * (dp - inner)).astype(BF16).reshape(2, part, part)
         attended = dot_tn(v2, low.reshape(2 * part, part)).astype(BF16)
         for b in range(2):
             left_s[1, pl.ds(block_row(hp * 2 + b, place), 64), tok] = attended[b * 64:(b + 1) * 64]
@@ -150,7 +151,7 @@
         ).astype(BF16)
         return carry
 
-    lax.fori_loop(0, clips * halves * (width // 128), attend_step, 0, unroll=4)
+    lax.fori_loop(0, clips * halves * (width // 128), attend_step, 0, unroll=8)
 
     half = width // 2
     copies = []
@@ -208,7 +209,7 @@
         return dgain, dbias
 
     zeros = jnp.zeros((8, width), F32)
-    dgain, dbias = lax.fori_loop(0, clips * frames // 2, back_step, (zeros, zeros))
+    dgain, dbias = lax.fori_loop(0, clips * frames // 2, back_step, (zeros, zeros), unroll=2)
     dgain = jnp.sum(dgain, axis=0, keepdims=True)
     dbias = jnp.sum(dbias, axis=0, keepdims=True)
     lane = lax.broadcasted_iota(jnp.int32, (1, 128), 1)
@@ -228,6 +229,8 @@
         low = both - hi - mid
         terms = jnp.where(row == 0, hi, jnp.where(row == 1, mid, jnp.where(row == 2, low, 0.0)))
         back_ref[(f % 2 - place[1]) % 2, f // 2, :16, width:] = terms.astype(BF16)
+    write(back_ref.at[1], theirs_hbm)
+    write(back_ref.at[0], back_hbm)
     for copy in copies:
         copy.wait()
 
@@ -239,17 +242,19 @@
     vm = pl.BlockSpec(memory_space=pltpu.VMEM)
     hbm = pl.BlockSpec(memory_space=pl.ANY)
     a, b = (8, 64, 1536), (4, 8, 64, 640)
+    back = (frames // 2, clips * positions, width + 128)
     return pl.pallas_call(
         main_kernel,
         out_shape=(
-            jax.ShapeDtypeStruct((2, frames // 2, clips * positions, width + 128), BF16),
+            jax.ShapeDtypeStruct(back, BF16),
+            jax.ShapeDtypeStruct(back, BF16),
             jax.ShapeDtypeStruct(a, BF16),
             jax.ShapeDtypeStruct(b, BF16),
             jax.ShapeDtypeStruct(a, F32),
             jax.ShapeDtypeStruct(b, F32),
         ),
         in_specs=[pl.BlockSpec(memory_space=pltpu.SMEM), hbm, vm, vm, hbm, hbm],
-        out_specs=(vm, hbm, hbm, hbm, hbm),
+        out_specs=(hbm,) * 6,
         scratch_shapes=[
             pltpu.VMEM(tokens.shape, BF16),
             pltpu.VMEM(wqkv.shape, BF16),
@@ -266,9 +271,10 @@
             pltpu.VMEM(b, BF16),
             pltpu.VMEM(a, F32),
             pltpu.VMEM(b, F32),
+            pltpu.VMEM((2,) + back, BF16),
             pltpu.SemaphoreType.DMA((frames // 2,)),
             pltpu.SemaphoreType.DMA((3 * width // CHUNK + 1,)),
-            pltpu.SemaphoreType.DMA((10,)),
+            pltpu.SemaphoreType.DMA((12,)),
         ],
         compiler_params=pltpu.CompilerParams(vmem_limit_bytes=63 * MIB),
         cost_estimate=pl.CostEstimate(flops=12 * 1024**3, bytes_accessed=20 * MIB, transcendentals=MIB),
@@ -277,52 +283,68 @@
 
 
 def message_kernel(place_ref, keep_ref, got_ref, back_ref, theirs_ref, own_ref, message_ref):
-    g = keep_ref[0] + got_ref[0].astype(F32)
-    message_ref[0, :, :1536] = g.astype(BF16)
-    message_ref[0, :32, 1536:] = back_ref[0, 0]
-    message_ref[0, 32:, 1536:] = theirs_ref[0]
-
-    @pl.when(pl.program_id(0) == place_ref[2])
-    def _():
-        own_ref[...] = g
-
-
-def run_message(place, keep, got, back, theirs):
-    lanes = back.shape[3]
-    rows = pl.BlockSpec((1, 64, 1536), lambda k, place: (k, 0, 0))
+    message_ref[:, :32, 1536:] = back_ref[...]
+    message_ref[:, 32:, 1536:] = theirs_ref[...]
+    for i in range(4):
+        g = keep_ref[i] + got_ref[i].astype(F32)
+        message_ref[i, :, :1536] = g.astype(BF16)
+
+        @pl.when(pl.program_id(0) * 4 + i == place_ref[2])
+        def _():
+            own_ref[...] = g
+
+
+def step_call(kernel, name, in_blocks, outs):
+    def spec(shape):
+        if len(shape) == 2:
+            return pl.BlockSpec(shape, lambda k, place: (0, 0))
+        return pl.BlockSpec((4,) + shape[1:], lambda k, place: (k, 0, 0))
+
     return pl.pallas_call(
-        message_kernel,
+        kernel,
         grid_spec=pltpu.PrefetchScalarGridSpec(
             num_scalar_prefetch=1,
-            grid=(8,),
-            in_specs=[
-                rows,
-                rows,
-                pl.BlockSpec((1, 1, 32, lanes), lambda k, place: (0, k, 0, 0)),
-                pl.BlockSpec((1, 32, lanes), lambda k, place: (k, 0, 0)),
-            ],
-            out_specs=(
-                pl.BlockSpec((64, 1536), lambda k, place: (0, 0)),
-                pl.BlockSpec((1, 64, 1536 + lanes), lambda k, place: (k, 0, 0)),
-            ),
+            grid=(2,),
+            in_specs=[spec(shape) for shape in in_blocks],
+            out_specs=tuple(spec(shape) for shape, _ in outs),
         ),
-        out_shape=(
-            jax.ShapeDtypeStruct((64, 1536), F32),
-            jax.ShapeDtypeStruct((8, 64, 1536 + lanes), BF16),
-        ),
+        out_shape=tuple(jax.ShapeDtypeStruct(shape, dtype) for shape, dtype in outs),
         compiler_params=pltpu.CompilerParams(vmem_limit_bytes=63 * MIB),
         cost_estimate=pl.CostEstimate(flops=MIB, bytes_accessed=9 * MIB, transcendentals=0),
-        name="message",
-    )(place, keep, got, back, theirs)
+        name=name,
+    )
+
+
+def run_message(place, keep, got, back, theirs):
+    ins = [keep.shape, got.shape, back.shape, theirs.shape]
+    outs = [((64, 1536), F32), ((8, 64, 1536 + back.shape[2]), BF16)]
+    return step_call(message_kernel, "message", ins, outs)(place, keep, got, back, theirs)
+
+
+def sum_kernel(place_ref, keep_ref, t1, t2, t3, own_ref, total_ref):
+    for i in range(4):
+        g = keep_ref[i] + t1[i].astype(F32) + t2[i].astype(F32) + t3[i].astype(F32)
+        total_ref[i] = g.astype(BF16)
+
+        @pl.when(pl.program_id(0) * 4 + i == place_ref[2])
+        def _():
+            own_ref[...] = g
+
+
+def run_sum(place, keep, got):
+    ins = [keep.shape] * 4
+    outs = [(keep.shape[1:], F32), (keep.shape, BF16)]
+    return step_call(sum_kernel, "sum_b", ins, outs)(place, keep, *got)
 
 
 def unpack_kernel(place_ref, message_ref, out_ref):
-    clips, _, width = out_ref.shape
-    for which in range(2):
-        at = pl.multiple_of((which + place_ref[1]) % 2 * 16, 16)
-        for c in range(clips):
-            row = which * 32 + c * 16
-            out_ref[c, pl.ds(at, 16), :] = message_ref[0, row:row + 16, 1536:1536 + width]
+    clips, rows, width = out_ref.shape
+    for i in range(rows // 32):
+        for which in range(2):
+            at = pl.multiple_of(i * 32 + (which + place_ref[1]) % 2 * 16, 16)
+            for c in range(clips):
+                row = which * 32 + c * 16
+                out_ref[c, pl.ds(at, 16), :] = message_ref[i, row:row + 16, 1536:1536 + width]
 
 
 def run_unpack(place, message, clips, width):
@@ -330,14 +352,37 @@
         unpack_kernel,
         grid_spec=pltpu.PrefetchScalarGridSpec(
             num_scalar_prefetch=1,
-            grid=(8,),
-            in_specs=[pl.BlockSpec((1,) + message.shape[1:], lambda k, place: (k, 0, 0))],
-            out_specs=pl.BlockSpec((clips, 32, width), lambda k, place: (0, k, 0)),
+            grid=(2,),
+            in_specs=[pl.BlockSpec((4,) + message.shape[1:], lambda k, place: (k, 0, 0))],
+            out_specs=pl.BlockSpec((clips, 128, width), lambda k, place: (0, k, 0)),
         ),
         out_shape=jax.ShapeDtypeStruct((clips, 256, width), BF16),
         compiler_params=pltpu.CompilerParams(vmem_limit_bytes=63 * MIB),
         name="unpack",
     )(place, message)
+
+
+def pack_kernel(video_ref, cot_ref, out_ref):
+    clips = video_ref.shape[0]
+    for d in range(4):
+        rows = slice(d * 16, d * 16 + 16)
+        for c in range(clips):
+            out_ref[d, c] = video_ref[c, 0, rows]
+            out_ref[d, clips + c] = cot_ref[c, 0, rows]
+
+
+def run_pack(video, cotangent):
+    clips, _, positions, width = video.shape
+    block = pl.BlockSpec((clips, 1, positions // 4, width), lambda k: (0, 0, k, 0))
+    return pl.pallas_call(
+        pack_kernel,
+        grid=(4,),
+        in_specs=[block, block],
+        out_specs=pl.BlockSpec((4, 2 * clips, 16, width), lambda k: (k, 0, 0, 0)),
+        out_shape=jax.ShapeDtypeStruct((16, 2 * clips, 16, width), BF16),
+        compiler_params=pltpu.CompilerParams(vmem_limit_bytes=63 * MIB),
+        name="pack",
+    )(video, cotangent)
 
 
 def place_kernel(scale, place_ref, d0, d1, d2, d3, qkv_ref, out_ref, gain_ref, bias_ref):
@@ -436,14 +481,15 @@
     place = jnp.stack([dp // 4, core, yz]).astype(jnp.int32)
     gain = norm_gain.reshape(1, width)
     bias = norm_bias.reshape(1, width)
-    tokens = jnp.concatenate([video, cotangent], axis=0).reshape(2 * clips, 16, positions // 16, width)
-    tokens = lax.all_to_all(tokens.transpose(1, 0, 2, 3), "frame", 0, 0, tiled=True)
-
-    back, send_a, send_b, keep_a, keep_b = run_main(place, tokens, gain, bias, qkv_weight, out_weight)
+    tokens = lax.all_to_all(run_pack(video, cotangent), "frame", 0, 0, tiled=True)
+    back, theirs, send_a, send_b, keep_a, keep_b = run_main(
+        place, tokens, gain, bias, qkv_weight, out_weight
+    )
 
     got_a = go_core(send_a)
-    theirs = go_core(back[1])
+    theirs = go_core(theirs)
     got_b = go_core(send_b)
+    got_a, got_b = lax.optimization_barrier((got_a, got_b))
     own_a, message = run_message(place, keep_a, got_a, back, theirs)
     message = trade_yz(message)
     terms_b = [keep_b[0] + got_b[0].astype(F32)]
@@ -451,15 +497,15 @@
     got_b = exchange(terms_b, go_x)
     message, got_b = lax.optimization_barrier((message, got_b))
 
-    b = combine(terms_b[0], got_b)
-    got_b = trade_yz(b.astype(BF16))
+    own_b, total_b = run_sum(place, terms_b[0], got_b)
+    got_b = trade_yz(total_b)
     a = reduce_yz(own_a, message[:, :, :1536], yz)
     terms_a = [a[:, k * 384 : (k + 1) * 384] for k in range(4)]
     got_a = exchange([t.astype(BF16) for t in terms_a], go_x)
     message, got_a, got_b = lax.optimization_barrier((message, got_a, got_b))
 
     a = combine(terms_a[0], got_a)
-    b = reduce_yz(pick(b, yz), got_b, yz)
+    b = reduce_yz(own_b, got_b, yz)
     small = jnp.sum(message[:, :, 1536 + width :].astype(F32), axis=(0, 1)).reshape(1, 128)
     own = jnp.concatenate([b, a, three_terms(small)], axis=1)
     own = combine(own, exchange([own.astype(BF16)] * 4, go_h))

time: 193 us -> 188 us (0.974)
  waiting for transfers between devices: 80.1 us -> 92 us
  local copies, waits for them, and re-layouts: 6.61 us -> 0.86 us
  other arithmetic: 14.3 us -> 8.98 us
  starting transfers between devices: 41.1 us -> 36.5 us
    ppermute x9, waiting for transfers between devices: 34.8 us -> 45.8 us  [go_x(): return lax.ppermute(a, 'dp', dp_pairs(lambda x, h: (x + k, h)))]
    convert_element_type x2 -> x0, other arithmetic: 8.2 us -> none  [the longest x1 4.59 us: local(): got_b = trade_yz(b.astype(BF16))]
    ppermute x9, starting transfers between devices: 14.4 us -> 8.9 us  [go_x(): return lax.ppermute(a, 'dp', dp_pairs(lambda x, h: (x + k, h)))]
    add x0 -> x1, other arithmetic: none -> 5.11 us  [local(): terms_b = [keep_b[0] + got_b[0].astype(F32)]]
    pallas_call x1, Pallas kernels: 6.19 us -> 3.27 us  [run_unpack(): pl.pallas_call(unpack_kernel, grid_spec=pltpu.PrefetchScalarGridSpec(num_...]
    pallas_call x2 -> x4, Pallas kernels: 40.4 us -> 43 us  [the longest x1 31.1 us: run_main(): pl.pallas_call(main_kernel, out_shape=(jax.ShapeDtypeStruct(back, BF16),...]
  transfers between devices with their start and end apart: 18 -> 18, of which waited for: 12 -> 14; matrix products, arithmetic and copies ran while one was open for 4% -> 4% of each run, Pallas kernels for 3% -> 2%
where the time goes in v8:
time: 188 us
  waiting for transfers between devices  92 us (49%)
  Pallas kernels  48.6 us (26%)
  starting transfers between devices  36.5 us (19%)
  other arithmetic  8.98 us (5%)
    ppermute x9, waiting for transfers between devices, go_x(): return lax.ppermute(a, 'dp', dp_pairs(lambda x, h: (x + k, h)))  45.8 us
    pallas_call x1, Pallas kernels, run_main(): pl.pallas_call(main_kernel, out_shape=(jax.ShapeDtypeStruct(back, BF16),...  31.1 us
    all_to_all x1, waiting for transfers between devices, local(): lax.all_to_all(run_pack(video, cotangent), 'frame', 0, 0, tiled=True)  26.1 us
    all_to_all x2, starting transfers between devices, trade_yz(): lax.all_to_all(a, 'frame', 0, 0, tiled=True, axis_index_groups=groups)  11.5 us
    ppermute x3, waiting for transfers between devices, go_h(): return lax.ppermute(a, 'dp', dp_pairs(lambda x, h: (x, h + k)))  10.9 us
    ppermute x3, starting transfers between devices, go_h(): return lax.ppermute(a, 'dp', dp_pairs(lambda x, h: (x, h + k)))  9.29 us
    ppermute x9, starting transfers between devices, go_x(): return lax.ppermute(a, 'dp', dp_pairs(lambda x, h: (x + k, h)))  8.9 us
    ppermute x3, waiting for transfers between devices, go_core(): return lax.ppermute(a, 'frame', frame_pairs(lambda y, z, c: (y, z, c + 1)))  7.72 us
  transfers between devices with their start and end apart: 18, of which 14 were waited for; matrix products, arithmetic and copies ran while one was open for 4% of the time, Pallas kernels for 2%

profile of v8, /device:TPU:32, one launch (start us, length us, event | category | flops | bytes accessed | tf_op | source)
XLA Modules:
  0.0 187.7 jit_solution(10835895973643257286)
XLA Ops:
  0.6 3.8 %pack.1 = bf16[16,4,16,1024]{3,2,1,0:T(8,128)(2,1)} custom-call(bf16[2,1,256,1024]{3,2,1,0:T(8,128)(2,1)} %video_ref.1, bf16[2,1,256,1024]{3,2,1,0:T(8,128)(2,1)} %cot_ref.1), custom_call_target="tpu_custom_call" | custom-call | tf_op jit(solution)/shard_map/pack/pallas_call | solution.py:377
  4.4 6.0 %all-to-all-start = ((bf16[16,4,16,1024]{3,2,1,0:T(8,128)(2,1)}), bf16[16,4,16,1024]{3,2,1,0:T(8,128)(2,1)}, u32[]{:S(2)}, u32[]{:S(2)}) async-start(bf16[16,4,16,1024]{3,2,1,0:T(8,128)(2,1)} %pack.1), calls=%async_computation | async-start | bytes 4194304 | tf_op jit(solution)/shard_map/all_to_all | solution.py:484
  10.4 0.7 pad_add_fusion.place_ref
  11.1 26.1 %all-to-all-done.tokens_hbm = bf16[16,4,16,1024]{3,2,1,0:T(8,128)(2,1)} async-done(((bf16[16,4,16,1024]{3,2,1,0:T(8,128)(2,1)}), bf16[16,4,16,1024]{3,2,1,0:T(8,128)(2,1)}, u32[]{:S(2)}, u32[]{:S(2)}) %all-to-all-start) | async-done | bytes 2097184 | tf_op jit(solution)/shard_map/all_to_all | solution.py:484
  37.2 31.1 %sublayer.1 = (bf16[8,32,1152]{2,1,0:T(8,128)(2,1)}, bf16[8,32,1152]{2,1,0:T(8,128)(2,1)}, bf16[8,64,1536]{2,1,0:T(8,128)(2,1)}, bf16[4,8,64,640]{3,2,1,0:T(8,12...) custom-call(s32[3]{0:T(128)} %pad_add_fusion.place_ref, bf16[16,4,16,1024]{3,2,1,0:T(8,128)(2,1)} %all-to-all-done.tokens_hbm, ...), custom_call_target="tpu_custom_call" | custom-call | flops 12884901888 | bytes 20971520 | tf_op jit(solution)/shard_map/sublayer/pallas_call | solution.py:246
  68.3 0.2 collective-permute-start.1
  68.5 0.4 collective-permute-start
  68.9 0.1 collective-permute-start.2
  69.0 7.7 %collective-permute-done.got_ref = bf16[8,64,1536]{2,1,0:T(8,128)(2,1)} collective-permute-done((bf16[8,64,1536]{2,1,0:T(8,128)(2,1)}, bf16[8,64,1536]{2,1,0:T(8,128)(2,1)}, u32[]{:S(2)}, u32[]{:S(2)}) %collective-permute-start) | collective-permute-done | bytes 1572896 | tf_op jit(solution)/shard_map/ppermute | solution.py:434
  76.7 0.8 copy-done.2
  77.5 4.7 %message.1 = (f32[64,1536]{1,0:T(8,128)}, bf16[8,64,2688]{2,1,0:T(8,128)(2,1)}) custom-call(s32[3]{0:T(128)} %pad_add_fusion.place_ref, f32[8,64,1536]{2,1,0:T(8,128)} %get-tuple-element.39.keep_ref, bf16[8,64,1536]{2,1,0:T(8,128)(2,1)} %collective-permute-done.got_ref, bf16[8,32,1152]{2,1,0:T(8,128)(2,1)} %get-tuple-element.41.back_ref, ...), custom_call_target="tpu_custom_call" | custom-call | flops 1048576 | bytes 9437184 | tf_op jit(solution)/shard_map/message/pallas_call | solution.py:321
  82.2 5.7 %all-to-all-start.1 = ((bf16[8,64,2688]{2,1,0:T(8,128)(2,1)}), bf16[8,64,2688]{2,1,0:T(8,128)(2,1)}, u32[]{:S(2)}, u32[]{:S(2)}) async-start(bf16[8,64,2688]{2,1,0:T(8,128)(2,1)} %get-tuple-element.43), calls=%async_computation.1 | async-start | bytes 5505024 | tf_op jit(solution)/shard_map/all_to_all | solution.py:439
  87.9 5.1 %add_bitcast_fusion = (f32[8,64,640]{2,1,0:T(8,128)}, bf16[8,64,640]{2,1,0:T(8,128)(2,1)S(1)}, bf16[8,64,640]{2,1,0:T(8,128)(2,1)S(1)}, bf16[8,64,640]{2,1,0:T(8,128)(2,1)S(1)}) fusion(f32[4,8,64,640]{3,2,1,0:T(8,128)} %get-tuple-element.35, bf16[4,8,64,640]{3,2,1,0:T(8,128)(2,1)} %collective-permute-done.1), kind=kLoop, calls=%fused_computation.5 | loop fusion | flops 3604480 | bytes 11141120 | tf_op jit(solution)/shard_map/add | solution.py:495
  93.0 2.6 %collective-permute-start.5 = (bf16[8,64,640]{2,1,0:T(8,128)(2,1)S(1)}, bf16[8,64,640]{2,1,0:T(8,128)(2,1)S(1)}, u32[]{:S(2)}, u32[]{:S(2)}) collective-permute-start(bf16[8,64,640]{2,1,0:T(8,128)(2,1)S(1)} %get-tuple-element.71), channel_id=1, source_target_pairs={{0,192},{16,208},{32,224},{48,240},{64,0},{80,16},{96,32},{112,48}... | collective-permute-start | bytes 1966088 | tf_op jit(solution)/shard_map/ppermute | solution.py:443
  95.6 0.8 collective-permute-start.4
  96.5 0.9 collective-permute-start.3
  97.3 26.4 %collective-permute-done.5.t3 = bf16[8,64,640]{2,1,0:T(8,128)(2,1)S(1)} collective-permute-done((bf16[8,64,640]{2,1,0:T(8,128)(2,1)S(1)}, bf16[8,64,640]{2,1,0:T(8,128)(2,1)S(1)}, u32[]{:S(2)}, u32[]{:S(2)}) %collective-permute-start.5) | collective-permute-done | bytes 655392 | tf_op jit(solution)/shard_map/ppermute | solution.py:443
  123.7 0.0 collective-permute-done.4.t2
  123.7 3.8 %collective-permute-done.3.t1 = bf16[8,64,640]{2,1,0:T(8,128)(2,1)} collective-permute-done((bf16[8,64,640]{2,1,0:T(8,128)(2,1)S(1)}, bf16[8,64,640]{2,1,0:T(8,128)(2,1)}, u32[]{:S(2)}, u32[]{:S(2)}) %collective-permute-start.3) | collective-permute-done | bytes 655392 | tf_op jit(solution)/shard_map/ppermute | solution.py:443
  127.5 0.0 all-to-all-done.1.message_ref
  127.5 3.5 %sum_b.1 = (f32[64,640]{1,0:T(8,128)}, bf16[8,64,640]{2,1,0:T(8,128)(2,1)}) custom-call(s32[3]{0:T(128)} %pad_add_fusion.place_ref, f32[8,64,640]{2,1,0:T(8,128)} %get-tuple-element.70.keep_ref, bf16[8,64,640]{2,1,0:T(8,128)(2,1)} %collective-permute-done.3.t1, bf16[8,64,640]{2,1,0:T(8,128)(2,1)} %collective-permute-done.4.t2, bf16[8,64,640]{2,1,0:T(8,128)(2,1)} %copy-done.1), custom_call_target="tpu_custom_call" | custom-call | flops 1048576 | bytes 9437184 | tf_op jit(solution)/shard_map/sum_b/pallas_call | solution.py:337
  131.0 5.9 %all-to-all-start.2 = ((bf16[8,64,640]{2,1,0:T(8,128)(2,1)}), bf16[8,64,640]{2,1,0:T(8,128)(2,1)S(1)}, u32[]{:S(2)}, u32[]{:S(2)}) async-start(bf16[8,64,640]{2,1,0:T(8,128)(2,1)} %get-tuple-element.50), calls=%async_computation.2 | async-start | bytes 1310720 | tf_op jit(solution)/shard_map/all_to_all | solution.py:439
  136.9 0.0 copy-start.6
  136.9 1.9 select_reduce_fusion
  138.8 0.8 collective-permute-start.8
  139.6 0.7 collective-permute-start.7
  140.3 0.8 collective-permute-start.6
  141.1 1.9 collective-permute-done.8
  143.0 2.7 %collective-permute-done.7 = bf16[64,384]{1,0:T(8,128)(2,1)S(1)} collective-permute-done((bf16[64,384]{1,0:T(8,128)(2,1)S(1)}, bf16[64,384]{1,0:T(8,128)(2,1)S(1)}, u32[]{:S(2)}, u32[]{:S(2)}) %collective-permute-start.7) | collective-permute-done | bytes 49184 | tf_op jit(solution)/shard_map/ppermute | solution.py:443
  145.7 0.3 collective-permute-done.6
  146.0 1.4 all-to-all-done.2
  147.4 1.0 convert_reduce_fusion
  148.4 0.2 select_reduce_fusion.1
  148.7 5.5 %collective-permute-start.11 = (bf16[64,1152]{1,0:T(8,128)(2,1)S(1)}, bf16[64,1152]{1,0:T(8,128)(2,1)S(1)}, u32[]{:S(2)}, u32[]{:S(2)}) collective-permute-start(bf16[64,1152]{1,0:T(8,128)(2,1)S(1)} %fusion.3), channel_id=1, source_target_pairs={{0,48},{16,0},{32,16},{48,32},{64,112},{80,64},{96,80},{112,96},{1... | collective-permute-start | bytes 442376 | tf_op jit(solution)/shard_map/ppermute | solution.py:447
  154.1 1.4 collective-permute-start.10
  155.6 2.4 %collective-permute-start.9 = (bf16[64,1152]{1,0:T(8,128)(2,1)S(1)}, bf16[64,1152]{1,0:T(8,128)(2,1)S(1)}, u32[]{:S(2)}, u32[]{:S(2)}) collective-permute-start(bf16[64,1152]{1,0:T(8,128)(2,1)S(1)} %fusion.3), channel_id=1, source_target_pairs={{0,16},{16,32},{32,48},{48,0},{64,80},{80,96},{96,112},{112,64},{1... | collective-permute-start | bytes 442376 | tf_op jit(solution)/shard_map/ppermute | solution.py:447
  158.0 4.7 %collective-permute-done.11 = bf16[64,1152]{1,0:T(8,128)(2,1)S(1)} collective-permute-done((bf16[64,1152]{1,0:T(8,128)(2,1)S(1)}, bf16[64,1152]{1,0:T(8,128)(2,1)S(1)}, u32[]{:S(2)}, u32[]{:S(2)}) %collective-permute-start.11) | collective-permute-done | bytes 147488 | tf_op jit(solution)/shard_map/ppermute | solution.py:447
  162.7 5.1 %collective-permute-done.10 = bf16[64,1152]{1,0:T(8,128)(2,1)S(1)} collective-permute-done((bf16[64,1152]{1,0:T(8,128)(2,1)S(1)}, bf16[64,1152]{1,0:T(8,128)(2,1)S(1)}, u32[]{:S(2)}, u32[]{:S(2)}) %collective-permute-start.10) | collective-permute-done | bytes 147488 | tf_op jit(solution)/shard_map/ppermute | solution.py:447
  167.7 1.1 collective-permute-done.9
  168.9 0.1 convert_add_fusion.d0
  169.0 0.1 collective-permute-start.14
  169.0 0.9 collective-permute-start.13
  169.9 1.3 collective-permute-start.12
  171.3 3.3 %unpack.1 = bf16[2,256,1024]{2,1,0:T(8,128)(2,1)} custom-call(s32[3]{0:T(128)} %pad_add_fusion.place_ref, bf16[8,64,2688]{2,1,0:T(8,128)(2,1)} %all-to-all-done.1.message_ref), custom_call_target="tpu_custom_call" | custom-call | tf_op jit(solution)/shard_map/unpack/pallas_call | solution.py:351
  174.5 4.4 %collective-permute-done.14.d3 = f32[64,1152]{1,0:T(8,128)S(1)} collective-permute-done((f32[64,1152]{1,0:T(8,128)S(1)}, f32[64,1152]{1,0:T(8,128)S(1)}, u32[]{:S(2)}, u32[]{:S(2)}) %collective-permute-start.14) | collective-permute-done | bytes 294944 | tf_op jit(solution)/shard_map/ppermute | solution.py:443
  179.0 1.6 collective-permute-done.13.d2
  180.6 4.7 %collective-permute-done.12.d1 = f32[64,1152]{1,0:T(8,128)} collective-permute-done((f32[64,1152]{1,0:T(8,128)S(1)}, f32[64,1152]{1,0:T(8,128)}, u32[]{:S(2)}, u32[]{:S(2)}) %collective-permute-start.12) | collective-permute-done | bytes 294944 | tf_op jit(solution)/shard_map/ppermute | solution.py:443
  185.4 2.3 %place_grads.1 = (f32[64,3072]{1,0:T(8,128)}, f32[64,1024]{1,0:T(8,128)}, f32[1,64]{1,0:T(1,128)}, f32[1,64]{1,0:T(1,128)}) custom-call(s32[3]{0:T(128)} %pad_add_fusion.place_ref, f32[64,1152]{1,0:T(8,128)} %copy-done, f32[64,1152]{1,0:T(8,128)} %collective-permute-done.12.d1, f32[64,1152]{1,0:T(8,128)} %copy-done.5, f32[64,1152]{1,0:T(8,128)} %copy-done.4), custom_call_target="tpu_custom_call" | custom-call | tf_op jit(solution)/shard_map/place_grads/pallas_call | solution.py:403
  (21 shorter events, 0.1 us)
Async XLA Ops:
  4.4 32.8 %all-to-all-start = ((bf16[16,4,16,1024]{3,2,1,0:T(8,128)(2,1)}), bf16[16,4,16,1024]{3,2,1,0:T(8,128)(2,1)}, u32[]{:S(2)}, u32[]{:S(2)}) async-start(bf16[16,4,16,1024]{3,2,1,0:T(8,128)(2,1)} %pack.1), calls=%async_computation | async-start | bytes 4194304 | tf_op jit(solution)/shard_map/all_to_all | solution.py:484
  68.3 8.4 %collective-permute-start.1 = (bf16[4,8,64,640]{3,2,1,0:T(8,128)(2,1)}, bf16[4,8,64,640]{3,2,1,0:T(8,128)(2,1)}, u32[]{:S(2)}, u32[]{:S(2)}) collective-permute-start(bf16[4,8,64,640]{3,2,1,0:T(8,128)(2,1)} %get-tuple-element.37), channel_id=1, source_target_pairs={{0,1},{1,0},{2,3},{3,2},{4,5},{5,4},{6,7},{7,6},{8,9},{9,8},{10,11... | collective-permute-start | bytes 7864328 | tf_op jit(solution)/shard_map/ppermute | solution.py:434
  68.5 8.2 %collective-permute-start = (bf16[8,64,1536]{2,1,0:T(8,128)(2,1)}, bf16[8,64,1536]{2,1,0:T(8,128)(2,1)}, u32[]{:S(2)}, u32[]{:S(2)}) collective-permute-start(bf16[8,64,1536]{2,1,0:T(8,128)(2,1)} %get-tuple-element.36), channel_id=1, source_target_pairs={{0,1},{1,0},{2,3},{3,2},{4,5},{5,4},{6,7},{7,6},{8,9},{9,8},{10,11... | collective-permute-start | bytes 4718600 | tf_op jit(solution)/shard_map/ppermute | solution.py:434
  68.9 7.8 %collective-permute-start.2 = (bf16[8,32,1152]{2,1,0:T(8,128)(2,1)}, bf16[8,32,1152]{2,1,0:T(8,128)(2,1)S(1)}, u32[]{:S(2)}, u32[]{:S(2)}) collective-permute-start(bf16[8,32,1152]{2,1,0:T(8,128)(2,1)} %get-tuple-element.42), channel_id=1, source_target_pairs={{0,1},{1,0},{2,3},{3,2},{4,5},{5,4},{6,7},{7,6},{8,9},{9,8},{10,11... | collective-permute-start | bytes 1769480 | tf_op jit(solution)/shard_map/ppermute | solution.py:434
  76.7 0.8 copy-start.2
  82.2 45.3 %all-to-all-start.1 = ((bf16[8,64,2688]{2,1,0:T(8,128)(2,1)}), bf16[8,64,2688]{2,1,0:T(8,128)(2,1)}, u32[]{:S(2)}, u32[]{:S(2)}) async-start(bf16[8,64,2688]{2,1,0:T(8,128)(2,1)} %get-tuple-element.43), calls=%async_computation.1 | async-start | bytes 5505024 | tf_op jit(solution)/shard_map/all_to_all | solution.py:439
  93.0 30.7 %collective-permute-start.5 = (bf16[8,64,640]{2,1,0:T(8,128)(2,1)S(1)}, bf16[8,64,640]{2,1,0:T(8,128)(2,1)S(1)}, u32[]{:S(2)}, u32[]{:S(2)}) collective-permute-start(bf16[8,64,640]{2,1,0:T(8,128)(2,1)S(1)} %get-tuple-element.71), channel_id=1, source_target_pairs={{0,192},{16,208},{32,224},{48,240},{64,0},{80,16},{96,32},{112,48}... | collective-permute-start | bytes 1966088 | tf_op jit(solution)/shard_map/ppermute | solution.py:443
  95.6 28.1 %collective-permute-start.4 = (bf16[8,64,640]{2,1,0:T(8,128)(2,1)S(1)}, bf16[8,64,640]{2,1,0:T(8,128)(2,1)}, u32[]{:S(2)}, u32[]{:S(2)}) collective-permute-start(bf16[8,64,640]{2,1,0:T(8,128)(2,1)S(1)} %get-tuple-element.72), channel_id=1, source_target_pairs={{0,128},{16,144},{32,160},{48,176},{64,192},{80,208},{96,224},{112... | collective-permute-start | bytes 1966088 | tf_op jit(solution)/shard_map/ppermute | solution.py:443
  96.5 31.1 %collective-permute-start.3 = (bf16[8,64,640]{2,1,0:T(8,128)(2,1)S(1)}, bf16[8,64,640]{2,1,0:T(8,128)(2,1)}, u32[]{:S(2)}, u32[]{:S(2)}) collective-permute-start(bf16[8,64,640]{2,1,0:T(8,128)(2,1)S(1)} %get-tuple-element.73), channel_id=1, source_target_pairs={{0,64},{16,80},{32,96},{48,112},{64,128},{80,144},{96,160},{112,17... | collective-permute-start | bytes 1966088 | tf_op jit(solution)/shard_map/ppermute | solution.py:443
  123.7 3.8 %copy-start.1 = (bf16[8,64,640]{2,1,0:T(8,128)(2,1)}, bf16[8,64,640]{2,1,0:T(8,128)(2,1)S(1)}, u32[]{:S(2)}) copy-start(bf16[8,64,640]{2,1,0:T(8,128)(2,1)S(1)} %collective-permute-done.5.t3) | copy-start | bytes 1966084
  131.0 5.9 %copy-start.3 = (f32[64,1536]{1,0:T(8,128)S(1)}, f32[64,1536]{1,0:T(8,128)}, u32[]{:S(2)}) copy-start(f32[64,1536]{1,0:T(8,128)} %get-tuple-element.49) | copy-start | bytes 1179652
  131.0 16.4 %all-to-all-start.2 = ((bf16[8,64,640]{2,1,0:T(8,128)(2,1)}), bf16[8,64,640]{2,1,0:T(8,128)(2,1)S(1)}, u32[]{:S(2)}, u32[]{:S(2)}) async-start(bf16[8,64,640]{2,1,0:T(8,128)(2,1)} %get-tuple-element.50), calls=%async_computation.2 | async-start | bytes 1310720 | tf_op jit(solution)/shard_map/all_to_all | solution.py:439
  136.9 11.5 %copy-start.6 = (f32[64,640]{1,0:T(8,128)S(1)}, f32[64,640]{1,0:T(8,128)}, u32[]{:S(2)}) copy-start(f32[64,640]{1,0:T(8,128)} %get-tuple-element.47) | copy-start | bytes 491524
  138.8 4.2 %collective-permute-start.8 = (bf16[64,384]{1,0:T(8,128)(2,1)S(1)}, bf16[64,384]{1,0:T(8,128)(2,1)S(1)}, u32[]{:S(2)}, u32[]{:S(2)}) collective-permute-start(bf16[64,384]{1,0:T(8,128)(2,1)S(1)} %get-tuple-element.74), channel_id=1, source_target_pairs={{0,192},{16,208},{32,224},{48,240},{64,0},{80,16},{96,32},{112,48}... | collective-permute-start | bytes 147464 | tf_op jit(solution)/shard_map/ppermute | solution.py:443
  139.6 6.1 %collective-permute-start.7 = (bf16[64,384]{1,0:T(8,128)(2,1)S(1)}, bf16[64,384]{1,0:T(8,128)(2,1)S(1)}, u32[]{:S(2)}, u32[]{:S(2)}) collective-permute-start(bf16[64,384]{1,0:T(8,128)(2,1)S(1)} %get-tuple-element.75), channel_id=1, source_target_pairs={{0,128},{16,144},{32,160},{48,176},{64,192},{80,208},{96,224},{112... | collective-permute-start | bytes 147464 | tf_op jit(solution)/shard_map/ppermute | solution.py:443
  140.3 5.6 %collective-permute-start.6 = (bf16[64,384]{1,0:T(8,128)(2,1)S(1)}, bf16[64,384]{1,0:T(8,128)(2,1)S(1)}, u32[]{:S(2)}, u32[]{:S(2)}) collective-permute-start(bf16[64,384]{1,0:T(8,128)(2,1)S(1)} %get-tuple-element.76), channel_id=1, source_target_pairs={{0,64},{16,80},{32,96},{48,112},{64,128},{80,144},{96,160},{112,17... | collective-permute-start | bytes 147464 | tf_op jit(solution)/shard_map/ppermute | solution.py:443
  148.7 14.0 %collective-permute-start.11 = (bf16[64,1152]{1,0:T(8,128)(2,1)S(1)}, bf16[64,1152]{1,0:T(8,128)(2,1)S(1)}, u32[]{:S(2)}, u32[]{:S(2)}) collective-permute-start(bf16[64,1152]{1,0:T(8,128)(2,1)S(1)} %fusion.3), channel_id=1, source_target_pairs={{0,48},{16,0},{32,16},{48,32},{64,112},{80,64},{96,80},{112,96},{1... | collective-permute-start | bytes 442376 | tf_op jit(solution)/shard_map/ppermute | solution.py:447
  154.1 13.6 %collective-permute-start.10 = (bf16[64,1152]{1,0:T(8,128)(2,1)S(1)}, bf16[64,1152]{1,0:T(8,128)(2,1)S(1)}, u32[]{:S(2)}, u32[]{:S(2)}) collective-permute-start(bf16[64,1152]{1,0:T(8,128)(2,1)S(1)} %fusion.3), channel_id=1, source_target_pairs={{0,32},{16,48},{32,0},{48,16},{64,96},{80,112},{96,64},{112,80},{1... | collective-permute-start | bytes 442376 | tf_op jit(solution)/shard_map/ppermute | solution.py:447
  155.6 13.3 %collective-permute-start.9 = (bf16[64,1152]{1,0:T(8,128)(2,1)S(1)}, bf16[64,1152]{1,0:T(8,128)(2,1)S(1)}, u32[]{:S(2)}, u32[]{:S(2)}) collective-permute-start(bf16[64,1152]{1,0:T(8,128)(2,1)S(1)} %fusion.3), channel_id=1, source_target_pairs={{0,16},{16,32},{32,48},{48,0},{64,80},{80,96},{96,112},{112,64},{1... | collective-permute-start | bytes 442376 | tf_op jit(solution)/shard_map/ppermute | solution.py:447
  168.9 5.6 %copy-start = (f32[64,1152]{1,0:T(8,128)}, f32[64,1152]{1,0:T(8,128)S(1)}, u32[]{:S(2)}) copy-start(f32[64,1152]{1,0:T(8,128)S(1)} %convert_add_fusion.d0) | copy-start | bytes 884740
  169.0 10.0 %collective-permute-start.14 = (f32[64,1152]{1,0:T(8,128)S(1)}, f32[64,1152]{1,0:T(8,128)S(1)}, u32[]{:S(2)}, u32[]{:S(2)}) collective-permute-start(f32[64,1152]{1,0:T(8,128)S(1)} %convert_add_fusion.d0), channel_id=1, source_target_pairs={{0,192},{16,208},{32,224},{48,240},{64,0},{80,16},{96,32},{112,48}... | collective-permute-start | bytes 884744 | tf_op jit(solution)/shard_map/ppermute | solution.py:443
  169.0 11.6 %collective-permute-start.13 = (f32[64,1152]{1,0:T(8,128)S(1)}, f32[64,1152]{1,0:T(8,128)S(1)}, u32[]{:S(2)}, u32[]{:S(2)}) collective-permute-start(f32[64,1152]{1,0:T(8,128)S(1)} %convert_add_fusion.d0), channel_id=1, source_target_pairs={{0,128},{16,144},{32,160},{48,176},{64,192},{80,208},{96,224},{112... | collective-permute-start | bytes 884744 | tf_op jit(solution)/shard_map/ppermute | solution.py:443
  169.9 15.4 %collective-permute-start.12 = (f32[64,1152]{1,0:T(8,128)S(1)}, f32[64,1152]{1,0:T(8,128)}, u32[]{:S(2)}, u32[]{:S(2)}) collective-permute-start(f32[64,1152]{1,0:T(8,128)S(1)} %convert_add_fusion.d0), channel_id=1, source_target_pairs={{0,64},{16,80},{32,96},{48,112},{64,128},{80,144},{96,160},{112,17... | collective-permute-start | bytes 884744 | tf_op jit(solution)/shard_map/ppermute | solution.py:443
  179.0 6.4 %copy-start.4 = (f32[64,1152]{1,0:T(8,128)}, f32[64,1152]{1,0:T(8,128)S(1)}, u32[]{:S(2)}) copy-start(f32[64,1152]{1,0:T(8,128)S(1)} %collective-permute-done.14.d3) | copy-start | bytes 884740
  180.6 4.7 %copy-start.5 = (f32[64,1152]{1,0:T(8,128)}, f32[64,1152]{1,0:T(8,128)S(1)}, u32[]{:S(2)}) copy-start(f32[64,1152]{1,0:T(8,128)S(1)} %collective-permute-done.13.d2) | copy-start | bytes 884740

commit v9 on v8

--- a/solution.py
+++ b/solution.py
@@ -362,27 +362,53 @@
     )(place, message)
 
 
-def pack_kernel(video_ref, cot_ref, out_ref):
+def pack_kernel(video_ref, cot_ref, out_ref, sems):
     clips = video_ref.shape[0]
-    for d in range(4):
-        rows = slice(d * 16, d * 16 + 16)
-        for c in range(clips):
-            out_ref[d, c] = video_ref[c, 0, rows]
-            out_ref[d, clips + c] = cot_ref[c, 0, rows]
+    copies = []
+    for c in range(clips):
+        copies.append(pltpu.make_async_copy(video_ref.at[c], out_ref.at[:, c], sems.at[2 * c]))
+        copies.append(pltpu.make_async_copy(cot_ref.at[c], out_ref.at[:, clips + c], sems.at[2 * c + 1]))
+    for copy in copies:
+        copy.start()
+    for copy in copies:
+        copy.wait()
 
 
 def run_pack(video, cotangent):
     clips, _, positions, width = video.shape
-    block = pl.BlockSpec((clips, 1, positions // 4, width), lambda k: (0, 0, k, 0))
+    shape = (clips, 16, positions // 16, width)
+    hbm = pl.BlockSpec(memory_space=pl.ANY)
     return pl.pallas_call(
         pack_kernel,
-        grid=(4,),
-        in_specs=[block, block],
-        out_specs=pl.BlockSpec((4, 2 * clips, 16, width), lambda k: (k, 0, 0, 0)),
-        out_shape=jax.ShapeDtypeStruct((16, 2 * clips, 16, width), BF16),
+        in_specs=[hbm, hbm],
+        out_specs=hbm,
+        out_shape=jax.ShapeDtypeStruct((16, 2 * clips, positions // 16, width), BF16),
+        scratch_shapes=[pltpu.SemaphoreType.DMA((2 * clips,))],
         compiler_params=pltpu.CompilerParams(vmem_limit_bytes=63 * MIB),
         name="pack",
-    )(video, cotangent)
+    )(video.reshape(shape), cotangent.reshape(shape))
+
+
+def terms_kernel(keep_ref, got_ref, own_ref, *term_refs):
+    own_ref[...] = keep_ref[0] + got_ref[0].astype(F32)
+    for i, term_ref in enumerate(term_refs):
+        term_ref[...] = (keep_ref[i + 1] + got_ref[i + 1].astype(F32)).astype(BF16)
+
+
+def run_terms(keep, got):
+    shape = keep.shape[1:]
+    ins = pl.BlockSpec((4, 2) + shape[1:], lambda k: (0, k, 0, 0))
+    out = pl.BlockSpec((2,) + shape[1:], lambda k: (k, 0, 0))
+    return pl.pallas_call(
+        terms_kernel,
+        grid=(4,),
+        in_specs=[ins, ins],
+        out_specs=(out,) * 4,
+        out_shape=tuple(jax.ShapeDtypeStruct(shape, dtype) for dtype in (F32, BF16, BF16, BF16)),
+        compiler_params=pltpu.CompilerParams(vmem_limit_bytes=63 * MIB),
+        cost_estimate=pl.CostEstimate(flops=MIB, bytes_accessed=11 * MIB, transcendentals=0),
+        name="terms_b",
+    )(keep, got)
 
 
 def place_kernel(scale, place_ref, d0, d1, d2, d3, qkv_ref, out_ref, gain_ref, bias_ref):
@@ -487,13 +513,12 @@
     )
 
     got_a = go_core(send_a)
-    theirs = go_core(theirs)
+    got_a, theirs, send_b = lax.optimization_barrier((got_a, go_core(theirs), send_b))
     got_b = go_core(send_b)
-    got_a, got_b = lax.optimization_barrier((got_a, got_b))
     own_a, message = run_message(place, keep_a, got_a, back, theirs)
+    terms_b = run_terms(keep_b, got_b)
+    message, terms_b = lax.optimization_barrier((message, terms_b))
     message = trade_yz(message)
-    terms_b = [keep_b[0] + got_b[0].astype(F32)]
-    terms_b += [(keep_b[k] + got_b[k].astype(F32)).astype(BF16) for k in range(1, 4)]
     got_b = exchange(terms_b, go_x)
     message, got_b = lax.optimization_barrier((message, got_b))
 

time: 188 us -> 245 us (1.30)
  Pallas kernels: 48.6 us -> 115 us
  waiting for transfers between devices: 92 us -> 84.1 us
  other arithmetic: 8.98 us -> 3.9 us
  starting transfers between devices: 36.5 us -> 40.9 us
    pallas_call x1 -> x2, Pallas kernels: 3.77 us -> 69.9 us  [the longest x1 64.7 us: run_pack(): pl.pallas_call(pack_kernel, in_specs=[hbm, hbm], out_specs=hbm, out_shape...]
    ppermute x9, starting transfers between devices: 8.9 us -> 14.1 us  [go_x(): return lax.ppermute(a, 'dp', dp_pairs(lambda x, h: (x + k, h)))]
    add x1 -> x0, other arithmetic: 5.11 us -> none  [local(): terms_b = [keep_b[0] + got_b[0].astype(F32)]]
    ppermute x3, waiting for transfers between devices: 7.72 us -> 4.18 us  [go_core(): return lax.ppermute(a, 'frame', frame_pairs(lambda y, z, c: (y, z, c + 1)))]
    ppermute x9, waiting for transfers between devices: 45.8 us -> 43 us  [go_x(): return lax.ppermute(a, 'dp', dp_pairs(lambda x, h: (x + k, h)))]
  transfers between devices with their start and end apart: 18 -> 18, of which waited for: 14 -> 15; matrix products, arithmetic and copies ran while one was open for 4% -> 1% of each run, Pallas kernels for 2% -> 3%
where the time goes in v9:
time: 245 us
  Pallas kernels  115 us (47%)
  waiting for transfers between devices  84.1 us (34%)
  starting transfers between devices  40.9 us (17%)
  other arithmetic  3.9 us (2%)
    pallas_call x1, Pallas kernels, run_pack(): pl.pallas_call(pack_kernel, in_specs=[hbm, hbm], out_specs=hbm, out_shape...  64.7 us
    ppermute x9, waiting for transfers between devices, go_x(): return lax.ppermute(a, 'dp', dp_pairs(lambda x, h: (x + k, h)))  43 us
    pallas_call x1, Pallas kernels, run_main(): pl.pallas_call(main_kernel, out_shape=(jax.ShapeDtypeStruct(back, BF16),...  31.1 us
    all_to_all x1, waiting for transfers between devices, local(): lax.all_to_all(run_pack(video, cotangent), 'frame', 0, 0, tiled=True)  26.1 us
    ppermute x9, starting transfers between devices, go_x(): return lax.ppermute(a, 'dp', dp_pairs(lambda x, h: (x + k, h)))  14.1 us
    all_to_all x2, starting transfers between devices, trade_yz(): lax.all_to_all(a, 'frame', 0, 0, tiled=True, axis_index_groups=groups)  10.9 us
    ppermute x3, waiting for transfers between devices, go_h(): return lax.ppermute(a, 'dp', dp_pairs(lambda x, h: (x, h + k)))  9.91 us
    ppermute x3, starting transfers between devices, go_h(): return lax.ppermute(a, 'dp', dp_pairs(lambda x, h: (x, h + k)))  9.12 us
  transfers between devices with their start and end apart: 18, of which 15 were waited for; matrix products, arithmetic and copies ran while one was open for 1% of the time, Pallas kernels for 3%

profile of v9, /device:TPU:32, one launch (start us, length us, event | category | flops | bytes accessed | tf_op | source)
XLA Modules:
  0.0 244.7 jit_solution(8564163917057800877)
XLA Ops:
  0.6 64.7 %pack.1 = bf16[16,4,16,1024]{3,2,1,0:T(8,128)(2,1)} custom-call(bf16[2,16,16,1024]{3,2,1,0:T(8,128)(2,1)} %bitcast.24, bf16[2,16,16,1024]{3,2,1,0:T(8,128)(2,1)} %bitcast.25), custom_call_target="tpu_custom_call" | custom-call | tf_op jit(solution)/shard_map/pack/pallas_call | solution.py:381
  65.3 6.0 %all-to-all-start = ((bf16[16,4,16,1024]{3,2,1,0:T(8,128)(2,1)}), bf16[16,4,16,1024]{3,2,1,0:T(8,128)(2,1)}, u32[]{:S(2)}, u32[]{:S(2)}) async-start(bf16[16,4,16,1024]{3,2,1,0:T(8,128)(2,1)} %pack.1), calls=%async_computation | async-start | bytes 4194304 | tf_op jit(solution)/shard_map/all_to_all | solution.py:510
  71.3 0.7 pad_add_fusion.place_ref
  72.0 26.1 %all-to-all-done.tokens_hbm = bf16[16,4,16,1024]{3,2,1,0:T(8,128)(2,1)} async-done(((bf16[16,4,16,1024]{3,2,1,0:T(8,128)(2,1)}), bf16[16,4,16,1024]{3,2,1,0:T(8,128)(2,1)}, u32[]{:S(2)}, u32[]{:S(2)}) %all-to-all-start) | async-done | bytes 2097184 | tf_op jit(solution)/shard_map/all_to_all | solution.py:510
  98.1 31.1 %sublayer.1 = (bf16[8,32,1152]{2,1,0:T(8,128)(2,1)}, bf16[8,32,1152]{2,1,0:T(8,128)(2,1)}, bf16[8,64,1536]{2,1,0:T(8,128)(2,1)}, bf16[4,8,64,640]{3,2,1,0:T(8,12...) custom-call(s32[3]{0:T(128)} %pad_add_fusion.place_ref, bf16[16,4,16,1024]{3,2,1,0:T(8,128)(2,1)} %all-to-all-done.tokens_hbm, ...), custom_call_target="tpu_custom_call" | custom-call | flops 12884901888 | bytes 20971520 | tf_op jit(solution)/shard_map/sublayer/pallas_call | solution.py:246
  129.2 0.2 collective-permute-start
  129.4 0.4 collective-permute-start.1
  129.8 3.7 %collective-permute-done.1.theirs_ref = bf16[8,32,1152]{2,1,0:T(8,128)(2,1)S(1)} collective-permute-done((bf16[8,32,1152]{2,1,0:T(8,128)(2,1)}, bf16[8,32,1152]{2,1,0:T(8,128)(2,1)S(1)}, u32[]{:S(2)}, u32[]{:S(2)}) %collective-permute-start.1) | collective-permute-done | bytes 589856 | tf_op jit(solution)/shard_map/ppermute | solution.py:460
  133.5 0.4 collective-permute-done.got_ref
  133.9 0.1 collective-permute-start.2
  134.0 0.3 copy-done.2
  134.3 4.7 %message.1 = (f32[64,1536]{1,0:T(8,128)}, bf16[8,64,2688]{2,1,0:T(8,128)(2,1)}) custom-call(s32[3]{0:T(128)} %pad_add_fusion.place_ref, f32[8,64,1536]{2,1,0:T(8,128)} %get-tuple-element.45.keep_ref, bf16[8,64,1536]{2,1,0:T(8,128)(2,1)} %collective-permute-done.got_ref, bf16[8,32,1152]{2,1,0:T(8,128)(2,1)} %get-tuple-element.50.back_ref, ...), custom_call_target="tpu_custom_call" | custom-call | flops 1048576 | bytes 9437184 | tf_op jit(solution)/shard_map/message/pallas_call | solution.py:321
  139.0 0.1 collective-permute-done.2.got_ref
  139.1 5.3 %terms_b.1 = (f32[8,64,640]{2,1,0:T(8,128)}, bf16[8,64,640]{2,1,0:T(8,128)(2,1)}, bf16[8,64,640]{2,1,0:T(8,128)(2,1)}, bf16[8,64,640]{2,1,0:T(8,128)(2,1)}) custom-call(f32[4,8,64,640]{3,2,1,0:T(8,128)} %get-tuple-element.53.keep_ref, bf16[4,8,64,640]{3,2,1,0:T(8,128)(2,1)} %collective-permute-done.2.got_ref), custom_call_target="tpu_custom_call" | custom-call | flops 1048576 | bytes 11534336 | tf_op jit(solution)/shard_map/terms_b/pallas_call | solution.py:402
  144.4 5.8 %all-to-all-start.1 = ((bf16[8,64,2688]{2,1,0:T(8,128)(2,1)}), bf16[8,64,2688]{2,1,0:T(8,128)(2,1)}, u32[]{:S(2)}, u32[]{:S(2)}) async-start(bf16[8,64,2688]{2,1,0:T(8,128)(2,1)} %get-tuple-element.60), calls=%async_computation.1 | async-start | bytes 5505024 | tf_op jit(solution)/shard_map/all_to_all | solution.py:465
  150.2 1.3 collective-permute-start.3
  151.6 2.7 %collective-permute-start.4 = (bf16[8,64,640]{2,1,0:T(8,128)(2,1)S(1)}, bf16[8,64,640]{2,1,0:T(8,128)(2,1)}, u32[]{:S(2)}, u32[]{:S(2)}) collective-permute-start(bf16[8,64,640]{2,1,0:T(8,128)(2,1)S(1)} %copy-done.7), channel_id=1, source_target_pairs={{0,128},{16,144},{32,160},{48,176},{64,192},{80,208},{96,224},{112... | collective-permute-start | bytes 1966088 | tf_op jit(solution)/shard_map/ppermute | solution.py:469
  154.3 1.4 collective-permute-start.5
  155.7 12.5 %collective-permute-done.3.t1 = bf16[8,64,640]{2,1,0:T(8,128)(2,1)S(1)} collective-permute-done((bf16[8,64,640]{2,1,0:T(8,128)(2,1)S(1)}, bf16[8,64,640]{2,1,0:T(8,128)(2,1)S(1)}, u32[]{:S(2)}, u32[]{:S(2)}) %collective-permute-start.3) | collective-permute-done | bytes 655392 | tf_op jit(solution)/shard_map/ppermute | solution.py:469
  168.3 14.7 %collective-permute-done.4.t2 = bf16[8,64,640]{2,1,0:T(8,128)(2,1)} collective-permute-done((bf16[8,64,640]{2,1,0:T(8,128)(2,1)S(1)}, bf16[8,64,640]{2,1,0:T(8,128)(2,1)}, u32[]{:S(2)}, u32[]{:S(2)}) %collective-permute-start.4) | collective-permute-done | bytes 655392 | tf_op jit(solution)/shard_map/ppermute | solution.py:469
  182.9 0.0 collective-permute-done.5.t3
  182.9 0.8 all-to-all-done.1.message_ref
  183.8 3.5 %sum_b.1 = (f32[64,640]{1,0:T(8,128)}, bf16[8,64,640]{2,1,0:T(8,128)(2,1)}) custom-call(s32[3]{0:T(128)} %pad_add_fusion.place_ref, f32[8,64,640]{2,1,0:T(8,128)} %get-tuple-element.59.keep_ref, bf16[8,64,640]{2,1,0:T(8,128)(2,1)} %copy-done.1, bf16[8,64,640]{2,1,0:T(8,128)(2,1)} %collective-permute-done.4.t2, bf16[8,64,640]{2,1,0:T(8,128)(2,1)} %collective-permute-done.5.t3), custom_call_target="tpu_custom_call" | custom-call | flops 1048576 | bytes 9437184 | tf_op jit(solution)/shard_map/sum_b/pallas_call | solution.py:337
  187.3 5.0 %all-to-all-start.2 = ((bf16[8,64,640]{2,1,0:T(8,128)(2,1)}), bf16[8,64,640]{2,1,0:T(8,128)(2,1)S(1)}, u32[]{:S(2)}, u32[]{:S(2)}) async-start(bf16[8,64,640]{2,1,0:T(8,128)(2,1)} %get-tuple-element.70), calls=%async_computation.2 | async-start | bytes 1310720 | tf_op jit(solution)/shard_map/all_to_all | solution.py:465
  192.3 1.9 select_reduce_fusion
  194.2 2.5 %collective-permute-start.8 = (bf16[64,384]{1,0:T(8,128)(2,1)S(1)}, bf16[64,384]{1,0:T(8,128)(2,1)S(1)}, u32[]{:S(2)}, u32[]{:S(2)}) collective-permute-start(bf16[64,384]{1,0:T(8,128)(2,1)S(1)} %get-tuple-element.90), channel_id=1, source_target_pairs={{0,192},{16,208},{32,224},{48,240},{64,0},{80,16},{96,32},{112,48}... | collective-permute-start | bytes 147464 | tf_op jit(solution)/shard_map/ppermute | solution.py:469
  196.8 1.1 collective-permute-start.7
  197.9 0.5 collective-permute-start.6
  198.4 0.4 collective-permute-done.8
  198.8 3.6 %collective-permute-done.7 = bf16[64,384]{1,0:T(8,128)(2,1)S(1)} collective-permute-done((bf16[64,384]{1,0:T(8,128)(2,1)S(1)}, bf16[64,384]{1,0:T(8,128)(2,1)S(1)}, u32[]{:S(2)}, u32[]{:S(2)}) %collective-permute-start.7) | collective-permute-done | bytes 49184 | tf_op jit(solution)/shard_map/ppermute | solution.py:469
  202.4 0.8 collective-permute-done.6
  203.2 0.0 all-to-all-done.2
  203.2 1.0 convert_reduce_fusion
  204.2 0.2 select_reduce_fusion.1
  204.5 5.3 %collective-permute-start.11 = (bf16[64,1152]{1,0:T(8,128)(2,1)S(1)}, bf16[64,1152]{1,0:T(8,128)(2,1)S(1)}, u32[]{:S(2)}, u32[]{:S(2)}) collective-permute-start(bf16[64,1152]{1,0:T(8,128)(2,1)S(1)} %fusion), channel_id=1, source_target_pairs={{0,48},{16,0},{32,16},{48,32},{64,112},{80,64},{96,80},{112,96},{1... | collective-permute-start | bytes 442376 | tf_op jit(solution)/shard_map/ppermute | solution.py:473
  209.8 1.4 collective-permute-start.10
  211.2 2.4 collective-permute-start.9
  213.6 3.4 %collective-permute-done.11 = bf16[64,1152]{1,0:T(8,128)(2,1)S(1)} collective-permute-done((bf16[64,1152]{1,0:T(8,128)(2,1)S(1)}, bf16[64,1152]{1,0:T(8,128)(2,1)S(1)}, u32[]{:S(2)}, u32[]{:S(2)}) %collective-permute-start.11) | collective-permute-done | bytes 147488 | tf_op jit(solution)/shard_map/ppermute | solution.py:473
  217.0 5.6 %collective-permute-done.10 = bf16[64,1152]{1,0:T(8,128)(2,1)S(1)} collective-permute-done((bf16[64,1152]{1,0:T(8,128)(2,1)S(1)}, bf16[64,1152]{1,0:T(8,128)(2,1)S(1)}, u32[]{:S(2)}, u32[]{:S(2)}) %collective-permute-start.10) | collective-permute-done | bytes 147488 | tf_op jit(solution)/shard_map/ppermute | solution.py:473
  222.7 0.9 collective-permute-done.9
  223.5 0.1 convert_add_fusion.d0
  223.6 3.1 %collective-permute-start.14 = (f32[64,1152]{1,0:T(8,128)S(1)}, f32[64,1152]{1,0:T(8,128)S(1)}, u32[]{:S(2)}, u32[]{:S(2)}) collective-permute-start(f32[64,1152]{1,0:T(8,128)S(1)} %convert_add_fusion.d0), channel_id=1, source_target_pairs={{0,192},{16,208},{32,224},{48,240},{64,0},{80,16},{96,32},{112,48}... | collective-permute-start | bytes 884744 | tf_op jit(solution)/shard_map/ppermute | solution.py:469
  226.7 0.3 collective-permute-start.13
  227.0 1.1 collective-permute-start.12
  228.1 3.3 %unpack.1 = bf16[2,256,1024]{2,1,0:T(8,128)(2,1)} custom-call(s32[3]{0:T(128)} %pad_add_fusion.place_ref, bf16[8,64,2688]{2,1,0:T(8,128)(2,1)} %all-to-all-done.1.message_ref), custom_call_target="tpu_custom_call" | custom-call | tf_op jit(solution)/shard_map/unpack/pallas_call | solution.py:351
  231.4 7.5 %collective-permute-done.14.d3 = f32[64,1152]{1,0:T(8,128)S(1)} collective-permute-done((f32[64,1152]{1,0:T(8,128)S(1)}, f32[64,1152]{1,0:T(8,128)S(1)}, u32[]{:S(2)}, u32[]{:S(2)}) %collective-permute-start.14) | collective-permute-done | bytes 294944 | tf_op jit(solution)/shard_map/ppermute | solution.py:469
  238.9 3.5 %collective-permute-done.12.d1 = f32[64,1152]{1,0:T(8,128)} collective-permute-done((f32[64,1152]{1,0:T(8,128)S(1)}, f32[64,1152]{1,0:T(8,128)}, u32[]{:S(2)}, u32[]{:S(2)}) %collective-permute-start.12) | collective-permute-done | bytes 294944 | tf_op jit(solution)/shard_map/ppermute | solution.py:469
  242.4 2.3 place_grads.1
  (25 shorter events, 0.1 us)
Async XLA Ops:
  65.3 32.8 %all-to-all-start = ((bf16[16,4,16,1024]{3,2,1,0:T(8,128)(2,1)}), bf16[16,4,16,1024]{3,2,1,0:T(8,128)(2,1)}, u32[]{:S(2)}, u32[]{:S(2)}) async-start(bf16[16,4,16,1024]{3,2,1,0:T(8,128)(2,1)} %pack.1), calls=%async_computation | async-start | bytes 4194304 | tf_op jit(solution)/shard_map/all_to_all | solution.py:510
  129.2 4.7 %collective-permute-start = (bf16[8,64,1536]{2,1,0:T(8,128)(2,1)}, bf16[8,64,1536]{2,1,0:T(8,128)(2,1)}, u32[]{:S(2)}, u32[]{:S(2)}) collective-permute-start(bf16[8,64,1536]{2,1,0:T(8,128)(2,1)} %get-tuple-element.46), channel_id=1, source_target_pairs={{0,1},{1,0},{2,3},{3,2},{4,5},{5,4},{6,7},{7,6},{8,9},{9,8},{10,11... | collective-permute-start | bytes 4718600 | tf_op jit(solution)/shard_map/ppermute | solution.py:460
  129.4 4.1 %collective-permute-start.1 = (bf16[8,32,1152]{2,1,0:T(8,128)(2,1)}, bf16[8,32,1152]{2,1,0:T(8,128)(2,1)S(1)}, u32[]{:S(2)}, u32[]{:S(2)}) collective-permute-start(bf16[8,32,1152]{2,1,0:T(8,128)(2,1)} %get-tuple-element.47), channel_id=1, source_target_pairs={{0,1},{1,0},{2,3},{3,2},{4,5},{5,4},{6,7},{7,6},{8,9},{9,8},{10,11... | collective-permute-start | bytes 1769480 | tf_op jit(solution)/shard_map/ppermute | solution.py:460
  133.5 0.8 copy-start.2
  133.9 5.3 %collective-permute-start.2 = (bf16[4,8,64,640]{3,2,1,0:T(8,128)(2,1)}, bf16[4,8,64,640]{3,2,1,0:T(8,128)(2,1)}, u32[]{:S(2)}, u32[]{:S(2)}) collective-permute-start(bf16[4,8,64,640]{3,2,1,0:T(8,128)(2,1)} %get-tuple-element.54), channel_id=1, source_target_pairs={{0,1},{1,0},{2,3},{3,2},{4,5},{5,4},{6,7},{7,6},{8,9},{9,8},{10,11... | collective-permute-start | bytes 7864328 | tf_op jit(solution)/shard_map/ppermute | solution.py:460
  144.4 5.8 %copy-start.8 = (bf16[8,64,640]{2,1,0:T(8,128)(2,1)S(1)}, bf16[8,64,640]{2,1,0:T(8,128)(2,1)}, u32[]{:S(2)}) copy-start(bf16[8,64,640]{2,1,0:T(8,128)(2,1)} %get-tuple-element.61) | copy-start | bytes 1966084
  144.4 7.2 %copy-start.7 = (bf16[8,64,640]{2,1,0:T(8,128)(2,1)S(1)}, bf16[8,64,640]{2,1,0:T(8,128)(2,1)}, u32[]{:S(2)}) copy-start(bf16[8,64,640]{2,1,0:T(8,128)(2,1)} %get-tuple-element.62) | copy-start | bytes 1966084
  144.4 9.9 %copy-start.6 = (bf16[8,64,640]{2,1,0:T(8,128)(2,1)S(1)}, bf16[8,64,640]{2,1,0:T(8,128)(2,1)}, u32[]{:S(2)}) copy-start(bf16[8,64,640]{2,1,0:T(8,128)(2,1)} %get-tuple-element.63) | copy-start | bytes 1966084
  144.4 39.4 %all-to-all-start.1 = ((bf16[8,64,2688]{2,1,0:T(8,128)(2,1)}), bf16[8,64,2688]{2,1,0:T(8,128)(2,1)}, u32[]{:S(2)}, u32[]{:S(2)}) async-start(bf16[8,64,2688]{2,1,0:T(8,128)(2,1)} %get-tuple-element.60), calls=%async_computation.1 | async-start | bytes 5505024 | tf_op jit(solution)/shard_map/all_to_all | solution.py:465
  150.2 18.0 %collective-permute-start.3 = (bf16[8,64,640]{2,1,0:T(8,128)(2,1)S(1)}, bf16[8,64,640]{2,1,0:T(8,128)(2,1)S(1)}, u32[]{:S(2)}, u32[]{:S(2)}) collective-permute-start(bf16[8,64,640]{2,1,0:T(8,128)(2,1)S(1)} %copy-done.8), channel_id=1, source_target_pairs={{0,64},{16,80},{32,96},{48,112},{64,128},{80,144},{96,160},{112,17... | collective-permute-start | bytes 1966088 | tf_op jit(solution)/shard_map/ppermute | solution.py:469
  151.6 31.4 %collective-permute-start.4 = (bf16[8,64,640]{2,1,0:T(8,128)(2,1)S(1)}, bf16[8,64,640]{2,1,0:T(8,128)(2,1)}, u32[]{:S(2)}, u32[]{:S(2)}) collective-permute-start(bf16[8,64,640]{2,1,0:T(8,128)(2,1)S(1)} %copy-done.7), channel_id=1, source_target_pairs={{0,128},{16,144},{32,160},{48,176},{64,192},{80,208},{96,224},{112... | collective-permute-start | bytes 1966088 | tf_op jit(solution)/shard_map/ppermute | solution.py:469
  154.3 28.6 %collective-permute-start.5 = (bf16[8,64,640]{2,1,0:T(8,128)(2,1)S(1)}, bf16[8,64,640]{2,1,0:T(8,128)(2,1)}, u32[]{:S(2)}, u32[]{:S(2)}) collective-permute-start(bf16[8,64,640]{2,1,0:T(8,128)(2,1)S(1)} %copy-done.6), channel_id=1, source_target_pairs={{0,192},{16,208},{32,224},{48,240},{64,0},{80,16},{96,32},{112,48}... | collective-permute-start | bytes 1966088 | tf_op jit(solution)/shard_map/ppermute | solution.py:469
  168.3 15.5 %copy-start.1 = (bf16[8,64,640]{2,1,0:T(8,128)(2,1)}, bf16[8,64,640]{2,1,0:T(8,128)(2,1)S(1)}, u32[]{:S(2)}) copy-start(bf16[8,64,640]{2,1,0:T(8,128)(2,1)S(1)} %collective-permute-done.3.t1) | copy-start | bytes 1966084
  187.3 17.0 %copy-start.5 = (f32[64,640]{1,0:T(8,128)S(1)}, f32[64,640]{1,0:T(8,128)}, u32[]{:S(2)}) copy-start(f32[64,640]{1,0:T(8,128)} %get-tuple-element.67) | copy-start | bytes 491524
  187.3 16.0 %all-to-all-start.2 = ((bf16[8,64,640]{2,1,0:T(8,128)(2,1)}), bf16[8,64,640]{2,1,0:T(8,128)(2,1)S(1)}, u32[]{:S(2)}, u32[]{:S(2)}) async-start(bf16[8,64,640]{2,1,0:T(8,128)(2,1)} %get-tuple-element.70), calls=%async_computation.2 | async-start | bytes 1310720 | tf_op jit(solution)/shard_map/all_to_all | solution.py:465
  194.2 4.6 %collective-permute-start.8 = (bf16[64,384]{1,0:T(8,128)(2,1)S(1)}, bf16[64,384]{1,0:T(8,128)(2,1)S(1)}, u32[]{:S(2)}, u32[]{:S(2)}) collective-permute-start(bf16[64,384]{1,0:T(8,128)(2,1)S(1)} %get-tuple-element.90), channel_id=1, source_target_pairs={{0,192},{16,208},{32,224},{48,240},{64,0},{80,16},{96,32},{112,48}... | collective-permute-start | bytes 147464 | tf_op jit(solution)/shard_map/ppermute | solution.py:469
  196.8 5.6 %collective-permute-start.7 = (bf16[64,384]{1,0:T(8,128)(2,1)S(1)}, bf16[64,384]{1,0:T(8,128)(2,1)S(1)}, u32[]{:S(2)}, u32[]{:S(2)}) collective-permute-start(bf16[64,384]{1,0:T(8,128)(2,1)S(1)} %get-tuple-element.91), channel_id=1, source_target_pairs={{0,128},{16,144},{32,160},{48,176},{64,192},{80,208},{96,224},{112... | collective-permute-start | bytes 147464 | tf_op jit(solution)/shard_map/ppermute | solution.py:469
  197.9 5.3 %collective-permute-start.6 = (bf16[64,384]{1,0:T(8,128)(2,1)S(1)}, bf16[64,384]{1,0:T(8,128)(2,1)S(1)}, u32[]{:S(2)}, u32[]{:S(2)}) collective-permute-start(bf16[64,384]{1,0:T(8,128)(2,1)S(1)} %get-tuple-element.92), channel_id=1, source_target_pairs={{0,64},{16,80},{32,96},{48,112},{64,128},{80,144},{96,160},{112,17... | collective-permute-start | bytes 147464 | tf_op jit(solution)/shard_map/ppermute | solution.py:469
  204.5 12.5 %collective-permute-start.11 = (bf16[64,1152]{1,0:T(8,128)(2,1)S(1)}, bf16[64,1152]{1,0:T(8,128)(2,1)S(1)}, u32[]{:S(2)}, u32[]{:S(2)}) collective-permute-start(bf16[64,1152]{1,0:T(8,128)(2,1)S(1)} %fusion), channel_id=1, source_target_pairs={{0,48},{16,0},{32,16},{48,32},{64,112},{80,64},{96,80},{112,96},{1... | collective-permute-start | bytes 442376 | tf_op jit(solution)/shard_map/ppermute | solution.py:473
  209.8 12.8 %collective-permute-start.10 = (bf16[64,1152]{1,0:T(8,128)(2,1)S(1)}, bf16[64,1152]{1,0:T(8,128)(2,1)S(1)}, u32[]{:S(2)}, u32[]{:S(2)}) collective-permute-start(bf16[64,1152]{1,0:T(8,128)(2,1)S(1)} %fusion), channel_id=1, source_target_pairs={{0,32},{16,48},{32,0},{48,16},{64,96},{80,112},{96,64},{112,80},{1... | collective-permute-start | bytes 442376 | tf_op jit(solution)/shard_map/ppermute | solution.py:473
  211.2 12.3 %collective-permute-start.9 = (bf16[64,1152]{1,0:T(8,128)(2,1)S(1)}, bf16[64,1152]{1,0:T(8,128)(2,1)S(1)}, u32[]{:S(2)}, u32[]{:S(2)}) collective-permute-start(bf16[64,1152]{1,0:T(8,128)(2,1)S(1)} %fusion), channel_id=1, source_target_pairs={{0,16},{16,32},{32,48},{48,0},{64,80},{80,96},{96,112},{112,64},{1... | collective-permute-start | bytes 442376 | tf_op jit(solution)/shard_map/ppermute | solution.py:473
  223.6 18.8 %copy-start = (f32[64,1152]{1,0:T(8,128)}, f32[64,1152]{1,0:T(8,128)S(1)}, u32[]{:S(2)}) copy-start(f32[64,1152]{1,0:T(8,128)S(1)} %convert_add_fusion.d0) | copy-start | bytes 884740
  223.6 15.3 %collective-permute-start.14 = (f32[64,1152]{1,0:T(8,128)S(1)}, f32[64,1152]{1,0:T(8,128)S(1)}, u32[]{:S(2)}, u32[]{:S(2)}) collective-permute-start(f32[64,1152]{1,0:T(8,128)S(1)} %convert_add_fusion.d0), channel_id=1, source_target_pairs={{0,192},{16,208},{32,224},{48,240},{64,0},{80,16},{96,32},{112,48}... | collective-permute-start | bytes 884744 | tf_op jit(solution)/shard_map/ppermute | solution.py:469
  226.7 12.2 %collective-permute-start.13 = (f32[64,1152]{1,0:T(8,128)S(1)}, f32[64,1152]{1,0:T(8,128)S(1)}, u32[]{:S(2)}, u32[]{:S(2)}) collective-permute-start(f32[64,1152]{1,0:T(8,128)S(1)} %convert_add_fusion.d0), channel_id=1, source_target_pairs={{0,128},{16,144},{32,160},{48,176},{64,192},{80,208},{96,224},{112... | collective-permute-start | bytes 884744 | tf_op jit(solution)/shard_map/ppermute | solution.py:469
  227.0 15.4 %collective-permute-start.12 = (f32[64,1152]{1,0:T(8,128)S(1)}, f32[64,1152]{1,0:T(8,128)}, u32[]{:S(2)}, u32[]{:S(2)}) collective-permute-start(f32[64,1152]{1,0:T(8,128)S(1)} %convert_add_fusion.d0), channel_id=1, source_target_pairs={{0,64},{16,80},{32,96},{48,112},{64,128},{80,144},{96,160},{112,17... | collective-permute-start | bytes 884744 | tf_op jit(solution)/shard_map/ppermute | solution.py:469
  238.9 3.5 %copy-start.3 = (f32[64,1152]{1,0:T(8,128)}, f32[64,1152]{1,0:T(8,128)S(1)}, u32[]{:S(2)}) copy-start(f32[64,1152]{1,0:T(8,128)S(1)} %collective-permute-done.14.d3) | copy-start | bytes 884740
  238.9 3.5 %copy-start.4 = (f32[64,1152]{1,0:T(8,128)}, f32[64,1152]{1,0:T(8,128)S(1)}, u32[]{:S(2)}) copy-start(f32[64,1152]{1,0:T(8,128)S(1)} %collective-permute-done.13.d2) | copy-start | bytes 884740

commit v10 on v9

--- a/solution.py
+++ b/solution.py
@@ -362,28 +362,32 @@
     )(place, message)
 
 
-def pack_kernel(video_ref, cot_ref, out_ref, sems):
+def pack_kernel(video_ref, cot_ref, out_ref, packed_s, sems):
     clips = video_ref.shape[0]
-    copies = []
+    loads = []
     for c in range(clips):
-        copies.append(pltpu.make_async_copy(video_ref.at[c], out_ref.at[:, c], sems.at[2 * c]))
-        copies.append(pltpu.make_async_copy(cot_ref.at[c], out_ref.at[:, clips + c], sems.at[2 * c + 1]))
-    for copy in copies:
-        copy.start()
-    for copy in copies:
-        copy.wait()
+        loads.append(pltpu.make_async_copy(video_ref.at[c], packed_s.at[:, c], sems.at[2 * c]))
+        loads.append(pltpu.make_async_copy(cot_ref.at[c], packed_s.at[:, clips + c], sems.at[2 * c + 1]))
+    for load in loads:
+        load.start()
+    for load in loads:
+        load.wait()
+    store = pltpu.make_async_copy(packed_s, out_ref, sems.at[2 * clips])
+    store.start()
+    store.wait()
 
 
 def run_pack(video, cotangent):
     clips, _, positions, width = video.shape
     shape = (clips, 16, positions // 16, width)
+    packed = (16, 2 * clips, positions // 16, width)
     hbm = pl.BlockSpec(memory_space=pl.ANY)
     return pl.pallas_call(
         pack_kernel,
         in_specs=[hbm, hbm],
         out_specs=hbm,
-        out_shape=jax.ShapeDtypeStruct((16, 2 * clips, positions // 16, width), BF16),
-        scratch_shapes=[pltpu.SemaphoreType.DMA((2 * clips,))],
+        out_shape=jax.ShapeDtypeStruct(packed, BF16),
+        scratch_shapes=[pltpu.VMEM(packed, BF16), pltpu.SemaphoreType.DMA((2 * clips + 1,))],
         compiler_params=pltpu.CompilerParams(vmem_limit_bytes=63 * MIB),
         name="pack",
     )(video.reshape(shape), cotangent.reshape(shape))
@@ -397,11 +401,11 @@
 
 def run_terms(keep, got):
     shape = keep.shape[1:]
-    ins = pl.BlockSpec((4, 2) + shape[1:], lambda k: (0, k, 0, 0))
-    out = pl.BlockSpec((2,) + shape[1:], lambda k: (k, 0, 0))
+    ins = pl.BlockSpec((4, 4) + shape[1:], lambda k: (0, k, 0, 0))
+    out = pl.BlockSpec((4,) + shape[1:], lambda k: (k, 0, 0))
     return pl.pallas_call(
         terms_kernel,
-        grid=(4,),
+        grid=(2,),
         in_specs=[ins, ins],
         out_specs=(out,) * 4,
         out_shape=tuple(jax.ShapeDtypeStruct(shape, dtype) for dtype in (F32, BF16, BF16, BF16)),

time: 245 us -> 183 us (0.75)
  Pallas kernels: 115 us -> 52.4 us
    pallas_call x1, Pallas kernels: 64.7 us -> 2.9 us  [run_pack(): pl.pallas_call(pack_kernel, in_specs=[hbm, hbm], out_specs=hbm, out_shape...]
  transfers between devices with their start and end apart: 18 -> 18, of which waited for: 15 -> 15; matrix products, arithmetic and copies ran while one was open for 1% -> 1% of each run, Pallas kernels for 3% -> 4%
where the time goes in v10:
time: 183 us; the launch traced here: 182 us
  waiting for transfers between devices  84.1 us (46%)
  Pallas kernels  52.4 us (29%)
  starting transfers between devices  40.9 us (22%)
  other arithmetic  3.9 us (2%)
    ppermute x9, waiting for transfers between devices, go_x(): return lax.ppermute(a, 'dp', dp_pairs(lambda x, h: (x + k, h)))  43 us
    pallas_call x1, Pallas kernels, run_main(): pl.pallas_call(main_kernel, out_shape=(jax.ShapeDtypeStruct(back, BF16),...  31.1 us
    all_to_all x1, waiting for transfers between devices, local(): lax.all_to_all(run_pack(video, cotangent), 'frame', 0, 0, tiled=True)  26.1 us
    ppermute x9, starting transfers between devices, go_x(): return lax.ppermute(a, 'dp', dp_pairs(lambda x, h: (x + k, h)))  14.1 us
    all_to_all x2, starting transfers between devices, trade_yz(): lax.all_to_all(a, 'frame', 0, 0, tiled=True, axis_index_groups=groups)  10.9 us
    ppermute x3, waiting for transfers between devices, go_h(): return lax.ppermute(a, 'dp', dp_pairs(lambda x, h: (x, h + k)))  9.91 us
    ppermute x3, starting transfers between devices, go_h(): return lax.ppermute(a, 'dp', dp_pairs(lambda x, h: (x, h + k)))  9.13 us
    all_to_all x1, starting transfers between devices, local(): lax.all_to_all(run_pack(video, cotangent), 'frame', 0, 0, tiled=True)  6.04 us
  transfers between devices with their start and end apart: 18, of which 15 were waited for; matrix products, arithmetic and copies ran while one was open for 1% of the time, Pallas kernels for 4%

profile of v10, /device:TPU:32, one launch (start us, length us, event | category | flops | bytes accessed | tf_op | source)
XLA Modules:
  0.0 182.3 jit_solution(6131433723866554422)
XLA Ops:
  0.6 2.9 %pack.1 = bf16[16,4,16,1024]{3,2,1,0:T(8,128)(2,1)} custom-call(bf16[2,16,16,1024]{3,2,1,0:T(8,128)(2,1)} %bitcast.24, bf16[2,16,16,1024]{3,2,1,0:T(8,128)(2,1)} %bitcast.25), custom_call_target="tpu_custom_call" | custom-call | tf_op jit(solution)/shard_map/pack/pallas_call | solution.py:385
  3.5 6.0 %all-to-all-start = ((bf16[16,4,16,1024]{3,2,1,0:T(8,128)(2,1)}), bf16[16,4,16,1024]{3,2,1,0:T(8,128)(2,1)}, u32[]{:S(2)}, u32[]{:S(2)}) async-start(bf16[16,4,16,1024]{3,2,1,0:T(8,128)(2,1)} %pack.1), calls=%async_computation | async-start | bytes 4194304 | tf_op jit(solution)/shard_map/all_to_all | solution.py:514
  9.6 0.7 pad_add_fusion.place_ref
  10.2 26.1 %all-to-all-done.tokens_hbm = bf16[16,4,16,1024]{3,2,1,0:T(8,128)(2,1)} async-done(((bf16[16,4,16,1024]{3,2,1,0:T(8,128)(2,1)}), bf16[16,4,16,1024]{3,2,1,0:T(8,128)(2,1)}, u32[]{:S(2)}, u32[]{:S(2)}) %all-to-all-start) | async-done | bytes 2097184 | tf_op jit(solution)/shard_map/all_to_all | solution.py:514
  36.4 31.1 %sublayer.1 = (bf16[8,32,1152]{2,1,0:T(8,128)(2,1)}, bf16[8,32,1152]{2,1,0:T(8,128)(2,1)}, bf16[8,64,1536]{2,1,0:T(8,128)(2,1)}, bf16[4,8,64,640]{3,2,1,0:T(8,12...) custom-call(s32[3]{0:T(128)} %pad_add_fusion.place_ref, bf16[16,4,16,1024]{3,2,1,0:T(8,128)(2,1)} %all-to-all-done.tokens_hbm, ...), custom_call_target="tpu_custom_call" | custom-call | flops 12884901888 | bytes 20971520 | tf_op jit(solution)/shard_map/sublayer/pallas_call | solution.py:246
  67.4 0.2 collective-permute-start
  67.6 0.4 collective-permute-start.1
  68.0 3.7 %collective-permute-done.1.theirs_ref = bf16[8,32,1152]{2,1,0:T(8,128)(2,1)S(1)} collective-permute-done((bf16[8,32,1152]{2,1,0:T(8,128)(2,1)}, bf16[8,32,1152]{2,1,0:T(8,128)(2,1)S(1)}, u32[]{:S(2)}, u32[]{:S(2)}) %collective-permute-start.1) | collective-permute-done | bytes 589856 | tf_op jit(solution)/shard_map/ppermute | solution.py:464
  71.7 0.4 collective-permute-done.got_ref
  72.1 0.1 collective-permute-start.2
  72.3 0.3 copy-done.2
  72.5 4.7 %message.1 = (f32[64,1536]{1,0:T(8,128)}, bf16[8,64,2688]{2,1,0:T(8,128)(2,1)}) custom-call(s32[3]{0:T(128)} %pad_add_fusion.place_ref, f32[8,64,1536]{2,1,0:T(8,128)} %get-tuple-element.45.keep_ref, bf16[8,64,1536]{2,1,0:T(8,128)(2,1)} %collective-permute-done.got_ref, bf16[8,32,1152]{2,1,0:T(8,128)(2,1)} %get-tuple-element.50.back_ref, ...), custom_call_target="tpu_custom_call" | custom-call | flops 1048576 | bytes 9437184 | tf_op jit(solution)/shard_map/message/pallas_call | solution.py:321
  77.2 0.1 collective-permute-done.2.got_ref
  77.4 4.6 %terms_b.1 = (f32[8,64,640]{2,1,0:T(8,128)}, bf16[8,64,640]{2,1,0:T(8,128)(2,1)}, bf16[8,64,640]{2,1,0:T(8,128)(2,1)}, bf16[8,64,640]{2,1,0:T(8,128)(2,1)}) custom-call(f32[4,8,64,640]{3,2,1,0:T(8,128)} %get-tuple-element.53.keep_ref, bf16[4,8,64,640]{3,2,1,0:T(8,128)(2,1)} %collective-permute-done.2.got_ref), custom_call_target="tpu_custom_call" | custom-call | flops 1048576 | bytes 11534336 | tf_op jit(solution)/shard_map/terms_b/pallas_call | solution.py:406
  82.0 5.8 %all-to-all-start.1 = ((bf16[8,64,2688]{2,1,0:T(8,128)(2,1)}), bf16[8,64,2688]{2,1,0:T(8,128)(2,1)}, u32[]{:S(2)}, u32[]{:S(2)}) async-start(bf16[8,64,2688]{2,1,0:T(8,128)(2,1)} %get-tuple-element.60), calls=%async_computation.1 | async-start | bytes 5505024 | tf_op jit(solution)/shard_map/all_to_all | solution.py:469
  87.8 1.3 collective-permute-start.3
  89.2 2.7 %collective-permute-start.4 = (bf16[8,64,640]{2,1,0:T(8,128)(2,1)S(1)}, bf16[8,64,640]{2,1,0:T(8,128)(2,1)}, u32[]{:S(2)}, u32[]{:S(2)}) collective-permute-start(bf16[8,64,640]{2,1,0:T(8,128)(2,1)S(1)} %copy-done.7), channel_id=1, source_target_pairs={{0,128},{16,144},{32,160},{48,176},{64,192},{80,208},{96,224},{112... | collective-permute-start | bytes 1966088 | tf_op jit(solution)/shard_map/ppermute | solution.py:473
  91.9 1.4 collective-permute-start.5
  93.3 12.5 %collective-permute-done.3.t1 = bf16[8,64,640]{2,1,0:T(8,128)(2,1)S(1)} collective-permute-done((bf16[8,64,640]{2,1,0:T(8,128)(2,1)S(1)}, bf16[8,64,640]{2,1,0:T(8,128)(2,1)S(1)}, u32[]{:S(2)}, u32[]{:S(2)}) %collective-permute-start.3) | collective-permute-done | bytes 655392 | tf_op jit(solution)/shard_map/ppermute | solution.py:473
  105.9 14.7 %collective-permute-done.4.t2 = bf16[8,64,640]{2,1,0:T(8,128)(2,1)} collective-permute-done((bf16[8,64,640]{2,1,0:T(8,128)(2,1)S(1)}, bf16[8,64,640]{2,1,0:T(8,128)(2,1)}, u32[]{:S(2)}, u32[]{:S(2)}) %collective-permute-start.4) | collective-permute-done | bytes 655392 | tf_op jit(solution)/shard_map/ppermute | solution.py:473
  120.5 0.0 collective-permute-done.5.t3
  120.5 0.8 all-to-all-done.1.message_ref
  121.4 3.5 %sum_b.1 = (f32[64,640]{1,0:T(8,128)}, bf16[8,64,640]{2,1,0:T(8,128)(2,1)}) custom-call(s32[3]{0:T(128)} %pad_add_fusion.place_ref, f32[8,64,640]{2,1,0:T(8,128)} %get-tuple-element.59.keep_ref, bf16[8,64,640]{2,1,0:T(8,128)(2,1)} %copy-done.1, bf16[8,64,640]{2,1,0:T(8,128)(2,1)} %collective-permute-done.4.t2, bf16[8,64,640]{2,1,0:T(8,128)(2,1)} %collective-permute-done.5.t3), custom_call_target="tpu_custom_call" | custom-call | flops 1048576 | bytes 9437184 | tf_op jit(solution)/shard_map/sum_b/pallas_call | solution.py:337
  124.9 5.0 %all-to-all-start.2 = ((bf16[8,64,640]{2,1,0:T(8,128)(2,1)}), bf16[8,64,640]{2,1,0:T(8,128)(2,1)S(1)}, u32[]{:S(2)}, u32[]{:S(2)}) async-start(bf16[8,64,640]{2,1,0:T(8,128)(2,1)} %get-tuple-element.70), calls=%async_computation.2 | async-start | bytes 1310720 | tf_op jit(solution)/shard_map/all_to_all | solution.py:469
  129.9 1.9 %select_reduce_fusion = f32[64,1536]{1,0:T(8,128)S(1)} fusion(bf16[8,64,2688]{2,1,0:T(8,128)(2,1)} %all-to-all-done.1.message_ref, f32[64,1536]{1,0:T(8,128)} %get-tuple-element.69, pred[8]{0:T(512)(128)(4,1)S(1)} %iota_compare_fusion.1), kind=kLoop, calls=%fused_computation | loop fusion | flops 2260992 | bytes 2359304 | tf_op jit(solution)/shard_map/reduce_sum | solution.py:496
  131.9 2.5 %collective-permute-start.8 = (bf16[64,384]{1,0:T(8,128)(2,1)S(1)}, bf16[64,384]{1,0:T(8,128)(2,1)S(1)}, u32[]{:S(2)}, u32[]{:S(2)}) collective-permute-start(bf16[64,384]{1,0:T(8,128)(2,1)S(1)} %get-tuple-element.90), channel_id=1, source_target_pairs={{0,192},{16,208},{32,224},{48,240},{64,0},{80,16},{96,32},{112,48}... | collective-permute-start | bytes 147464 | tf_op jit(solution)/shard_map/ppermute | solution.py:473
  134.4 1.1 collective-permute-start.7
  135.5 0.5 collective-permute-start.6
  136.0 0.4 collective-permute-done.8
  136.4 3.6 %collective-permute-done.7 = bf16[64,384]{1,0:T(8,128)(2,1)S(1)} collective-permute-done((bf16[64,384]{1,0:T(8,128)(2,1)S(1)}, bf16[64,384]{1,0:T(8,128)(2,1)S(1)}, u32[]{:S(2)}, u32[]{:S(2)}) %collective-permute-start.7) | collective-permute-done | bytes 49184 | tf_op jit(solution)/shard_map/ppermute | solution.py:473
  140.0 0.8 collective-permute-done.6
  140.8 1.0 convert_reduce_fusion
  141.8 0.2 select_reduce_fusion.1
  142.1 5.3 %collective-permute-start.11 = (bf16[64,1152]{1,0:T(8,128)(2,1)S(1)}, bf16[64,1152]{1,0:T(8,128)(2,1)S(1)}, u32[]{:S(2)}, u32[]{:S(2)}) collective-permute-start(bf16[64,1152]{1,0:T(8,128)(2,1)S(1)} %fusion), channel_id=1, source_target_pairs={{0,48},{16,0},{32,16},{48,32},{64,112},{80,64},{96,80},{112,96},{1... | collective-permute-start | bytes 442376 | tf_op jit(solution)/shard_map/ppermute | solution.py:477
  147.4 1.4 collective-permute-start.10
  148.9 2.4 %collective-permute-start.9 = (bf16[64,1152]{1,0:T(8,128)(2,1)S(1)}, bf16[64,1152]{1,0:T(8,128)(2,1)S(1)}, u32[]{:S(2)}, u32[]{:S(2)}) collective-permute-start(bf16[64,1152]{1,0:T(8,128)(2,1)S(1)} %fusion), channel_id=1, source_target_pairs={{0,16},{16,32},{32,48},{48,0},{64,80},{80,96},{96,112},{112,64},{1... | collective-permute-start | bytes 442376 | tf_op jit(solution)/shard_map/ppermute | solution.py:477
  151.2 3.4 %collective-permute-done.11 = bf16[64,1152]{1,0:T(8,128)(2,1)S(1)} collective-permute-done((bf16[64,1152]{1,0:T(8,128)(2,1)S(1)}, bf16[64,1152]{1,0:T(8,128)(2,1)S(1)}, u32[]{:S(2)}, u32[]{:S(2)}) %collective-permute-start.11) | collective-permute-done | bytes 147488 | tf_op jit(solution)/shard_map/ppermute | solution.py:477
  154.6 5.6 %collective-permute-done.10 = bf16[64,1152]{1,0:T(8,128)(2,1)S(1)} collective-permute-done((bf16[64,1152]{1,0:T(8,128)(2,1)S(1)}, bf16[64,1152]{1,0:T(8,128)(2,1)S(1)}, u32[]{:S(2)}, u32[]{:S(2)}) %collective-permute-start.10) | collective-permute-done | bytes 147488 | tf_op jit(solution)/shard_map/ppermute | solution.py:477
  160.3 0.9 collective-permute-done.9
  161.1 0.1 convert_add_fusion.d0
  161.2 3.1 %collective-permute-start.14 = (f32[64,1152]{1,0:T(8,128)S(1)}, f32[64,1152]{1,0:T(8,128)S(1)}, u32[]{:S(2)}, u32[]{:S(2)}) collective-permute-start(f32[64,1152]{1,0:T(8,128)S(1)} %convert_add_fusion.d0), channel_id=1, source_target_pairs={{0,192},{16,208},{32,224},{48,240},{64,0},{80,16},{96,32},{112,48}... | collective-permute-start | bytes 884744 | tf_op jit(solution)/shard_map/ppermute | solution.py:473
  164.3 0.3 collective-permute-start.13
  164.6 1.1 collective-permute-start.12
  165.7 3.3 %unpack.1 = bf16[2,256,1024]{2,1,0:T(8,128)(2,1)} custom-call(s32[3]{0:T(128)} %pad_add_fusion.place_ref, bf16[8,64,2688]{2,1,0:T(8,128)(2,1)} %all-to-all-done.1.message_ref), custom_call_target="tpu_custom_call" | custom-call | tf_op jit(solution)/shard_map/unpack/pallas_call | solution.py:351
  169.0 7.5 %collective-permute-done.14.d3 = f32[64,1152]{1,0:T(8,128)S(1)} collective-permute-done((f32[64,1152]{1,0:T(8,128)S(1)}, f32[64,1152]{1,0:T(8,128)S(1)}, u32[]{:S(2)}, u32[]{:S(2)}) %collective-permute-start.14) | collective-permute-done | bytes 294944 | tf_op jit(solution)/shard_map/ppermute | solution.py:473
  176.5 0.0 collective-permute-done.13.d2
  176.5 3.5 %collective-permute-done.12.d1 = f32[64,1152]{1,0:T(8,128)} collective-permute-done((f32[64,1152]{1,0:T(8,128)S(1)}, f32[64,1152]{1,0:T(8,128)}, u32[]{:S(2)}, u32[]{:S(2)}) %collective-permute-start.12) | collective-permute-done | bytes 294944 | tf_op jit(solution)/shard_map/ppermute | solution.py:473
  180.0 2.3 %place_grads.1 = (f32[64,3072]{1,0:T(8,128)}, f32[64,1024]{1,0:T(8,128)}, f32[1,64]{1,0:T(1,128)}, f32[1,64]{1,0:T(1,128)}) custom-call(s32[3]{0:T(128)} %pad_add_fusion.place_ref, f32[64,1152]{1,0:T(8,128)} %copy-done, f32[64,1152]{1,0:T(8,128)} %collective-permute-done.12.d1, f32[64,1152]{1,0:T(8,128)} %copy-done.4, f32[64,1152]{1,0:T(8,128)} %copy-done.3), custom_call_target="tpu_custom_call" | custom-call | tf_op jit(solution)/shard_map/place_grads/pallas_call | solution.py:433
  (25 shorter events, 0.1 us)
Async XLA Ops:
  3.5 32.8 %all-to-all-start = ((bf16[16,4,16,1024]{3,2,1,0:T(8,128)(2,1)}), bf16[16,4,16,1024]{3,2,1,0:T(8,128)(2,1)}, u32[]{:S(2)}, u32[]{:S(2)}) async-start(bf16[16,4,16,1024]{3,2,1,0:T(8,128)(2,1)} %pack.1), calls=%async_computation | async-start | bytes 4194304 | tf_op jit(solution)/shard_map/all_to_all | solution.py:514
  67.4 4.7 %collective-permute-start = (bf16[8,64,1536]{2,1,0:T(8,128)(2,1)}, bf16[8,64,1536]{2,1,0:T(8,128)(2,1)}, u32[]{:S(2)}, u32[]{:S(2)}) collective-permute-start(bf16[8,64,1536]{2,1,0:T(8,128)(2,1)} %get-tuple-element.46), channel_id=1, source_target_pairs={{0,1},{1,0},{2,3},{3,2},{4,5},{5,4},{6,7},{7,6},{8,9},{9,8},{10,11... | collective-permute-start | bytes 4718600 | tf_op jit(solution)/shard_map/ppermute | solution.py:464
  67.6 4.1 %collective-permute-start.1 = (bf16[8,32,1152]{2,1,0:T(8,128)(2,1)}, bf16[8,32,1152]{2,1,0:T(8,128)(2,1)S(1)}, u32[]{:S(2)}, u32[]{:S(2)}) collective-permute-start(bf16[8,32,1152]{2,1,0:T(8,128)(2,1)} %get-tuple-element.47), channel_id=1, source_target_pairs={{0,1},{1,0},{2,3},{3,2},{4,5},{5,4},{6,7},{7,6},{8,9},{9,8},{10,11... | collective-permute-start | bytes 1769480 | tf_op jit(solution)/shard_map/ppermute | solution.py:464
  71.7 0.8 copy-start.2
  72.1 5.3 %collective-permute-start.2 = (bf16[4,8,64,640]{3,2,1,0:T(8,128)(2,1)}, bf16[4,8,64,640]{3,2,1,0:T(8,128)(2,1)}, u32[]{:S(2)}, u32[]{:S(2)}) collective-permute-start(bf16[4,8,64,640]{3,2,1,0:T(8,128)(2,1)} %get-tuple-element.54), channel_id=1, source_target_pairs={{0,1},{1,0},{2,3},{3,2},{4,5},{5,4},{6,7},{7,6},{8,9},{9,8},{10,11... | collective-permute-start | bytes 7864328 | tf_op jit(solution)/shard_map/ppermute | solution.py:464
  82.0 5.8 %copy-start.8 = (bf16[8,64,640]{2,1,0:T(8,128)(2,1)S(1)}, bf16[8,64,640]{2,1,0:T(8,128)(2,1)}, u32[]{:S(2)}) copy-start(bf16[8,64,640]{2,1,0:T(8,128)(2,1)} %get-tuple-element.61) | copy-start | bytes 1966084
  82.0 7.2 %copy-start.7 = (bf16[8,64,640]{2,1,0:T(8,128)(2,1)S(1)}, bf16[8,64,640]{2,1,0:T(8,128)(2,1)}, u32[]{:S(2)}) copy-start(bf16[8,64,640]{2,1,0:T(8,128)(2,1)} %get-tuple-element.62) | copy-start | bytes 1966084
  82.0 9.9 %copy-start.6 = (bf16[8,64,640]{2,1,0:T(8,128)(2,1)S(1)}, bf16[8,64,640]{2,1,0:T(8,128)(2,1)}, u32[]{:S(2)}) copy-start(bf16[8,64,640]{2,1,0:T(8,128)(2,1)} %get-tuple-element.63) | copy-start | bytes 1966084
  82.0 39.4 %all-to-all-start.1 = ((bf16[8,64,2688]{2,1,0:T(8,128)(2,1)}), bf16[8,64,2688]{2,1,0:T(8,128)(2,1)}, u32[]{:S(2)}, u32[]{:S(2)}) async-start(bf16[8,64,2688]{2,1,0:T(8,128)(2,1)} %get-tuple-element.60), calls=%async_computation.1 | async-start | bytes 5505024 | tf_op jit(solution)/shard_map/all_to_all | solution.py:469
  87.8 18.0 %collective-permute-start.3 = (bf16[8,64,640]{2,1,0:T(8,128)(2,1)S(1)}, bf16[8,64,640]{2,1,0:T(8,128)(2,1)S(1)}, u32[]{:S(2)}, u32[]{:S(2)}) collective-permute-start(bf16[8,64,640]{2,1,0:T(8,128)(2,1)S(1)} %copy-done.8), channel_id=1, source_target_pairs={{0,64},{16,80},{32,96},{48,112},{64,128},{80,144},{96,160},{112,17... | collective-permute-start | bytes 1966088 | tf_op jit(solution)/shard_map/ppermute | solution.py:473
  89.2 31.4 %collective-permute-start.4 = (bf16[8,64,640]{2,1,0:T(8,128)(2,1)S(1)}, bf16[8,64,640]{2,1,0:T(8,128)(2,1)}, u32[]{:S(2)}, u32[]{:S(2)}) collective-permute-start(bf16[8,64,640]{2,1,0:T(8,128)(2,1)S(1)} %copy-done.7), channel_id=1, source_target_pairs={{0,128},{16,144},{32,160},{48,176},{64,192},{80,208},{96,224},{112... | collective-permute-start | bytes 1966088 | tf_op jit(solution)/shard_map/ppermute | solution.py:473
  91.9 28.6 %collective-permute-start.5 = (bf16[8,64,640]{2,1,0:T(8,128)(2,1)S(1)}, bf16[8,64,640]{2,1,0:T(8,128)(2,1)}, u32[]{:S(2)}, u32[]{:S(2)}) collective-permute-start(bf16[8,64,640]{2,1,0:T(8,128)(2,1)S(1)} %copy-done.6), channel_id=1, source_target_pairs={{0,192},{16,208},{32,224},{48,240},{64,0},{80,16},{96,32},{112,48}... | collective-permute-start | bytes 1966088 | tf_op jit(solution)/shard_map/ppermute | solution.py:473
  105.9 15.5 %copy-start.1 = (bf16[8,64,640]{2,1,0:T(8,128)(2,1)}, bf16[8,64,640]{2,1,0:T(8,128)(2,1)S(1)}, u32[]{:S(2)}) copy-start(bf16[8,64,640]{2,1,0:T(8,128)(2,1)S(1)} %collective-permute-done.3.t1) | copy-start | bytes 1966084
  124.9 17.0 %copy-start.5 = (f32[64,640]{1,0:T(8,128)S(1)}, f32[64,640]{1,0:T(8,128)}, u32[]{:S(2)}) copy-start(f32[64,640]{1,0:T(8,128)} %get-tuple-element.67) | copy-start | bytes 491524
  124.9 16.0 %all-to-all-start.2 = ((bf16[8,64,640]{2,1,0:T(8,128)(2,1)}), bf16[8,64,640]{2,1,0:T(8,128)(2,1)S(1)}, u32[]{:S(2)}, u32[]{:S(2)}) async-start(bf16[8,64,640]{2,1,0:T(8,128)(2,1)} %get-tuple-element.70), calls=%async_computation.2 | async-start | bytes 1310720 | tf_op jit(solution)/shard_map/all_to_all | solution.py:469
  131.9 4.5 %collective-permute-start.8 = (bf16[64,384]{1,0:T(8,128)(2,1)S(1)}, bf16[64,384]{1,0:T(8,128)(2,1)S(1)}, u32[]{:S(2)}, u32[]{:S(2)}) collective-permute-start(bf16[64,384]{1,0:T(8,128)(2,1)S(1)} %get-tuple-element.90), channel_id=1, source_target_pairs={{0,192},{16,208},{32,224},{48,240},{64,0},{80,16},{96,32},{112,48}... | collective-permute-start | bytes 147464 | tf_op jit(solution)/shard_map/ppermute | solution.py:473
  134.4 5.6 %collective-permute-start.7 = (bf16[64,384]{1,0:T(8,128)(2,1)S(1)}, bf16[64,384]{1,0:T(8,128)(2,1)S(1)}, u32[]{:S(2)}, u32[]{:S(2)}) collective-permute-start(bf16[64,384]{1,0:T(8,128)(2,1)S(1)} %get-tuple-element.91), channel_id=1, source_target_pairs={{0,128},{16,144},{32,160},{48,176},{64,192},{80,208},{96,224},{112... | collective-permute-start | bytes 147464 | tf_op jit(solution)/shard_map/ppermute | solution.py:473
  135.5 5.3 %collective-permute-start.6 = (bf16[64,384]{1,0:T(8,128)(2,1)S(1)}, bf16[64,384]{1,0:T(8,128)(2,1)S(1)}, u32[]{:S(2)}, u32[]{:S(2)}) collective-permute-start(bf16[64,384]{1,0:T(8,128)(2,1)S(1)} %get-tuple-element.92), channel_id=1, source_target_pairs={{0,64},{16,80},{32,96},{48,112},{64,128},{80,144},{96,160},{112,17... | collective-permute-start | bytes 147464 | tf_op jit(solution)/shard_map/ppermute | solution.py:473
  142.1 12.5 %collective-permute-start.11 = (bf16[64,1152]{1,0:T(8,128)(2,1)S(1)}, bf16[64,1152]{1,0:T(8,128)(2,1)S(1)}, u32[]{:S(2)}, u32[]{:S(2)}) collective-permute-start(bf16[64,1152]{1,0:T(8,128)(2,1)S(1)} %fusion), channel_id=1, source_target_pairs={{0,48},{16,0},{32,16},{48,32},{64,112},{80,64},{96,80},{112,96},{1... | collective-permute-start | bytes 442376 | tf_op jit(solution)/shard_map/ppermute | solution.py:477
  147.4 12.8 %collective-permute-start.10 = (bf16[64,1152]{1,0:T(8,128)(2,1)S(1)}, bf16[64,1152]{1,0:T(8,128)(2,1)S(1)}, u32[]{:S(2)}, u32[]{:S(2)}) collective-permute-start(bf16[64,1152]{1,0:T(8,128)(2,1)S(1)} %fusion), channel_id=1, source_target_pairs={{0,32},{16,48},{32,0},{48,16},{64,96},{80,112},{96,64},{112,80},{1... | collective-permute-start | bytes 442376 | tf_op jit(solution)/shard_map/ppermute | solution.py:477
  148.9 12.3 %collective-permute-start.9 = (bf16[64,1152]{1,0:T(8,128)(2,1)S(1)}, bf16[64,1152]{1,0:T(8,128)(2,1)S(1)}, u32[]{:S(2)}, u32[]{:S(2)}) collective-permute-start(bf16[64,1152]{1,0:T(8,128)(2,1)S(1)} %fusion), channel_id=1, source_target_pairs={{0,16},{16,32},{32,48},{48,0},{64,80},{80,96},{96,112},{112,64},{1... | collective-permute-start | bytes 442376 | tf_op jit(solution)/shard_map/ppermute | solution.py:477
  161.2 18.8 %copy-start = (f32[64,1152]{1,0:T(8,128)}, f32[64,1152]{1,0:T(8,128)S(1)}, u32[]{:S(2)}) copy-start(f32[64,1152]{1,0:T(8,128)S(1)} %convert_add_fusion.d0) | copy-start | bytes 884740
  161.2 15.3 %collective-permute-start.14 = (f32[64,1152]{1,0:T(8,128)S(1)}, f32[64,1152]{1,0:T(8,128)S(1)}, u32[]{:S(2)}, u32[]{:S(2)}) collective-permute-start(f32[64,1152]{1,0:T(8,128)S(1)} %convert_add_fusion.d0), channel_id=1, source_target_pairs={{0,192},{16,208},{32,224},{48,240},{64,0},{80,16},{96,32},{112,48}... | collective-permute-start | bytes 884744 | tf_op jit(solution)/shard_map/ppermute | solution.py:473
  164.3 12.2 %collective-permute-start.13 = (f32[64,1152]{1,0:T(8,128)S(1)}, f32[64,1152]{1,0:T(8,128)S(1)}, u32[]{:S(2)}, u32[]{:S(2)}) collective-permute-start(f32[64,1152]{1,0:T(8,128)S(1)} %convert_add_fusion.d0), channel_id=1, source_target_pairs={{0,128},{16,144},{32,160},{48,176},{64,192},{80,208},{96,224},{112... | collective-permute-start | bytes 884744 | tf_op jit(solution)/shard_map/ppermute | solution.py:473
  164.6 15.4 %collective-permute-start.12 = (f32[64,1152]{1,0:T(8,128)S(1)}, f32[64,1152]{1,0:T(8,128)}, u32[]{:S(2)}, u32[]{:S(2)}) collective-permute-start(f32[64,1152]{1,0:T(8,128)S(1)} %convert_add_fusion.d0), channel_id=1, source_target_pairs={{0,64},{16,80},{32,96},{48,112},{64,128},{80,144},{96,160},{112,17... | collective-permute-start | bytes 884744 | tf_op jit(solution)/shard_map/ppermute | solution.py:473
  176.5 3.5 %copy-start.3 = (f32[64,1152]{1,0:T(8,128)}, f32[64,1152]{1,0:T(8,128)S(1)}, u32[]{:S(2)}) copy-start(f32[64,1152]{1,0:T(8,128)S(1)} %collective-permute-done.14.d3) | copy-start | bytes 884740
  176.5 3.5 %copy-start.4 = (f32[64,1152]{1,0:T(8,128)}, f32[64,1152]{1,0:T(8,128)S(1)}, u32[]{:S(2)}) copy-start(f32[64,1152]{1,0:T(8,128)S(1)} %collective-permute-done.13.d2) | copy-start | bytes 884740

commit v11 on v10

--- a/solution.py
+++ b/solution.py
@@ -531,12 +531,13 @@
     a = reduce_yz(own_a, message[:, :, :1536], yz)
     terms_a = [a[:, k * 384 : (k + 1) * 384] for k in range(4)]
     got_a = exchange([t.astype(BF16) for t in terms_a], go_x)
-    message, got_a, got_b = lax.optimization_barrier((message, got_a, got_b))
+    small = jnp.sum(message[:, :, 1536 + width :].astype(F32), axis=(0, 1)).reshape(1, 128)
+    terms = three_terms(small)
+    message, terms, got_a, got_b = lax.optimization_barrier((message, terms, got_a, got_b))
 
     a = combine(terms_a[0], got_a)
     b = reduce_yz(own_b, got_b, yz)
-    small = jnp.sum(message[:, :, 1536 + width :].astype(F32), axis=(0, 1)).reshape(1, 128)
-    own = jnp.concatenate([b, a, three_terms(small)], axis=1)
+    own = jnp.concatenate([b, a, terms], axis=1)
     own = combine(own, exchange([own.astype(BF16)] * 4, go_h))
     pieces = [own] + exchange([own] * 4, go_x)
 

time: 183 us -> 182 us (level)
  transfers between devices with their start and end apart: 18 -> 18, of which waited for: 15 -> 14; matrix products, arithmetic and copies ran while one was open for 1% -> 2% of each run, Pallas kernels for 4% -> 4%
where the time goes in v11:
time: 182 us; the launch traced here: 181 us
  waiting for transfers between devices  83.1 us (46%)
  Pallas kernels  52.4 us (29%)
  starting transfers between devices  40.9 us (22%)
  other arithmetic  3.89 us (2%)
    ppermute x9, waiting for transfers between devices, go_x(): return lax.ppermute(a, 'dp', dp_pairs(lambda x, h: (x + k, h)))  42 us
    pallas_call x1, Pallas kernels, run_main(): pl.pallas_call(main_kernel, out_shape=(jax.ShapeDtypeStruct(back, BF16),...  31.1 us
    all_to_all x1, waiting for transfers between devices, local(): lax.all_to_all(run_pack(video, cotangent), 'frame', 0, 0, tiled=True)  26.1 us
    ppermute x9, starting transfers between devices, go_x(): return lax.ppermute(a, 'dp', dp_pairs(lambda x, h: (x + k, h)))  14.1 us
    all_to_all x2, starting transfers between devices, trade_yz(): lax.all_to_all(a, 'frame', 0, 0, tiled=True, axis_index_groups=groups)  10.9 us
    ppermute x3, waiting for transfers between devices, go_h(): return lax.ppermute(a, 'dp', dp_pairs(lambda x, h: (x, h + k)))  9.91 us
    ppermute x3, starting transfers between devices, go_h(): return lax.ppermute(a, 'dp', dp_pairs(lambda x, h: (x, h + k)))  9.13 us
    all_to_all x1, starting transfers between devices, local(): lax.all_to_all(run_pack(video, cotangent), 'frame', 0, 0, tiled=True)  6.04 us
  transfers between devices with their start and end apart: 18, of which 14 were waited for; matrix products, arithmetic and copies ran while one was open for 2% of the time, Pallas kernels for 4%

profile of v11, /device:TPU:32, one launch (start us, length us, event | category | flops | bytes accessed | tf_op | source)
XLA Modules:
  0.0 181.3 jit_solution(3565354955145542253)
XLA Ops:
  0.6 2.9 %pack.1 = bf16[16,4,16,1024]{3,2,1,0:T(8,128)(2,1)} custom-call(bf16[2,16,16,1024]{3,2,1,0:T(8,128)(2,1)} %bitcast.24, bf16[2,16,16,1024]{3,2,1,0:T(8,128)(2,1)} %bitcast.25), custom_call_target="tpu_custom_call" | custom-call | tf_op jit(solution)/shard_map/pack/pallas_call | solution.py:385
  3.5 6.0 %all-to-all-start = ((bf16[16,4,16,1024]{3,2,1,0:T(8,128)(2,1)}), bf16[16,4,16,1024]{3,2,1,0:T(8,128)(2,1)}, u32[]{:S(2)}, u32[]{:S(2)}) async-start(bf16[16,4,16,1024]{3,2,1,0:T(8,128)(2,1)} %pack.1), calls=%async_computation | async-start | bytes 4194304 | tf_op jit(solution)/shard_map/all_to_all | solution.py:514
  9.6 0.7 pad_add_fusion.place_ref
  10.2 26.1 %all-to-all-done.tokens_hbm = bf16[16,4,16,1024]{3,2,1,0:T(8,128)(2,1)} async-done(((bf16[16,4,16,1024]{3,2,1,0:T(8,128)(2,1)}), bf16[16,4,16,1024]{3,2,1,0:T(8,128)(2,1)}, u32[]{:S(2)}, u32[]{:S(2)}) %all-to-all-start) | async-done | bytes 2097184 | tf_op jit(solution)/shard_map/all_to_all | solution.py:514
  36.4 31.1 %sublayer.1 = (bf16[8,32,1152]{2,1,0:T(8,128)(2,1)}, bf16[8,32,1152]{2,1,0:T(8,128)(2,1)}, bf16[8,64,1536]{2,1,0:T(8,128)(2,1)}, bf16[4,8,64,640]{3,2,1,0:T(8,12...) custom-call(s32[3]{0:T(128)} %pad_add_fusion.place_ref, bf16[16,4,16,1024]{3,2,1,0:T(8,128)(2,1)} %all-to-all-done.tokens_hbm, ...), custom_call_target="tpu_custom_call" | custom-call | flops 12884901888 | bytes 20971520 | tf_op jit(solution)/shard_map/sublayer/pallas_call | solution.py:246
  67.4 0.2 collective-permute-start
  67.6 0.4 collective-permute-start.1
  68.0 3.7 %collective-permute-done.1.theirs_ref = bf16[8,32,1152]{2,1,0:T(8,128)(2,1)S(1)} collective-permute-done((bf16[8,32,1152]{2,1,0:T(8,128)(2,1)}, bf16[8,32,1152]{2,1,0:T(8,128)(2,1)S(1)}, u32[]{:S(2)}, u32[]{:S(2)}) %collective-permute-start.1) | collective-permute-done | bytes 589856 | tf_op jit(solution)/shard_map/ppermute | solution.py:464
  71.7 0.4 collective-permute-done.got_ref
  72.1 0.1 collective-permute-start.2
  72.3 0.3 copy-done.2
  72.5 4.7 %message.1 = (f32[64,1536]{1,0:T(8,128)}, bf16[8,64,2688]{2,1,0:T(8,128)(2,1)}) custom-call(s32[3]{0:T(128)} %pad_add_fusion.place_ref, f32[8,64,1536]{2,1,0:T(8,128)} %get-tuple-element.46.keep_ref, bf16[8,64,1536]{2,1,0:T(8,128)(2,1)} %collective-permute-done.got_ref, bf16[8,32,1152]{2,1,0:T(8,128)(2,1)} %get-tuple-element.51.back_ref, ...), custom_call_target="tpu_custom_call" | custom-call | flops 1048576 | bytes 9437184 | tf_op jit(solution)/shard_map/message/pallas_call | solution.py:321
  77.2 0.1 collective-permute-done.2.got_ref
  77.4 4.6 %terms_b.1 = (f32[8,64,640]{2,1,0:T(8,128)}, bf16[8,64,640]{2,1,0:T(8,128)(2,1)}, bf16[8,64,640]{2,1,0:T(8,128)(2,1)}, bf16[8,64,640]{2,1,0:T(8,128)(2,1)}) custom-call(f32[4,8,64,640]{3,2,1,0:T(8,128)} %get-tuple-element.54.keep_ref, bf16[4,8,64,640]{3,2,1,0:T(8,128)(2,1)} %collective-permute-done.2.got_ref), custom_call_target="tpu_custom_call" | custom-call | flops 1048576 | bytes 11534336 | tf_op jit(solution)/shard_map/terms_b/pallas_call | solution.py:406
  82.0 5.8 %all-to-all-start.1 = ((bf16[8,64,2688]{2,1,0:T(8,128)(2,1)}), bf16[8,64,2688]{2,1,0:T(8,128)(2,1)}, u32[]{:S(2)}, u32[]{:S(2)}) async-start(bf16[8,64,2688]{2,1,0:T(8,128)(2,1)} %get-tuple-element.61), calls=%async_computation.1 | async-start | bytes 5505024 | tf_op jit(solution)/shard_map/all_to_all | solution.py:469
  87.8 1.3 collective-permute-start.3
  89.2 2.7 %collective-permute-start.4 = (bf16[8,64,640]{2,1,0:T(8,128)(2,1)S(1)}, bf16[8,64,640]{2,1,0:T(8,128)(2,1)}, u32[]{:S(2)}, u32[]{:S(2)}) collective-permute-start(bf16[8,64,640]{2,1,0:T(8,128)(2,1)S(1)} %copy-done.7), channel_id=1, source_target_pairs={{0,128},{16,144},{32,160},{48,176},{64,192},{80,208},{96,224},{112... | collective-permute-start | bytes 1966088 | tf_op jit(solution)/shard_map/ppermute | solution.py:473
  91.9 1.4 collective-permute-start.5
  93.3 12.5 %collective-permute-done.3.t1 = bf16[8,64,640]{2,1,0:T(8,128)(2,1)S(1)} collective-permute-done((bf16[8,64,640]{2,1,0:T(8,128)(2,1)S(1)}, bf16[8,64,640]{2,1,0:T(8,128)(2,1)S(1)}, u32[]{:S(2)}, u32[]{:S(2)}) %collective-permute-start.3) | collective-permute-done | bytes 655392 | tf_op jit(solution)/shard_map/ppermute | solution.py:473
  105.9 14.7 %collective-permute-done.4.t2 = bf16[8,64,640]{2,1,0:T(8,128)(2,1)} collective-permute-done((bf16[8,64,640]{2,1,0:T(8,128)(2,1)S(1)}, bf16[8,64,640]{2,1,0:T(8,128)(2,1)}, u32[]{:S(2)}, u32[]{:S(2)}) %collective-permute-start.4) | collective-permute-done | bytes 655392 | tf_op jit(solution)/shard_map/ppermute | solution.py:473
  120.5 0.0 collective-permute-done.5.t3
  120.5 0.8 all-to-all-done.1.message_ref
  121.4 3.5 %sum_b.1 = (f32[64,640]{1,0:T(8,128)}, bf16[8,64,640]{2,1,0:T(8,128)(2,1)}) custom-call(s32[3]{0:T(128)} %pad_add_fusion.place_ref, f32[8,64,640]{2,1,0:T(8,128)} %get-tuple-element.60.keep_ref, bf16[8,64,640]{2,1,0:T(8,128)(2,1)} %copy-done.1, bf16[8,64,640]{2,1,0:T(8,128)(2,1)} %collective-permute-done.4.t2, bf16[8,64,640]{2,1,0:T(8,128)(2,1)} %collective-permute-done.5.t3), custom_call_target="tpu_custom_call" | custom-call | flops 1048576 | bytes 9437184 | tf_op jit(solution)/shard_map/sum_b/pallas_call | solution.py:337
  124.9 5.0 %all-to-all-start.2 = ((bf16[8,64,640]{2,1,0:T(8,128)(2,1)}), bf16[8,64,640]{2,1,0:T(8,128)(2,1)S(1)}, u32[]{:S(2)}, u32[]{:S(2)}) async-start(bf16[8,64,640]{2,1,0:T(8,128)(2,1)} %get-tuple-element.71), calls=%async_computation.2 | async-start | bytes 1310720 | tf_op jit(solution)/shard_map/all_to_all | solution.py:469
  129.9 1.9 %select_reduce_fusion = f32[64,1536]{1,0:T(8,128)S(1)} fusion(bf16[8,64,2688]{2,1,0:T(8,128)(2,1)} %all-to-all-done.1.message_ref, f32[64,1536]{1,0:T(8,128)} %get-tuple-element.70, pred[8]{0:T(512)(128)(4,1)S(1)} %iota_compare_fusion.1), kind=kLoop, calls=%fused_computation | loop fusion | flops 2260992 | bytes 2359304 | tf_op jit(solution)/shard_map/reduce_sum | solution.py:496
  131.9 2.5 %collective-permute-start.8 = (bf16[64,384]{1,0:T(8,128)(2,1)S(1)}, bf16[64,384]{1,0:T(8,128)(2,1)S(1)}, u32[]{:S(2)}, u32[]{:S(2)}) collective-permute-start(bf16[64,384]{1,0:T(8,128)(2,1)S(1)} %get-tuple-element.92), channel_id=1, source_target_pairs={{0,192},{16,208},{32,224},{48,240},{64,0},{80,16},{96,32},{112,48}... | collective-permute-start | bytes 147464 | tf_op jit(solution)/shard_map/ppermute | solution.py:473
  134.4 1.1 collective-permute-start.7
  135.5 0.5 collective-permute-start.6
  136.0 1.0 convert_reduce_fusion
  137.0 0.0 collective-permute-done.8
  137.0 2.9 %collective-permute-done.7 = bf16[64,384]{1,0:T(8,128)(2,1)S(1)} collective-permute-done((bf16[64,384]{1,0:T(8,128)(2,1)S(1)}, bf16[64,384]{1,0:T(8,128)(2,1)S(1)}, u32[]{:S(2)}, u32[]{:S(2)}) %collective-permute-start.7) | collective-permute-done | bytes 49184 | tf_op jit(solution)/shard_map/ppermute | solution.py:473
  140.0 0.8 collective-permute-done.6
  140.8 0.0 all-to-all-done.2
  140.8 0.2 select_reduce_fusion.1
  141.1 5.3 %collective-permute-start.11 = (bf16[64,1152]{1,0:T(8,128)(2,1)S(1)}, bf16[64,1152]{1,0:T(8,128)(2,1)S(1)}, u32[]{:S(2)}, u32[]{:S(2)}) collective-permute-start(bf16[64,1152]{1,0:T(8,128)(2,1)S(1)} %fusion), channel_id=1, source_target_pairs={{0,48},{16,0},{32,16},{48,32},{64,112},{80,64},{96,80},{112,96},{1... | collective-permute-start | bytes 442376 | tf_op jit(solution)/shard_map/ppermute | solution.py:477
  146.4 1.4 collective-permute-start.10
  147.8 2.4 %collective-permute-start.9 = (bf16[64,1152]{1,0:T(8,128)(2,1)S(1)}, bf16[64,1152]{1,0:T(8,128)(2,1)S(1)}, u32[]{:S(2)}, u32[]{:S(2)}) collective-permute-start(bf16[64,1152]{1,0:T(8,128)(2,1)S(1)} %fusion), channel_id=1, source_target_pairs={{0,16},{16,32},{32,48},{48,0},{64,80},{80,96},{96,112},{112,64},{1... | collective-permute-start | bytes 442376 | tf_op jit(solution)/shard_map/ppermute | solution.py:477
  150.2 3.4 %collective-permute-done.11 = bf16[64,1152]{1,0:T(8,128)(2,1)S(1)} collective-permute-done((bf16[64,1152]{1,0:T(8,128)(2,1)S(1)}, bf16[64,1152]{1,0:T(8,128)(2,1)S(1)}, u32[]{:S(2)}, u32[]{:S(2)}) %collective-permute-start.11) | collective-permute-done | bytes 147488 | tf_op jit(solution)/shard_map/ppermute | solution.py:477
  153.6 5.6 %collective-permute-done.10 = bf16[64,1152]{1,0:T(8,128)(2,1)S(1)} collective-permute-done((bf16[64,1152]{1,0:T(8,128)(2,1)S(1)}, bf16[64,1152]{1,0:T(8,128)(2,1)S(1)}, u32[]{:S(2)}, u32[]{:S(2)}) %collective-permute-start.10) | collective-permute-done | bytes 147488 | tf_op jit(solution)/shard_map/ppermute | solution.py:477
  159.2 0.9 collective-permute-done.9
  160.1 0.1 convert_add_fusion.d0
  160.2 3.1 %collective-permute-start.14 = (f32[64,1152]{1,0:T(8,128)S(1)}, f32[64,1152]{1,0:T(8,128)S(1)}, u32[]{:S(2)}, u32[]{:S(2)}) collective-permute-start(f32[64,1152]{1,0:T(8,128)S(1)} %convert_add_fusion.d0), channel_id=1, source_target_pairs={{0,192},{16,208},{32,224},{48,240},{64,0},{80,16},{96,32},{112,48}... | collective-permute-start | bytes 884744 | tf_op jit(solution)/shard_map/ppermute | solution.py:473
  163.3 0.3 collective-permute-start.13
  163.6 1.1 collective-permute-start.12
  164.7 3.3 %unpack.1 = bf16[2,256,1024]{2,1,0:T(8,128)(2,1)} custom-call(s32[3]{0:T(128)} %pad_add_fusion.place_ref, bf16[8,64,2688]{2,1,0:T(8,128)(2,1)} %all-to-all-done.1.message_ref), custom_call_target="tpu_custom_call" | custom-call | tf_op jit(solution)/shard_map/unpack/pallas_call | solution.py:351
  167.9 7.5 %collective-permute-done.14.d3 = f32[64,1152]{1,0:T(8,128)S(1)} collective-permute-done((f32[64,1152]{1,0:T(8,128)S(1)}, f32[64,1152]{1,0:T(8,128)S(1)}, u32[]{:S(2)}, u32[]{:S(2)}) %collective-permute-start.14) | collective-permute-done | bytes 294944 | tf_op jit(solution)/shard_map/ppermute | solution.py:473
  175.5 3.5 %collective-permute-done.12.d1 = f32[64,1152]{1,0:T(8,128)} collective-permute-done((f32[64,1152]{1,0:T(8,128)S(1)}, f32[64,1152]{1,0:T(8,128)}, u32[]{:S(2)}, u32[]{:S(2)}) %collective-permute-start.12) | collective-permute-done | bytes 294944 | tf_op jit(solution)/shard_map/ppermute | solution.py:473
  179.0 2.3 %place_grads.1 = (f32[64,3072]{1,0:T(8,128)}, f32[64,1024]{1,0:T(8,128)}, f32[1,64]{1,0:T(1,128)}, f32[1,64]{1,0:T(1,128)}) custom-call(s32[3]{0:T(128)} %pad_add_fusion.place_ref, f32[64,1152]{1,0:T(8,128)} %copy-done, f32[64,1152]{1,0:T(8,128)} %collective-permute-done.12.d1, f32[64,1152]{1,0:T(8,128)} %copy-done.4, f32[64,1152]{1,0:T(8,128)} %copy-done.3), custom_call_target="tpu_custom_call" | custom-call | tf_op jit(solution)/shard_map/place_grads/pallas_call | solution.py:433
  (25 shorter events, 0.1 us)
Async XLA Ops:
  3.5 32.8 %all-to-all-start = ((bf16[16,4,16,1024]{3,2,1,0:T(8,128)(2,1)}), bf16[16,4,16,1024]{3,2,1,0:T(8,128)(2,1)}, u32[]{:S(2)}, u32[]{:S(2)}) async-start(bf16[16,4,16,1024]{3,2,1,0:T(8,128)(2,1)} %pack.1), calls=%async_computation | async-start | bytes 4194304 | tf_op jit(solution)/shard_map/all_to_all | solution.py:514
  67.4 4.7 %collective-permute-start = (bf16[8,64,1536]{2,1,0:T(8,128)(2,1)}, bf16[8,64,1536]{2,1,0:T(8,128)(2,1)}, u32[]{:S(2)}, u32[]{:S(2)}) collective-permute-start(bf16[8,64,1536]{2,1,0:T(8,128)(2,1)} %get-tuple-element.47), channel_id=1, source_target_pairs={{0,1},{1,0},{2,3},{3,2},{4,5},{5,4},{6,7},{7,6},{8,9},{9,8},{10,11... | collective-permute-start | bytes 4718600 | tf_op jit(solution)/shard_map/ppermute | solution.py:464
  67.6 4.1 %collective-permute-start.1 = (bf16[8,32,1152]{2,1,0:T(8,128)(2,1)}, bf16[8,32,1152]{2,1,0:T(8,128)(2,1)S(1)}, u32[]{:S(2)}, u32[]{:S(2)}) collective-permute-start(bf16[8,32,1152]{2,1,0:T(8,128)(2,1)} %get-tuple-element.48), channel_id=1, source_target_pairs={{0,1},{1,0},{2,3},{3,2},{4,5},{5,4},{6,7},{7,6},{8,9},{9,8},{10,11... | collective-permute-start | bytes 1769480 | tf_op jit(solution)/shard_map/ppermute | solution.py:464
  71.7 0.8 copy-start.2
  72.1 5.3 %collective-permute-start.2 = (bf16[4,8,64,640]{3,2,1,0:T(8,128)(2,1)}, bf16[4,8,64,640]{3,2,1,0:T(8,128)(2,1)}, u32[]{:S(2)}, u32[]{:S(2)}) collective-permute-start(bf16[4,8,64,640]{3,2,1,0:T(8,128)(2,1)} %get-tuple-element.55), channel_id=1, source_target_pairs={{0,1},{1,0},{2,3},{3,2},{4,5},{5,4},{6,7},{7,6},{8,9},{9,8},{10,11... | collective-permute-start | bytes 7864328 | tf_op jit(solution)/shard_map/ppermute | solution.py:464
  82.0 5.8 %copy-start.8 = (bf16[8,64,640]{2,1,0:T(8,128)(2,1)S(1)}, bf16[8,64,640]{2,1,0:T(8,128)(2,1)}, u32[]{:S(2)}) copy-start(bf16[8,64,640]{2,1,0:T(8,128)(2,1)} %get-tuple-element.62) | copy-start | bytes 1966084
  82.0 7.2 %copy-start.7 = (bf16[8,64,640]{2,1,0:T(8,128)(2,1)S(1)}, bf16[8,64,640]{2,1,0:T(8,128)(2,1)}, u32[]{:S(2)}) copy-start(bf16[8,64,640]{2,1,0:T(8,128)(2,1)} %get-tuple-element.63) | copy-start | bytes 1966084
  82.0 9.9 %copy-start.6 = (bf16[8,64,640]{2,1,0:T(8,128)(2,1)S(1)}, bf16[8,64,640]{2,1,0:T(8,128)(2,1)}, u32[]{:S(2)}) copy-start(bf16[8,64,640]{2,1,0:T(8,128)(2,1)} %get-tuple-element.64) | copy-start | bytes 1966084
  82.0 39.4 %all-to-all-start.1 = ((bf16[8,64,2688]{2,1,0:T(8,128)(2,1)}), bf16[8,64,2688]{2,1,0:T(8,128)(2,1)}, u32[]{:S(2)}, u32[]{:S(2)}) async-start(bf16[8,64,2688]{2,1,0:T(8,128)(2,1)} %get-tuple-element.61), calls=%async_computation.1 | async-start | bytes 5505024 | tf_op jit(solution)/shard_map/all_to_all | solution.py:469
  87.8 18.0 %collective-permute-start.3 = (bf16[8,64,640]{2,1,0:T(8,128)(2,1)S(1)}, bf16[8,64,640]{2,1,0:T(8,128)(2,1)S(1)}, u32[]{:S(2)}, u32[]{:S(2)}) collective-permute-start(bf16[8,64,640]{2,1,0:T(8,128)(2,1)S(1)} %copy-done.8), channel_id=1, source_target_pairs={{0,64},{16,80},{32,96},{48,112},{64,128},{80,144},{96,160},{112,17... | collective-permute-start | bytes 1966088 | tf_op jit(solution)/shard_map/ppermute | solution.py:473
  89.2 31.4 %collective-permute-start.4 = (bf16[8,64,640]{2,1,0:T(8,128)(2,1)S(1)}, bf16[8,64,640]{2,1,0:T(8,128)(2,1)}, u32[]{:S(2)}, u32[]{:S(2)}) collective-permute-start(bf16[8,64,640]{2,1,0:T(8,128)(2,1)S(1)} %copy-done.7), channel_id=1, source_target_pairs={{0,128},{16,144},{32,160},{48,176},{64,192},{80,208},{96,224},{112... | collective-permute-start | bytes 1966088 | tf_op jit(solution)/shard_map/ppermute | solution.py:473
  91.9 28.6 %collective-permute-start.5 = (bf16[8,64,640]{2,1,0:T(8,128)(2,1)S(1)}, bf16[8,64,640]{2,1,0:T(8,128)(2,1)}, u32[]{:S(2)}, u32[]{:S(2)}) collective-permute-start(bf16[8,64,640]{2,1,0:T(8,128)(2,1)S(1)} %copy-done.6), channel_id=1, source_target_pairs={{0,192},{16,208},{32,224},{48,240},{64,0},{80,16},{96,32},{112,48}... | collective-permute-start | bytes 1966088 | tf_op jit(solution)/shard_map/ppermute | solution.py:473
  105.9 15.5 %copy-start.1 = (bf16[8,64,640]{2,1,0:T(8,128)(2,1)}, bf16[8,64,640]{2,1,0:T(8,128)(2,1)S(1)}, u32[]{:S(2)}) copy-start(bf16[8,64,640]{2,1,0:T(8,128)(2,1)S(1)} %collective-permute-done.3.t1) | copy-start | bytes 1966084
  124.9 16.0 %copy-start.5 = (f32[64,640]{1,0:T(8,128)S(1)}, f32[64,640]{1,0:T(8,128)}, u32[]{:S(2)}) copy-start(f32[64,640]{1,0:T(8,128)} %get-tuple-element.68) | copy-start | bytes 491524
  124.9 16.0 %all-to-all-start.2 = ((bf16[8,64,640]{2,1,0:T(8,128)(2,1)}), bf16[8,64,640]{2,1,0:T(8,128)(2,1)S(1)}, u32[]{:S(2)}, u32[]{:S(2)}) async-start(bf16[8,64,640]{2,1,0:T(8,128)(2,1)} %get-tuple-element.71), calls=%async_computation.2 | async-start | bytes 1310720 | tf_op jit(solution)/shard_map/all_to_all | solution.py:469
  131.9 5.2 %collective-permute-start.8 = (bf16[64,384]{1,0:T(8,128)(2,1)S(1)}, bf16[64,384]{1,0:T(8,128)(2,1)S(1)}, u32[]{:S(2)}, u32[]{:S(2)}) collective-permute-start(bf16[64,384]{1,0:T(8,128)(2,1)S(1)} %get-tuple-element.92), channel_id=1, source_target_pairs={{0,192},{16,208},{32,224},{48,240},{64,0},{80,16},{96,32},{112,48}... | collective-permute-start | bytes 147464 | tf_op jit(solution)/shard_map/ppermute | solution.py:473
  134.4 5.6 %collective-permute-start.7 = (bf16[64,384]{1,0:T(8,128)(2,1)S(1)}, bf16[64,384]{1,0:T(8,128)(2,1)S(1)}, u32[]{:S(2)}, u32[]{:S(2)}) collective-permute-start(bf16[64,384]{1,0:T(8,128)(2,1)S(1)} %get-tuple-element.93), channel_id=1, source_target_pairs={{0,128},{16,144},{32,160},{48,176},{64,192},{80,208},{96,224},{112... | collective-permute-start | bytes 147464 | tf_op jit(solution)/shard_map/ppermute | solution.py:473
  135.5 5.3 %collective-permute-start.6 = (bf16[64,384]{1,0:T(8,128)(2,1)S(1)}, bf16[64,384]{1,0:T(8,128)(2,1)S(1)}, u32[]{:S(2)}, u32[]{:S(2)}) collective-permute-start(bf16[64,384]{1,0:T(8,128)(2,1)S(1)} %get-tuple-element.94), channel_id=1, source_target_pairs={{0,64},{16,80},{32,96},{48,112},{64,128},{80,144},{96,160},{112,17... | collective-permute-start | bytes 147464 | tf_op jit(solution)/shard_map/ppermute | solution.py:473
  141.1 12.5 %collective-permute-start.11 = (bf16[64,1152]{1,0:T(8,128)(2,1)S(1)}, bf16[64,1152]{1,0:T(8,128)(2,1)S(1)}, u32[]{:S(2)}, u32[]{:S(2)}) collective-permute-start(bf16[64,1152]{1,0:T(8,128)(2,1)S(1)} %fusion), channel_id=1, source_target_pairs={{0,48},{16,0},{32,16},{48,32},{64,112},{80,64},{96,80},{112,96},{1... | collective-permute-start | bytes 442376 | tf_op jit(solution)/shard_map/ppermute | solution.py:477
  146.4 12.8 %collective-permute-start.10 = (bf16[64,1152]{1,0:T(8,128)(2,1)S(1)}, bf16[64,1152]{1,0:T(8,128)(2,1)S(1)}, u32[]{:S(2)}, u32[]{:S(2)}) collective-permute-start(bf16[64,1152]{1,0:T(8,128)(2,1)S(1)} %fusion), channel_id=1, source_target_pairs={{0,32},{16,48},{32,0},{48,16},{64,96},{80,112},{96,64},{112,80},{1... | collective-permute-start | bytes 442376 | tf_op jit(solution)/shard_map/ppermute | solution.py:477
  147.8 12.3 %collective-permute-start.9 = (bf16[64,1152]{1,0:T(8,128)(2,1)S(1)}, bf16[64,1152]{1,0:T(8,128)(2,1)S(1)}, u32[]{:S(2)}, u32[]{:S(2)}) collective-permute-start(bf16[64,1152]{1,0:T(8,128)(2,1)S(1)} %fusion), channel_id=1, source_target_pairs={{0,16},{16,32},{32,48},{48,0},{64,80},{80,96},{96,112},{112,64},{1... | collective-permute-start | bytes 442376 | tf_op jit(solution)/shard_map/ppermute | solution.py:477
  160.2 18.8 %copy-start = (f32[64,1152]{1,0:T(8,128)}, f32[64,1152]{1,0:T(8,128)S(1)}, u32[]{:S(2)}) copy-start(f32[64,1152]{1,0:T(8,128)S(1)} %convert_add_fusion.d0) | copy-start | bytes 884740
  160.2 15.3 %collective-permute-start.14 = (f32[64,1152]{1,0:T(8,128)S(1)}, f32[64,1152]{1,0:T(8,128)S(1)}, u32[]{:S(2)}, u32[]{:S(2)}) collective-permute-start(f32[64,1152]{1,0:T(8,128)S(1)} %convert_add_fusion.d0), channel_id=1, source_target_pairs={{0,192},{16,208},{32,224},{48,240},{64,0},{80,16},{96,32},{112,48}... | collective-permute-start | bytes 884744 | tf_op jit(solution)/shard_map/ppermute | solution.py:473
  163.3 12.2 %collective-permute-start.13 = (f32[64,1152]{1,0:T(8,128)S(1)}, f32[64,1152]{1,0:T(8,128)S(1)}, u32[]{:S(2)}, u32[]{:S(2)}) collective-permute-start(f32[64,1152]{1,0:T(8,128)S(1)} %convert_add_fusion.d0), channel_id=1, source_target_pairs={{0,128},{16,144},{32,160},{48,176},{64,192},{80,208},{96,224},{112... | collective-permute-start | bytes 884744 | tf_op jit(solution)/shard_map/ppermute | solution.py:473
  163.6 15.4 %collective-permute-start.12 = (f32[64,1152]{1,0:T(8,128)S(1)}, f32[64,1152]{1,0:T(8,128)}, u32[]{:S(2)}, u32[]{:S(2)}) collective-permute-start(f32[64,1152]{1,0:T(8,128)S(1)} %convert_add_fusion.d0), channel_id=1, source_target_pairs={{0,64},{16,80},{32,96},{48,112},{64,128},{80,144},{96,160},{112,17... | collective-permute-start | bytes 884744 | tf_op jit(solution)/shard_map/ppermute | solution.py:473
  175.5 3.5 %copy-start.3 = (f32[64,1152]{1,0:T(8,128)}, f32[64,1152]{1,0:T(8,128)S(1)}, u32[]{:S(2)}) copy-start(f32[64,1152]{1,0:T(8,128)S(1)} %collective-permute-done.14.d3) | copy-start | bytes 884740
  175.5 3.5 %copy-start.4 = (f32[64,1152]{1,0:T(8,128)}, f32[64,1152]{1,0:T(8,128)S(1)}, u32[]{:S(2)}) copy-start(f32[64,1152]{1,0:T(8,128)S(1)} %collective-permute-done.13.d2) | copy-start | bytes 884740

commit v12 on v11

--- a/solution.py
+++ b/solution.py
@@ -440,6 +440,7 @@
         ),
         in_specs=[pl.BlockSpec(memory_space=pltpu.SMEM)] + [vm] * 4,
         out_specs=(vm,) * 4,
+        compiler_params=pltpu.CompilerParams(vmem_limit_bytes=8 * MIB),
         name="place_grads",
     )(place, *pieces)
 

time: 182 us -> 182 us (level)
  no operation moved by 1% of the time
where the time goes in v12:
time: 182 us; the launch traced here: 181 us
  waiting for transfers between devices  83.1 us (46%)
  Pallas kernels  52.1 us (29%)
  starting transfers between devices  40.9 us (22%)
  other arithmetic  3.9 us (2%)
    ppermute x9, waiting for transfers between devices, go_x(): return lax.ppermute(a, 'dp', dp_pairs(lambda x, h: (x + k, h)))  42 us
    pallas_call x1, Pallas kernels, run_main(): pl.pallas_call(main_kernel, out_shape=(jax.ShapeDtypeStruct(back, BF16),...  31.1 us
    all_to_all x1, waiting for transfers between devices, local(): lax.all_to_all(run_pack(video, cotangent), 'frame', 0, 0, tiled=True)  26.1 us
    ppermute x9, starting transfers between devices, go_x(): return lax.ppermute(a, 'dp', dp_pairs(lambda x, h: (x + k, h)))  14.1 us
    all_to_all x2, starting transfers between devices, trade_yz(): lax.all_to_all(a, 'frame', 0, 0, tiled=True, axis_index_groups=groups)  10.9 us
    ppermute x3, waiting for transfers between devices, go_h(): return lax.ppermute(a, 'dp', dp_pairs(lambda x, h: (x, h + k)))  9.93 us
    ppermute x3, starting transfers between devices, go_h(): return lax.ppermute(a, 'dp', dp_pairs(lambda x, h: (x, h + k)))  9.14 us
    all_to_all x1, starting transfers between devices, local(): lax.all_to_all(run_pack(video, cotangent), 'frame', 0, 0, tiled=True)  6.03 us
  transfers between devices with their start and end apart: 18, of which 14 were waited for; matrix products, arithmetic and copies ran while one was open for 2% of the time, Pallas kernels for 4%

profile of v12, /device:TPU:32, one launch (start us, length us, event | category | flops | bytes accessed | tf_op | source)
XLA Modules:
  0.0 181.0 jit_solution(11236786521963086958)
XLA Ops:
  0.6 2.9 %pack.1 = bf16[16,4,16,1024]{3,2,1,0:T(8,128)(2,1)} custom-call(bf16[2,16,16,1024]{3,2,1,0:T(8,128)(2,1)} %bitcast.24, bf16[2,16,16,1024]{3,2,1,0:T(8,128)(2,1)} %bitcast.25), custom_call_target="tpu_custom_call" | custom-call | tf_op jit(solution)/shard_map/pack/pallas_call | solution.py:385
  3.5 6.0 %all-to-all-start = ((bf16[16,4,16,1024]{3,2,1,0:T(8,128)(2,1)}), bf16[16,4,16,1024]{3,2,1,0:T(8,128)(2,1)}, u32[]{:S(2)}, u32[]{:S(2)}) async-start(bf16[16,4,16,1024]{3,2,1,0:T(8,128)(2,1)} %pack.1), calls=%async_computation | async-start | bytes 4194304 | tf_op jit(solution)/shard_map/all_to_all | solution.py:515
  9.6 0.7 pad_add_fusion.place_ref
  10.2 26.1 %all-to-all-done.tokens_hbm = bf16[16,4,16,1024]{3,2,1,0:T(8,128)(2,1)} async-done(((bf16[16,4,16,1024]{3,2,1,0:T(8,128)(2,1)}), bf16[16,4,16,1024]{3,2,1,0:T(8,128)(2,1)}, u32[]{:S(2)}, u32[]{:S(2)}) %all-to-all-start) | async-done | bytes 2097184 | tf_op jit(solution)/shard_map/all_to_all | solution.py:515
  36.3 31.1 %sublayer.1 = (bf16[8,32,1152]{2,1,0:T(8,128)(2,1)}, bf16[8,32,1152]{2,1,0:T(8,128)(2,1)}, bf16[8,64,1536]{2,1,0:T(8,128)(2,1)}, bf16[4,8,64,640]{3,2,1,0:T(8,12...) custom-call(s32[3]{0:T(128)} %pad_add_fusion.place_ref, bf16[16,4,16,1024]{3,2,1,0:T(8,128)(2,1)} %all-to-all-done.tokens_hbm, ...), custom_call_target="tpu_custom_call" | custom-call | flops 12884901888 | bytes 20971520 | tf_op jit(solution)/shard_map/sublayer/pallas_call | solution.py:246
  67.4 0.2 collective-permute-start
  67.6 0.4 collective-permute-start.1
  68.0 3.7 %collective-permute-done.1.theirs_ref = bf16[8,32,1152]{2,1,0:T(8,128)(2,1)S(1)} collective-permute-done((bf16[8,32,1152]{2,1,0:T(8,128)(2,1)}, bf16[8,32,1152]{2,1,0:T(8,128)(2,1)S(1)}, u32[]{:S(2)}, u32[]{:S(2)}) %collective-permute-start.1) | collective-permute-done | bytes 589856 | tf_op jit(solution)/shard_map/ppermute | solution.py:465
  71.7 0.4 collective-permute-done.got_ref
  72.1 0.1 collective-permute-start.2
  72.2 0.3 copy-done.2
  72.5 4.7 %message.1 = (f32[64,1536]{1,0:T(8,128)}, bf16[8,64,2688]{2,1,0:T(8,128)(2,1)}) custom-call(s32[3]{0:T(128)} %pad_add_fusion.place_ref, f32[8,64,1536]{2,1,0:T(8,128)} %get-tuple-element.46.keep_ref, bf16[8,64,1536]{2,1,0:T(8,128)(2,1)} %collective-permute-done.got_ref, bf16[8,32,1152]{2,1,0:T(8,128)(2,1)} %get-tuple-element.51.back_ref, ...), custom_call_target="tpu_custom_call" | custom-call | flops 1048576 | bytes 9437184 | tf_op jit(solution)/shard_map/message/pallas_call | solution.py:321
  77.2 0.1 collective-permute-done.2.got_ref
  77.3 4.6 %terms_b.1 = (f32[8,64,640]{2,1,0:T(8,128)}, bf16[8,64,640]{2,1,0:T(8,128)(2,1)}, bf16[8,64,640]{2,1,0:T(8,128)(2,1)}, bf16[8,64,640]{2,1,0:T(8,128)(2,1)}) custom-call(f32[4,8,64,640]{3,2,1,0:T(8,128)} %get-tuple-element.54.keep_ref, bf16[4,8,64,640]{3,2,1,0:T(8,128)(2,1)} %collective-permute-done.2.got_ref), custom_call_target="tpu_custom_call" | custom-call | flops 1048576 | bytes 11534336 | tf_op jit(solution)/shard_map/terms_b/pallas_call | solution.py:406
  82.0 5.8 %all-to-all-start.1 = ((bf16[8,64,2688]{2,1,0:T(8,128)(2,1)}), bf16[8,64,2688]{2,1,0:T(8,128)(2,1)}, u32[]{:S(2)}, u32[]{:S(2)}) async-start(bf16[8,64,2688]{2,1,0:T(8,128)(2,1)} %get-tuple-element.61), calls=%async_computation.1 | async-start | bytes 5505024 | tf_op jit(solution)/shard_map/all_to_all | solution.py:470
  87.8 1.3 collective-permute-start.3
  89.2 2.7 %collective-permute-start.4 = (bf16[8,64,640]{2,1,0:T(8,128)(2,1)S(1)}, bf16[8,64,640]{2,1,0:T(8,128)(2,1)}, u32[]{:S(2)}, u32[]{:S(2)}) collective-permute-start(bf16[8,64,640]{2,1,0:T(8,128)(2,1)S(1)} %copy-done.5), channel_id=1, source_target_pairs={{0,128},{16,144},{32,160},{48,176},{64,192},{80,208},{96,224},{112... | collective-permute-start | bytes 1966088 | tf_op jit(solution)/shard_map/ppermute | solution.py:474
  91.9 1.4 collective-permute-start.5
  93.3 12.5 %collective-permute-done.3.t1 = bf16[8,64,640]{2,1,0:T(8,128)(2,1)S(1)} collective-permute-done((bf16[8,64,640]{2,1,0:T(8,128)(2,1)S(1)}, bf16[8,64,640]{2,1,0:T(8,128)(2,1)S(1)}, u32[]{:S(2)}, u32[]{:S(2)}) %collective-permute-start.3) | collective-permute-done | bytes 655392 | tf_op jit(solution)/shard_map/ppermute | solution.py:474
  105.8 14.7 %collective-permute-done.4.t2 = bf16[8,64,640]{2,1,0:T(8,128)(2,1)} collective-permute-done((bf16[8,64,640]{2,1,0:T(8,128)(2,1)S(1)}, bf16[8,64,640]{2,1,0:T(8,128)(2,1)}, u32[]{:S(2)}, u32[]{:S(2)}) %collective-permute-start.4) | collective-permute-done | bytes 655392 | tf_op jit(solution)/shard_map/ppermute | solution.py:474
  120.5 0.0 collective-permute-done.5.t3
  120.5 0.8 all-to-all-done.1.message_ref
  121.4 3.5 %sum_b.1 = (f32[64,640]{1,0:T(8,128)}, bf16[8,64,640]{2,1,0:T(8,128)(2,1)}) custom-call(s32[3]{0:T(128)} %pad_add_fusion.place_ref, f32[8,64,640]{2,1,0:T(8,128)} %get-tuple-element.60.keep_ref, bf16[8,64,640]{2,1,0:T(8,128)(2,1)} %copy-done.1, bf16[8,64,640]{2,1,0:T(8,128)(2,1)} %collective-permute-done.4.t2, bf16[8,64,640]{2,1,0:T(8,128)(2,1)} %collective-permute-done.5.t3), custom_call_target="tpu_custom_call" | custom-call | flops 1048576 | bytes 9437184 | tf_op jit(solution)/shard_map/sum_b/pallas_call | solution.py:337
  124.8 5.0 %all-to-all-start.2 = ((bf16[8,64,640]{2,1,0:T(8,128)(2,1)}), bf16[8,64,640]{2,1,0:T(8,128)(2,1)S(1)}, u32[]{:S(2)}, u32[]{:S(2)}) async-start(bf16[8,64,640]{2,1,0:T(8,128)(2,1)} %get-tuple-element.71), calls=%async_computation.2 | async-start | bytes 1310720 | tf_op jit(solution)/shard_map/all_to_all | solution.py:470
  129.9 1.9 %select_reduce_fusion = f32[64,1536]{1,0:T(8,128)S(1)} fusion(bf16[8,64,2688]{2,1,0:T(8,128)(2,1)} %all-to-all-done.1.message_ref, f32[64,1536]{1,0:T(8,128)} %get-tuple-element.70, pred[8]{0:T(512)(128)(4,1)S(1)} %iota_compare_fusion.1), kind=kLoop, calls=%fused_computation | loop fusion | flops 2260992 | bytes 2359304 | tf_op jit(solution)/shard_map/reduce_sum | solution.py:497
  131.8 2.5 %collective-permute-start.8 = (bf16[64,384]{1,0:T(8,128)(2,1)S(1)}, bf16[64,384]{1,0:T(8,128)(2,1)S(1)}, u32[]{:S(2)}, u32[]{:S(2)}) collective-permute-start(bf16[64,384]{1,0:T(8,128)(2,1)S(1)} %get-tuple-element.92), channel_id=1, source_target_pairs={{0,192},{16,208},{32,224},{48,240},{64,0},{80,16},{96,32},{112,48}... | collective-permute-start | bytes 147464 | tf_op jit(solution)/shard_map/ppermute | solution.py:474
  134.4 1.1 collective-permute-start.7
  135.5 0.5 collective-permute-start.6
  136.0 1.0 convert_reduce_fusion
  137.0 0.0 collective-permute-done.8
  137.0 2.9 %collective-permute-done.7 = bf16[64,384]{1,0:T(8,128)(2,1)S(1)} collective-permute-done((bf16[64,384]{1,0:T(8,128)(2,1)S(1)}, bf16[64,384]{1,0:T(8,128)(2,1)S(1)}, u32[]{:S(2)}, u32[]{:S(2)}) %collective-permute-start.7) | collective-permute-done | bytes 49184 | tf_op jit(solution)/shard_map/ppermute | solution.py:474
  139.9 0.8 collective-permute-done.6
  140.8 0.0 all-to-all-done.2
  140.8 0.2 select_reduce_fusion.1
  141.1 5.3 %collective-permute-start.11 = (bf16[64,1152]{1,0:T(8,128)(2,1)S(1)}, bf16[64,1152]{1,0:T(8,128)(2,1)S(1)}, u32[]{:S(2)}, u32[]{:S(2)}) collective-permute-start(bf16[64,1152]{1,0:T(8,128)(2,1)S(1)} %fusion), channel_id=1, source_target_pairs={{0,48},{16,0},{32,16},{48,32},{64,112},{80,64},{96,80},{112,96},{1... | collective-permute-start | bytes 442376 | tf_op jit(solution)/shard_map/ppermute | solution.py:478
  146.4 1.4 collective-permute-start.10
  147.8 2.4 %collective-permute-start.9 = (bf16[64,1152]{1,0:T(8,128)(2,1)S(1)}, bf16[64,1152]{1,0:T(8,128)(2,1)S(1)}, u32[]{:S(2)}, u32[]{:S(2)}) collective-permute-start(bf16[64,1152]{1,0:T(8,128)(2,1)S(1)} %fusion), channel_id=1, source_target_pairs={{0,16},{16,32},{32,48},{48,0},{64,80},{80,96},{96,112},{112,64},{1... | collective-permute-start | bytes 442376 | tf_op jit(solution)/shard_map/ppermute | solution.py:478
  150.2 3.4 %collective-permute-done.11 = bf16[64,1152]{1,0:T(8,128)(2,1)S(1)} collective-permute-done((bf16[64,1152]{1,0:T(8,128)(2,1)S(1)}, bf16[64,1152]{1,0:T(8,128)(2,1)S(1)}, u32[]{:S(2)}, u32[]{:S(2)}) %collective-permute-start.11) | collective-permute-done | bytes 147488 | tf_op jit(solution)/shard_map/ppermute | solution.py:478
  153.6 5.6 %collective-permute-done.10 = bf16[64,1152]{1,0:T(8,128)(2,1)S(1)} collective-permute-done((bf16[64,1152]{1,0:T(8,128)(2,1)S(1)}, bf16[64,1152]{1,0:T(8,128)(2,1)S(1)}, u32[]{:S(2)}, u32[]{:S(2)}) %collective-permute-start.10) | collective-permute-done | bytes 147488 | tf_op jit(solution)/shard_map/ppermute | solution.py:478
  159.2 0.9 collective-permute-done.9
  160.1 0.1 convert_add_fusion.d0
  160.2 3.1 %collective-permute-start.14 = (f32[64,1152]{1,0:T(8,128)S(1)}, f32[64,1152]{1,0:T(8,128)S(1)}, u32[]{:S(2)}, u32[]{:S(2)}) collective-permute-start(f32[64,1152]{1,0:T(8,128)S(1)} %convert_add_fusion.d0), channel_id=1, source_target_pairs={{0,192},{16,208},{32,224},{48,240},{64,0},{80,16},{96,32},{112,48}... | collective-permute-start | bytes 884744 | tf_op jit(solution)/shard_map/ppermute | solution.py:474
  163.3 0.3 collective-permute-start.13
  163.6 1.1 collective-permute-start.12
  164.7 3.3 %unpack.1 = bf16[2,256,1024]{2,1,0:T(8,128)(2,1)} custom-call(s32[3]{0:T(128)} %pad_add_fusion.place_ref, bf16[8,64,2688]{2,1,0:T(8,128)(2,1)} %all-to-all-done.1.message_ref), custom_call_target="tpu_custom_call" | custom-call | tf_op jit(solution)/shard_map/unpack/pallas_call | solution.py:351
  167.9 7.5 %collective-permute-done.14.d3 = f32[64,1152]{1,0:T(8,128)S(1)} collective-permute-done((f32[64,1152]{1,0:T(8,128)S(1)}, f32[64,1152]{1,0:T(8,128)S(1)}, u32[]{:S(2)}, u32[]{:S(2)}) %collective-permute-start.14) | collective-permute-done | bytes 294944 | tf_op jit(solution)/shard_map/ppermute | solution.py:474
  175.5 3.5 %collective-permute-done.12.d1 = f32[64,1152]{1,0:T(8,128)} collective-permute-done((f32[64,1152]{1,0:T(8,128)S(1)}, f32[64,1152]{1,0:T(8,128)}, u32[]{:S(2)}, u32[]{:S(2)}) %collective-permute-start.12) | collective-permute-done | bytes 294944 | tf_op jit(solution)/shard_map/ppermute | solution.py:474
  179.0 2.0 %place_grads.1 = (f32[64,3072]{1,0:T(8,128)}, f32[64,1024]{1,0:T(8,128)}, f32[1,64]{1,0:T(1,128)}, f32[1,64]{1,0:T(1,128)}) custom-call(s32[3]{0:T(128)S(1)} %copy-done, f32[64,1152]{1,0:T(8,128)S(1)} %convert_add_fusion.d0, f32[64,1152]{1,0:T(8,128)} %collective-permute-done.12.d1, f32[64,1152]{1,0:T(8,128)S(1)} %collective-permute-done.13.d2, ...), custom_call_target="tpu_custom_call" | custom-call | tf_op jit(solution)/shard_map/place_grads/pallas_call | solution.py:433
  (21 shorter events, 0.1 us)
Async XLA Ops:
  3.5 32.8 %all-to-all-start = ((bf16[16,4,16,1024]{3,2,1,0:T(8,128)(2,1)}), bf16[16,4,16,1024]{3,2,1,0:T(8,128)(2,1)}, u32[]{:S(2)}, u32[]{:S(2)}) async-start(bf16[16,4,16,1024]{3,2,1,0:T(8,128)(2,1)} %pack.1), calls=%async_computation | async-start | bytes 4194304 | tf_op jit(solution)/shard_map/all_to_all | solution.py:515
  67.4 4.7 %collective-permute-start = (bf16[8,64,1536]{2,1,0:T(8,128)(2,1)}, bf16[8,64,1536]{2,1,0:T(8,128)(2,1)}, u32[]{:S(2)}, u32[]{:S(2)}) collective-permute-start(bf16[8,64,1536]{2,1,0:T(8,128)(2,1)} %get-tuple-element.47), channel_id=1, source_target_pairs={{0,1},{1,0},{2,3},{3,2},{4,5},{5,4},{6,7},{7,6},{8,9},{9,8},{10,11... | collective-permute-start | bytes 4718600 | tf_op jit(solution)/shard_map/ppermute | solution.py:465
  67.6 4.1 %collective-permute-start.1 = (bf16[8,32,1152]{2,1,0:T(8,128)(2,1)}, bf16[8,32,1152]{2,1,0:T(8,128)(2,1)S(1)}, u32[]{:S(2)}, u32[]{:S(2)}) collective-permute-start(bf16[8,32,1152]{2,1,0:T(8,128)(2,1)} %get-tuple-element.48), channel_id=1, source_target_pairs={{0,1},{1,0},{2,3},{3,2},{4,5},{5,4},{6,7},{7,6},{8,9},{9,8},{10,11... | collective-permute-start | bytes 1769480 | tf_op jit(solution)/shard_map/ppermute | solution.py:465
  71.7 0.8 copy-start.2
  72.1 5.3 %collective-permute-start.2 = (bf16[4,8,64,640]{3,2,1,0:T(8,128)(2,1)}, bf16[4,8,64,640]{3,2,1,0:T(8,128)(2,1)}, u32[]{:S(2)}, u32[]{:S(2)}) collective-permute-start(bf16[4,8,64,640]{3,2,1,0:T(8,128)(2,1)} %get-tuple-element.55), channel_id=1, source_target_pairs={{0,1},{1,0},{2,3},{3,2},{4,5},{5,4},{6,7},{7,6},{8,9},{9,8},{10,11... | collective-permute-start | bytes 7864328 | tf_op jit(solution)/shard_map/ppermute | solution.py:465
  82.0 5.8 %copy-start.6 = (bf16[8,64,640]{2,1,0:T(8,128)(2,1)S(1)}, bf16[8,64,640]{2,1,0:T(8,128)(2,1)}, u32[]{:S(2)}) copy-start(bf16[8,64,640]{2,1,0:T(8,128)(2,1)} %get-tuple-element.62) | copy-start | bytes 1966084
  82.0 7.2 %copy-start.5 = (bf16[8,64,640]{2,1,0:T(8,128)(2,1)S(1)}, bf16[8,64,640]{2,1,0:T(8,128)(2,1)}, u32[]{:S(2)}) copy-start(bf16[8,64,640]{2,1,0:T(8,128)(2,1)} %get-tuple-element.63) | copy-start | bytes 1966084
  82.0 9.9 %copy-start.4 = (bf16[8,64,640]{2,1,0:T(8,128)(2,1)S(1)}, bf16[8,64,640]{2,1,0:T(8,128)(2,1)}, u32[]{:S(2)}) copy-start(bf16[8,64,640]{2,1,0:T(8,128)(2,1)} %get-tuple-element.64) | copy-start | bytes 1966084
  82.0 39.4 %all-to-all-start.1 = ((bf16[8,64,2688]{2,1,0:T(8,128)(2,1)}), bf16[8,64,2688]{2,1,0:T(8,128)(2,1)}, u32[]{:S(2)}, u32[]{:S(2)}) async-start(bf16[8,64,2688]{2,1,0:T(8,128)(2,1)} %get-tuple-element.61), calls=%async_computation.1 | async-start | bytes 5505024 | tf_op jit(solution)/shard_map/all_to_all | solution.py:470
  87.8 18.0 %collective-permute-start.3 = (bf16[8,64,640]{2,1,0:T(8,128)(2,1)S(1)}, bf16[8,64,640]{2,1,0:T(8,128)(2,1)S(1)}, u32[]{:S(2)}, u32[]{:S(2)}) collective-permute-start(bf16[8,64,640]{2,1,0:T(8,128)(2,1)S(1)} %copy-done.6), channel_id=1, source_target_pairs={{0,64},{16,80},{32,96},{48,112},{64,128},{80,144},{96,160},{112,17... | collective-permute-start | bytes 1966088 | tf_op jit(solution)/shard_map/ppermute | solution.py:474
  89.2 31.4 %collective-permute-start.4 = (bf16[8,64,640]{2,1,0:T(8,128)(2,1)S(1)}, bf16[8,64,640]{2,1,0:T(8,128)(2,1)}, u32[]{:S(2)}, u32[]{:S(2)}) collective-permute-start(bf16[8,64,640]{2,1,0:T(8,128)(2,1)S(1)} %copy-done.5), channel_id=1, source_target_pairs={{0,128},{16,144},{32,160},{48,176},{64,192},{80,208},{96,224},{112... | collective-permute-start | bytes 1966088 | tf_op jit(solution)/shard_map/ppermute | solution.py:474
  91.9 28.7 %collective-permute-start.5 = (bf16[8,64,640]{2,1,0:T(8,128)(2,1)S(1)}, bf16[8,64,640]{2,1,0:T(8,128)(2,1)}, u32[]{:S(2)}, u32[]{:S(2)}) collective-permute-start(bf16[8,64,640]{2,1,0:T(8,128)(2,1)S(1)} %copy-done.4), channel_id=1, source_target_pairs={{0,192},{16,208},{32,224},{48,240},{64,0},{80,16},{96,32},{112,48}... | collective-permute-start | bytes 1966088 | tf_op jit(solution)/shard_map/ppermute | solution.py:474
  105.8 15.5 %copy-start.1 = (bf16[8,64,640]{2,1,0:T(8,128)(2,1)}, bf16[8,64,640]{2,1,0:T(8,128)(2,1)S(1)}, u32[]{:S(2)}) copy-start(bf16[8,64,640]{2,1,0:T(8,128)(2,1)S(1)} %collective-permute-done.3.t1) | copy-start | bytes 1966084
  124.8 16.0 %copy-start.3 = (f32[64,640]{1,0:T(8,128)S(1)}, f32[64,640]{1,0:T(8,128)}, u32[]{:S(2)}) copy-start(f32[64,640]{1,0:T(8,128)} %get-tuple-element.68) | copy-start | bytes 491524
  124.8 16.0 %all-to-all-start.2 = ((bf16[8,64,640]{2,1,0:T(8,128)(2,1)}), bf16[8,64,640]{2,1,0:T(8,128)(2,1)S(1)}, u32[]{:S(2)}, u32[]{:S(2)}) async-start(bf16[8,64,640]{2,1,0:T(8,128)(2,1)} %get-tuple-element.71), calls=%async_computation.2 | async-start | bytes 1310720 | tf_op jit(solution)/shard_map/all_to_all | solution.py:470
  131.8 5.2 %collective-permute-start.8 = (bf16[64,384]{1,0:T(8,128)(2,1)S(1)}, bf16[64,384]{1,0:T(8,128)(2,1)S(1)}, u32[]{:S(2)}, u32[]{:S(2)}) collective-permute-start(bf16[64,384]{1,0:T(8,128)(2,1)S(1)} %get-tuple-element.92), channel_id=1, source_target_pairs={{0,192},{16,208},{32,224},{48,240},{64,0},{80,16},{96,32},{112,48}... | collective-permute-start | bytes 147464 | tf_op jit(solution)/shard_map/ppermute | solution.py:474
  134.4 5.6 %collective-permute-start.7 = (bf16[64,384]{1,0:T(8,128)(2,1)S(1)}, bf16[64,384]{1,0:T(8,128)(2,1)S(1)}, u32[]{:S(2)}, u32[]{:S(2)}) collective-permute-start(bf16[64,384]{1,0:T(8,128)(2,1)S(1)} %get-tuple-element.93), channel_id=1, source_target_pairs={{0,128},{16,144},{32,160},{48,176},{64,192},{80,208},{96,224},{112... | collective-permute-start | bytes 147464 | tf_op jit(solution)/shard_map/ppermute | solution.py:474
  135.5 5.3 %collective-permute-start.6 = (bf16[64,384]{1,0:T(8,128)(2,1)S(1)}, bf16[64,384]{1,0:T(8,128)(2,1)S(1)}, u32[]{:S(2)}, u32[]{:S(2)}) collective-permute-start(bf16[64,384]{1,0:T(8,128)(2,1)S(1)} %get-tuple-element.94), channel_id=1, source_target_pairs={{0,64},{16,80},{32,96},{48,112},{64,128},{80,144},{96,160},{112,17... | collective-permute-start | bytes 147464 | tf_op jit(solution)/shard_map/ppermute | solution.py:474
  141.0 37.9 %copy-start = (s32[3]{0:T(128)S(1)}, s32[3]{0:T(128)}, u32[]{:S(2)}) copy-start(s32[3]{0:T(128)} %pad_add_fusion.place_ref) | copy-start | bytes 40
  141.1 12.5 %collective-permute-start.11 = (bf16[64,1152]{1,0:T(8,128)(2,1)S(1)}, bf16[64,1152]{1,0:T(8,128)(2,1)S(1)}, u32[]{:S(2)}, u32[]{:S(2)}) collective-permute-start(bf16[64,1152]{1,0:T(8,128)(2,1)S(1)} %fusion), channel_id=1, source_target_pairs={{0,48},{16,0},{32,16},{48,32},{64,112},{80,64},{96,80},{112,96},{1... | collective-permute-start | bytes 442376 | tf_op jit(solution)/shard_map/ppermute | solution.py:478
  146.4 12.8 %collective-permute-start.10 = (bf16[64,1152]{1,0:T(8,128)(2,1)S(1)}, bf16[64,1152]{1,0:T(8,128)(2,1)S(1)}, u32[]{:S(2)}, u32[]{:S(2)}) collective-permute-start(bf16[64,1152]{1,0:T(8,128)(2,1)S(1)} %fusion), channel_id=1, source_target_pairs={{0,32},{16,48},{32,0},{48,16},{64,96},{80,112},{96,64},{112,80},{1... | collective-permute-start | bytes 442376 | tf_op jit(solution)/shard_map/ppermute | solution.py:478
  147.8 12.3 %collective-permute-start.9 = (bf16[64,1152]{1,0:T(8,128)(2,1)S(1)}, bf16[64,1152]{1,0:T(8,128)(2,1)S(1)}, u32[]{:S(2)}, u32[]{:S(2)}) collective-permute-start(bf16[64,1152]{1,0:T(8,128)(2,1)S(1)} %fusion), channel_id=1, source_target_pairs={{0,16},{16,32},{32,48},{48,0},{64,80},{80,96},{96,112},{112,64},{1... | collective-permute-start | bytes 442376 | tf_op jit(solution)/shard_map/ppermute | solution.py:478
  160.2 15.3 %collective-permute-start.14 = (f32[64,1152]{1,0:T(8,128)S(1)}, f32[64,1152]{1,0:T(8,128)S(1)}, u32[]{:S(2)}, u32[]{:S(2)}) collective-permute-start(f32[64,1152]{1,0:T(8,128)S(1)} %convert_add_fusion.d0), channel_id=1, source_target_pairs={{0,192},{16,208},{32,224},{48,240},{64,0},{80,16},{96,32},{112,48}... | collective-permute-start | bytes 884744 | tf_op jit(solution)/shard_map/ppermute | solution.py:474
  163.3 12.2 %collective-permute-start.13 = (f32[64,1152]{1,0:T(8,128)S(1)}, f32[64,1152]{1,0:T(8,128)S(1)}, u32[]{:S(2)}, u32[]{:S(2)}) collective-permute-start(f32[64,1152]{1,0:T(8,128)S(1)} %convert_add_fusion.d0), channel_id=1, source_target_pairs={{0,128},{16,144},{32,160},{48,176},{64,192},{80,208},{96,224},{112... | collective-permute-start | bytes 884744 | tf_op jit(solution)/shard_map/ppermute | solution.py:474
  163.6 15.4 %collective-permute-start.12 = (f32[64,1152]{1,0:T(8,128)S(1)}, f32[64,1152]{1,0:T(8,128)}, u32[]{:S(2)}, u32[]{:S(2)}) collective-permute-start(f32[64,1152]{1,0:T(8,128)S(1)} %convert_add_fusion.d0), channel_id=1, source_target_pairs={{0,64},{16,80},{32,96},{48,112},{64,128},{80,144},{96,160},{112,17... | collective-permute-start | bytes 884744 | tf_op jit(solution)/shard_map/ppermute | solution.py:474
